TPU v7x, 32 devices: a whole 2x2x4 slice. The times are simulated.
32 devices in a mesh: head: 4 (over x, core), blk: 8 (over z, y).
Axes of the slice: x: 2, y: 2, z: 4, core: 2. Of those that a mesh axis runs over, the one named last changes fastest.
Arguments:
- tokens: bfloat16 [8192, 2048], P(('blk', 'head')), may hold values from -6 to 6
- doc_lengths: int32 [4], replicated, may hold values from 1 to 4096, 8192 in all
- norm1_gain: bfloat16 [2048], P(('head', 'blk')), may hold values from 0.25 to 1.75
- w_query: bfloat16 [2048, 1536], P(('head', 'blk')), may hold values from -0.125 to 0.125
- w_key: bfloat16 [2048, 384], P(('head', 'blk')), may hold values from -0.125 to 0.125
- w_value: bfloat16 [2048, 384], P(('head', 'blk')), may hold values from -0.125 to 0.125
- query_gain: bfloat16 [64], replicated, may hold values from 0.25 to 1.75
- key_gain: bfloat16 [64], replicated, may hold values from 0.25 to 1.75
- w_out: bfloat16 [1536, 2048], P(('head', 'blk')), may hold values from -1.25 to 1.25
- norm2_gain: bfloat16 [2048], P(('head', 'blk')), may hold values from 0.25 to 1.75
- w_gate: bfloat16 [2048, 5120], P(('head', 'blk')), may hold values from -0.125 to 0.125
- w_up: bfloat16 [2048, 5120], P(('head', 'blk')), may hold values from -0.125 to 0.125
- w_down: bfloat16 [5120, 2048], P(('head', 'blk')), may hold values from -0.078125 to 0.078125
- cotangent: bfloat16 [8192, 2048], P(('blk', 'head')), may hold values from -6 to 6
Outputs:
- out_act: bfloat16 [8192, 2048], P(('blk', 'head'))
- d_tokens: float32 [8192, 2048], P(('blk', 'head'))
- d_norm1_gain: float32 [2048], P(('head', 'blk'))
- d_w_query: float32 [2048, 1536], P(('head', 'blk'))
- d_w_key: float32 [2048, 384], P(('head', 'blk'))
- d_w_value: float32 [2048, 384], P(('head', 'blk'))
- d_query_gain: float32 [64], replicated
- d_key_gain: float32 [64], replicated
- d_w_out: float32 [1536, 2048], P(('head', 'blk'))
- d_norm2_gain: float32 [2048], P(('head', 'blk'))
- d_w_gate: float32 [2048, 5120], P(('head', 'blk'))
- d_w_up: float32 [2048, 5120], P(('head', 'blk'))
- d_w_down: float32 [5120, 2048], P(('head', 'blk'))
Inputs may be any that keep to these rules, and one draw needn't show every extreme that they name: `doc_lengths`: the documents lie end to end in order from token 0; their lengths sum to 8192 and one is exactly 4096 long.
All inputs are finite; a program needn't handle non-finite values.
Results may differ from a plain program's by a relative error of at most 0.018.
Values may be sent and summed in bfloat16 or wider, within the bound.
A program may use at most 320 MiB of HBM per device.

v0:
```python
from functools import reduce
import math

import jax
import jax.numpy as jnp
import numpy as np
from jax import lax
from jax.sharding import PartitionSpec as P

QHEADS = 24
KVHEADS = 6
HEAD = 64
MAXDOC = 4096


EPS = 1e-06
SCALE = 0.125
NEG = -1e30
HIGHEST = lax.Precision.HIGHEST


def shifted(block, axis, distance):
    devices = range(lax.axis_size(axis))
    route = [(i - distance, i) for i in devices if i - distance in devices]
    return lax.ppermute(block, axis, route)


def passed_along(block, axis, distance):
    devices = range(lax.axis_size(axis))
    route = [((i - distance) % len(devices), i) for i in devices]
    return lax.ppermute(block, axis, route)


def norm_rows(tensor, gain_vec):
    return tensor * lax.rsqrt(jnp.mean(tensor * tensor, axis=-1, keepdims=True) + EPS) * gain_vec


def rotate(tensor, cosine, sine_table):
    half_width = tensor.shape[-1] // 2
    first_half = tensor[..., :half_width]
    second = tensor[..., half_width:]
    return jnp.concatenate(
        [first_half * cosine - second * sine_table, second * cosine + first_half * sine_table],
        axis=-1,
    )


def prepare(query_raw, key_raw, query_g, key_g, cosine, sine_table):
    tok_rows = query_raw.shape[0]
    query_rot = rotate(
        norm_rows(query_raw.reshape(tok_rows, QHEADS, HEAD), query_g), cosine, sine_table
    )
    key_rot = rotate(norm_rows(key_raw.reshape(tok_rows, KVHEADS, HEAD), key_g), cosine, sine_table)
    return (query_rot, key_rot)


def swiglu(gate_val, up_val):
    return jax.nn.silu(gate_val) * up_val


def doc_number(position, starts):
    return jnp.sum((starts <= position[..., None]).astype(jnp.int32), axis=-1) - 1


def matmul(left_side, right_side):
    return jnp.dot(left_side, right_side, preferred_element_type=jnp.float32)


def shards(
    tokens,
    doc_lengths,
    norm1_gain,
    w_query,
    w_key,
    w_value,
    query_gain,
    key_gain,
    w_out,
    norm2_gain,
    w_gate,
    w_up,
    w_down,
    cotangent,
):
    tok_rows = tokens.shape[0]
    blocks = lax.axis_size("blk")
    groups = lax.axis_size("head")
    group_id = lax.axis_index("head")
    blk_place = lax.axis_index("blk")
    block_len = groups * tok_rows
    reach_steps = (MAXDOC - 2) // block_len + 1
    per_group = QHEADS // groups
    head_ratio = QHEADS // KVHEADS
    starts = jnp.cumsum(doc_lengths) - doc_lengths
    gathered = (
        lax.all_gather(norm1_gain, ("head", "blk"), axis=0, tiled=True),
        lax.all_gather(w_query, ("head", "blk"), axis=0, tiled=True),
        lax.all_gather(w_key, ("head", "blk"), axis=0, tiled=True),
        lax.all_gather(w_value, ("head", "blk"), axis=0, tiled=True),
        lax.all_gather(w_out, ("head", "blk"), axis=0, tiled=True),
        lax.all_gather(norm2_gain, ("head", "blk"), axis=0, tiled=True),
        lax.all_gather(w_gate, ("head", "blk"), axis=0, tiled=True),
        lax.all_gather(w_up, ("head", "blk"), axis=0, tiled=True),
        lax.all_gather(w_down, ("head", "blk"), axis=0, tiled=True),
    )
    offsets = jnp.arange(tok_rows, dtype=jnp.int32)
    token_pos = blk_place * block_len + group_id * tok_rows + offsets
    inside = starts[None, :] <= token_pos[:, None]
    in_doc = token_pos - jnp.max(jnp.where(inside, starts[None, :], 0), axis=1)
    rope_freq = jnp.exp(-math.log(10000.0) * jnp.arange(HEAD // 2, dtype=jnp.float32) / (HEAD // 2))
    rope_angle = in_doc.astype(jnp.float32)[:, None] * rope_freq[None, :]
    cosine = jnp.cos(rope_angle)[:, None, :]
    sine_table = jnp.sin(rope_angle)[:, None, :]
    inputs = tokens.astype(jnp.float32)
    gain_one = gathered[0].astype(jnp.float32)
    query_g = query_gain.astype(jnp.float32)
    key_g = key_gain.astype(jnp.float32)
    normed_one = norm_rows(inputs, gain_one).astype(jnp.bfloat16)
    query_raw = matmul(normed_one, gathered[1])
    key_raw = matmul(normed_one, gathered[2])
    value_raw = matmul(normed_one, gathered[3])
    query_rot, key_rot = prepare(query_raw, key_raw, query_g, key_g, cosine, sine_table)
    firsts = np.arange(groups) * per_group // head_ratio
    copy_index = np.stack([firsts, firsts + 1], axis=1)
    key_copies = key_rot.astype(jnp.bfloat16)[:, copy_index]
    value_copies = value_raw.astype(jnp.bfloat16).reshape(tok_rows, KVHEADS, HEAD)[:, copy_index]
    pairs_out = jnp.concatenate([key_copies, value_copies], axis=-1).reshape(
        tok_rows, groups, 4 * HEAD
    )
    query_out = query_rot.astype(jnp.bfloat16).reshape(tok_rows, groups, per_group * HEAD)
    query_in, pairs_in = (
        lax.all_to_all(query_out, "head", split_axis=1, concat_axis=1, tiled=True),
        lax.all_to_all(pairs_out, "head", split_axis=1, concat_axis=1, tiled=True),
    )
    queries = query_in.reshape(block_len, per_group, HEAD)
    kv_own = pairs_in.reshape(block_len, 2, 2 * HEAD)
    first_kv = group_id * per_group // head_ratio
    head_kv = (
        group_id * per_group + jnp.arange(per_group, dtype=jnp.int32)
    ) // head_ratio - first_kv
    select = (head_kv[:, None] == jnp.arange(2, dtype=jnp.int32)[None, :]).astype(jnp.float32)
    seg_pos = (jnp.arange(groups, dtype=jnp.int32)[None, :] * tok_rows + offsets[:, None]).reshape(
        block_len
    )
    query_pos = blk_place * block_len + seg_pos
    query_doc = doc_number(query_pos, starts)

    def block_terms(kv_block, distance):
        source = (blk_place - distance) % blocks
        key_pos = source * block_len + seg_pos
        key_doc = doc_number(key_pos, starts)
        allowed = (query_doc[:, None] == key_doc[None, :]) & (
            key_pos[None, :] <= query_pos[:, None]
        )
        spread = jnp.take(kv_block, head_kv, axis=1)
        key_part = spread[..., :HEAD]
        value_part = spread[..., HEAD:]
        scores = (
            jnp.einsum("qhd,khd->hqk", queries, key_part, preferred_element_type=jnp.float32)
            * SCALE
        )
        return (allowed[None], jnp.where(allowed[None], scores, NEG), key_part, value_part)

    def forward_step(state_in, kv_block, distance):
        run_max, run_sum, out_acc = state_in
        allowed, scores, key_part, value_part = block_terms(kv_block, distance)
        new_max = jnp.maximum(run_max, jnp.max(scores, axis=-1))
        weights = jnp.where(allowed, jnp.exp(scores - new_max[..., None]), 0.0)
        rescale = jnp.exp(run_max - new_max)
        new_sum = run_sum * rescale + jnp.sum(weights, axis=-1)
        new_acc = out_acc * rescale[..., None] + jnp.einsum(
            "hqk,khd->hqd",
            weights.astype(jnp.bfloat16),
            value_part,
            preferred_element_type=jnp.float32,
        )
        return (new_max, new_sum, new_acc)

    empty_state = (
        jnp.full((per_group, block_len), NEG, jnp.float32),
        jnp.zeros((per_group, block_len), jnp.float32),
        jnp.zeros((per_group, block_len, HEAD), jnp.float32),
    )
    first_state = forward_step(empty_state, kv_own, jnp.int32(0))

    def forward_turn(distance, loop_state):
        kv_block, state_in = loop_state
        kv_block = shifted(kv_block, "blk", 1)
        return (kv_block, forward_step(state_in, kv_block, distance))

    kv_spent, final_state = lax.fori_loop(1, reach_steps + 1, forward_turn, (kv_own, first_state))
    run_max, run_sum, out_acc = final_state
    log_total = run_max + jnp.log(run_sum)
    attn_keep = jnp.transpose(out_acc / run_sum[..., None], (1, 0, 2))
    attn_out = attn_keep.astype(jnp.bfloat16).reshape(tok_rows, groups, per_group * HEAD)
    mixed = lax.all_to_all(attn_out, "head", split_axis=1, concat_axis=1, tiled=True).reshape(
        tok_rows, QHEADS * HEAD
    )
    resid = inputs + matmul(mixed, gathered[4])
    gain_two = gathered[5].astype(jnp.float32)
    normed_two = norm_rows(resid, gain_two).astype(jnp.bfloat16)
    gate_val = matmul(normed_two, gathered[6])
    up_val = matmul(normed_two, gathered[7])
    hidden = swiglu(gate_val, up_val).astype(jnp.bfloat16)
    out_act = (resid + matmul(hidden, gathered[8])).astype(jnp.bfloat16)
    grad_top = cotangent.astype(jnp.float32)
    grad_w_down = matmul(hidden.T, cotangent)
    grad_hidden = matmul(cotangent, gathered[8].T)
    swiglu_out, swiglu_pull = jax.vjp(swiglu, gate_val, up_val)
    grad_gate, grad_up = swiglu_pull(grad_hidden)
    grad_gate = grad_gate.astype(jnp.bfloat16)
    grad_up = grad_up.astype(jnp.bfloat16)
    grad_w_gate = matmul(normed_two.T, grad_gate)
    grad_w_up = matmul(normed_two.T, grad_up)
    grad_normed = matmul(grad_gate, gathered[6].T) + matmul(grad_up, gathered[7].T)
    norm_two_out, norm_two_pull = jax.vjp(norm_rows, resid, gain_two)
    grad_resid_part, grad_gain_two = norm_two_pull(grad_normed)
    grad_resid = grad_top + grad_resid_part
    ffn_parts = (
        lax.psum_scatter(grad_gain_two, ("head", "blk"), scatter_dimension=0, tiled=True),
        lax.psum_scatter(grad_w_gate, ("head", "blk"), scatter_dimension=0, tiled=True),
        lax.psum_scatter(grad_w_up, ("head", "blk"), scatter_dimension=0, tiled=True),
        lax.psum_scatter(grad_w_down, ("head", "blk"), scatter_dimension=0, tiled=True),
    )
    grad_attn = grad_resid.astype(jnp.bfloat16)
    grad_w_out = matmul(mixed.T, grad_attn)
    grad_mixed = (
        matmul(grad_attn, gathered[4].T)
        .astype(jnp.bfloat16)
        .reshape(tok_rows, groups, per_group * HEAD)
    )
    grad_mix = lax.all_to_all(grad_mixed, "head", split_axis=1, concat_axis=1, tiled=True).reshape(
        block_len, per_group, HEAD
    )
    row_dots = jnp.sum(grad_mix.astype(jnp.float32) * attn_keep, axis=-1).T

    def backward_step(kv_block, kv_grad, query_grad, distance):
        allowed, scores, key_part, value_part = block_terms(kv_block, distance)
        probs = jnp.where(allowed, jnp.exp(scores - log_total[..., None]), 0.0)
        grad_prob = jnp.einsum(
            "qhd,khd->hqk", grad_mix, value_part, preferred_element_type=jnp.float32
        )
        grad_score = (probs * (grad_prob - row_dots[..., None])).astype(jnp.bfloat16)
        query_grad = (
            query_grad
            + jnp.einsum("hqk,khd->qhd", grad_score, key_part, preferred_element_type=jnp.float32)
            * SCALE
        )
        key_terms = (
            jnp.einsum("hqk,qhd->khd", grad_score, queries, preferred_element_type=jnp.float32)
            * SCALE
        )
        value_terms = jnp.einsum(
            "hqk,qhd->khd", probs.astype(jnp.bfloat16), grad_mix, preferred_element_type=jnp.float32
        )
        both_terms = jnp.concatenate([key_terms, value_terms], axis=-1)
        kv_grad = kv_grad + jnp.einsum("khe,hj->kje", both_terms, select, precision=HIGHEST)
        return (kv_grad, query_grad)

    start_grad, start_query = backward_step(
        kv_own,
        jnp.zeros((block_len, 2, 2 * HEAD), jnp.float32),
        jnp.zeros((block_len, per_group, HEAD), jnp.float32),
        jnp.int32(0),
    )

    def backward_turn(distance, loop_state):
        kv_block, kv_grad, query_grad = loop_state
        kv_block = shifted(kv_block, "blk", 1)
        kv_grad = passed_along(kv_grad.astype(jnp.bfloat16), "blk", 1).astype(kv_grad.dtype)
        kv_grad, query_grad = backward_step(kv_block, kv_grad, query_grad, distance)
        return (kv_block, kv_grad, query_grad)

    kv_spent_back, kv_grad, query_grad = lax.fori_loop(
        1, reach_steps + 1, backward_turn, (kv_own, start_grad, start_query)
    )
    home_by = -reach_steps % blocks
    kv_grad = passed_along(kv_grad.astype(jnp.bfloat16), "blk", home_by).astype(kv_grad.dtype)
    query_back, kv_back = (
        lax.all_to_all(
            query_grad.reshape(tok_rows, groups, per_group * HEAD).astype(jnp.bfloat16),
            "head",
            split_axis=1,
            concat_axis=1,
            tiled=True,
        ).astype(jnp.float32),
        lax.all_to_all(
            kv_grad.reshape(tok_rows, groups, 4 * HEAD).astype(jnp.bfloat16),
            "head",
            split_axis=1,
            concat_axis=1,
            tiled=True,
        ).astype(jnp.float32),
    )
    grad_queries = query_back.reshape(tok_rows, QHEADS, HEAD)
    kv_parts = kv_back.reshape(tok_rows, groups, 2, 2, HEAD)
    head_grads = []
    for head_id in range(KVHEADS):
        members = [
            kv_parts[:, group_at, slot_at]
            for group_at in range(groups)
            for slot_at in range(2)
            if copy_index[group_at, slot_at] == head_id
        ]
        head_grads.append(reduce(jnp.add, members))
    kv_heads = jnp.stack(head_grads, axis=1)
    grad_keys = kv_heads[:, :, 0]
    grad_values = kv_heads[:, :, 1]

    def prep_local(query_in_raw, key_in_raw, query_gain_in, key_gain_in):
        return prepare(query_in_raw, key_in_raw, query_gain_in, key_gain_in, cosine, sine_table)

    prep_out, prep_pull = jax.vjp(prep_local, query_raw, key_raw, query_g, key_g)
    grad_query_raw, grad_key_raw, grad_query_g, grad_key_g = prep_pull((grad_queries, grad_keys))
    query_low = grad_query_raw.astype(jnp.bfloat16)
    key_low = grad_key_raw.astype(jnp.bfloat16)
    value_low = grad_values.reshape(tok_rows, KVHEADS * HEAD).astype(jnp.bfloat16)
    grad_w_query = matmul(normed_one.T, query_low)
    grad_w_key = matmul(normed_one.T, key_low)
    grad_w_value = matmul(normed_one.T, value_low)
    grad_normed_one = (
        matmul(query_low, gathered[1].T)
        + matmul(key_low, gathered[2].T)
        + matmul(value_low, gathered[3].T)
    )
    norm_one_out, norm_one_pull = jax.vjp(norm_rows, inputs, gain_one)
    grad_input_part, grad_gain_one = norm_one_pull(grad_normed_one)
    d_tokens = grad_resid + grad_input_part
    attn_parts = (
        lax.psum_scatter(grad_gain_one, ("head", "blk"), scatter_dimension=0, tiled=True),
        lax.psum_scatter(grad_w_query, ("head", "blk"), scatter_dimension=0, tiled=True),
        lax.psum_scatter(grad_w_key, ("head", "blk"), scatter_dimension=0, tiled=True),
        lax.psum_scatter(grad_w_value, ("head", "blk"), scatter_dimension=0, tiled=True),
        lax.psum_scatter(grad_w_out, ("head", "blk"), scatter_dimension=0, tiled=True),
    )
    gain_sums = lax.psum((grad_query_g, grad_key_g), ("head", "blk"))
    return (
        out_act,
        d_tokens,
        attn_parts[0],
        attn_parts[1],
        attn_parts[2],
        attn_parts[3],
        gain_sums[0],
        gain_sums[1],
        attn_parts[4],
        ffn_parts[0],
        ffn_parts[1],
        ffn_parts[2],
        ffn_parts[3],
    )


def solution(mesh):
    in_specs = (
        P(("blk", "head"), None),
        P(),
        P(("head", "blk")),
        P(("head", "blk"), None),
        P(("head", "blk"), None),
        P(("head", "blk"), None),
        P(),
        P(),
        P(("head", "blk"), None),
        P(("head", "blk")),
        P(("head", "blk"), None),
        P(("head", "blk"), None),
        P(("head", "blk"), None),
        P(("blk", "head"), None),
    )
    out_specs = (
        P(("blk", "head"), None),
        P(("blk", "head"), None),
        P(("head", "blk")),
        P(("head", "blk"), None),
        P(("head", "blk"), None),
        P(("head", "blk"), None),
        P(),
        P(),
        P(("head", "blk"), None),
        P(("head", "blk")),
        P(("head", "blk"), None),
        P(("head", "blk"), None),
        P(("head", "blk"), None),
    )
    return jax.shard_map(shards, mesh=mesh, in_specs=in_specs, out_specs=out_specs, check_vma=False)
```

profile of v0, /device:TPU:0, one launch (start us, length us, event | category | flops | bytes accessed | tf_op | source)
XLA Modules:
  0.0 4447.1 jit_solution(2734365608295401895)
XLA Ops:
  13.7 42.2 all-reduce.9
  71.1 54.6 %all-gather.8.cloned.1.call-done = bf16[2048,384]{1,0:T(8,128)(2,1)} async-done(((bf16[64,384]{1,0:T(8,128)(2,1)}), bf16[2048,384]{1,0:T(8,128)(2,1)}) %all-gather.8.cloned.1.call-update) | async-done | bytes 1572880 | tf_op jit(solution)/shard_map/all_gather | solution.py:98
  133.9 64.3 %all-gather.12.cloned.1.call-done = bf16[2048,1536]{1,0:T(8,128)(2,1)} async-done(((bf16[64,1536]{1,0:T(8,128)(2,1)}), bf16[2048,1536]{1,0:T(8,128)(2,1)}) %all-gather.12.cloned.1.call-update) | async-done | bytes 6291472 | tf_op jit(solution)/shard_map/all_gather | solution.py:97
  264.1 221.2 %while.44 = (s32[]{:T(128)}, bf16[1024,2,128]{2,0,1:T(8,128)(2,1)S(1)}, f32[6,1024]{1,0:T(8,128)S(1)}, f32[6,1024]{1,0:T(8,128)}, f32[6,1024,64]{1,2,0:T(8,128)}...) while((s32[]{:T(128)}, ...), condition=%wide.region_13.15_spmd.clone.clone, body=%wide.region_9.14_spmd.clone.clone.sunk | while | flops 1697149056 | bytes 205386368 | solution.py:191
  300.9 14.0 multiply_add_fusion.13
  354.0 13.6 multiply_add_fusion.13
  383.4 13.5 collective-permute-done
  418.9 13.4 multiply_add_fusion.13
  471.8 13.5 multiply_add_fusion.13
  501.0 20.7 all-to-all-done.2
  542.3 23.9 all-gather.18.cloned.1.call-done
  578.4 128.9 %all-gather.20.cloned.1.call-done = bf16[5120,2048]{1,0:T(8,128)(2,1)} async-done(((bf16[160,2048]{1,0:T(8,128)(2,1)}), bf16[5120,2048]{1,0:T(8,128)(2,1)}) %all-gather.20.cloned.1.call-update) | async-done | bytes 20971536 | tf_op jit(solution)/shard_map/all_gather | solution.py:104
  707.3 23.0 multiply_convert_fusion.1
  785.9 16.6 fusion.66
  816.8 17.3 multiply_convert_fusion
  859.5 366.6 %while.45 = (s32[]{:T(128)}, bf16[1024,2,128]{2,0,1:T(8,128)(2,1)S(1)}, bf16[1024,2,128]{2,1,0:T(2,128)(2,1)}, f32[1024,6,64]{0,2,1:T(8,128)}, s32[1024]{0:T(102...) while((s32[]{:T(128)}, ...), condition=%wide.region_19.21_spmd.clone.clone, body=%wide.region_17.20_spmd.clone.clone.sunk | while | flops 4127604736 | bytes 179917520 | solution.py:274
  902.5 17.0 fusion.223
  996.2 16.9 fusion.223
  1087.3 16.9 fusion.223
  1175.9 16.9 fusion.223
  1281.1 14.1 all_to_all.31
  1305.8 18.3 fusion.132
  1324.2 18.3 fusion.133
  1343.7 18.3 fusion.134
  1362.1 14.3 fusion.67
  1385.2 38.5 all-reduce.8
  1429.1 39.6 reduce-scatter.12.cloned.1.call-done
  1468.6 161.1 %reduce-scatter.14.cloned.1.call-done = f32[48,2048]{1,0:T(8,128)} async-done(((f32[1536,2048]{1,0:T(8,128)}), f32[48,2048]{1,0:T(8,128)}) %reduce-scatter.14.cloned.1.call-update) | async-done | bytes 393232 | tf_op jit(solution)/shard_map/reduce_scatter | solution.py:334
  1629.8 162.4 %reduce-scatter.8.cloned.1.call-done = f32[64,1536]{1,0:T(8,128)} async-done(((f32[2048,1536]{1,0:T(8,128)}), f32[64,1536]{1,0:T(8,128)}) %reduce-scatter.8.cloned.1.call-update) | async-done | bytes 393232 | tf_op jit(solution)/shard_map/reduce_scatter | solution.py:331
  1792.2 882.1 %reduce-scatter.16.cloned.1.call-done = f32[64,5120]{1,0:T(8,128)} async-done(((f32[2048,5120]{1,0:T(8,128)}), f32[64,5120]{1,0:T(8,128)}) %reduce-scatter.16.cloned.1.call-update) | async-done | bytes 1310736 | tf_op jit(solution)/shard_map/reduce_scatter | solution.py:221
  2674.3 883.1 %reduce-scatter.18.cloned.1.call-done = f32[64,5120]{1,0:T(8,128)} async-done(((f32[2048,5120]{1,0:T(8,128)}), f32[64,5120]{1,0:T(8,128)}) %reduce-scatter.18.cloned.1.call-update) | async-done | bytes 1310736 | tf_op jit(solution)/shard_map/reduce_scatter | solution.py:222
  3557.4 883.0 %reduce-scatter.20.cloned.1.call-done = f32[160,2048]{1,0:T(8,128)} async-done(((f32[5120,2048]{1,0:T(8,128)}), f32[160,2048]{1,0:T(8,128)}) %reduce-scatter.20.cloned.1.call-update) | async-done | bytes 1310736 | tf_op jit(solution)/shard_map/reduce_scatter | solution.py:223
  (545 shorter events, 769.7 us)
Async XLA Ops:
  7.2 61.6 %all-gather.10.cloned.1.call-start = ((), (), s32[]{:S(2)}) async-start(), calls=%async_computation.14 | async-start | bytes 1622016 | tf_op jit(solution)/shard_map/all_gather | solution.py:99
  8.0 117.7 %all-gather.8.cloned.1.call-start = ((), (), s32[]{:S(2)}) async-start(), calls=%async_computation.13 | async-start | bytes 1622016 | tf_op jit(solution)/shard_map/all_gather | solution.py:98
  8.7 189.5 %all-gather.12.cloned.1.call-start = ((), (), s32[]{:S(2)}) async-start(), calls=%async_computation.15 | async-start | bytes 6488064 | tf_op jit(solution)/shard_map/all_gather | solution.py:97
  9.5 513.7 %all-gather.14.cloned.1.call-start = ((), (), s32[]{:S(2)}) async-start(), calls=%async_computation.16 | async-start | bytes 6488064 | tf_op jit(solution)/shard_map/all_gather | solution.py:100
  10.0 519.7 %all-gather.16.cloned.1.call-start = ((), (), s32[]{:S(2)}) async-start(), calls=%async_computation.17 | async-start | bytes 21626880 | tf_op jit(solution)/shard_map/all_gather | solution.py:102
  10.6 555.5 %all-gather.18.cloned.1.call-start = ((), (), s32[]{:S(2)}) async-start(), calls=%async_computation.18 | async-start | bytes 21626880 | tf_op jit(solution)/shard_map/all_gather | solution.py:103
  11.2 696.1 %all-gather.20.cloned.1.call-start = ((), (), s32[]{:S(2)}) async-start(), calls=%async_computation.19 | async-start | bytes 21626880 | tf_op jit(solution)/shard_map/all_gather | solution.py:104
  130.5 75.5 %all-to-all-start = ((bf16[256,4,256]{2,0,1:T(8,128)(2,1)}), bf16[256,4,256]{2,0,1:T(8,128)(2,1)S(1)}, u32[]{:S(2)}, u32[]{:S(2)}) async-start(bf16[256,4,256]{2,0,1:T(8,128)(2,1)} %copy.201), calls=%async_computation | async-start | bytes 1048576 | tf_op jit(solution)/shard_map/all_to_all | solution.py:133
  205.9 15.6 all-to-all-start.1
  264.3 14.6 collective-permute-start
  315.0 14.8 collective-permute-start
  367.7 29.1 collective-permute-start
  432.3 17.5 collective-permute-start
  496.3 25.4 all-to-all-start.2
  542.3 165.1 %copy-start.29 = (bf16[256,2048]{1,0:T(8,128)(2,1)S(1)}, bf16[256,2048]{1,0:T(8,128)(2,1)}, u32[]{:S(2)}) copy-start(bf16[256,2048]{1,0:T(8,128)(2,1)} %param.36) | copy-start | bytes 3145732
  764.5 15.1 all-to-all-start.3
  768.0 661.1 %reduce-scatter.10.cloned.1.call-start = ((), (), s32[]{:S(2)}) async-start(), calls=%async_computation.21 | async-start | bytes 3244032 | tf_op jit(solution)/shard_map/reduce_scatter | solution.py:332
  859.6 15.7 collective-permute-start.1
  863.1 83.6 %collective-permute-start.2 = (bf16[1024,2,128]{2,1,0:T(2,128)(2,1)}, bf16[1024,2,128]{2,1,0:T(2,128)(2,1)}, u32[]{:S(2)}, u32[]{:S(2)}) collective-permute-start(bf16[1024,2,128]{2,1,0:T(2,128)(2,1)} %get-tuple-element.1341), channel_id=1, source_target_pairs={{7,0},{0,1},{1,2},{2,3},{3,4},{4,5},{5,6},{6,7},{15,8},{8,9},{9,10... | collective-permute-start | bytes 1572872 | tf_op jit(solution)/shard_map/while/body/eval_jaxpr/ppermute | solution.py:31
  952.3 16.7 collective-permute-start.1
  956.7 83.6 %collective-permute-start.2 = (bf16[1024,2,128]{2,1,0:T(2,128)(2,1)}, bf16[1024,2,128]{2,1,0:T(2,128)(2,1)}, u32[]{:S(2)}, u32[]{:S(2)}) collective-permute-start(bf16[1024,2,128]{2,1,0:T(2,128)(2,1)} %get-tuple-element.1341), channel_id=1, source_target_pairs={{7,0},{0,1},{1,2},{2,3},{3,4},{4,5},{5,6},{6,7},{15,8},{8,9},{9,10... | collective-permute-start | bytes 1572872 | tf_op jit(solution)/shard_map/while/body/eval_jaxpr/ppermute | solution.py:31
  1046.0 14.1 collective-permute-start.1
  1050.4 81.0 %collective-permute-start.2 = (bf16[1024,2,128]{2,1,0:T(2,128)(2,1)}, bf16[1024,2,128]{2,1,0:T(2,128)(2,1)}, u32[]{:S(2)}, u32[]{:S(2)}) collective-permute-start(bf16[1024,2,128]{2,1,0:T(2,128)(2,1)} %get-tuple-element.1341), channel_id=1, source_target_pairs={{7,0},{0,1},{1,2},{2,3},{3,4},{4,5},{5,6},{6,7},{15,8},{8,9},{9,10... | collective-permute-start | bytes 1572872 | tf_op jit(solution)/shard_map/while/body/eval_jaxpr/ppermute | solution.py:31
  1137.1 11.7 collective-permute-start.1
  1142.1 77.9 %collective-permute-start.2 = (bf16[1024,2,128]{2,1,0:T(2,128)(2,1)}, bf16[1024,2,128]{2,1,0:T(2,128)(2,1)}, u32[]{:S(2)}, u32[]{:S(2)}) collective-permute-start(bf16[1024,2,128]{2,1,0:T(2,128)(2,1)} %get-tuple-element.1341), channel_id=1, source_target_pairs={{7,0},{0,1},{1,2},{2,3},{3,4},{4,5},{5,6},{6,7},{15,8},{8,9},{9,10... | collective-permute-start | bytes 1572872 | tf_op jit(solution)/shard_map/while/body/eval_jaxpr/ppermute | solution.py:31
  1226.1 18.6 collective-permute-start.3
  1261.3 207.4 %reduce-scatter.12.cloned.1.call-start = ((), (), s32[]{:S(2)}) async-start(), calls=%async_computation.22 | async-start | bytes 3244032 | tf_op jit(solution)/shard_map/reduce_scatter | solution.py:333
  1264.5 365.2 %reduce-scatter.14.cloned.1.call-start = ((), (), s32[]{:S(2)}) async-start(), calls=%async_computation.23 | async-start | bytes 12976128 | tf_op jit(solution)/shard_map/reduce_scatter | solution.py:334
  1273.7 518.5 %reduce-scatter.8.cloned.1.call-start = ((), (), s32[]{:S(2)}) async-start(), calls=%async_computation.20 | async-start | bytes 12976128 | tf_op jit(solution)/shard_map/reduce_scatter | solution.py:331
  1304.6 1369.6 %reduce-scatter.16.cloned.1.call-start = ((), (), s32[]{:S(2)}) async-start(), calls=%async_computation.24 | async-start | bytes 43253760 | tf_op jit(solution)/shard_map/reduce_scatter | solution.py:221
  1324.1 2233.3 %reduce-scatter.18.cloned.1.call-start = ((), (), s32[]{:S(2)}) async-start(), calls=%async_computation.25 | async-start | bytes 43253760 | tf_op jit(solution)/shard_map/reduce_scatter | solution.py:222
  1342.5 3097.8 %reduce-scatter.20.cloned.1.call-start = ((), (), s32[]{:S(2)}) async-start(), calls=%async_computation.26 | async-start | bytes 43253760 | tf_op jit(solution)/shard_map/reduce_scatter | solution.py:223
  (105 other events, 1858.1 us)
Sparse Core Ops, SparseCore 0:
  11.0 57.7 all-gather.9
  71.7 53.9 all-gather.7
  128.6 69.5 all-gather.11
  201.0 68.8 all-gather.13
  272.6 141.8 all-gather.15
  417.2 148.9 all-gather.17
  569.0 138.3 all-gather.19
  1261.4 100.0 reduce-scatter.9
  1367.5 101.0 reduce-scatter.11
  1475.1 154.6 reduce-scatter.13
  1637.4 154.7 reduce-scatter.7
  1794.9 879.3 reduce-scatter.15
  2677.1 880.1 reduce-scatter.17
  3560.1 880.1 reduce-scatter.19
where the time goes:
time: 4460 us; the launch traced here: 4450 us
  waiting for transfers between devices  3410 us (76%)
  matrix products  600 us (13%)
  other arithmetic  139 us (3%)
  blocking collectives  106 us (2%)
  local copies, waits for them, and re-layouts  101 us (2%)
  starting transfers between devices  77.2 us (2%)
    reduce_scatter x1, waiting for transfers between devices, shards(): lax.psum_scatter(grad_w_up, ('head', 'blk'), scatter_dimension=0, tiled=T...  883 us
    reduce_scatter x1, waiting for transfers between devices, shards(): lax.psum_scatter(grad_w_down, ('head', 'blk'), scatter_dimension=0, tiled...  883 us
    reduce_scatter x1, waiting for transfers between devices, shards(): lax.psum_scatter(grad_w_gate, ('head', 'blk'), scatter_dimension=0, tiled...  882 us
    dot_general x21, matrix products, matmul(): return jnp.dot(left_side, right_side, preferred_element_type=jnp.float32)  190 us
    reduce_scatter x1, waiting for transfers between devices, shards(): lax.psum_scatter(grad_w_query, ('head', 'blk'), scatter_dimension=0, tile...  162 us
    reduce_scatter x1, waiting for transfers between devices, shards(): lax.psum_scatter(grad_w_out, ('head', 'blk'), scatter_dimension=0, tiled=...  161 us
    all_gather x1, waiting for transfers between devices, shards(): lax.all_gather(w_down, ('head', 'blk'), axis=0, tiled=True)  129 us
  transfers between devices with their start and end apart: 31, of which 23 were waited for; matrix products, arithmetic and copies ran while one was open for 15% of the time, Pallas kernels for 0%

commit v1 on v0

v1 whole, which is shorter than its diff:
```python
import functools
import math

import jax
import jax.numpy as jnp
from jax import lax
from jax.experimental import pallas as pl
from jax.experimental.pallas import tpu as pltpu
from jax.sharding import PartitionSpec as P

QHEADS = 24
KVHEADS = 6
HEAD = 64
MAXDOC = 4096

EPS = 1e-06
SCALE = 0.125
LOG2E = 1.4426950408889634
NEG = -1e30
TILE = 256
BACK = 4
BF = jnp.bfloat16
F32 = jnp.float32


def matmul(left_side, right_side):
    return jnp.dot(left_side, right_side, preferred_element_type=F32)


def matmul_tn(left_side, right_side):
    return lax.dot_general(
        left_side, right_side, (((0,), (0,)), ((), ())), preferred_element_type=F32
    )


def matmul_nt(left_side, right_side):
    return lax.dot_general(
        left_side, right_side, (((1,), (1,)), ((), ())), preferred_element_type=F32
    )


def swap(block, axis, bit):
    count = lax.axis_size(axis)
    return lax.ppermute(block, axis, [(i, i ^ bit) for i in range(count)])


def ring(block, step):
    count = lax.axis_size("blk")
    return lax.ppermute(block, "blk", [(i, (i + step) % count) for i in range(count)])


def put(full, part, index, axis=0):
    return lax.dynamic_update_index_in_dim(full, part, index, axis)


def take(full, index, axis=0):
    return lax.dynamic_index_in_dim(full, index, axis, keepdims=False)


def gather_head(part):
    me = lax.axis_index("head")
    far = swap(part, "head", 2)
    near = swap(part, "head", 1)
    diagonal = swap(far, "head", 1)
    full = jnp.zeros((4,) + part.shape, part.dtype)
    full = put(full, part, me)
    full = put(full, near, me ^ 1)
    full = put(full, far, me ^ 2)
    return put(full, diagonal, me ^ 3)


def scatter_head(terms):
    me = lax.axis_index("head")
    got_far = swap(take(terms, me ^ 3), "head", 1)
    far = (take(terms, me ^ 2).astype(F32) + got_far.astype(F32)).astype(terms.dtype)
    got_near = swap(take(terms, me ^ 1), "head", 1)
    arrived = swap(far, "head", 2)
    return take(terms, me).astype(F32) + got_near.astype(F32) + arrived.astype(F32)


def gather_blk(part, axis=0):
    count = lax.axis_size("blk")
    line = count // 2
    place, side = lax.axis_index("blk") // 2, lax.axis_index("blk") % 2
    shape = part.shape[:axis] + (count,) + part.shape[axis:]
    full = jnp.zeros(shape, part.dtype)
    held = part
    for step in range(line):
        if step:
            held = ring(held, 2)
        other = swap(held, "blk", 1)
        source = (place - step) % line
        full = put(full, held, 2 * source + side, axis)
        full = put(full, other, 2 * source + 1 - side, axis)
    return full


def scatter_blk(chunk):
    count = lax.axis_size("blk")
    line = count // 2
    place, side = lax.axis_index("blk") // 2, lax.axis_index("blk") % 2
    total = None
    for step in range(1, line + 1):
        target = (place - step) % line
        mine = chunk(2 * target + side)
        got = swap(chunk(2 * target + 1 - side), "blk", 1)
        term = mine.astype(F32) + got.astype(F32)
        if total is not None:
            term = term + total.astype(F32)
        if step < line:
            total = ring(term.astype(BF), 2)
        else:
            total = term
    return total


def nt(left_side, right_side):
    return lax.dot_general(
        left_side, right_side, (((1,), (1,)), ((), ())), preferred_element_type=F32
    )


def nn(left_side, right_side):
    return lax.dot_general(
        left_side, right_side, (((1,), (0,)), ((), ())), preferred_element_type=F32
    )


def head_groups(meta_ref):
    odd = meta_ref[0]
    return ((4, 2 * odd, odd), (2, 4 * (1 - odd), 1 - odd))


def attend_kernel(meta_ref, query_ref, key_ref, value_ref, start_ref, out_ref, acc_ref):
    rows = query_ref.shape[1]
    base = key_ref.shape[1] - rows
    lane = lax.broadcasted_iota(jnp.int32, (TILE, 2 * HEAD), 1)
    for count, first, slot in head_groups(meta_ref):
        for tile in range(rows // TILE):
            q_at = tile * TILE
            low, high = meta_ref[1 + 2 * tile], meta_ref[2 + 2 * tile]
            queries = query_ref[pl.ds(first, count), q_at : q_at + TILE, :].reshape(
                count * TILE, 2 * HEAD
            )
            acc = acc_ref.at[pl.ds(0, count * TILE)]
            acc[...] = jnp.zeros((count * TILE, 2 * HEAD), F32)
            start_col = start_ref[q_at : q_at + TILE, :]
            q_pos = base + q_at + lax.broadcasted_iota(jnp.int32, (TILE, 1), 0)

            def step(at, carry, masked):
                k_at = pl.multiple_of(at * TILE, TILE)
                scores = nt(queries, key_ref[slot, pl.ds(k_at, TILE), :])
                if masked:
                    k_pos = k_at + lax.broadcasted_iota(jnp.int32, (1, TILE), 1)
                    allowed = (start_col <= k_pos) & (k_pos <= q_pos)
                    scores = jnp.where(
                        allowed[None], scores.reshape(count, TILE, TILE), NEG
                    ).reshape(count * TILE, TILE)
                weights = jnp.exp2(scores).astype(BF)
                acc[...] += nn(weights, value_ref[slot, pl.ds(k_at, TILE), :])
                return carry

            begin = low // TILE
            clear = jnp.minimum((high + TILE - 1) // TILE, (base + q_at) // TILE)
            last = (base + q_at) // TILE
            lax.fori_loop(begin, clear, functools.partial(step, masked=True), 0)
            lax.fori_loop(clear, last, functools.partial(step, masked=False), 0)
            step(last, 0, True)
            for j in range(count):
                part = acc_ref[j * TILE : (j + 1) * TILE, :]
                total = part[:, HEAD : HEAD + 1]
                out_ref[first + j, q_at : q_at + TILE, :] = jnp.where(
                    lane < HEAD, part / total, jnp.log2(total)
                )


def attend(meta, queries, keys, values, starts):
    heads, rows, _ = queries.shape
    return pl.pallas_call(
        attend_kernel,
        out_shape=jax.ShapeDtypeStruct((heads, rows, 2 * HEAD), F32),
        in_specs=[pl.BlockSpec(memory_space=pltpu.SMEM)]
        + [pl.BlockSpec(memory_space=pltpu.VMEM)] * 4,
        out_specs=pl.BlockSpec(memory_space=pltpu.VMEM),
        scratch_shapes=[pltpu.VMEM((4 * TILE, 2 * HEAD), F32)],
        compiler_params=pltpu.CompilerParams(vmem_limit_bytes=48 << 20),
        cost_estimate=pl.CostEstimate(
            flops=30_000_000_000, bytes_accessed=20_000_000, transcendentals=20_000_000
        ),
        name="attend",
    )(meta, queries, keys, values, starts)


def attend_back_kernel(
    meta_ref,
    key_ref,
    value_ref,
    key_t_ref,
    query_t_ref,
    grad_t_ref,
    query_ref,
    grad_ref,
    start_ref,
    dq_ref,
    dkv_ref,
):
    rows = query_ref.shape[1]
    base = key_ref.shape[1] - rows
    dkv_ref[...] = jnp.zeros_like(dkv_ref)
    dq_ref[...] = jnp.zeros_like(dq_ref)
    for count, first, slot in head_groups(meta_ref):
        for tile in range(rows // TILE):
            q_at = tile * TILE
            q_cols = slice(q_at, q_at + TILE)
            low, high = meta_ref[1 + 2 * tile], meta_ref[2 + 2 * tile]
            start_row = start_ref[:, q_cols]
            q_pos = base + q_at + lax.broadcasted_iota(jnp.int32, (1, TILE), 1)

            def step(at, carry, masked):
                k_at = pl.multiple_of(at * TILE, TILE)
                k_rows = pl.ds(k_at, TILE)
                keys = key_ref[slot, k_rows, :]
                values = value_ref[slot, k_rows, :]
                key_t = key_t_ref[slot, :, k_rows]
                if masked:
                    k_pos = k_at + lax.broadcasted_iota(jnp.int32, (TILE, 1), 0)
                    allowed = (start_row <= k_pos) & (k_pos <= q_pos)
                total = dkv_ref[slot, k_rows, :]
                for j in range(count):
                    scores = nn(keys, query_t_ref[first + j, :, q_cols])
                    if masked:
                        scores = jnp.where(allowed, scores, NEG)
                    probs = jnp.exp2(scores)
                    diff = nn(values, grad_t_ref[first + j, :, q_cols])
                    grad_score = (probs * diff).astype(BF)
                    total = (
                        total
                        + nn(probs.astype(BF), grad_ref[first + j, q_cols, :])
                        + nn(grad_score, query_ref[first + j, q_cols, :])
                    )
                    dq_ref[first + j, :, q_cols] += nn(key_t, grad_score)
                dkv_ref[slot, k_rows, :] = total
                return carry

            begin = low // TILE
            clear = jnp.minimum((high + TILE - 1) // TILE, (base + q_at) // TILE)
            last = (base + q_at) // TILE
            lax.fori_loop(begin, clear, functools.partial(step, masked=True), 0)
            lax.fori_loop(clear, last, functools.partial(step, masked=False), 0)
            step(last, 0, True)


def attend_back(meta, keys, values, keys_t, queries_t, grads_t, queries, grads, starts):
    heads, rows, _ = queries.shape
    return pl.pallas_call(
        attend_back_kernel,
        out_shape=(
            jax.ShapeDtypeStruct((heads, HEAD, rows), F32),
            jax.ShapeDtypeStruct((2, keys.shape[1], 2 * HEAD), F32),
        ),
        in_specs=[pl.BlockSpec(memory_space=pltpu.SMEM)]
        + [pl.BlockSpec(memory_space=pltpu.VMEM)] * 8,
        out_specs=(pl.BlockSpec(memory_space=pltpu.VMEM),) * 2,
        compiler_params=pltpu.CompilerParams(vmem_limit_bytes=56 << 20),
        cost_estimate=pl.CostEstimate(
            flops=70_000_000_000, bytes_accessed=40_000_000, transcendentals=20_000_000
        ),
        name="attend_back",
    )(meta, keys, values, keys_t, queries_t, grads_t, queries, grads, starts)


def norm_rows(tensor, gain_vec):
    return tensor * lax.rsqrt(jnp.mean(tensor * tensor, axis=-1, keepdims=True) + EPS) * gain_vec


def rotate(tensor, cosine, sine_table):
    half_width = tensor.shape[-1] // 2
    first_half = tensor[..., :half_width]
    second = tensor[..., half_width:]
    return jnp.concatenate(
        [first_half * cosine - second * sine_table, second * cosine + first_half * sine_table],
        axis=-1,
    )


def split_low(value, parts):
    out = []
    for _ in range(parts):
        term = lax.reduce_precision(value, 8, 7)
        out.append(term.astype(BF))
        value = value - term
    return out


def shards(
    tokens,
    doc_lengths,
    norm1_gain,
    w_query,
    w_key,
    w_value,
    query_gain,
    key_gain,
    w_out,
    norm2_gain,
    w_gate,
    w_up,
    w_down,
    cotangent,
):
    tok_rows, width = tokens.shape
    blocks = lax.axis_size("blk")
    groups = lax.axis_size("head")
    group_id = lax.axis_index("head")
    blk_place = lax.axis_index("blk")
    block_len = groups * tok_rows
    per_group = QHEADS // groups
    head_ratio = QHEADS // KVHEADS
    w_rows = w_query.shape[0]
    hidden_cols = w_gate.shape[1] // groups
    q_cols = per_group * HEAD
    firsts = [g * per_group // head_ratio for g in range(groups)]
    odd = group_id % 2

    columns = []
    for g in range(groups):
        kv = slice(firsts[g] * HEAD, (firsts[g] + 2) * HEAD)
        columns += [
            w_query[:, g * q_cols : (g + 1) * q_cols],
            w_key[:, kv],
            w_value[:, kv],
            norm1_gain[:, None],
            norm2_gain[:, None],
            jnp.zeros((w_rows, 126), BF),
        ]
    qkv_cols = q_cols + 4 * HEAD
    qkv_wide = qkv_cols + 2 * HEAD
    w_in = jnp.concatenate(columns, axis=1).reshape(w_rows, groups, qkv_wide)
    w_in = lax.all_to_all(w_in, "head", split_axis=1, concat_axis=1, tiled=True)
    w_in = gather_blk(jnp.swapaxes(w_in, 0, 1), 1).reshape(width, qkv_wide)
    w_qkv = w_in[:, :qkv_cols]
    gains = w_in[:, qkv_cols : qkv_cols + 2].astype(F32).T
    gain_one, gain_two = gains[0], gains[1]

    block_tokens = gather_head(tokens).reshape(block_len, width)

    def spread(weight):
        split = weight.reshape(w_rows, groups, hidden_cols)
        split = lax.all_to_all(split, "head", split_axis=1, concat_axis=1, tiled=True)
        return gather_blk(jnp.swapaxes(split, 0, 1), 1).reshape(width, hidden_cols)

    starts = jnp.cumsum(doc_lengths) - doc_lengths
    offsets = jnp.arange(block_len, dtype=jnp.int32)
    token_pos = blk_place * block_len + offsets
    inside = starts[None, :] <= token_pos[:, None]
    token_start = jnp.max(jnp.where(inside, starts[None, :], 0), axis=1)
    in_doc = token_pos - token_start
    rope_freq = jnp.exp(-math.log(10000.0) * jnp.arange(HEAD // 2, dtype=F32) / (HEAD // 2))
    rope_angle = in_doc.astype(F32)[:, None] * rope_freq[None, :]
    cosine = jnp.cos(rope_angle)[:, None, :]
    sine_table = jnp.sin(rope_angle)[:, None, :]
    window_start = token_start - (blk_place - BACK) * block_len
    tiles = block_len // TILE
    edges = jnp.stack(
        [window_start[:: TILE], window_start[TILE - 1 :: TILE]], axis=1
    ).reshape(2 * tiles)
    meta = jnp.concatenate([odd[None].astype(jnp.int32), edges.astype(jnp.int32)])

    query_g = query_gain.astype(F32)
    key_g = key_gain.astype(F32)
    block_inputs = block_tokens.astype(F32)
    normed_one = norm_rows(block_inputs, gain_one).astype(BF)
    raw = matmul(normed_one, w_qkv)

    def prepare(query_raw, key_raw, query_gain_in, key_gain_in):
        return (
            rotate(norm_rows(query_raw, query_gain_in), cosine, sine_table),
            rotate(norm_rows(key_raw, key_gain_in), cosine, sine_table),
        )

    query_raw = raw[:, :q_cols].reshape(block_len, per_group, HEAD)
    key_raw = raw[:, q_cols : q_cols + 2 * HEAD].reshape(block_len, 2, HEAD)
    value_own = raw[:, q_cols + 2 * HEAD :].reshape(block_len, 2, HEAD).astype(BF)
    (query_rot, key_rot), prep_pull = jax.vjp(prepare, query_raw, key_raw, query_g, key_g)
    queries = jnp.swapaxes(query_rot.astype(BF), 0, 1)
    kv_own = jnp.swapaxes(
        jnp.concatenate([key_rot.astype(BF), value_own], axis=-1), 0, 1
    )

    even = blk_place % 2 == 0
    kv_two = ring(kv_own, 2)
    kv_one = swap(jnp.where(even, kv_own, kv_two), "blk", 1)
    kv_four = ring(kv_two, 2)
    kv_three = swap(jnp.where(even, kv_two, kv_four), "blk", 1)
    window = jnp.concatenate([kv_four, kv_three, kv_two, kv_one, kv_own], axis=1)
    key_win, value_win = window[..., :HEAD], window[..., HEAD:]
    ones = jnp.ones(key_win.shape, BF)
    keys_wide = jnp.concatenate([key_win, key_win, ones, ones], axis=-1)
    values_wide = jnp.concatenate([value_win, ones], axis=-1)

    scaled = split_low(queries.astype(F32) * (SCALE * LOG2E), 2)
    attended = attend(
        meta,
        jnp.concatenate(scaled, axis=-1),
        keys_wide[..., : 2 * HEAD],
        values_wide,
        window_start[:, None],
    )
    attn_keep = attended[..., :HEAD]
    log_total = attended[..., HEAD]
    attn_out = jnp.swapaxes(attn_keep.astype(BF), 0, 1).reshape(groups, tok_rows, q_cols)
    mixed = lax.all_to_all(attn_out, "head", split_axis=0, concat_axis=0, tiled=True)
    mixed = jnp.swapaxes(mixed, 0, 1).reshape(tok_rows, QHEADS * HEAD)

    w_o = gather_head(gather_blk(w_out, 0)).reshape(QHEADS * HEAD, width)
    inputs = tokens.astype(F32)
    resid = inputs + matmul(mixed, w_o)
    normed_two_own = norm_rows(resid, gain_two).astype(BF)

    w_g, w_u = spread(w_gate), spread(w_up)
    w_d = gather_blk(w_down, 0).reshape(hidden_cols, width)
    top = gather_head(cotangent).reshape(block_len, width)
    normed_two = gather_head(normed_two_own).reshape(block_len, width)
    gate_val = matmul(normed_two, w_g)
    up_val = matmul(normed_two, w_u)
    gate_sig = jax.nn.sigmoid(gate_val)
    gate_silu = gate_val * gate_sig
    hidden = (gate_silu * up_val).astype(BF)
    out_part = matmul(hidden, w_d).astype(BF).reshape(groups, tok_rows, width)
    out_act = (resid + scatter_head(out_part)).astype(BF)
    grad_hidden = matmul_nt(top, w_d)
    grad_gate = (grad_hidden * up_val * gate_sig * (1 + gate_val * (1 - gate_sig))).astype(BF)
    grad_up = (grad_hidden * gate_silu).astype(BF)
    grad_part = (matmul_nt(grad_gate, w_g) + matmul_nt(grad_up, w_u)).astype(BF)
    grad_normed = scatter_head(grad_part.reshape(groups, tok_rows, width))
    norm_two_out, norm_two_pull = jax.vjp(norm_rows, resid, gain_two)
    grad_resid_part, grad_gain_two = norm_two_pull(grad_normed)
    grad_resid = cotangent.astype(F32) + grad_resid_part
    grad_attn = grad_resid.astype(BF)

    def by_rows(grad):
        parts = grad.astype(BF).reshape(groups, blocks, w_rows, grad.shape[1])
        return scatter_blk(lambda b: take(parts, b, 1))

    def to_owner(grad):
        back = lax.all_to_all(
            grad.astype(BF), "head", split_axis=0, concat_axis=0, tiled=True
        )
        return jnp.swapaxes(back, 0, 1).astype(F32)

    down_parts = matmul_tn(hidden, top).astype(BF).reshape(blocks, w_down.shape[0], width)
    d_w_down = scatter_blk(lambda b: take(down_parts, b))
    d_w_gate = to_owner(by_rows(matmul_tn(normed_two, grad_gate))).reshape(w_gate.shape)
    d_w_up = to_owner(by_rows(matmul_tn(normed_two, grad_up))).reshape(w_up.shape)

    out_parts = matmul_tn(mixed, grad_attn).astype(BF).reshape(groups, -1, width)
    out_slab = scatter_head(out_parts).astype(BF).reshape(blocks, w_out.shape[0], width)
    d_w_out = scatter_blk(lambda b: take(out_slab, b))
    grad_mixed = matmul_nt(grad_attn, w_o).astype(BF).reshape(tok_rows, groups, q_cols)
    grad_mix = lax.all_to_all(
        jnp.swapaxes(grad_mixed, 0, 1), "head", split_axis=0, concat_axis=0, tiled=True
    )
    grad_mix = jnp.swapaxes(grad_mix.reshape(block_len, per_group, HEAD), 0, 1)
    row_dots = jnp.sum(grad_mix.astype(F32) * attn_keep, axis=-1, keepdims=True)
    low_logs = split_low(-log_total[..., None], 3)
    low_dots = split_low(-row_dots, 2)
    blank = jnp.zeros(queries.shape, BF)
    query_t = jnp.concatenate(
        scaled + low_logs + [blank, blank[..., : HEAD - 3]], axis=-1
    )
    grad_t = jnp.concatenate([grad_mix] + low_dots + [blank[..., : HEAD - 2]], axis=-1)
    dq_t, dkv = attend_back(
        meta,
        keys_wide,
        values_wide,
        jnp.swapaxes(key_win, 1, 2),
        jnp.swapaxes(query_t, 1, 2),
        jnp.swapaxes(grad_t, 1, 2),
        jnp.concatenate([queries, blank], axis=-1),
        jnp.concatenate([blank, grad_mix], axis=-1),
        window_start[None, :],
    )
    grad_queries = jnp.transpose(dq_t, (2, 0, 1)) * SCALE

    four, three, two, one, own = [
        dkv[:, i * block_len : (i + 1) * block_len] for i in range(BACK + 1)
    ]
    got_one = swap(one.astype(BF), "blk", 1).astype(F32)
    got_three = swap(three.astype(BF), "blk", 1).astype(F32)
    four = four + jnp.where(even, 0.0, got_three)
    two = two + jnp.where(even, got_three, got_one)
    own = own + jnp.where(even, got_one, 0.0)
    two = two + ring(four.astype(BF), -2).astype(F32)
    own = own + ring(two.astype(BF), -2).astype(F32)
    kv_grad = jnp.swapaxes(own, 0, 1)
    grad_keys = kv_grad[..., :HEAD] * SCALE
    grad_values = kv_grad[..., HEAD:]

    grad_query_raw, grad_key_raw, grad_query_g, grad_key_g = prep_pull((grad_queries, grad_keys))
    raw_grads = jnp.concatenate(
        [
            grad_query_raw.reshape(block_len, q_cols),
            grad_key_raw.reshape(block_len, 2 * HEAD),
            grad_values.reshape(block_len, 2 * HEAD),
        ],
        axis=1,
    ).astype(BF)
    grad_w_in = matmul_tn(normed_one, raw_grads)
    normed_part = matmul_nt(raw_grads, w_qkv).astype(BF)
    grad_normed_one = scatter_head(normed_part.reshape(groups, tok_rows, width))
    norm_one_out, norm_one_pull = jax.vjp(norm_rows, inputs, gain_one)
    grad_input_part, grad_gain_one = norm_one_pull(grad_normed_one)
    d_tokens = grad_resid + grad_input_part
    grad_w_in = jnp.concatenate(
        [
            grad_w_in,
            grad_gain_one[:, None],
            grad_gain_two[:, None],
            jnp.zeros((width, 126), F32),
        ],
        axis=1,
    )
    owned = to_owner(by_rows(grad_w_in))
    d_w_query = owned[:, :, :q_cols].reshape(w_rows, QHEADS * HEAD)
    key_heads, value_heads = [], []
    for head_id in range(KVHEADS):
        keys_of, values_of = [], []
        for g in range(groups):
            for slot in range(2):
                if firsts[g] + slot == head_id:
                    at = q_cols + slot * HEAD
                    keys_of.append(owned[:, g, at : at + HEAD])
                    at += 2 * HEAD
                    values_of.append(owned[:, g, at : at + HEAD])
        key_heads.append(functools.reduce(jnp.add, keys_of))
        value_heads.append(functools.reduce(jnp.add, values_of))
    d_w_key = jnp.concatenate(key_heads, axis=1)
    d_w_value = jnp.concatenate(value_heads, axis=1)
    d_norm1_gain = jnp.sum(owned[:, :, qkv_cols], axis=1)
    d_norm2_gain = jnp.sum(owned[:, :, qkv_cols + 1], axis=1)
    gain_sums = lax.psum((grad_query_g, grad_key_g), ("head", "blk"))
    return (
        out_act,
        d_tokens,
        d_norm1_gain,
        d_w_query,
        d_w_key,
        d_w_value,
        gain_sums[0],
        gain_sums[1],
        d_w_out,
        d_norm2_gain,
        d_w_gate,
        d_w_up,
        d_w_down,
    )


def solution(mesh):
    by_token = P(("blk", "head"), None)
    by_row = P(("head", "blk"), None)
    by_entry = P(("head", "blk"))
    in_specs = (
        by_token,
        P(),
        by_entry,
        by_row,
        by_row,
        by_row,
        P(),
        P(),
        by_row,
        by_entry,
        by_row,
        by_row,
        by_row,
        by_token,
    )
    out_specs = (
        by_token,
        by_token,
        by_entry,
        by_row,
        by_row,
        by_row,
        P(),
        P(),
        by_row,
        by_entry,
        by_row,
        by_row,
        by_row,
    )
    return jax.shard_map(shards, mesh=mesh, in_specs=in_specs, out_specs=out_specs, check_vma=False)
```

time: 4460 us -> 1190 us (0.27)
  waiting for transfers between devices: 3410 us -> 385 us
  matrix products: 600 us -> 111 us
  starting transfers between devices: 77.2 us -> 224 us
  local copies, waits for them, and re-layouts: 101 us -> 215 us
    reduce_scatter x7 -> x0, waiting for transfers between devices: 3010 us -> none  [the longest x1 883 us: shards(): lax.psum_scatter(grad_w_up, ('head', 'blk'), scatter_dimension=0, tiled=T...]
    dot_general x60 -> x15, matrix products: 600 us -> 111 us  [the longest x5 41.2 us: matmul(): return jnp.dot(left_side, right_side, preferred_element_type=F32)]
    ppermute x13 -> x102, waiting for transfers between devices: 73.6 us -> 369 us  [the longest x34 193 us: ring(): lax.ppermute(block, 'blk', [(i, (i + step) % count) for i in range(count)])]
    all_gather x7 -> x0, waiting for transfers between devices: 283 us -> none  [the longest x1 129 us: shards(): lax.all_gather(w_down, ('head', 'blk'), axis=0, tiled=True)]
    ppermute x13 -> x102, starting transfers between devices: 61 us -> 192 us  [the longest x34 120 us: ring(): lax.ppermute(block, 'blk', [(i, (i + step) % count) for i in range(count)])]
    psum x0 -> x1, blocking collectives: none -> 81.8 us  [shards(): gain_sums = lax.psum((grad_query_g, grad_key_g), ('head', 'blk'))]
    unnamed x2 -> x0, blocking collectives: 80.7 us -> none
    dynamic_update_slice x0 -> x55, local copies, waits for them, and re-layouts: none -> 80.7 us  [put(): return lax.dynamic_update_index_in_dim(full, part, index, axis)]
  transfers between devices with their start and end apart: 31 -> 110, of which waited for: 23 -> 43; matrix products, arithmetic and copies ran while one was open for 15% -> 31% of each run, Pallas kernels for 0% -> 3%
where the time goes in v1:
time: 1190 us; the launch traced here: 1170 us
  waiting for transfers between devices  385 us (32%)
  starting transfers between devices  224 us (19%)
  local copies, waits for them, and re-layouts  215 us (18%)
  other arithmetic  111 us (9%)
  matrix products  111 us (9%)
  blocking collectives  81.8 us (7%)
  Pallas kernels  40.3 us (3%)
    ppermute x34, waiting for transfers between devices, ring(): lax.ppermute(block, 'blk', [(i, (i + step) % count) for i in range(count)])  193 us
    ppermute x68, waiting for transfers between devices, swap(): return lax.ppermute(block, axis, [(i, i ^ bit) for i in range(count)])  176 us
    ppermute x34, starting transfers between devices, ring(): lax.ppermute(block, 'blk', [(i, (i + step) % count) for i in range(count)])  120 us
    psum x1, blocking collectives, shards(): gain_sums = lax.psum((grad_query_g, grad_key_g), ('head', 'blk'))  81.8 us
    dynamic_update_slice x55, local copies, waits for them, and re-layouts, put(): return lax.dynamic_update_index_in_dim(full, part, index, axis)  80.7 us
    ppermute x68, starting transfers between devices, swap(): return lax.ppermute(block, axis, [(i, i ^ bit) for i in range(count)])  72.2 us
    dot_general x5, matrix products, matmul(): return jnp.dot(left_side, right_side, preferred_element_type=F32)  41.2 us
    dot_general x5, matrix products, matmul_nt(): lax.dot_general(left_side, right_side, (((1,), (1,)), ((), ())), preferre...  40 us
  transfers between devices with their start and end apart: 110, of which 43 were waited for; matrix products, arithmetic and copies ran while one was open for 31% of the time, Pallas kernels for 3%

profile of v1, /device:TPU:0, one launch (start us, length us, event | category | flops | bytes accessed | tf_op | source)
XLA Modules:
  0.0 1171.0 jit_solution(3580937719811071332)
XLA Ops:
  126.3 21.0 %collective-permute-done.5 = bf16[4,64,768]{2,1,0:T(8,128)(2,1)S(1)} collective-permute-done((bf16[4,64,768]{2,1,0:T(8,128)(2,1)S(1)}, bf16[4,64,768]{2,1,0:T(8,128)(2,1)S(1)}, u32[]{:S(2)}, u32[]{:S(2)}) %collective-permute-start.5) | collective-permute-done | bytes 393248 | tf_op jit(solution)/shard_map/ppermute | solution.py:44
  153.6 13.3 %collective-permute-done.28 = bf16[4,64,1280]{2,1,0:T(8,128)(2,1)S(1)} collective-permute-done((bf16[4,64,1280]{2,1,0:T(8,128)(2,1)}, bf16[4,64,1280]{2,1,0:T(8,128)(2,1)S(1)}, u32[]{:S(2)}, u32[]{:S(2)}) %collective-permute-start.28) | collective-permute-done | bytes 655392 | tf_op jit(solution)/shard_map/ppermute | solution.py:49
  170.2 10.8 collective-permute-done.44
  232.2 11.7 collective-permute-done.46
  296.2 15.6 %collective-permute-done.10 = bf16[2,1024,128]{1,2,0:T(8,128)(2,1)S(1)} collective-permute-done((bf16[2,1024,128]{1,2,0:T(8,128)(2,1)S(1)}, bf16[2,1024,128]{1,2,0:T(8,128)(2,1)S(1)}, u32[]{:S(2)}, u32[]{:S(2)}) %collective-permute-start.10) | collective-permute-done | bytes 524320 | tf_op jit(solution)/shard_map/ppermute | solution.py:49
  328.4 25.9 %collective-permute-done.12 = bf16[2,1024,128]{1,2,0:T(8,128)(2,1)S(1)} collective-permute-done((bf16[2,1024,128]{1,2,0:T(8,128)(2,1)S(1)}, bf16[2,1024,128]{1,2,0:T(8,128)(2,1)S(1)}, u32[]{:S(2)}, u32[]{:S(2)}) %collective-permute-start.12) | collective-permute-done | bytes 524320 | tf_op jit(solution)/shard_map/ppermute | solution.py:44
  356.5 10.5 fusion.89
  382.4 14.0 %attend.1 = f32[6,1024,128]{2,1,0:T(8,128)} custom-call(s32[9]{0:T(128)S(1)} %pad_add_fusion.3.meta_ref, bf16[6,1024,128]{2,1,0:T(8,128)(2,1)S(1)} %copy-done, bf16[2,5120,128]{2,1,0:T(8,128)(2,1)S(1)} %copy.388.key_ref, bf16[2,5120,128]{2,1,0:T(8,128)(2,1)} %concatenate.72.clone.value_ref, s32[1024,1]{1,0:T(8,128)S(1)} %copy.390.start_ref), custom_call_target="tpu_custom_call" | custom-call | flops 30000001024 | bytes 20000000 | tf_op jit(solution)/shard_map/attend/pallas_call | solution.py:179
  430.0 18.5 %collective-permute-done.25 = bf16[256,2048]{1,0:T(8,128)(2,1)} collective-permute-done((bf16[256,2048]{1,0:T(8,128)(2,1)S(1)}, bf16[256,2048]{1,0:T(8,128)(2,1)}, u32[]{:S(2)}, u32[]{:S(2)}) %collective-permute-start.25) | collective-permute-done | bytes 1048608 | tf_op jit(solution)/shard_map/ppermute | solution.py:44
  454.7 12.0 %concatenate.75 = bf16[6,1024,256]{2,1,0:T(8,128)(2,1)} concatenate(bf16[6,1024,64]{2,1,0:T(8,128)(2,1)} %copy-done.12, bf16[6,1024,64]{2,1,0:T(8,128)(2,1)} %copy-done.13, bf16[6,1024,1]{2,1,0:T(8,128)(2,1)} %get-tuple-element.70, bf16[6,1024,1]{2,1,0:T(8,128)(2,1)} %get-tuple-element.69, bf16[6,1024,1]{2,1,0:T(8,128)(2,1)} %get-tuple-element.68, ...), dimensions={2} | concatenate | bytes 6291456 | tf_op jit(solution)/shard_map/concatenate | solution.py:468
  478.6 9.0 fusion.88
  487.6 12.3 %multiply_convert_fusion.2 = (bf16[1024,1280]{1,0:T(8,128)(2,1)}, bf16[1024,1280]{1,0:T(8,128)(2,1)}, bf16[1024,1280]{1,0:T(8,128)(2,1)S(1)}) fusion(f32[1024,1280]{1,0:T(8,128)S(1)} %bitcast.562, f32[1024,1280]{1,0:T(8,128)S(1)} %fusion.88, bf16[1024,2048]{1,0:T(8,128)(2,1)S(1)} %bitcast.534, bf16[2048,1280]{1,0:T(8,128)(2,1)} %bitcast.73), kind=kOutput, calls=%fused_computation.9 | convolution fusion | flops 5388369920 | bytes 27787264 | tf_op jit(solution)/shard_map/dot_general | solution.py:27
  499.9 8.7 convolution_convert_fusion.2
  508.7 12.3 %fusion.90 = f32[1024,2048]{1,0:T(8,128)} fusion(bf16[1024,1280]{1,0:T(8,128)(2,1)S(1)} %copy-done.84, bf16[2048,1280]{1,0:T(8,128)(2,1)} %bitcast.90), kind=kOutput, calls=%fused_computation.327 | convolution fusion | flops 5368709120 | bytes 16252928 | tf_op jit(solution)/shard_map/dot_general | solution.py:37
  549.2 10.0 add_convert_fusion
  559.2 8.7 convolution_convert_fusion.5
  568.3 10.4 collective-permute-done.91
  581.7 24.7 %collective-permute-done.84 = bf16[4,64,1280]{2,1,0:T(8,128)(2,1)} collective-permute-done((bf16[4,64,1280]{2,1,0:T(8,128)(2,1)}, bf16[4,64,1280]{2,1,0:T(8,128)(2,1)}, u32[]{:S(2)}, u32[]{:S(2)}) %collective-permute-start.84) | collective-permute-done | bytes 655392 | tf_op jit(solution)/shard_map/ppermute | solution.py:44
  609.7 10.8 collective-permute-start.92
  620.9 28.6 %collective-permute-start.85 = (bf16[4,64,1280]{2,1,0:T(8,128)(2,1)S(1)}, bf16[4,64,1280]{2,1,0:T(8,128)(2,1)S(1)}, u32[]{:S(2)}, u32[]{:S(2)}) collective-permute-start(bf16[4,64,1280]{2,1,0:T(8,128)(2,1)S(1)} %fusion.40), channel_id=1, source_target_pairs={{0,2},{1,3},{2,4},{3,5},{4,6},{5,7},{6,0},{7,1},{8,10},{9,11},{10,... | collective-permute-start | bytes 1966088 | tf_op jit(solution)/shard_map/ppermute | solution.py:49
  650.3 13.5 %collective-permute-done.92 = bf16[4,64,1280]{2,1,0:T(8,128)(2,1)S(1)} collective-permute-done((bf16[4,64,1280]{2,1,0:T(8,128)(2,1)S(1)}, bf16[4,64,1280]{2,1,0:T(8,128)(2,1)S(1)}, u32[]{:S(2)}, u32[]{:S(2)}) %collective-permute-start.92) | collective-permute-done | bytes 655392 | tf_op jit(solution)/shard_map/ppermute | solution.py:49
  667.0 10.8 collective-permute-done.85
  681.1 10.9 collective-permute-done.99
  694.3 11.6 collective-permute-done.93
  707.7 12.3 %collective-permute-done.86 = bf16[4,64,1280]{2,1,0:T(8,128)(2,1)S(1)} collective-permute-done((bf16[4,64,1280]{2,1,0:T(8,128)(2,1)S(1)}, bf16[4,64,1280]{2,1,0:T(8,128)(2,1)S(1)}, u32[]{:S(2)}, u32[]{:S(2)}) %collective-permute-start.86) | collective-permute-done | bytes 655392 | tf_op jit(solution)/shard_map/ppermute | solution.py:49
  724.0 8.9 collective-permute-done.100
  737.7 19.3 %collective-permute-done.50 = bf16[256,2048]{1,0:T(8,128)(2,1)S(1)} collective-permute-done((bf16[256,2048]{1,0:T(8,128)(2,1)S(1)}, bf16[256,2048]{1,0:T(8,128)(2,1)S(1)}, u32[]{:S(2)}, u32[]{:S(2)}) %collective-permute-start.50) | collective-permute-done | bytes 1048608 | tf_op jit(solution)/shard_map/ppermute | solution.py:44
  784.5 11.3 collective-permute-done.87
  825.5 26.3 %attend_back.1 = (f32[6,64,1024]{2,1,0:T(8,128)}, f32[2,5120,128]{2,1,0:T(8,128)}) custom-call(s32[9]{0:T(128)} %copy-done.1, bf16[2,5120,256]{2,1,0:T(8,128)(2,1)} %maximum_maximum_fusion.key_ref, bf16[2,5120,128]{2,1,0:T(8,128)(2,1)} %concatenate.72.clone.value_ref, bf16[2,64,5120]{2,1,0:T(8,128)(2,1)} %get-tuple-element.73.key_t_ref, ...), custom_call_target="tpu_custom_call" | custom-call | flops 70000001024 | bytes 40000000 | tf_op jit(solution)/shard_map/attend_back/pallas_call | solution.py:255
  890.2 62.6 %collective-permute-start.59 = (bf16[2,1024,128]{1,2,0:T(8,128)(2,1)}, bf16[2,1024,128]{1,2,0:T(8,128)(2,1)}, u32[]{:S(2)}, u32[]{:S(2)}) collective-permute-start(bf16[2,1024,128]{1,2,0:T(8,128)(2,1)} %fusion.55), channel_id=1, source_target_pairs={{0,6},{1,7},{2,0},{3,1},{4,2},{5,3},{6,4},{7,5},{8,14},{9,15},{10,... | collective-permute-start | bytes 1572872 | tf_op jit(solution)/shard_map/ppermute | solution.py:49
  1003.7 81.8 %all-reduce.7 = (f32[64]{0:T(128)}, f32[64]{0:T(128)}) all-reduce(f32[64]{0:T(128)S(1)} %get-tuple-element.17, f32[64]{0:T(128)S(1)} %get-tuple-element.27), channel_id=1, replica_groups=mesh['head'=4,'blk'=8] {'head','blk'}, use_global_device_ids=true, to_apply=%region_16.17 | all-reduce | flops 128 | bytes 1024 | tf_op jit(solution)/shard_map/psum | solution.py:541
  1105.8 11.3 collective-permute-done.67
  (622 shorter events, 598.6 us)
Async XLA Ops:
  5.3 108.6 %collective-permute-start = (bf16[256,2048]{1,0:T(8,128)(2,1)}, bf16[256,2048]{1,0:T(8,128)(2,1)}, u32[]{:S(2)}, u32[]{:S(2)}) collective-permute-start(bf16[256,2048]{1,0:T(8,128)(2,1)} %param.14), channel_id=1, source_target_pairs={{0,8},{8,0},{16,24},{24,16},{1,9},{9,1},{17,25},{25,17},{2,10},{10... | collective-permute-start | bytes 3145736 | tf_op jit(solution)/shard_map/ppermute | solution.py:44
  5.3 113.5 %collective-permute-start.1 = (bf16[256,2048]{1,0:T(8,128)(2,1)}, bf16[256,2048]{1,0:T(8,128)(2,1)}, u32[]{:S(2)}, u32[]{:S(2)}) collective-permute-start(bf16[256,2048]{1,0:T(8,128)(2,1)} %param.14), channel_id=1, source_target_pairs={{0,16},{8,24},{16,0},{24,8},{1,17},{9,25},{17,1},{25,9},{2,18},{10... | collective-permute-start | bytes 3145736 | tf_op jit(solution)/shard_map/ppermute | solution.py:44
  14.6 73.0 %collective-permute-start.41 = (bf16[160,2048]{1,0:T(8,128)(2,1)}, bf16[160,2048]{1,0:T(8,128)(2,1)}, u32[]{:S(2)}, u32[]{:S(2)}) collective-permute-start(bf16[160,2048]{1,0:T(8,128)(2,1)} %param.26), channel_id=1, source_target_pairs={{0,1},{1,0},{2,3},{3,2},{4,5},{5,4},{6,7},{7,6},{8,9},{9,8},{10,11... | collective-permute-start | bytes 1966088 | tf_op jit(solution)/shard_map/ppermute | solution.py:44
  151.2 134.9 %collective-permute-start.21 = (bf16[8,48,2048]{2,1,0:T(8,128)(2,1)}, bf16[8,48,2048]{2,1,0:T(8,128)(2,1)}, u32[]{:S(2)}, u32[]{:S(2)}) collective-permute-start(bf16[8,48,2048]{2,1,0:T(8,128)(2,1)} %bitcast_dynamic-update-slice_fusion.48), channel_id=1, source_target_pairs={{0,8},{8,0},{16,24},{24,16},{1,9},{9,1},{17,25},{25,17},{2,10},{10... | collective-permute-start | bytes 4718600 | tf_op jit(solution)/shard_map/ppermute | solution.py:44
  152.1 136.9 %collective-permute-start.22 = (bf16[8,48,2048]{2,1,0:T(8,128)(2,1)}, bf16[8,48,2048]{2,1,0:T(8,128)(2,1)}, u32[]{:S(2)}, u32[]{:S(2)}) collective-permute-start(bf16[8,48,2048]{2,1,0:T(8,128)(2,1)} %bitcast_dynamic-update-slice_fusion.48), channel_id=1, source_target_pairs={{0,16},{8,24},{16,0},{24,8},{1,17},{9,25},{17,1},{25,9},{2,18},{10... | collective-permute-start | bytes 4718600 | tf_op jit(solution)/shard_map/ppermute | solution.py:44
  183.4 63.6 %collective-permute-start.2 = (bf16[256,2048]{1,0:T(8,128)(2,1)}, bf16[256,2048]{1,0:T(8,128)(2,1)S(1)}, u32[]{:S(2)}, u32[]{:S(2)}) collective-permute-start(bf16[256,2048]{1,0:T(8,128)(2,1)} %collective-permute-done.1), channel_id=1, source_target_pairs={{0,8},{8,0},{16,24},{24,16},{1,9},{9,1},{17,25},{25,17},{2,10},{10... | collective-permute-start | bytes 3145736 | tf_op jit(solution)/shard_map/ppermute | solution.py:44
  231.2 52.4 %collective-permute-start.53 = (bf16[256,2048]{1,0:T(8,128)(2,1)}, bf16[256,2048]{1,0:T(8,128)(2,1)}, u32[]{:S(2)}, u32[]{:S(2)}) collective-permute-start(bf16[256,2048]{1,0:T(8,128)(2,1)} %collective-permute-done.52), channel_id=1, source_target_pairs={{0,8},{8,0},{16,24},{24,16},{1,9},{9,1},{17,25},{25,17},{2,10},{10... | collective-permute-start | bytes 3145736 | tf_op jit(solution)/shard_map/ppermute | solution.py:44
  243.9 49.3 %collective-permute-start.38 = (bf16[4,64,1280]{2,1,0:T(8,128)(2,1)}, bf16[4,64,1280]{2,1,0:T(8,128)(2,1)}, u32[]{:S(2)}, u32[]{:S(2)}) collective-permute-start(bf16[4,64,1280]{2,1,0:T(8,128)(2,1)} %collective-permute-done.37), channel_id=1, source_target_pairs={{0,1},{1,0},{2,3},{3,2},{4,5},{5,4},{6,7},{7,6},{8,9},{9,8},{10,11... | collective-permute-start | bytes 1966088 | tf_op jit(solution)/shard_map/ppermute | solution.py:44
  247.0 49.2 %collective-permute-start.39 = (bf16[4,64,1280]{2,1,0:T(8,128)(2,1)}, bf16[4,64,1280]{2,1,0:T(8,128)(2,1)}, u32[]{:S(2)}, u32[]{:S(2)}) collective-permute-start(bf16[4,64,1280]{2,1,0:T(8,128)(2,1)} %collective-permute-done.37), channel_id=1, source_target_pairs={{0,2},{1,3},{2,4},{3,5},{4,6},{5,7},{6,0},{7,1},{8,10},{9,11},{10,... | collective-permute-start | bytes 1966088 | tf_op jit(solution)/shard_map/ppermute | solution.py:49
  296.2 110.2 %collective-permute-start.23 = (bf16[8,48,2048]{2,1,0:T(8,128)(2,1)}, bf16[8,48,2048]{2,1,0:T(8,128)(2,1)}, u32[]{:S(2)}, u32[]{:S(2)}) collective-permute-start(bf16[8,48,2048]{2,1,0:T(8,128)(2,1)} %collective-permute-done.22), channel_id=1, source_target_pairs={{0,8},{8,0},{16,24},{24,16},{1,9},{9,1},{17,25},{25,17},{2,10},{10... | collective-permute-start | bytes 4718600 | tf_op jit(solution)/shard_map/ppermute | solution.py:44
  314.3 52.7 %collective-permute-start.40 = (bf16[4,64,1280]{2,1,0:T(8,128)(2,1)}, bf16[4,64,1280]{2,1,0:T(8,128)(2,1)S(1)}, u32[]{:S(2)}, u32[]{:S(2)}) collective-permute-start(bf16[4,64,1280]{2,1,0:T(8,128)(2,1)} %collective-permute-done.39), channel_id=1, source_target_pairs={{0,1},{1,0},{2,3},{3,2},{4,5},{5,4},{6,7},{7,6},{8,9},{9,8},{10,11... | collective-permute-start | bytes 1966088 | tf_op jit(solution)/shard_map/ppermute | solution.py:44
  316.3 88.2 %collective-permute-start.33 = (bf16[4,64,1280]{2,1,0:T(8,128)(2,1)}, bf16[4,64,1280]{2,1,0:T(8,128)(2,1)}, u32[]{:S(2)}, u32[]{:S(2)}) collective-permute-start(bf16[4,64,1280]{2,1,0:T(8,128)(2,1)} %collective-permute-done.32), channel_id=1, source_target_pairs={{0,1},{1,0},{2,3},{3,2},{4,5},{5,4},{6,7},{7,6},{8,9},{9,8},{10,11... | collective-permute-start | bytes 1966088 | tf_op jit(solution)/shard_map/ppermute | solution.py:44
  422.7 48.7 %collective-permute-start.24 = (bf16[256,2048]{1,0:T(8,128)(2,1)S(1)}, bf16[256,2048]{1,0:T(8,128)(2,1)}, u32[]{:S(2)}, u32[]{:S(2)}) collective-permute-start(bf16[256,2048]{1,0:T(8,128)(2,1)S(1)} %get-tuple-element.34), channel_id=1, source_target_pairs={{0,8},{8,0},{16,24},{24,16},{1,9},{9,1},{17,25},{25,17},{2,10},{10... | collective-permute-start | bytes 3145736 | tf_op jit(solution)/shard_map/ppermute | solution.py:44
  530.7 49.2 %collective-permute-start.98 = (bf16[160,2048]{1,0:T(8,128)(2,1)}, bf16[160,2048]{1,0:T(8,128)(2,1)}, u32[]{:S(2)}, u32[]{:S(2)}) collective-permute-start(bf16[160,2048]{1,0:T(8,128)(2,1)} %get-tuple-element.43), channel_id=1, source_target_pairs={{0,1},{1,0},{2,3},{3,2},{4,5},{5,4},{6,7},{7,6},{8,9},{9,8},{10,11... | collective-permute-start | bytes 1966088 | tf_op jit(solution)/shard_map/ppermute | solution.py:44
  534.6 145.0 %collective-permute-start.97 = (bf16[160,2048]{1,0:T(8,128)(2,1)}, bf16[160,2048]{1,0:T(8,128)(2,1)}, u32[]{:S(2)}, u32[]{:S(2)}) collective-permute-start(bf16[160,2048]{1,0:T(8,128)(2,1)} %get-tuple-element.44), channel_id=1, source_target_pairs={{0,1},{1,0},{2,3},{3,2},{4,5},{5,4},{6,7},{7,6},{8,9},{9,8},{10,11... | collective-permute-start | bytes 1966088 | tf_op jit(solution)/shard_map/ppermute | solution.py:44
  538.0 112.0 %collective-permute-start.90 = (bf16[4,64,1280]{2,1,0:T(8,128)(2,1)}, bf16[4,64,1280]{2,1,0:T(8,128)(2,1)}, u32[]{:S(2)}, u32[]{:S(2)}) collective-permute-start(bf16[4,64,1280]{2,1,0:T(8,128)(2,1)} %get-tuple-element.47), channel_id=1, source_target_pairs={{0,1},{1,0},{2,3},{3,2},{4,5},{5,4},{6,7},{7,6},{8,9},{9,8},{10,11... | collective-permute-start | bytes 1966088 | tf_op jit(solution)/shard_map/ppermute | solution.py:44
  547.2 59.2 %collective-permute-start.84 = (bf16[4,64,1280]{2,1,0:T(8,128)(2,1)}, bf16[4,64,1280]{2,1,0:T(8,128)(2,1)}, u32[]{:S(2)}, u32[]{:S(2)}) collective-permute-start(bf16[4,64,1280]{2,1,0:T(8,128)(2,1)} %get-tuple-element.53), channel_id=1, source_target_pairs={{0,1},{1,0},{2,3},{3,2},{4,5},{5,4},{6,7},{7,6},{8,9},{9,8},{10,11... | collective-permute-start | bytes 1966088 | tf_op jit(solution)/shard_map/ppermute | solution.py:44
  606.4 59.1 %collective-permute-start.83 = (bf16[4,64,1280]{2,1,0:T(8,128)(2,1)S(1)}, bf16[4,64,1280]{2,1,0:T(8,128)(2,1)S(1)}, u32[]{:S(2)}, u32[]{:S(2)}) collective-permute-start(bf16[4,64,1280]{2,1,0:T(8,128)(2,1)S(1)} %copy-done.51), channel_id=1, source_target_pairs={{0,1},{1,0},{2,3},{3,2},{4,5},{5,4},{6,7},{7,6},{8,9},{9,8},{10,11... | collective-permute-start | bytes 1966088 | tf_op jit(solution)/shard_map/ppermute | solution.py:44
  609.7 54.2 %collective-permute-start.92 = (bf16[4,64,1280]{2,1,0:T(8,128)(2,1)S(1)}, bf16[4,64,1280]{2,1,0:T(8,128)(2,1)S(1)}, u32[]{:S(2)}, u32[]{:S(2)}) collective-permute-start(bf16[4,64,1280]{2,1,0:T(8,128)(2,1)S(1)} %fusion.33), channel_id=1, source_target_pairs={{0,2},{1,3},{2,4},{3,5},{4,6},{5,7},{6,0},{7,1},{8,10},{9,11},{10,... | collective-permute-start | bytes 1966088 | tf_op jit(solution)/shard_map/ppermute | solution.py:49
  620.9 57.0 %collective-permute-start.85 = (bf16[4,64,1280]{2,1,0:T(8,128)(2,1)S(1)}, bf16[4,64,1280]{2,1,0:T(8,128)(2,1)S(1)}, u32[]{:S(2)}, u32[]{:S(2)}) collective-permute-start(bf16[4,64,1280]{2,1,0:T(8,128)(2,1)S(1)} %fusion.40), channel_id=1, source_target_pairs={{0,2},{1,3},{2,4},{3,5},{4,6},{5,7},{6,0},{7,1},{8,10},{9,11},{10,... | collective-permute-start | bytes 1966088 | tf_op jit(solution)/shard_map/ppermute | solution.py:49
  679.6 44.3 %collective-permute-start.96 = (bf16[160,2048]{1,0:T(8,128)(2,1)S(1)}, bf16[160,2048]{1,0:T(8,128)(2,1)S(1)}, u32[]{:S(2)}, u32[]{:S(2)}) collective-permute-start(bf16[160,2048]{1,0:T(8,128)(2,1)S(1)} %get-tuple-element.45), channel_id=1, source_target_pairs={{0,1},{1,0},{2,3},{3,2},{4,5},{5,4},{6,7},{7,6},{8,9},{9,8},{10,11... | collective-permute-start | bytes 1966088 | tf_op jit(solution)/shard_map/ppermute | solution.py:44
  720.0 61.3 %collective-permute-start.95 = (bf16[160,2048]{1,0:T(8,128)(2,1)S(1)}, bf16[160,2048]{1,0:T(8,128)(2,1)}, u32[]{:S(2)}, u32[]{:S(2)}) collective-permute-start(bf16[160,2048]{1,0:T(8,128)(2,1)S(1)} %get-tuple-element.42), channel_id=1, source_target_pairs={{0,1},{1,0},{2,3},{3,2},{4,5},{5,4},{6,7},{7,6},{8,9},{9,8},{10,11... | collective-permute-start | bytes 1966088 | tf_op jit(solution)/shard_map/ppermute | solution.py:44
  736.2 48.3 %collective-permute-start.81 = (bf16[4,64,1280]{2,1,0:T(8,128)(2,1)S(1)}, bf16[4,64,1280]{2,1,0:T(8,128)(2,1)}, u32[]{:S(2)}, u32[]{:S(2)}) collective-permute-start(bf16[4,64,1280]{2,1,0:T(8,128)(2,1)S(1)} %get-tuple-element.50), channel_id=1, source_target_pairs={{0,1},{1,0},{2,3},{3,2},{4,5},{5,4},{6,7},{7,6},{8,9},{9,8},{10,11... | collective-permute-start | bytes 1966088 | tf_op jit(solution)/shard_map/ppermute | solution.py:44
  778.6 210.5 %collective-permute-start.72 = (bf16[384,2048]{1,0:T(8,128)(2,1)}, bf16[384,2048]{1,0:T(8,128)(2,1)}, u32[]{:S(2)}, u32[]{:S(2)}) collective-permute-start(bf16[384,2048]{1,0:T(8,128)(2,1)} %get-tuple-element.41), channel_id=1, source_target_pairs={{0,8},{8,0},{16,24},{24,16},{1,9},{9,1},{17,25},{25,17},{2,10},{10... | collective-permute-start | bytes 4718600 | tf_op jit(solution)/shard_map/ppermute | solution.py:44
  781.3 304.1 %collective-permute-start.71 = (bf16[384,2048]{1,0:T(8,128)(2,1)}, bf16[384,2048]{1,0:T(8,128)(2,1)}, u32[]{:S(2)}, u32[]{:S(2)}) collective-permute-start(bf16[384,2048]{1,0:T(8,128)(2,1)} %get-tuple-element.40), channel_id=1, source_target_pairs={{0,8},{8,0},{16,24},{24,16},{1,9},{9,1},{17,25},{25,17},{2,10},{10... | collective-permute-start | bytes 4718600 | tf_op jit(solution)/shard_map/ppermute | solution.py:44
  798.2 171.5 %all-to-all-start.7 = ((bf16[4,64,1280]{2,1,0:T(8,128)(2,1)}), bf16[4,64,1280]{2,1,0:T(8,128)(2,1)}, u32[]{:S(2)}, u32[]{:S(2)}) async-start(bf16[4,64,1280]{2,1,0:T(8,128)(2,1)} %fusion.39), calls=%async_computation.7 | async-start | bytes 1310720 | tf_op jit(solution)/shard_map/all_to_all | solution.py:446
  876.3 81.1 %collective-permute-start.57 = (bf16[2,1024,128]{1,2,0:T(8,128)(2,1)}, bf16[2,1024,128]{1,2,0:T(8,128)(2,1)S(1)}, u32[]{:S(2)}, u32[]{:S(2)}) collective-permute-start(bf16[2,1024,128]{1,2,0:T(8,128)(2,1)} %get-tuple-element.72), channel_id=1, source_target_pairs={{0,1},{1,0},{2,3},{3,2},{4,5},{5,4},{6,7},{7,6},{8,9},{9,8},{10,11... | collective-permute-start | bytes 1572872 | tf_op jit(solution)/shard_map/ppermute | solution.py:44
  890.2 73.5 %collective-permute-start.59 = (bf16[2,1024,128]{1,2,0:T(8,128)(2,1)}, bf16[2,1024,128]{1,2,0:T(8,128)(2,1)}, u32[]{:S(2)}, u32[]{:S(2)}) collective-permute-start(bf16[2,1024,128]{1,2,0:T(8,128)(2,1)} %fusion.55), channel_id=1, source_target_pairs={{0,6},{1,7},{2,0},{3,1},{4,2},{5,3},{6,4},{7,5},{8,14},{9,15},{10,... | collective-permute-start | bytes 1572872 | tf_op jit(solution)/shard_map/ppermute | solution.py:49
  992.0 93.4 %collective-permute-start.73 = (bf16[384,2048]{1,0:T(8,128)(2,1)S(1)}, bf16[384,2048]{1,0:T(8,128)(2,1)}, u32[]{:S(2)}, u32[]{:S(2)}) collective-permute-start(bf16[384,2048]{1,0:T(8,128)(2,1)S(1)} %fusion.6), channel_id=1, source_target_pairs={{0,16},{8,24},{16,0},{24,8},{1,17},{9,25},{17,1},{25,9},{2,18},{10... | collective-permute-start | bytes 4718600 | tf_op jit(solution)/shard_map/ppermute | solution.py:44
  994.0 100.0 %collective-permute-start.61 = (bf16[256,2048]{1,0:T(8,128)(2,1)}, bf16[256,2048]{1,0:T(8,128)(2,1)}, u32[]{:S(2)}, u32[]{:S(2)}) collective-permute-start(bf16[256,2048]{1,0:T(8,128)(2,1)} %get-tuple-element.54), channel_id=1, source_target_pairs={{0,8},{8,0},{16,24},{24,16},{1,9},{9,1},{17,25},{25,17},{2,10},{10... | collective-permute-start | bytes 3145736 | tf_op jit(solution)/shard_map/ppermute | solution.py:44
  997.6 96.6 %collective-permute-start.63 = (bf16[256,2048]{1,0:T(8,128)(2,1)}, bf16[256,2048]{1,0:T(8,128)(2,1)}, u32[]{:S(2)}, u32[]{:S(2)}) collective-permute-start(bf16[256,2048]{1,0:T(8,128)(2,1)} %fusion.18), channel_id=1, source_target_pairs={{0,16},{8,24},{16,0},{24,8},{1,17},{9,25},{17,1},{25,9},{2,18},{10... | collective-permute-start | bytes 3145736 | tf_op jit(solution)/shard_map/ppermute | solution.py:44
  1094.1 52.0 %collective-permute-start.74 = (bf16[48,2048]{1,0:T(8,128)(2,1)S(1)}, bf16[48,2048]{1,0:T(8,128)(2,1)S(1)}, u32[]{:S(2)}, u32[]{:S(2)}) collective-permute-start(bf16[48,2048]{1,0:T(8,128)(2,1)S(1)} %get-tuple-element.78), channel_id=1, source_target_pairs={{0,1},{1,0},{2,3},{3,2},{4,5},{5,4},{6,7},{7,6},{8,9},{9,8},{10,11... | collective-permute-start | bytes 589832 | tf_op jit(solution)/shard_map/ppermute | solution.py:44
  (168 other events, 4632.3 us)

commit v2 on v1

--- a/solution.py
+++ b/solution.py
@@ -78,27 +78,81 @@
     return take(terms, me).astype(F32) + got_near.astype(F32) + arrived.astype(F32)
 
 
+def place_of():
+    at = lax.axis_index("blk")
+    return at // 2, at % 2, lax.axis_size("blk") // 2
+
+
+class LineGather:
+    def __init__(self, part, axis=0):
+        self.place, _, self.line = place_of()
+        self.axis = axis
+        shape = part.shape[:axis] + (self.line,) + part.shape[axis:]
+        self.full = put(jnp.zeros(shape, part.dtype), part, self.place, axis)
+        self.held = part
+        self.step = 0
+
+    def send(self):
+        self.step += 1
+        self.held = ring(self.held, 2)
+        return self.held
+
+    def keep(self):
+        source = (self.place - self.step) % self.line
+        self.full = put(self.full, self.held, source, self.axis)
+
+    def ahead(self, steps):
+        for _ in range(steps):
+            self.send()
+            self.keep()
+
+
+class LineScatter:
+    def __init__(self, chunk):
+        self.place, _, self.line = place_of()
+        self.chunk = chunk
+        self.step = 1
+        self.total = chunk((self.place - 1) % self.line)
+
+    def send(self):
+        self.total = ring(self.total.astype(BF), 2)
+        return self.total
+
+    def add(self):
+        self.step += 1
+        mine = self.chunk((self.place - self.step) % self.line)
+        self.total = self.total.astype(F32) + mine.astype(F32)
+
+    def ahead(self, steps):
+        for _ in range(steps):
+            self.send()
+            self.add()
+
+
 def gather_blk(part, axis=0):
-    count = lax.axis_size("blk")
-    line = count // 2
-    place, side = lax.axis_index("blk") // 2, lax.axis_index("blk") % 2
-    shape = part.shape[:axis] + (count,) + part.shape[axis:]
+    place, side, line = place_of()
+    shape = part.shape[:axis] + (line, 2) + part.shape[axis:]
     full = jnp.zeros(shape, part.dtype)
     held = part
+
+    def store(full, block, source, side):
+        block = block.reshape(block.shape[:axis] + (1, 1) + block.shape[axis:])
+        at = [0] * full.ndim
+        at[axis], at[axis + 1] = source, side
+        return lax.dynamic_update_slice(full, block, at)
+
     for step in range(line):
         if step:
             held = ring(held, 2)
         other = swap(held, "blk", 1)
         source = (place - step) % line
-        full = put(full, held, 2 * source + side, axis)
-        full = put(full, other, 2 * source + 1 - side, axis)
+        full = store(full, held, source, side)
+        full = store(full, other, source, 1 - side)
     return full
 
 
 def scatter_blk(chunk):
-    count = lax.axis_size("blk")
-    line = count // 2
-    place, side = lax.axis_index("blk") // 2, lax.axis_index("blk") % 2
+    place, side, line = place_of()
     total = None
     for step in range(1, line + 1):
         target = (place - step) % line
@@ -112,6 +166,76 @@
         else:
             total = term
     return total
+
+
+def gather_pair(part):
+    me = lax.axis_index("head")
+    side = lax.axis_index("blk") % 2
+    half = part.shape[0] // 2
+    near = swap(part, "head", 1)
+    far = swap(part, "head", 2)
+    across = swap(part, "blk", 1)
+    corner = jnp.concatenate(
+        [swap(far[:half], "blk", 1), swap(across[half:], "head", 2)], axis=0
+    )
+    full = jnp.zeros((2, 4) + part.shape, part.dtype)
+
+    def store(full, block, side, head):
+        return lax.dynamic_update_slice(
+            full, block[None, None], [side, head] + [0] * part.ndim
+        )
+
+    full = store(full, part, side, me)
+    full = store(full, near, side, me ^ 1)
+    for block, to_side, to_head in (
+        (far, side, me ^ 2),
+        (across, 1 - side, me),
+        (corner, 1 - side, me ^ 2),
+    ):
+        full = store(full, block, to_side, to_head)
+        full = store(full, swap(block, "head", 1), to_side, to_head ^ 1)
+    return full
+
+
+def scatter_pair(terms):
+    me = lax.axis_index("head")
+    side = lax.axis_index("blk") % 2
+    half = terms.shape[2] // 2
+
+    def pick(to_side, to_head):
+        rest = [0] * (terms.ndim - 2)
+        return lax.dynamic_slice(
+            terms, [to_side, to_head] + rest, (1, 1) + terms.shape[2:]
+        ).reshape(terms.shape[2:])
+
+    def both(to_side, to_head):
+        got = swap(pick(to_side, to_head ^ 1), "head", 1)
+        return pick(to_side, to_head).astype(F32) + got.astype(F32)
+
+    corner = both(1 - side, me ^ 2).astype(BF)
+    top = swap(corner[:half], "blk", 1)
+    bottom = swap(corner[half:], "head", 2)
+    far = both(side, me ^ 2)
+    across = both(1 - side, me)
+    far = jnp.concatenate([far[:half] + top.astype(F32), far[half:]], axis=0)
+    across = jnp.concatenate([across[:half], across[half:] + bottom.astype(F32)], axis=0)
+    got_far = swap(far.astype(BF), "head", 2)
+    got_across = swap(across.astype(BF), "blk", 1)
+    return both(side, me) + got_far.astype(F32) + got_across.astype(F32)
+
+
+def sum_all(values):
+    for bit in (1, 2):
+        values = values + swap(values, "head", bit)
+    bit = 1
+    while bit < lax.axis_size("blk"):
+        values = values + swap(values, "blk", bit)
+        bit *= 2
+    return values
+
+
+def sync(*trees):
+    return lax.optimization_barrier(trees)
 
 
 def nt(left_side, right_side):
@@ -317,7 +441,10 @@
     per_group = QHEADS // groups
     head_ratio = QHEADS // KVHEADS
     w_rows = w_query.shape[0]
-    hidden_cols = w_gate.shape[1] // groups
+    line = blocks // 2
+    side = blk_place % 2
+    ff_rows = w_down.shape[0]
+    ff_cols = line * ff_rows
     q_cols = per_group * HEAD
     firsts = [g * per_group // head_ratio for g in range(groups)]
     odd = group_id % 2
@@ -337,17 +464,35 @@
     qkv_wide = qkv_cols + 2 * HEAD
     w_in = jnp.concatenate(columns, axis=1).reshape(w_rows, groups, qkv_wide)
     w_in = lax.all_to_all(w_in, "head", split_axis=1, concat_axis=1, tiled=True)
+    down = LineGather(w_down)
+    down.ahead(line - 4)
+    down_moved = down.send()
     w_in = gather_blk(jnp.swapaxes(w_in, 0, 1), 1).reshape(width, qkv_wide)
+    block_tokens = gather_head(tokens).reshape(block_len, width)
+
+    def by_unit(weight):
+        return weight.reshape(w_rows, groups, line, 2, ff_rows)
+
+    both = jnp.stack([by_unit(w_gate), by_unit(w_up)], axis=3)
+    both = jnp.transpose(both, (4, 1, 0, 3, 2, 5)).reshape(2, groups, w_rows, 2 * ff_cols)
+    w_in, block_tokens, both, down_moved = sync(w_in, block_tokens, both, down_moved)
+    down.held = down_moved
+    down.keep()
+
+    other = swap(take(both, 1 - side), "blk", 1)
+    both = put(jnp.zeros(both.shape, BF), take(both, side), side)
+    both = put(both, other, 1 - side)
+    both = lax.all_to_all(
+        jnp.swapaxes(both, 0, 1), "head", split_axis=0, concat_axis=0, tiled=True
+    )
+    gate_up = LineGather(both, 1)
+    gate_up.ahead(line - 4)
+    down_moved = down.send()
+    gate_up_moved = gate_up.send()
+
     w_qkv = w_in[:, :qkv_cols]
     gains = w_in[:, qkv_cols : qkv_cols + 2].astype(F32).T
     gain_one, gain_two = gains[0], gains[1]
-
-    block_tokens = gather_head(tokens).reshape(block_len, width)
-
-    def spread(weight):
-        split = weight.reshape(w_rows, groups, hidden_cols)
-        split = lax.all_to_all(split, "head", split_axis=1, concat_axis=1, tiled=True)
-        return gather_blk(jnp.swapaxes(split, 0, 1), 1).reshape(width, hidden_cols)
 
     starts = jnp.cumsum(doc_lengths) - doc_lengths
     offsets = jnp.arange(block_len, dtype=jnp.int32)
@@ -362,7 +507,7 @@
     window_start = token_start - (blk_place - BACK) * block_len
     tiles = block_len // TILE
     edges = jnp.stack(
-        [window_start[:: TILE], window_start[TILE - 1 :: TILE]], axis=1
+        [window_start[::TILE], window_start[TILE - 1 :: TILE]], axis=1
     ).reshape(2 * tiles)
     meta = jnp.concatenate([odd[None].astype(jnp.int32), edges.astype(jnp.int32)])
 
@@ -386,8 +531,13 @@
     kv_own = jnp.swapaxes(
         jnp.concatenate([key_rot.astype(BF), value_own], axis=-1), 0, 1
     )
-
-    even = blk_place % 2 == 0
+    kv_own, down_moved, gate_up_moved = sync(kv_own, down_moved, gate_up_moved)
+    down.held, gate_up.held = down_moved, gate_up_moved
+    down.keep()
+    gate_up.keep()
+
+    down_moved = down.send()
+    even = side == 0
     kv_two = ring(kv_own, 2)
     kv_one = swap(jnp.where(even, kv_own, kv_two), "blk", 1)
     kv_four = ring(kv_two, 2)
@@ -399,6 +549,14 @@
     values_wide = jnp.concatenate([value_win, ones], axis=-1)
 
     scaled = split_low(queries.astype(F32) * (SCALE * LOG2E), 2)
+    keys_wide, values_wide, down_moved, w_out, cotangent = sync(
+        keys_wide, values_wide, down_moved, w_out, cotangent
+    )
+    down.held = down_moved
+    down.keep()
+    gate_up_moved = gate_up.send()
+    top = gather_pair(cotangent).reshape(2 * block_len, width)
+    w_o = gather_blk(w_out, 0).reshape(blocks * w_out.shape[0], width)
     attended = attend(
         meta,
         jnp.concatenate(scaled, axis=-1),
@@ -406,60 +564,59 @@
         values_wide,
         window_start[:, None],
     )
+    attended, gate_up_moved, top, w_o = sync(attended, gate_up_moved, top, w_o)
+    gate_up.held = gate_up_moved
+    gate_up.keep()
+    gate_up_moved = gate_up.send()
+    w_o = gather_head(w_o).reshape(QHEADS * HEAD, width)
     attn_keep = attended[..., :HEAD]
     log_total = attended[..., HEAD]
     attn_out = jnp.swapaxes(attn_keep.astype(BF), 0, 1).reshape(groups, tok_rows, q_cols)
     mixed = lax.all_to_all(attn_out, "head", split_axis=0, concat_axis=0, tiled=True)
     mixed = jnp.swapaxes(mixed, 0, 1).reshape(tok_rows, QHEADS * HEAD)
-
-    w_o = gather_head(gather_blk(w_out, 0)).reshape(QHEADS * HEAD, width)
     inputs = tokens.astype(F32)
     resid = inputs + matmul(mixed, w_o)
     normed_two_own = norm_rows(resid, gain_two).astype(BF)
 
-    w_g, w_u = spread(w_gate), spread(w_up)
-    w_d = gather_blk(w_down, 0).reshape(hidden_cols, width)
-    top = gather_head(cotangent).reshape(block_len, width)
-    normed_two = gather_head(normed_two_own).reshape(block_len, width)
-    gate_val = matmul(normed_two, w_g)
-    up_val = matmul(normed_two, w_u)
+    normed_two = gather_pair(normed_two_own).reshape(2 * block_len, width)
+    gate_up.held = gate_up_moved
+    gate_up.keep()
+    w_gu = gate_up.full
+    w_gu = w_gu.reshape(width, 2 * ff_cols)
+    w_d = down.full.reshape(ff_cols, width)
+    gate_up_val = matmul(normed_two, w_gu)
+    gate_val, up_val = gate_up_val[:, :ff_cols], gate_up_val[:, ff_cols:]
     gate_sig = jax.nn.sigmoid(gate_val)
     gate_silu = gate_val * gate_sig
     hidden = (gate_silu * up_val).astype(BF)
-    out_part = matmul(hidden, w_d).astype(BF).reshape(groups, tok_rows, width)
-    out_act = (resid + scatter_head(out_part)).astype(BF)
+    out_part = matmul(hidden, w_d).astype(BF).reshape(2, groups, tok_rows, width)
     grad_hidden = matmul_nt(top, w_d)
     grad_gate = (grad_hidden * up_val * gate_sig * (1 + gate_val * (1 - gate_sig))).astype(BF)
     grad_up = (grad_hidden * gate_silu).astype(BF)
-    grad_part = (matmul_nt(grad_gate, w_g) + matmul_nt(grad_up, w_u)).astype(BF)
-    grad_normed = scatter_head(grad_part.reshape(groups, tok_rows, width))
+    grad_gu = jnp.concatenate([grad_gate, grad_up], axis=1)
+    grad_part = matmul_nt(grad_gu, w_gu).astype(BF)
+    grad_part, hidden, grad_gu, out_part = sync(grad_part, hidden, grad_gu, out_part)
+
+    down_parts = matmul_tn(hidden, top).astype(BF).reshape(line, ff_rows, width)
+    gu_parts = matmul_tn(normed_two, grad_gu).astype(BF)
+    gu_parts = gu_parts.reshape(groups, line, 2, w_rows, 2 * ff_cols)
+    grad_normed = scatter_pair(grad_part.reshape(2, groups, tok_rows, width))
     norm_two_out, norm_two_pull = jax.vjp(norm_rows, resid, gain_two)
     grad_resid_part, grad_gain_two = norm_two_pull(grad_normed)
     grad_resid = cotangent.astype(F32) + grad_resid_part
     grad_attn = grad_resid.astype(BF)
-
-    def by_rows(grad):
-        parts = grad.astype(BF).reshape(groups, blocks, w_rows, grad.shape[1])
-        return scatter_blk(lambda b: take(parts, b, 1))
-
-    def to_owner(grad):
-        back = lax.all_to_all(
-            grad.astype(BF), "head", split_axis=0, concat_axis=0, tiled=True
-        )
-        return jnp.swapaxes(back, 0, 1).astype(F32)
-
-    down_parts = matmul_tn(hidden, top).astype(BF).reshape(blocks, w_down.shape[0], width)
-    d_w_down = scatter_blk(lambda b: take(down_parts, b))
-    d_w_gate = to_owner(by_rows(matmul_tn(normed_two, grad_gate))).reshape(w_gate.shape)
-    d_w_up = to_owner(by_rows(matmul_tn(normed_two, grad_up))).reshape(w_up.shape)
-
-    out_parts = matmul_tn(mixed, grad_attn).astype(BF).reshape(groups, -1, width)
-    out_slab = scatter_head(out_parts).astype(BF).reshape(blocks, w_out.shape[0], width)
-    d_w_out = scatter_blk(lambda b: take(out_slab, b))
+    grad_attn, down_parts, gu_parts, out_part = sync(grad_attn, down_parts, gu_parts, out_part)
+
+    down_sum = LineScatter(lambda p: take(down_parts, p))
+    gu_sum = LineScatter(lambda p: take(gu_parts, p, 1))
+    down_sum.ahead(line - 4)
+    gu_sum.ahead(line - 4)
+    down_moved, gu_moved = down_sum.send(), gu_sum.send()
     grad_mixed = matmul_nt(grad_attn, w_o).astype(BF).reshape(tok_rows, groups, q_cols)
     grad_mix = lax.all_to_all(
         jnp.swapaxes(grad_mixed, 0, 1), "head", split_axis=0, concat_axis=0, tiled=True
     )
+    out_parts = matmul_tn(mixed, grad_attn).astype(BF).reshape(groups, -1, width)
     grad_mix = jnp.swapaxes(grad_mix.reshape(block_len, per_group, HEAD), 0, 1)
     row_dots = jnp.sum(grad_mix.astype(F32) * attn_keep, axis=-1, keepdims=True)
     low_logs = split_low(-log_total[..., None], 3)
@@ -469,34 +626,75 @@
         scaled + low_logs + [blank, blank[..., : HEAD - 3]], axis=-1
     )
     grad_t = jnp.concatenate([grad_mix] + low_dots + [blank[..., : HEAD - 2]], axis=-1)
+    query_t, grad_t = jnp.swapaxes(query_t, 1, 2), jnp.swapaxes(grad_t, 1, 2)
+    query_t, grad_t, down_moved, gu_moved, out_part, out_parts = sync(
+        query_t, grad_t, down_moved, gu_moved, out_part, out_parts
+    )
+    down_sum.total, gu_sum.total = down_moved, gu_moved
+    down_sum.add()
+    gu_sum.add()
+    down_moved, gu_moved = down_sum.send(), gu_sum.send()
+    out_act = (resid + scatter_pair(out_part)).astype(BF)
+    out_slab = scatter_head(out_parts).astype(BF).reshape(blocks, w_out.shape[0], width)
     dq_t, dkv = attend_back(
         meta,
         keys_wide,
         values_wide,
         jnp.swapaxes(key_win, 1, 2),
-        jnp.swapaxes(query_t, 1, 2),
-        jnp.swapaxes(grad_t, 1, 2),
+        query_t,
+        grad_t,
         jnp.concatenate([queries, blank], axis=-1),
         jnp.concatenate([blank, grad_mix], axis=-1),
         window_start[None, :],
     )
+    dq_t, dkv, down_moved, gu_moved, out_act, out_slab = sync(
+        dq_t, dkv, down_moved, gu_moved, out_act, out_slab
+    )
+    down_sum.total, gu_sum.total = down_moved, gu_moved
+    down_sum.add()
+    gu_sum.add()
     grad_queries = jnp.transpose(dq_t, (2, 0, 1)) * SCALE
 
     four, three, two, one, own = [
         dkv[:, i * block_len : (i + 1) * block_len] for i in range(BACK + 1)
     ]
+    got_three = swap(three.astype(BF), "blk", 1).astype(F32)
     got_one = swap(one.astype(BF), "blk", 1).astype(F32)
-    got_three = swap(three.astype(BF), "blk", 1).astype(F32)
     four = four + jnp.where(even, 0.0, got_three)
     two = two + jnp.where(even, got_three, got_one)
     own = own + jnp.where(even, got_one, 0.0)
     two = two + ring(four.astype(BF), -2).astype(F32)
     own = own + ring(two.astype(BF), -2).astype(F32)
+    down_moved, gu_moved = down_sum.send(), gu_sum.send()
+    own, down_moved, gu_moved = sync(own, down_moved, gu_moved)
+    down_sum.total, gu_sum.total = down_moved, gu_moved
+    down_sum.add()
+    gu_sum.add()
+    d_w_down = down_sum.total
     kv_grad = jnp.swapaxes(own, 0, 1)
     grad_keys = kv_grad[..., :HEAD] * SCALE
     grad_values = kv_grad[..., HEAD:]
 
+    def to_owner(grad):
+        back = lax.all_to_all(
+            grad.astype(BF), "head", split_axis=0, concat_axis=0, tiled=True
+        )
+        return jnp.swapaxes(back, 0, 1).astype(F32)
+
+    gu_own = gu_sum.total.astype(BF)
+    mine = take(gu_own, side, 1)
+    got = swap(take(gu_own, 1 - side, 1), "blk", 1)
+    gu_own = put(jnp.zeros((groups, w_rows, 2, 2 * ff_cols), BF), mine, side, 2)
+    gu_own = put(gu_own, got, 1 - side, 2)
+    gu_own = to_owner(gu_own)
+    gu_own = gu_own.reshape(w_rows, groups, 2, 2, line, ff_rows)
+    gu_own = jnp.transpose(gu_own, (3, 0, 1, 4, 2, 5)).reshape((2,) + w_gate.shape)
+    d_w_gate, d_w_up = gu_own[0], gu_own[1]
+
+    d_w_out = scatter_blk(lambda b: take(out_slab, b))
+
     grad_query_raw, grad_key_raw, grad_query_g, grad_key_g = prep_pull((grad_queries, grad_keys))
+    gain_sums = sum_all(jnp.stack([grad_query_g, grad_key_g]))
     raw_grads = jnp.concatenate(
         [
             grad_query_raw.reshape(block_len, q_cols),
@@ -520,7 +718,8 @@
         ],
         axis=1,
     )
-    owned = to_owner(by_rows(grad_w_in))
+    in_parts = grad_w_in.astype(BF).reshape(groups, blocks, w_rows, qkv_wide)
+    owned = to_owner(scatter_blk(lambda b: take(in_parts, b, 1)))
     d_w_query = owned[:, :, :q_cols].reshape(w_rows, QHEADS * HEAD)
     key_heads, value_heads = [], []
     for head_id in range(KVHEADS):
@@ -538,7 +737,6 @@
     d_w_value = jnp.concatenate(value_heads, axis=1)
     d_norm1_gain = jnp.sum(owned[:, :, qkv_cols], axis=1)
     d_norm2_gain = jnp.sum(owned[:, :, qkv_cols + 1], axis=1)
-    gain_sums = lax.psum((grad_query_g, grad_key_g), ("head", "blk"))
     return (
         out_act,
         d_tokens,

time: 1190 us -> 1100 us (0.924)
  blocking collectives: 81.8 us -> 0 us
  waiting for transfers between devices: 385 us -> 337 us
  starting transfers between devices: 224 us -> 243 us
  other arithmetic: 111 us -> 126 us
    psum x1 -> x0, blocking collectives: 81.8 us -> none  [shards(): gain_sums = lax.psum((grad_query_g, grad_key_g), ('head', 'blk'))]
    ppermute x34 -> x28, waiting for transfers between devices: 193 us -> 139 us  [ring(): lax.ppermute(block, 'blk', [(i, (i + step) % count) for i in range(count)])]
    dynamic_update_slice x55 -> x20, local copies, waits for them, and re-layouts: 80.7 us -> 36.4 us  [put(): return lax.dynamic_update_index_in_dim(full, part, index, axis)]
    optimization_barrier x0 -> x5, local copies, waits for them, and re-layouts: none -> 20.9 us  [sync(): return lax.optimization_barrier(trees)]
    ppermute x68 -> x71, starting transfers between devices: 72.2 us -> 89.9 us  [swap(): return lax.ppermute(block, axis, [(i, i ^ bit) for i in range(count)])]
    slice x0 -> x14, local copies, waits for them, and re-layouts: none -> 16.4 us  [the longest x3 11.9 us: shards(): d_w_gate, d_w_up = (gu_own[0], gu_own[1])]
    dynamic_update_slice x0 -> x31, local copies, waits for them, and re-layouts: none -> 16.1 us  [the longest x16 10.6 us: store(): return lax.dynamic_update_slice(full, block, at)]
    ppermute x34 -> x28, starting transfers between devices: 120 us -> 128 us  [ring(): lax.ppermute(block, 'blk', [(i, (i + step) % count) for i in range(count)])]
  transfers between devices with their start and end apart: 110 -> 105, of which waited for: 43 -> 42; matrix products, arithmetic and copies ran while one was open for 31% -> 32% of each run, Pallas kernels for 3% -> 4%
where the time goes in v2:
time: 1100 us; the launch traced here: 1080 us
  waiting for transfers between devices  337 us (31%)
  starting transfers between devices  243 us (22%)
  local copies, waits for them, and re-layouts  220 us (20%)
  other arithmetic  126 us (11%)
  matrix products  114 us (10%)
  Pallas kernels  40.2 us (4%)
    ppermute x71, waiting for transfers between devices, swap(): return lax.ppermute(block, axis, [(i, i ^ bit) for i in range(count)])  175 us
    ppermute x28, waiting for transfers between devices, ring(): lax.ppermute(block, 'blk', [(i, (i + step) % count) for i in range(count)])  139 us
    ppermute x28, starting transfers between devices, ring(): lax.ppermute(block, 'blk', [(i, (i + step) % count) for i in range(count)])  128 us
    ppermute x71, starting transfers between devices, swap(): return lax.ppermute(block, axis, [(i, i ^ bit) for i in range(count)])  89.9 us
    dot_general x4, matrix products, matmul_nt(): lax.dot_general(left_side, right_side, (((1,), (1,)), ((), ())), preferre...  40 us
    dot_general x4, matrix products, matmul(): return jnp.dot(left_side, right_side, preferred_element_type=F32)  37.8 us
    dynamic_update_slice x20, local copies, waits for them, and re-layouts, put(): return lax.dynamic_update_index_in_dim(full, part, index, axis)  36.4 us
    dot_general x4, matrix products, matmul_tn(): lax.dot_general(left_side, right_side, (((0,), (0,)), ((), ())), preferre...  36.3 us
  transfers between devices with their start and end apart: 105, of which 42 were waited for; matrix products, arithmetic and copies ran while one was open for 32% of the time, Pallas kernels for 4%

profile of v2, /device:TPU:0, one launch (start us, length us, event | category | flops | bytes accessed | tf_op | source)
XLA Modules:
  0.0 1083.8 jit_solution(4712287593368280223)
XLA Ops:
  58.8 9.6 collective-permute-done.5
  80.9 9.4 collective-permute-done.12
  101.0 12.2 %all-to-all-done.1 = bf16[4,2,64,1280]{3,2,1,0:T(8,128)(2,1)} async-done(((bf16[4,2,64,1280]{3,2,1,0:T(8,128)(2,1)}), bf16[4,2,64,1280]{3,2,1,0:T(8,128)(2,1)}, u32[]{:S(2)}, u32[]{:S(2)}) %all-to-all-start.1) | async-done | bytes 1310752 | tf_op jit(solution)/shard_map/all_to_all | solution.py:485
  127.7 20.5 %collective-permute-done.13 = bf16[4,2,64,1280]{3,2,1,0:T(8,128)(2,1)} collective-permute-done((bf16[4,2,64,1280]{3,2,1,0:T(8,128)(2,1)}, bf16[4,2,64,1280]{3,2,1,0:T(8,128)(2,1)}, u32[]{:S(2)}, u32[]{:S(2)}) %collective-permute-start.13) | collective-permute-done | bytes 1310752 | tf_op jit(solution)/shard_map/ppermute | solution.py:49
  149.3 13.6 %collective-permute-done.14 = bf16[2,1024,128]{1,2,0:T(8,128)(2,1)S(1)} collective-permute-done((bf16[2,1024,128]{1,2,0:T(8,128)(2,1)S(1)}, bf16[2,1024,128]{1,2,0:T(8,128)(2,1)S(1)}, u32[]{:S(2)}, u32[]{:S(2)}) %collective-permute-start.14) | collective-permute-done | bytes 524320 | tf_op jit(solution)/shard_map/ppermute | solution.py:49
  165.6 11.0 %collective-permute-done.15 = bf16[2,1024,128]{1,2,0:T(8,128)(2,1)S(1)} collective-permute-done((bf16[2,1024,128]{1,2,0:T(8,128)(2,1)S(1)}, bf16[2,1024,128]{1,2,0:T(8,128)(2,1)S(1)}, u32[]{:S(2)}, u32[]{:S(2)}) %collective-permute-start.15) | collective-permute-done | bytes 524320 | tf_op jit(solution)/shard_map/ppermute | solution.py:49
  227.9 14.0 %attend.1 = f32[6,1024,128]{2,1,0:T(8,128)} custom-call(s32[9]{0:T(128)S(1)} %pad_add_fusion.3.meta_ref, bf16[6,1024,128]{2,1,0:T(8,128)(2,1)S(1)} %pad_maximum_fusion.1.query_ref, bf16[2,5120,128]{2,1,0:T(8,128)(2,1)S(1)} %slice.276.key_ref, bf16[2,5120,128]{2,1,0:T(8,128)(2,1)} %copy.317.value_ref, s32[1024,1]{1,0:T(8,128)S(1)} %copy.303.start_ref), custom_call_target="tpu_custom_call" | custom-call | flops 30000001024 | bytes 20000000 | tf_op jit(solution)/shard_map/attend/pallas_call | solution.py:303
  243.9 30.9 %collective-permute-start.31 = (bf16[48,2048]{1,0:T(8,128)(2,1)}, bf16[48,2048]{1,0:T(8,128)(2,1)S(1)}, u32[]{:S(2)}, u32[]{:S(2)}) collective-permute-start(bf16[48,2048]{1,0:T(8,128)(2,1)} %collective-permute-done.29), channel_id=1, source_target_pairs={{0,2},{1,3},{2,4},{3,5},{4,6},{5,7},{6,0},{7,1},{8,10},{9,11},{10,... | collective-permute-start | bytes 589832 | tf_op jit(solution)/shard_map/ppermute | solution.py:49
  274.8 15.6 %collective-permute-start.30 = (bf16[48,2048]{1,0:T(8,128)(2,1)}, bf16[48,2048]{1,0:T(8,128)(2,1)S(1)}, u32[]{:S(2)}, u32[]{:S(2)}) collective-permute-start(bf16[48,2048]{1,0:T(8,128)(2,1)} %collective-permute-done.29), channel_id=1, source_target_pairs={{0,1},{1,0},{2,3},{3,2},{4,5},{5,4},{6,7},{7,6},{8,9},{9,8},{10,11... | collective-permute-start | bytes 589832 | tf_op jit(solution)/shard_map/ppermute | solution.py:44
  314.5 11.0 %collective-permute-done.25 = bf16[128,2048]{1,0:T(8,128)(2,1)S(1)} collective-permute-done((bf16[128,2048]{1,0:T(8,128)(2,1)S(1)}, bf16[128,2048]{1,0:T(8,128)(2,1)S(1)}, u32[]{:S(2)}, u32[]{:S(2)}) %collective-permute-start.25) | collective-permute-done | bytes 524320 | tf_op jit(solution)/shard_map/ppermute | solution.py:44
  348.8 20.4 %collective-permute-done.36 = bf16[384,2048]{1,0:T(8,128)(2,1)} collective-permute-done((bf16[384,2048]{1,0:T(8,128)(2,1)}, bf16[384,2048]{1,0:T(8,128)(2,1)}, u32[]{:S(2)}, u32[]{:S(2)}) %collective-permute-start.36) | collective-permute-done | bytes 1572896 | tf_op jit(solution)/shard_map/ppermute | solution.py:44
  395.2 18.9 %collective-permute-done.39 = bf16[256,2048]{1,0:T(8,128)(2,1)S(1)} collective-permute-done((bf16[256,2048]{1,0:T(8,128)(2,1)S(1)}, bf16[256,2048]{1,0:T(8,128)(2,1)S(1)}, u32[]{:S(2)}, u32[]{:S(2)}) %collective-permute-start.39) | collective-permute-done | bytes 1048608 | tf_op jit(solution)/shard_map/ppermute | solution.py:44
  417.0 10.7 collective-permute-done.43
  431.6 17.4 %fusion.87 = f32[2048,1280]{0,1:T(8,128)} fusion(bf16[2048,2048]{1,0:T(8,128)(2,1)S(1)} %bitcast.414, bf16[2048,1280]{1,0:T(8,128)(2,1)} %bitcast.89), kind=kOutput, calls=%fused_computation.328 | convolution fusion | flops 10737418240 | bytes 24117248 | tf_op jit(solution)/shard_map/dot_general | solution.py:27
  449.0 16.2 %multiply_convert_fusion.2 = (bf16[2048,640]{0,1:T(8,128)(2,1)}, bf16[2048,640]{0,1:T(8,128)(2,1)}, bf16[2048,640]{0,1:T(8,128)(2,1)}) fusion(f32[2048,1280]{0,1:T(8,128)} %fusion.87, bf16[2048,2048]{1,0:T(8,128)(2,1)} %bitcast.416, bf16[640,2048]{1,0:T(8,128)(2,1)} %bitcast.449), kind=kOutput, calls=%fused_computation.13 | convolution fusion | flops 5388369920 | bytes 29360128 | tf_op jit(solution)/shard_map/dot_general | solution.py:37
  465.2 14.6 %convolution_convert_fusion.2 = bf16[2048,2048]{1,0:T(8,128)(2,1)S(1)} fusion(bf16[2048,1280]{1,0:T(8,128)(2,1)} %bitcast.89, bf16[2048,640]{0,1:T(8,128)(2,1)} %get-tuple-element.115, bf16[2048,640]{0,1:T(8,128)(2,1)} %get-tuple-element.114), kind=kOutput, calls=%fused_computation.7 | convolution fusion | flops 10752098304 | bytes 18874368 | tf_op jit(solution)/shard_map/dot_general | solution.py:37
  488.6 9.5 convolution_convert_fusion.1
  511.6 12.0 %concatenate.99 = bf16[6,1024,256]{2,1,0:T(8,128)(2,1)} concatenate(bf16[6,1024,64]{2,1,0:T(8,128)(2,1)} %copy-done.10, bf16[6,1024,64]{2,1,0:T(8,128)(2,1)} %copy-done.9, bf16[6,1024,1]{2,1,0:T(8,128)(2,1)} %get-tuple-element.147, bf16[6,1024,1]{2,1,0:T(8,128)(2,1)} %get-tuple-element.146, bf16[6,1024,1]{2,1,0:T(8,128)(2,1)} %get-tuple-element.145, ...), dimensions={2} | concatenate | bytes 6291456 | tf_op jit(solution)/shard_map/concatenate | solution.py:625
  530.3 17.2 %convolution_convert_fusion.3 = bf16[2048,1280]{1,0:T(8,128)(2,1)} fusion(bf16[2048,2048]{1,0:T(8,128)(2,1)} %bitcast.415, bf16[2048,1280]{0,1:T(8,128)(2,1)} %pad_maximum_fusion), kind=kOutput, calls=%fused_computation.8 | convolution fusion | flops 10740039680 | bytes 18874368 | tf_op jit(solution)/shard_map/dot_general | solution.py:31
  550.1 12.4 %collective-permute-done.50 = bf16[128,2048]{1,0:T(8,128)(2,1)S(1)} collective-permute-done((bf16[128,2048]{1,0:T(8,128)(2,1)S(1)}, bf16[128,2048]{1,0:T(8,128)(2,1)S(1)}, u32[]{:S(2)}, u32[]{:S(2)}) %collective-permute-start.50) | collective-permute-done | bytes 524320 | tf_op jit(solution)/shard_map/ppermute | solution.py:44
  571.4 13.2 %collective-permute-done.54 = bf16[256,2048]{1,0:T(8,128)(2,1)S(1)} collective-permute-done((bf16[256,2048]{1,0:T(8,128)(2,1)S(1)}, bf16[256,2048]{1,0:T(8,128)(2,1)S(1)}, u32[]{:S(2)}, u32[]{:S(2)}) %collective-permute-start.54) | collective-permute-done | bytes 1048608 | tf_op jit(solution)/shard_map/ppermute | solution.py:44
  641.6 14.9 %collective-permute-done.56 = bf16[4,2,64,1280]{3,2,1,0:T(8,128)(2,1)} collective-permute-done((bf16[4,2,64,1280]{3,2,1,0:T(8,128)(2,1)}, bf16[4,2,64,1280]{3,2,1,0:T(8,128)(2,1)}, u32[]{:S(2)}, u32[]{:S(2)}) %collective-permute-start.56) | collective-permute-done | bytes 1310752 | tf_op jit(solution)/shard_map/ppermute | solution.py:49
  672.3 26.2 %attend_back.1 = (f32[6,64,1024]{2,1,0:T(8,128)}, f32[2,5120,128]{2,1,0:T(8,128)}) custom-call(s32[9]{0:T(128)} %copy-done, bf16[2,5120,256]{2,1,0:T(8,128)(2,1)} %maximum_maximum_fusion.key_ref, bf16[2,5120,128]{2,1,0:T(8,128)(2,1)} %copy.317.value_ref, bf16[2,64,5120]{2,1,0:T(8,128)(2,1)} %get-tuple-element.150.key_t_ref, ...), custom_call_target="tpu_custom_call" | custom-call | flops 70000001024 | bytes 40000000 | tf_op jit(solution)/shard_map/attend_back/pallas_call | solution.py:379
  703.7 27.1 %collective-permute-start.62 = (bf16[128,2048]{1,0:T(8,128)(2,1)S(1)}, bf16[128,2048]{1,0:T(8,128)(2,1)S(1)}, u32[]{:S(2)}, u32[]{:S(2)}) collective-permute-start(bf16[128,2048]{1,0:T(8,128)(2,1)S(1)} %get-tuple-element.159), channel_id=1, source_target_pairs={{0,1},{1,0},{2,3},{3,2},{4,5},{5,4},{6,7},{7,6},{8,9},{9,8},{10,11... | collective-permute-start | bytes 1572872 | tf_op jit(solution)/shard_map/ppermute | solution.py:44
  733.5 12.1 %collective-permute-done.65 = bf16[128,2048]{1,0:T(8,128)(2,1)S(1)} collective-permute-done((bf16[128,2048]{1,0:T(8,128)(2,1)S(1)}, bf16[128,2048]{1,0:T(8,128)(2,1)S(1)}, u32[]{:S(2)}, u32[]{:S(2)}) %collective-permute-start.65) | collective-permute-done | bytes 524320 | tf_op jit(solution)/shard_map/ppermute | solution.py:44
  749.6 51.4 %collective-permute-start.58 = (bf16[4,2,64,1280]{3,2,1,0:T(8,128)(2,1)S(1)}, bf16[4,2,64,1280]{3,2,1,0:T(8,128)(2,1)S(1)}, u32[]{:S(2)}, u32[]{:S(2)}) collective-permute-start(bf16[4,2,64,1280]{3,2,1,0:T(8,128)(2,1)S(1)} %fusion.14), channel_id=1, source_target_pairs={{0,2},{1,3},{2,4},{3,5},{4,6},{5,7},{6,0},{7,1},{8,10},{9,11},{10,... | collective-permute-start | bytes 3932168 | tf_op jit(solution)/shard_map/ppermute | solution.py:49
  801.2 18.5 %collective-permute-start.57 = (bf16[160,2048]{1,0:T(8,128)(2,1)S(1)}, bf16[160,2048]{1,0:T(8,128)(2,1)S(1)}, u32[]{:S(2)}, u32[]{:S(2)}) collective-permute-start(bf16[160,2048]{1,0:T(8,128)(2,1)S(1)} %fusion.36), channel_id=1, source_target_pairs={{0,2},{1,3},{2,4},{3,5},{4,6},{5,7},{6,0},{7,1},{8,10},{9,11},{10,... | collective-permute-start | bytes 1966088 | tf_op jit(solution)/shard_map/ppermute | solution.py:49
  823.6 17.0 %collective-permute-done.57 = bf16[160,2048]{1,0:T(8,128)(2,1)S(1)} collective-permute-done((bf16[160,2048]{1,0:T(8,128)(2,1)S(1)}, bf16[160,2048]{1,0:T(8,128)(2,1)S(1)}, u32[]{:S(2)}, u32[]{:S(2)}) %collective-permute-start.57) | collective-permute-done | bytes 655392 | tf_op jit(solution)/shard_map/ppermute | solution.py:49
  843.1 15.3 %collective-permute-start.74 = (bf16[160,2048]{1,0:T(8,128)(2,1)}, bf16[160,2048]{1,0:T(8,128)(2,1)}, u32[]{:S(2)}, u32[]{:S(2)}) collective-permute-start(bf16[160,2048]{1,0:T(8,128)(2,1)} %fusion.35), channel_id=1, source_target_pairs={{0,2},{1,3},{2,4},{3,5},{4,6},{5,7},{6,0},{7,1},{8,10},{9,11},{10,... | collective-permute-start | bytes 1966088 | tf_op jit(solution)/shard_map/ppermute | solution.py:49
  885.4 8.9 collective-permute-done.71
  904.8 34.7 %collective-permute-done.72 = bf16[2,1024,128]{1,2,0:T(8,128)(2,1)S(1)} collective-permute-done((bf16[2,1024,128]{1,2,0:T(8,128)(2,1)S(1)}, bf16[2,1024,128]{1,2,0:T(8,128)(2,1)S(1)}, u32[]{:S(2)}, u32[]{:S(2)}) %collective-permute-start.72) | collective-permute-done | bytes 524320 | tf_op jit(solution)/shard_map/ppermute | solution.py:49
  983.3 14.7 %collective-permute-done.78 = bf16[256,2048]{1,0:T(8,128)(2,1)S(1)} collective-permute-done((bf16[256,2048]{1,0:T(8,128)(2,1)S(1)}, bf16[256,2048]{1,0:T(8,128)(2,1)S(1)}, u32[]{:S(2)}, u32[]{:S(2)}) %collective-permute-start.78) | collective-permute-done | bytes 1048608 | tf_op jit(solution)/shard_map/ppermute | solution.py:44
  (621 shorter events, 529.6 us)
Async XLA Ops:
  0.7 48.4 %collective-permute-start.7 = (bf16[256,2048]{1,0:T(8,128)(2,1)}, bf16[256,2048]{1,0:T(8,128)(2,1)}, u32[]{:S(2)}, u32[]{:S(2)}) collective-permute-start(bf16[256,2048]{1,0:T(8,128)(2,1)} %param.14), channel_id=1, source_target_pairs={{0,8},{8,0},{16,24},{24,16},{1,9},{9,1},{17,25},{25,17},{2,10},{10... | collective-permute-start | bytes 3145736 | tf_op jit(solution)/shard_map/ppermute | solution.py:44
  1.2 47.8 %collective-permute-start.8 = (bf16[256,2048]{1,0:T(8,128)(2,1)}, bf16[256,2048]{1,0:T(8,128)(2,1)}, u32[]{:S(2)}, u32[]{:S(2)}) collective-permute-start(bf16[256,2048]{1,0:T(8,128)(2,1)} %param.14), channel_id=1, source_target_pairs={{0,16},{8,24},{16,0},{24,8},{1,17},{9,25},{17,1},{25,9},{2,18},{10... | collective-permute-start | bytes 3145736 | tf_op jit(solution)/shard_map/ppermute | solution.py:44
  12.2 65.7 %collective-permute-start.10 = (bf16[160,2048]{1,0:T(8,128)(2,1)}, bf16[160,2048]{1,0:T(8,128)(2,1)}, u32[]{:S(2)}, u32[]{:S(2)}) collective-permute-start(bf16[160,2048]{1,0:T(8,128)(2,1)} %param.26), channel_id=1, source_target_pairs={{0,2},{1,3},{2,4},{3,5},{4,6},{5,7},{6,0},{7,1},{8,10},{9,11},{10,... | collective-permute-start | bytes 1966088 | tf_op jit(solution)/shard_map/ppermute | solution.py:49
  80.1 47.6 %collective-permute-start.11 = (bf16[160,2048]{1,0:T(8,128)(2,1)}, bf16[160,2048]{1,0:T(8,128)(2,1)}, u32[]{:S(2)}, u32[]{:S(2)}) collective-permute-start(bf16[160,2048]{1,0:T(8,128)(2,1)} %collective-permute-done.10), channel_id=1, source_target_pairs={{0,2},{1,3},{2,4},{3,5},{4,6},{5,7},{6,0},{7,1},{8,10},{9,11},{10,... | collective-permute-start | bytes 1966088 | tf_op jit(solution)/shard_map/ppermute | solution.py:49
  113.2 35.0 %collective-permute-start.13 = (bf16[4,2,64,1280]{3,2,1,0:T(8,128)(2,1)}, bf16[4,2,64,1280]{3,2,1,0:T(8,128)(2,1)}, u32[]{:S(2)}, u32[]{:S(2)}) collective-permute-start(bf16[4,2,64,1280]{3,2,1,0:T(8,128)(2,1)} %all-to-all-done.1), channel_id=1, source_target_pairs={{0,2},{1,3},{2,4},{3,5},{4,6},{5,7},{6,0},{7,1},{8,10},{9,11},{10,... | collective-permute-start | bytes 3932168 | tf_op jit(solution)/shard_map/ppermute | solution.py:49
  196.1 132.4 %collective-permute-start.19 = (bf16[4,2,64,1280]{3,2,1,0:T(8,128)(2,1)}, bf16[4,2,64,1280]{3,2,1,0:T(8,128)(2,1)}, u32[]{:S(2)}, u32[]{:S(2)}) collective-permute-start(bf16[4,2,64,1280]{3,2,1,0:T(8,128)(2,1)} %collective-permute-done.13), channel_id=1, source_target_pairs={{0,2},{1,3},{2,4},{3,5},{4,6},{5,7},{6,0},{7,1},{8,10},{9,11},{10,... | collective-permute-start | bytes 3932168 | tf_op jit(solution)/shard_map/ppermute | solution.py:49
  215.8 58.9 %collective-permute-start.28 = (bf16[48,2048]{1,0:T(8,128)(2,1)S(1)}, bf16[48,2048]{1,0:T(8,128)(2,1)}, u32[]{:S(2)}, u32[]{:S(2)}) collective-permute-start(bf16[48,2048]{1,0:T(8,128)(2,1)S(1)} %copy-done.52), channel_id=1, source_target_pairs={{0,1},{1,0},{2,3},{3,2},{4,5},{5,4},{6,7},{7,6},{8,9},{9,8},{10,11... | collective-permute-start | bytes 589832 | tf_op jit(solution)/shard_map/ppermute | solution.py:44
  216.1 92.9 %collective-permute-start.23 = (bf16[256,2048]{1,0:T(8,128)(2,1)}, bf16[256,2048]{1,0:T(8,128)(2,1)}, u32[]{:S(2)}, u32[]{:S(2)}) collective-permute-start(bf16[256,2048]{1,0:T(8,128)(2,1)} %param.27), channel_id=1, source_target_pairs={{0,1},{1,0},{2,3},{3,2},{4,5},{5,4},{6,7},{7,6},{8,9},{9,8},{10,11... | collective-permute-start | bytes 3145736 | tf_op jit(solution)/shard_map/ppermute | solution.py:44
  217.9 93.2 %collective-permute-start.21 = (bf16[256,2048]{1,0:T(8,128)(2,1)}, bf16[256,2048]{1,0:T(8,128)(2,1)}, u32[]{:S(2)}, u32[]{:S(2)}) collective-permute-start(bf16[256,2048]{1,0:T(8,128)(2,1)} %param.27), channel_id=1, source_target_pairs={{0,16},{8,24},{16,0},{24,8},{1,17},{9,25},{17,1},{25,9},{2,18},{10... | collective-permute-start | bytes 3145736 | tf_op jit(solution)/shard_map/ppermute | solution.py:44
  243.9 49.7 %collective-permute-start.31 = (bf16[48,2048]{1,0:T(8,128)(2,1)}, bf16[48,2048]{1,0:T(8,128)(2,1)S(1)}, u32[]{:S(2)}, u32[]{:S(2)}) collective-permute-start(bf16[48,2048]{1,0:T(8,128)(2,1)} %collective-permute-done.29), channel_id=1, source_target_pairs={{0,2},{1,3},{2,4},{3,5},{4,6},{5,7},{6,0},{7,1},{8,10},{9,11},{10,... | collective-permute-start | bytes 589832 | tf_op jit(solution)/shard_map/ppermute | solution.py:49
  331.7 37.6 %collective-permute-start.36 = (bf16[384,2048]{1,0:T(8,128)(2,1)}, bf16[384,2048]{1,0:T(8,128)(2,1)}, u32[]{:S(2)}, u32[]{:S(2)}) collective-permute-start(bf16[384,2048]{1,0:T(8,128)(2,1)} %bitcast.59), channel_id=1, source_target_pairs={{0,16},{8,24},{16,0},{24,8},{1,17},{9,25},{17,1},{25,9},{2,18},{10... | collective-permute-start | bytes 4718600 | tf_op jit(solution)/shard_map/ppermute | solution.py:44
  335.3 40.0 %collective-permute-start.35 = (bf16[384,2048]{1,0:T(8,128)(2,1)}, bf16[384,2048]{1,0:T(8,128)(2,1)}, u32[]{:S(2)}, u32[]{:S(2)}) collective-permute-start(bf16[384,2048]{1,0:T(8,128)(2,1)} %bitcast.59), channel_id=1, source_target_pairs={{0,8},{8,0},{16,24},{24,16},{1,9},{9,1},{17,25},{25,17},{2,10},{10... | collective-permute-start | bytes 4718600 | tf_op jit(solution)/shard_map/ppermute | solution.py:44
  339.4 53.3 %collective-permute-start.46 = (bf16[4,2,64,1280]{3,2,1,0:T(8,128)(2,1)}, bf16[4,2,64,1280]{3,2,1,0:T(8,128)(2,1)}, u32[]{:S(2)}, u32[]{:S(2)}) collective-permute-start(bf16[4,2,64,1280]{3,2,1,0:T(8,128)(2,1)} %collective-permute-done.19), channel_id=1, source_target_pairs={{0,2},{1,3},{2,4},{3,5},{4,6},{5,7},{6,0},{7,1},{8,10},{9,11},{10,... | collective-permute-start | bytes 3932168 | tf_op jit(solution)/shard_map/ppermute | solution.py:49
  344.4 37.7 %all-to-all-start.2 = ((bf16[4,256,384]{2,1,0:T(8,128)(2,1)}), bf16[4,256,384]{2,1,0:T(8,128)(2,1)}, u32[]{:S(2)}, u32[]{:S(2)}) async-start(bf16[4,256,384]{2,1,0:T(8,128)(2,1)} %copy.305), calls=%async_computation.2 | async-start | bytes 1572864 | tf_op jit(solution)/shard_map/all_to_all | solution.py:575
  549.4 35.2 %collective-permute-start.54 = (bf16[256,2048]{1,0:T(8,128)(2,1)S(1)}, bf16[256,2048]{1,0:T(8,128)(2,1)S(1)}, u32[]{:S(2)}, u32[]{:S(2)}) collective-permute-start(bf16[256,2048]{1,0:T(8,128)(2,1)S(1)} %pad_maximum_fusion.4), channel_id=1, source_target_pairs={{0,1},{1,0},{2,3},{3,2},{4,5},{5,4},{6,7},{7,6},{8,9},{9,8},{10,11... | collective-permute-start | bytes 3145736 | tf_op jit(solution)/shard_map/ppermute | solution.py:44
  611.8 44.8 %collective-permute-start.56 = (bf16[4,2,64,1280]{3,2,1,0:T(8,128)(2,1)}, bf16[4,2,64,1280]{3,2,1,0:T(8,128)(2,1)}, u32[]{:S(2)}, u32[]{:S(2)}) collective-permute-start(bf16[4,2,64,1280]{3,2,1,0:T(8,128)(2,1)} %dynamic-slice_bitcast_fusion.2), channel_id=1, source_target_pairs={{0,2},{1,3},{2,4},{3,5},{4,6},{5,7},{6,0},{7,1},{8,10},{9,11},{10,... | collective-permute-start | bytes 3932168 | tf_op jit(solution)/shard_map/ppermute | solution.py:49
  667.3 155.4 %collective-permute-start.67 = (bf16[384,2048]{1,0:T(8,128)(2,1)}, bf16[384,2048]{1,0:T(8,128)(2,1)S(1)}, u32[]{:S(2)}, u32[]{:S(2)}) collective-permute-start(bf16[384,2048]{1,0:T(8,128)(2,1)} %get-tuple-element.131), channel_id=1, source_target_pairs={{0,8},{8,0},{16,24},{24,16},{1,9},{9,1},{17,25},{25,17},{2,10},{10... | collective-permute-start | bytes 4718600 | tf_op jit(solution)/shard_map/ppermute | solution.py:44
  667.3 65.2 %collective-permute-start.68 = (bf16[384,2048]{1,0:T(8,128)(2,1)S(1)}, bf16[384,2048]{1,0:T(8,128)(2,1)S(1)}, u32[]{:S(2)}, u32[]{:S(2)}) collective-permute-start(bf16[384,2048]{1,0:T(8,128)(2,1)S(1)} %get-tuple-element.132), channel_id=1, source_target_pairs={{0,8},{8,0},{16,24},{24,16},{1,9},{9,1},{17,25},{25,17},{2,10},{10... | collective-permute-start | bytes 4718600 | tf_op jit(solution)/shard_map/ppermute | solution.py:44
  698.5 51.1 %collective-permute-start.59 = (bf16[256,2048]{1,0:T(8,128)(2,1)S(1)}, bf16[256,2048]{1,0:T(8,128)(2,1)S(1)}, u32[]{:S(2)}, u32[]{:S(2)}) collective-permute-start(bf16[256,2048]{1,0:T(8,128)(2,1)S(1)} %get-tuple-element.117), channel_id=1, source_target_pairs={{0,8},{8,0},{16,24},{24,16},{1,9},{9,1},{17,25},{25,17},{2,10},{10... | collective-permute-start | bytes 3145736 | tf_op jit(solution)/shard_map/ppermute | solution.py:44
  703.7 42.2 %collective-permute-start.62 = (bf16[128,2048]{1,0:T(8,128)(2,1)S(1)}, bf16[128,2048]{1,0:T(8,128)(2,1)S(1)}, u32[]{:S(2)}, u32[]{:S(2)}) collective-permute-start(bf16[128,2048]{1,0:T(8,128)(2,1)S(1)} %get-tuple-element.159), channel_id=1, source_target_pairs={{0,1},{1,0},{2,3},{3,2},{4,5},{5,4},{6,7},{7,6},{8,9},{9,8},{10,11... | collective-permute-start | bytes 1572872 | tf_op jit(solution)/shard_map/ppermute | solution.py:44
  733.1 89.6 %collective-permute-start.69 = (bf16[384,2048]{1,0:T(8,128)(2,1)S(1)}, bf16[384,2048]{1,0:T(8,128)(2,1)S(1)}, u32[]{:S(2)}, u32[]{:S(2)}) collective-permute-start(bf16[384,2048]{1,0:T(8,128)(2,1)S(1)} %fusion.9), channel_id=1, source_target_pairs={{0,16},{8,24},{16,0},{24,8},{1,17},{9,25},{17,1},{25,9},{2,18},{10... | collective-permute-start | bytes 4718600 | tf_op jit(solution)/shard_map/ppermute | solution.py:44
  745.8 55.3 %collective-permute-start.66 = (bf16[256,2048]{1,0:T(8,128)(2,1)S(1)}, bf16[256,2048]{1,0:T(8,128)(2,1)S(1)}, u32[]{:S(2)}, u32[]{:S(2)}) collective-permute-start(bf16[256,2048]{1,0:T(8,128)(2,1)S(1)} %pad_maximum_fusion.6), channel_id=1, source_target_pairs={{0,1},{1,0},{2,3},{3,2},{4,5},{5,4},{6,7},{7,6},{8,9},{9,8},{10,11... | collective-permute-start | bytes 3145736 | tf_op jit(solution)/shard_map/ppermute | solution.py:44
  746.2 73.6 %collective-permute-start.63 = (bf16[256,2048]{1,0:T(8,128)(2,1)S(1)}, bf16[256,2048]{1,0:T(8,128)(2,1)S(1)}, u32[]{:S(2)}, u32[]{:S(2)}) collective-permute-start(bf16[256,2048]{1,0:T(8,128)(2,1)S(1)} %pad_maximum_fusion.5), channel_id=1, source_target_pairs={{0,16},{8,24},{16,0},{24,8},{1,17},{9,25},{17,1},{25,9},{2,18},{10... | collective-permute-start | bytes 3145736 | tf_op jit(solution)/shard_map/ppermute | solution.py:44
  749.6 91.1 %collective-permute-start.58 = (bf16[4,2,64,1280]{3,2,1,0:T(8,128)(2,1)S(1)}, bf16[4,2,64,1280]{3,2,1,0:T(8,128)(2,1)S(1)}, u32[]{:S(2)}, u32[]{:S(2)}) collective-permute-start(bf16[4,2,64,1280]{3,2,1,0:T(8,128)(2,1)S(1)} %fusion.14), channel_id=1, source_target_pairs={{0,2},{1,3},{2,4},{3,5},{4,6},{5,7},{6,0},{7,1},{8,10},{9,11},{10,... | collective-permute-start | bytes 3932168 | tf_op jit(solution)/shard_map/ppermute | solution.py:49
  801.2 39.5 %collective-permute-start.57 = (bf16[160,2048]{1,0:T(8,128)(2,1)S(1)}, bf16[160,2048]{1,0:T(8,128)(2,1)S(1)}, u32[]{:S(2)}, u32[]{:S(2)}) collective-permute-start(bf16[160,2048]{1,0:T(8,128)(2,1)S(1)} %fusion.36), channel_id=1, source_target_pairs={{0,2},{1,3},{2,4},{3,5},{4,6},{5,7},{6,0},{7,1},{8,10},{9,11},{10,... | collective-permute-start | bytes 1966088 | tf_op jit(solution)/shard_map/ppermute | solution.py:49
  843.1 111.7 %collective-permute-start.74 = (bf16[160,2048]{1,0:T(8,128)(2,1)}, bf16[160,2048]{1,0:T(8,128)(2,1)}, u32[]{:S(2)}, u32[]{:S(2)}) collective-permute-start(bf16[160,2048]{1,0:T(8,128)(2,1)} %fusion.35), channel_id=1, source_target_pairs={{0,2},{1,3},{2,4},{3,5},{4,6},{5,7},{6,0},{7,1},{8,10},{9,11},{10,... | collective-permute-start | bytes 1966088 | tf_op jit(solution)/shard_map/ppermute | solution.py:49
  859.6 36.3 %collective-permute-start.93 = (bf16[48,2048]{1,0:T(8,128)(2,1)S(1)}, bf16[48,2048]{1,0:T(8,128)(2,1)S(1)}, u32[]{:S(2)}, u32[]{:S(2)}) collective-permute-start(bf16[48,2048]{1,0:T(8,128)(2,1)S(1)} %get-tuple-element.155), channel_id=1, source_target_pairs={{0,1},{1,0},{2,3},{3,2},{4,5},{5,4},{6,7},{7,6},{8,9},{9,8},{10,11... | collective-permute-start | bytes 589832 | tf_op jit(solution)/shard_map/ppermute | solution.py:44
  895.7 43.8 %collective-permute-start.72 = (bf16[2,1024,128]{1,2,0:T(8,128)(2,1)S(1)}, bf16[2,1024,128]{1,2,0:T(8,128)(2,1)S(1)}, u32[]{:S(2)}, u32[]{:S(2)}) collective-permute-start(bf16[2,1024,128]{1,2,0:T(8,128)(2,1)S(1)} %fusion.45), channel_id=1, source_target_pairs={{0,6},{1,7},{2,0},{3,1},{4,2},{5,3},{6,4},{7,5},{8,14},{9,15},{10,... | collective-permute-start | bytes 1572872 | tf_op jit(solution)/shard_map/ppermute | solution.py:49
  895.8 51.8 %collective-permute-start.92 = (bf16[48,2048]{1,0:T(8,128)(2,1)}, bf16[48,2048]{1,0:T(8,128)(2,1)}, u32[]{:S(2)}, u32[]{:S(2)}) collective-permute-start(bf16[48,2048]{1,0:T(8,128)(2,1)} %get-tuple-element.156), channel_id=1, source_target_pairs={{0,1},{1,0},{2,3},{3,2},{4,5},{5,4},{6,7},{7,6},{8,9},{9,8},{10,11... | collective-permute-start | bytes 589832 | tf_op jit(solution)/shard_map/ppermute | solution.py:44
  896.2 58.6 %collective-permute-start.75 = (bf16[4,2,64,1280]{3,2,1,0:T(8,128)(2,1)}, bf16[4,2,64,1280]{3,2,1,0:T(8,128)(2,1)}, u32[]{:S(2)}, u32[]{:S(2)}) collective-permute-start(bf16[4,2,64,1280]{3,2,1,0:T(8,128)(2,1)} %fusion.13), channel_id=1, source_target_pairs={{0,2},{1,3},{2,4},{3,5},{4,6},{5,7},{6,0},{7,1},{8,10},{9,11},{10,... | collective-permute-start | bytes 3932168 | tf_op jit(solution)/shard_map/ppermute | solution.py:49
  904.5 43.3 %collective-permute-start.96 = (bf16[48,2048]{1,0:T(8,128)(2,1)}, bf16[48,2048]{1,0:T(8,128)(2,1)}, u32[]{:S(2)}, u32[]{:S(2)}) collective-permute-start(bf16[48,2048]{1,0:T(8,128)(2,1)} %fusion.60), channel_id=1, source_target_pairs={{0,2},{1,3},{2,4},{3,5},{4,6},{5,7},{6,0},{7,1},{8,10},{9,11},{10,... | collective-permute-start | bytes 589832 | tf_op jit(solution)/shard_map/ppermute | solution.py:49
  982.7 39.2 %collective-permute-start.90 = (f32[2,64]{1,0:T(2,128)S(1)}, f32[2,64]{1,0:T(2,128)}, u32[]{:S(2)}, u32[]{:S(2)}) collective-permute-start(f32[2,64]{1,0:T(2,128)S(1)} %add.693), channel_id=1, source_target_pairs={{0,4},{1,5},{2,6},{3,7},{4,0},{5,1},{6,2},{7,3},{8,12},{9,13},{10,... | collective-permute-start | bytes 1544 | tf_op jit(solution)/shard_map/ppermute | solution.py:44
  (156 other events, 3416.5 us)

commit v3 on v2

--- a/solution.py
+++ b/solution.py
@@ -391,6 +391,493 @@
         ),
         name="attend_back",
     )(meta, keys, values, keys_t, queries_t, grads_t, queries, grads, starts)
+
+
+MESH = pl.DeviceIdType.MESH
+HEADS_OUT, SLAB, NEAR, FAR, ACROSS, FAR_ON, ACROSS_ON = 0, 3, 7, 8, 9, 10, 11
+CORNER_TOP, CORNER_LOW, CORNER_ON, TO_MATE = 12, 13, 14, 15
+BACK_TOP, BACK_LOW, BACK_FAR, BACK_ACROSS, HEADS_BACK, SUM_ON = 19, 20, 21, 22, 23, 26
+TRANSFERS = 30
+SPANS = ((0, 256), (256, 256), (512, 128))
+
+
+def transposed(block):
+    return jnp.swapaxes(block, 0, 1)
+
+
+def middle_kernel(
+    slabs,
+    line,
+    attn_ref,
+    tokens_ref,
+    w_out_ref,
+    gain_ref,
+    w_down_ref,
+    top_ref,
+    *refs,
+):
+    slab_refs = refs[:slabs]
+    (
+        resid_out,
+        grad_out,
+        grad_low_out,
+        mixed_out,
+        heads_out,
+        part_out,
+        gu_out,
+        gu_next,
+        down_out,
+        gain_out,
+        mixed,
+        acts,
+        tops,
+        w_gu,
+        w_dn,
+        hidden,
+        grad_gu,
+        pairs,
+        got,
+        stage,
+        in_far,
+        in_across,
+        in_top,
+        in_low,
+        resid,
+        turned,
+        gu_stage,
+        sends,
+        recvs,
+        locals_,
+    ) = refs[slabs:]
+    me, at = lax.axis_index("head"), lax.axis_index("blk")
+    count = lax.axis_size("blk")
+    side, place = at % 2, at // 2
+    odd = me % 2
+    mate, beside, corner = me + 1 - 2 * odd, (me + 2) % 4, (me + 3 - 2 * odd) % 4
+    other = at + 1 - 2 * side
+    after, before = (at + 2) % count, (at + count - 2) % count
+    rows, width = tokens_ref.shape
+    half = rows // 2
+    cols = mixed.shape[1] // 4
+    units = w_dn.shape[0]
+    slab_rows = slab_refs[0].shape[1]
+
+    barrier = pltpu.get_barrier_semaphore()
+    peers = ((mate, at), (beside, at), (corner, at), (me, other), (me, after), (me, before))
+    for peer in peers:
+        pl.semaphore_signal(barrier, inc=1, device_id=peer, device_id_type=MESH)
+    pl.semaphore_wait(barrier, len(peers))
+
+    def remote(index, source, target, device):
+        return pltpu.make_async_remote_copy(
+            src_ref=source,
+            dst_ref=target,
+            send_sem=sends.at[index],
+            recv_sem=recvs.at[index],
+            device_id=device,
+            device_id_type=MESH,
+        )
+
+    def local(index, source, target):
+        return pltpu.make_async_copy(source, target, locals_.at[index])
+
+    def mixed_cols(head):
+        return mixed.at[:, pl.ds(pl.multiple_of(head * cols, 128), cols)]
+
+    heads = [
+        remote(HEADS_OUT + i, attn_ref.at[to], mixed_cols(me), (to, at))
+        for i, to in enumerate((mate, beside, corner))
+    ]
+    for copy in heads:
+        copy.start()
+    own_heads = local(0, attn_ref.at[me], mixed_cols(me))
+    own_heads.start()
+    load_out = [
+        local(1 + i, w_out_ref.at[pl.ds(i * rows, rows)], pairs.at[i]) for i in range(6)
+    ]
+    for copy in load_out:
+        copy.start()
+
+    def slab_at(head, source):
+        start = pl.multiple_of((head * line + source) * slab_rows, 16)
+        return w_gu.at[pl.ds(start, slab_rows)]
+
+    last = (place + line - (slabs - 1)) % line
+    slab_on = [
+        remote(SLAB + h, slab_refs[-1].at[h], slab_at(h, last), (me, after)) for h in range(4)
+    ]
+    for copy in slab_on:
+        copy.start()
+    load_slabs = [
+        local(7 + 4 * i + h, ref.at[h], slab_at(h, (place + line - i) % line))
+        for i, ref in enumerate(slab_refs)
+        for h in range(4)
+    ]
+    for copy in load_slabs:
+        copy.start()
+    base_sem = 7 + 4 * slabs
+    load_down = local(base_sem, w_down_ref, w_dn)
+    load_down.start()
+    load_top = local(base_sem + 1, top_ref, tops)
+    load_top.start()
+
+    for copy in heads:
+        copy.wait_recv()
+    own_heads.wait()
+    for copy in load_out:
+        copy.wait()
+    keep_mixed = local(base_sem + 2, mixed, mixed_out)
+    keep_mixed.start()
+
+    def resid_cols(step, carry):
+        span = pl.ds(pl.multiple_of(step * 256, 256), 256)
+        weight = pairs[0:6, :, span].reshape(6 * rows, 256)
+        resid[:, span] = tokens_ref[:, span].astype(F32) + nn(mixed[...], weight)
+        return carry
+
+    lax.fori_loop(0, width // 256, resid_cols, 0)
+    slot = side * 4 + me
+
+    def norm_tile(step, carry):
+        tile = pl.ds(pl.multiple_of(step * 32, 32), 32)
+        block = resid[tile, :]
+        scale = lax.rsqrt(jnp.mean(block * block, axis=1, keepdims=True) + EPS)
+        acts[slot, tile, :] = (block * scale * gain_ref[...]).astype(BF)
+        return carry
+
+    lax.fori_loop(0, rows // 32, norm_tile, 0)
+    keep_resid = local(base_sem + 3, resid, resid_out)
+    keep_resid.start()
+
+    far_slot, across_slot = side * 4 + beside, (1 - side) * 4 + me
+    corner_slot = (1 - side) * 4 + beside
+    near = remote(NEAR, acts.at[slot], acts.at[slot], (mate, at))
+    far = remote(FAR, acts.at[slot], acts.at[slot], (beside, at))
+    across = remote(ACROSS, acts.at[slot], acts.at[slot], (me, other))
+    far_on = remote(FAR_ON, acts.at[far_slot], acts.at[far_slot], (mate, at))
+    across_on = remote(ACROSS_ON, acts.at[across_slot], acts.at[across_slot], (mate, at))
+    corner_on = remote(CORNER_ON, acts.at[corner_slot], acts.at[corner_slot], (mate, at))
+    far_top = acts.at[far_slot, pl.ds(0, half)]
+    across_low = acts.at[across_slot, pl.ds(half, half)]
+    corner_top = remote(CORNER_TOP, far_top, far_top, (me, other))
+    corner_low = remote(CORNER_LOW, across_low, across_low, (beside, at))
+    near.start()
+    far.start()
+    across.start()
+    for copy in load_slabs:
+        copy.wait()
+    for copy in slab_on:
+        copy.wait_recv()
+    load_down.wait()
+    load_top.wait()
+
+    def chunk(c, carry):
+        its_side = (side + c // 2) % 2
+        its_head = (me + 2 * (c % 2)) % 4
+        pair = its_side * 4 + its_head - its_head % 2
+
+        @pl.when(c == 0)
+        def _():
+            near.wait_recv()
+
+        @pl.when(c == 1)
+        def _():
+            far.wait_recv()
+            far_on.start()
+            corner_top.start()
+            across.wait_recv()
+            across_on.start()
+            corner_low.start()
+            far_on.wait_recv()
+
+        @pl.when(c == 2)
+        def _():
+            corner_top.wait_recv()
+            corner_low.wait_recv()
+            corner_on.start()
+            across_on.wait_recv()
+
+        @pl.when(c == 3)
+        def _():
+            corner_on.wait_recv()
+
+        for first, size in SPANS:
+            block = acts[pl.ds(pair, 2)].reshape(2 * rows, width)
+            gate = nn(block, w_gu[:, first : first + size])
+            up = nn(block, w_gu[:, units + first : units + first + size])
+            grad = nt(
+                tops[pl.ds(pair, 2)].reshape(2 * rows, width), w_dn[first : first + size, :]
+            )
+            sig = jax.nn.sigmoid(gate)
+            silu = gate * sig
+            shape = (2, rows, size)
+            hidden[pl.ds(pair, 2), :, first : first + size] = (
+                (silu * up).astype(BF).reshape(shape)
+            )
+            grad_gu[pl.ds(pair, 2), :, first : first + size] = (
+                (grad * up * sig * (1 + gate * (1 - sig))).astype(BF).reshape(shape)
+            )
+            grad_gu[pl.ds(pair, 2), :, units + first : units + first + size] = (
+                (grad * silu).astype(BF).reshape(shape)
+            )
+
+        def grad_cols(step, carry):
+            span = pl.ds(pl.multiple_of(step * 256, 256), 256)
+            block = grad_gu[pl.ds(pair, 2)].reshape(2 * rows, 2 * units)
+            part = nt(block, w_gu[span, :])
+            pairs[pl.ds(2 * c, 2), :, span] = part.astype(BF).reshape(2, rows, 256)
+            return carry
+
+        lax.fori_loop(0, width // 256, grad_cols, 0)
+        remote(TO_MATE + c, pairs.at[2 * c + 1 - odd], got.at[c], (mate, at)).start()
+
+        @pl.when(c > 0)
+        def _():
+            local(base_sem + 4, stage, part_out.at[pl.ds(0, 2)]).wait()
+
+        def out_cols(step, carry):
+            span = pl.ds(pl.multiple_of(step * 256, 256), 256)
+            block = hidden[pl.ds(pair, 2)].reshape(2 * rows, units)
+            part = nn(block, w_dn[:, span])
+            stage[:, :, span] = part.astype(BF).reshape(2, rows, 256)
+            return carry
+
+        lax.fori_loop(0, width // 256, out_cols, 0)
+        local(base_sem + 4, stage, part_out.at[pl.ds(pair, 2)]).start()
+        return carry
+
+    lax.fori_loop(0, 4, chunk, 0)
+
+    def to_mate(c):
+        return remote(TO_MATE + c, pairs.at[2 * c + 1 - odd], got.at[c], (mate, at))
+
+    def add_rows(c, first, extra):
+        def tile(step, carry):
+            span = pl.ds(pl.multiple_of(first + step * 32, 32), 32)
+            total = pairs[2 * c + odd, span, :].astype(F32) + got[c, span, :].astype(F32)
+            for ref in extra:
+                total = total + ref[pl.ds(pl.multiple_of(step * 32, 32), 32), :].astype(F32)
+            pairs[2 * c + odd, span, :] = total.astype(BF)
+            return carry
+
+        lax.fori_loop(0, half // 32, tile, 0)
+
+    back_top = remote(
+        BACK_TOP, pairs.at[6 + odd, pl.ds(0, half)], in_top, (me, other)
+    )
+    back_low = remote(
+        BACK_LOW, pairs.at[6 + odd, pl.ds(half, half)], in_low, (beside, at)
+    )
+    back_far = remote(BACK_FAR, pairs.at[2 + odd], in_far, (beside, at))
+    back_across = remote(BACK_ACROSS, pairs.at[4 + odd], in_across, (me, other))
+    to_mate(3).wait_recv()
+    add_rows(3, 0, ())
+    back_top.start()
+    add_rows(3, half, ())
+    back_low.start()
+    to_mate(1).wait_recv()
+    to_mate(2).wait_recv()
+    add_rows(1, half, ())
+    add_rows(2, 0, ())
+
+    local(base_sem + 4, stage, part_out.at[pl.ds(0, 2)]).wait()
+
+    def gu_rows(step, carry):
+        span = pl.ds(pl.multiple_of(step * 256, 256), 256)
+        turned[...] = transposed(acts[:, :, span].reshape(8 * rows, 256))
+        buffer = step % 2
+
+        @pl.when(step > 1)
+        def _():
+            local(base_sem + 5 + buffer, gu_stage.at[buffer], gu_out.at[pl.ds(0, 256)]).wait()
+
+        for n in range(2 * units // 256):
+            part = nn(
+                turned[...],
+                grad_gu[:, :, n * 256 : (n + 1) * 256].reshape(8 * rows, 256),
+            )
+            gu_stage[buffer, :, n * 256 : (n + 1) * 256] = part.astype(BF)
+        local(base_sem + 5 + buffer, gu_stage.at[buffer], gu_out.at[span]).start()
+        return carry
+
+    lax.fori_loop(0, 5, gu_rows, 0)
+    back_top.wait_recv()
+    add_rows(1, 0, (in_top,))
+    back_far.start()
+    back_low.wait_recv()
+    add_rows(2, half, (in_low,))
+    back_across.start()
+    lax.fori_loop(5, width // 256, gu_rows, 0)
+    for buffer in range(2):
+        local(base_sem + 5 + buffer, gu_stage.at[buffer], gu_out.at[pl.ds(0, 256)]).wait()
+
+    target = (place + line - 1) % line
+    sum_on = [
+        remote(
+            SUM_ON + h,
+            gu_out.at[pl.ds(pl.multiple_of((h * line + target) * slab_rows, 16), slab_rows)],
+            gu_next.at[h],
+            (me, after),
+        )
+        for h in range(4)
+    ]
+    for copy in sum_on:
+        copy.start()
+
+    for copy in (near, far, across, far_on, across_on, corner_on, corner_top, corner_low):
+        copy.wait_send()
+    load_again = [
+        local(1 + i, w_out_ref.at[pl.ds(i * rows, rows)], acts.at[i]) for i in range(6)
+    ]
+    for copy in load_again:
+        copy.start()
+
+    for i, (first, size) in enumerate(SPANS):
+        turned[0:size, :] = transposed(
+            hidden[:, :, first : first + size].reshape(8 * rows, size)
+        )
+        buffer = i % 2
+        if i > 1:
+            local(base_sem + 7, stage.at[0], down_out.at[pl.ds(0, rows)]).wait()
+
+        def down_cols(step, carry):
+            span = pl.ds(pl.multiple_of(step * 256, 256), 256)
+            part = nn(turned[0:size, :], tops[:, :, span].reshape(8 * rows, 256))
+            stage[buffer, 0:size, span] = part.astype(BF)
+            return carry
+
+        lax.fori_loop(0, width // 256, down_cols, 0)
+        local(
+            base_sem + 7 + buffer,
+            stage.at[buffer, pl.ds(0, size)],
+            down_out.at[pl.ds(first, size)],
+        ).start()
+
+    to_mate(0).wait_recv()
+    back_far.wait_recv()
+    back_across.wait_recv()
+    keep_resid.wait()
+    gain_out[...] = jnp.zeros_like(gain_out)
+    low = got.at[0]
+
+    def norm_back(step, carry):
+        tile = pl.ds(pl.multiple_of(step * 32, 32), 32)
+        grad = (
+            pairs[odd, tile, :].astype(F32)
+            + got[0, tile, :].astype(F32)
+            + in_far[tile, :].astype(F32)
+            + in_across[tile, :].astype(F32)
+        )
+        block = resid[tile, :]
+        scale = lax.rsqrt(jnp.mean(block * block, axis=1, keepdims=True) + EPS)
+        gain_out[...] += jnp.sum(grad * block * scale, axis=0, keepdims=True)
+        inner = grad * gain_ref[...]
+        mean = jnp.mean(inner * block, axis=1, keepdims=True)
+        total = (
+            tops[slot, tile, :].astype(F32)
+            + scale * inner
+            - block * (scale * scale * scale * mean)
+        )
+        resid[tile, :] = total
+        low[tile, :] = total.astype(BF)
+        return carry
+
+    lax.fori_loop(0, rows // 32, norm_back, 0)
+    keep_grad = local(base_sem + 3, resid, grad_out)
+    keep_grad.start()
+    keep_low = local(base_sem + 4, low, grad_low_out)
+    keep_low.start()
+    keep_mixed.wait()
+    for copy in load_again:
+        copy.wait()
+
+    def heads_cols(step, carry):
+        span = pl.ds(pl.multiple_of(step * 256, 256), 256)
+        mixed[:, span] = nt(low[...], acts[step]).astype(BF)
+        return carry
+
+    lax.fori_loop(0, 6, heads_cols, 0)
+    heads_on = [
+        remote(HEADS_BACK + i, mixed_cols(to), heads_out.at[me], (to, at))
+        for i, to in enumerate((mate, beside, corner))
+    ]
+    for copy in heads_on:
+        copy.start()
+    own_back = local(0, mixed_cols(me), heads_out.at[me])
+    own_back.start()
+
+    own_back.wait()
+    keep_grad.wait()
+    keep_low.wait()
+    local(base_sem + 7, stage.at[0, pl.ds(0, SPANS[2][1])], down_out.at[pl.ds(0, SPANS[2][1])]).wait()
+    local(base_sem + 8, stage.at[1], down_out.at[pl.ds(0, rows)]).wait()
+    for copy in heads_on + sum_on:
+        copy.wait()
+    for copy in heads + slab_on:
+        copy.wait_send()
+    for c in range(4):
+        to_mate(c).wait_send()
+    for copy in (back_top, back_low, back_far, back_across):
+        copy.wait_send()
+
+
+def middle(attn_out, tokens, w_o, gain, slabs, w_d, top):
+    rows, width = tokens.shape
+    units = w_d.shape[0]
+    cols = attn_out.shape[2]
+    line = lax.axis_size("blk") // 2
+    slab_shape = slabs[0].shape
+    anywhere = pl.BlockSpec(memory_space=pl.ANY)
+    vmem = pl.BlockSpec(memory_space=pltpu.VMEM)
+    shape = jax.ShapeDtypeStruct
+    eight = (8, rows, width)
+    return pl.pallas_call(
+        functools.partial(middle_kernel, len(slabs), line),
+        out_shape=(
+            shape((rows, width), F32),
+            shape((rows, width), F32),
+            shape((rows, width), BF),
+            shape((rows, 4 * cols), BF),
+            shape(attn_out.shape, BF),
+            shape(eight, BF),
+            shape((width, 2 * units), BF),
+            shape(slab_shape, BF),
+            shape((units, width), BF),
+            shape((1, width), F32),
+        ),
+        in_specs=[anywhere, vmem, anywhere, vmem, anywhere, anywhere]
+        + [anywhere] * len(slabs),
+        out_specs=(anywhere,) * 9 + (vmem,),
+        scratch_shapes=[
+            pltpu.VMEM((rows, 4 * cols), BF),
+            pltpu.VMEM(eight, BF),
+            pltpu.VMEM(eight, BF),
+            pltpu.VMEM((width, 2 * units), BF),
+            pltpu.VMEM((units, width), BF),
+            pltpu.VMEM((8, rows, units), BF),
+            pltpu.VMEM((8, rows, 2 * units), BF),
+            pltpu.VMEM(eight, BF),
+            pltpu.VMEM((4, rows, width), BF),
+            pltpu.VMEM((2, rows, width), BF),
+            pltpu.VMEM((rows, width), BF),
+            pltpu.VMEM((rows, width), BF),
+            pltpu.VMEM((rows // 2, width), BF),
+            pltpu.VMEM((rows // 2, width), BF),
+            pltpu.VMEM((rows, width), F32),
+            pltpu.VMEM((256, 8 * rows), BF),
+            pltpu.VMEM((2, 256, 2 * units), BF),
+            pltpu.SemaphoreType.DMA((TRANSFERS,)),
+            pltpu.SemaphoreType.DMA((TRANSFERS,)),
+            pltpu.SemaphoreType.DMA((16 + 4 * len(slabs),)),
+        ],
+        compiler_params=pltpu.CompilerParams(
+            collective_id=1, has_side_effects=True, vmem_limit_bytes=60 << 20
+        ),
+        cost_estimate=pl.CostEstimate(
+            flops=60_000_000_000, bytes_accessed=100_000_000, transcendentals=2_000_000
+        ),
+        name="middle",
+    )(attn_out, tokens, w_o, gain, w_d, top, *slabs)
 
 
 def norm_rows(tensor, gain_vec):
@@ -485,10 +972,11 @@
     both = lax.all_to_all(
         jnp.swapaxes(both, 0, 1), "head", split_axis=0, concat_axis=0, tiled=True
     )
-    gate_up = LineGather(both, 1)
-    gate_up.ahead(line - 4)
+    slabs = [both.reshape(groups, 2 * w_rows, 2 * ff_cols)]
+    for _ in range(line - 3):
+        slabs.append(ring(slabs[-1], 2))
     down_moved = down.send()
-    gate_up_moved = gate_up.send()
+    top = gather_pair(cotangent)
 
     w_qkv = w_in[:, :qkv_cols]
     gains = w_in[:, qkv_cols : qkv_cols + 2].astype(F32).T
@@ -531,10 +1019,9 @@
     kv_own = jnp.swapaxes(
         jnp.concatenate([key_rot.astype(BF), value_own], axis=-1), 0, 1
     )
-    kv_own, down_moved, gate_up_moved = sync(kv_own, down_moved, gate_up_moved)
-    down.held, gate_up.held = down_moved, gate_up_moved
+    kv_own, down_moved, slabs = sync(kv_own, down_moved, slabs)
+    down.held = down_moved
     down.keep()
-    gate_up.keep()
 
     down_moved = down.send()
     even = side == 0
@@ -549,14 +1036,14 @@
     values_wide = jnp.concatenate([value_win, ones], axis=-1)
 
     scaled = split_low(queries.astype(F32) * (SCALE * LOG2E), 2)
-    keys_wide, values_wide, down_moved, w_out, cotangent = sync(
-        keys_wide, values_wide, down_moved, w_out, cotangent
+    keys_wide, values_wide, down_moved, w_out, top, slabs = sync(
+        keys_wide, values_wide, down_moved, w_out, top, slabs
     )
     down.held = down_moved
     down.keep()
-    gate_up_moved = gate_up.send()
-    top = gather_pair(cotangent).reshape(2 * block_len, width)
+    slabs.append(ring(slabs[-1], 2))
     w_o = gather_blk(w_out, 0).reshape(blocks * w_out.shape[0], width)
+    w_o = gather_head(w_o).reshape(QHEADS * HEAD, width)
     attended = attend(
         meta,
         jnp.concatenate(scaled, axis=-1),
@@ -564,58 +1051,40 @@
         values_wide,
         window_start[:, None],
     )
-    attended, gate_up_moved, top, w_o = sync(attended, gate_up_moved, top, w_o)
-    gate_up.held = gate_up_moved
-    gate_up.keep()
-    gate_up_moved = gate_up.send()
-    w_o = gather_head(w_o).reshape(QHEADS * HEAD, width)
+    attended, slabs, w_o = sync(attended, slabs, w_o)
     attn_keep = attended[..., :HEAD]
     log_total = attended[..., HEAD]
     attn_out = jnp.swapaxes(attn_keep.astype(BF), 0, 1).reshape(groups, tok_rows, q_cols)
-    mixed = lax.all_to_all(attn_out, "head", split_axis=0, concat_axis=0, tiled=True)
-    mixed = jnp.swapaxes(mixed, 0, 1).reshape(tok_rows, QHEADS * HEAD)
+
+    (
+        resid,
+        grad_resid,
+        grad_attn,
+        mixed,
+        grad_mix,
+        out_part,
+        gu_parts,
+        gu_moved,
+        down_parts,
+        grad_gain_two,
+    ) = middle(
+        attn_out,
+        tokens,
+        w_o,
+        gain_two[None, :],
+        slabs,
+        down.full.reshape(ff_cols, width),
+        top.reshape(2 * groups, tok_rows, width),
+    )
+    grad_gain_two = grad_gain_two[0]
     inputs = tokens.astype(F32)
-    resid = inputs + matmul(mixed, w_o)
-    normed_two_own = norm_rows(resid, gain_two).astype(BF)
-
-    normed_two = gather_pair(normed_two_own).reshape(2 * block_len, width)
-    gate_up.held = gate_up_moved
-    gate_up.keep()
-    w_gu = gate_up.full
-    w_gu = w_gu.reshape(width, 2 * ff_cols)
-    w_d = down.full.reshape(ff_cols, width)
-    gate_up_val = matmul(normed_two, w_gu)
-    gate_val, up_val = gate_up_val[:, :ff_cols], gate_up_val[:, ff_cols:]
-    gate_sig = jax.nn.sigmoid(gate_val)
-    gate_silu = gate_val * gate_sig
-    hidden = (gate_silu * up_val).astype(BF)
-    out_part = matmul(hidden, w_d).astype(BF).reshape(2, groups, tok_rows, width)
-    grad_hidden = matmul_nt(top, w_d)
-    grad_gate = (grad_hidden * up_val * gate_sig * (1 + gate_val * (1 - gate_sig))).astype(BF)
-    grad_up = (grad_hidden * gate_silu).astype(BF)
-    grad_gu = jnp.concatenate([grad_gate, grad_up], axis=1)
-    grad_part = matmul_nt(grad_gu, w_gu).astype(BF)
-    grad_part, hidden, grad_gu, out_part = sync(grad_part, hidden, grad_gu, out_part)
-
-    down_parts = matmul_tn(hidden, top).astype(BF).reshape(line, ff_rows, width)
-    gu_parts = matmul_tn(normed_two, grad_gu).astype(BF)
-    gu_parts = gu_parts.reshape(groups, line, 2, w_rows, 2 * ff_cols)
-    grad_normed = scatter_pair(grad_part.reshape(2, groups, tok_rows, width))
-    norm_two_out, norm_two_pull = jax.vjp(norm_rows, resid, gain_two)
-    grad_resid_part, grad_gain_two = norm_two_pull(grad_normed)
-    grad_resid = cotangent.astype(F32) + grad_resid_part
-    grad_attn = grad_resid.astype(BF)
-    grad_attn, down_parts, gu_parts, out_part = sync(grad_attn, down_parts, gu_parts, out_part)
-
+    down_parts = down_parts.reshape(line, ff_rows, width)
+    gu_parts = gu_parts.reshape(groups, line, 2 * w_rows, 2 * ff_cols)
     down_sum = LineScatter(lambda p: take(down_parts, p))
     gu_sum = LineScatter(lambda p: take(gu_parts, p, 1))
-    down_sum.ahead(line - 4)
-    gu_sum.ahead(line - 4)
-    down_moved, gu_moved = down_sum.send(), gu_sum.send()
-    grad_mixed = matmul_nt(grad_attn, w_o).astype(BF).reshape(tok_rows, groups, q_cols)
-    grad_mix = lax.all_to_all(
-        jnp.swapaxes(grad_mixed, 0, 1), "head", split_axis=0, concat_axis=0, tiled=True
-    )
+    gu_sum.total = gu_moved
+    gu_sum.add()
+    out_part = out_part.reshape(2, groups, tok_rows, width)
     out_parts = matmul_tn(mixed, grad_attn).astype(BF).reshape(groups, -1, width)
     grad_mix = jnp.swapaxes(grad_mix.reshape(block_len, per_group, HEAD), 0, 1)
     row_dots = jnp.sum(grad_mix.astype(F32) * attn_keep, axis=-1, keepdims=True)
@@ -627,12 +1096,8 @@
     )
     grad_t = jnp.concatenate([grad_mix] + low_dots + [blank[..., : HEAD - 2]], axis=-1)
     query_t, grad_t = jnp.swapaxes(query_t, 1, 2), jnp.swapaxes(grad_t, 1, 2)
-    query_t, grad_t, down_moved, gu_moved, out_part, out_parts = sync(
-        query_t, grad_t, down_moved, gu_moved, out_part, out_parts
-    )
-    down_sum.total, gu_sum.total = down_moved, gu_moved
-    down_sum.add()
-    gu_sum.add()
+    down_sum.ahead(line - 4)
+    gu_sum.ahead(line - 4)
     down_moved, gu_moved = down_sum.send(), gu_sum.send()
     out_act = (resid + scatter_pair(out_part)).astype(BF)
     out_slab = scatter_head(out_parts).astype(BF).reshape(blocks, w_out.shape[0], width)
@@ -670,6 +1135,8 @@
     down_sum.total, gu_sum.total = down_moved, gu_moved
     down_sum.add()
     gu_sum.add()
+    down_sum.send()
+    down_sum.add()
     d_w_down = down_sum.total
     kv_grad = jnp.swapaxes(own, 0, 1)
     grad_keys = kv_grad[..., :HEAD] * SCALE
@@ -681,7 +1148,7 @@
         )
         return jnp.swapaxes(back, 0, 1).astype(F32)
 
-    gu_own = gu_sum.total.astype(BF)
+    gu_own = gu_sum.total.astype(BF).reshape(groups, 2, w_rows, 2 * ff_cols)
     mine = take(gu_own, side, 1)
     got = swap(take(gu_own, 1 - side, 1), "blk", 1)
     gu_own = put(jnp.zeros((groups, w_rows, 2, 2 * ff_cols), BF), mine, side, 2)

time: 1100 us -> 1030 us (0.936)
  Pallas kernels: 40.2 us -> 203 us
  starting transfers between devices: 243 us -> 134 us
  matrix products: 114 us -> 21.4 us
  other arithmetic: 126 us -> 110 us
  waiting for transfers between devices: 337 us -> 324 us
    pallas_call x0 -> x1, Pallas kernels: none -> 162 us  [middle(): pl.pallas_call(functools.partial(middle_kernel, len(slabs), line), out_sh...]
    ppermute x28 -> x26, starting transfers between devices: 128 us -> 44.4 us  [ring(): lax.ppermute(block, 'blk', [(i, (i + step) % count) for i in range(count)])]
    ppermute x71 -> x55, waiting for transfers between devices: 175 us -> 116 us  [swap(): return lax.ppermute(block, axis, [(i, i ^ bit) for i in range(count)])]
    ppermute x28 -> x26, waiting for transfers between devices: 139 us -> 194 us  [ring(): lax.ppermute(block, 'blk', [(i, (i + step) % count) for i in range(count)])]
    dot_general x4 -> x1, matrix products: 40 us -> 5.48 us  [matmul_nt(): lax.dot_general(left_side, right_side, (((1,), (1,)), ((), ())), preferre...]
    dot_general x4 -> x1, matrix products: 37.8 us -> 5.96 us  [matmul(): return jnp.dot(left_side, right_side, preferred_element_type=F32)]
    dot_general x4 -> x2, matrix products: 36.3 us -> 9.97 us  [matmul_tn(): lax.dot_general(left_side, right_side, (((0,), (0,)), ((), ())), preferre...]
    ppermute x71 -> x55, starting transfers between devices: 89.9 us -> 74.2 us  [swap(): return lax.ppermute(block, axis, [(i, i ^ bit) for i in range(count)])]
  transfers between devices with their start and end apart: 105 -> 85, of which waited for: 42 -> 35; matrix products, arithmetic and copies ran while one was open for 32% -> 29% of each run, Pallas kernels for 4% -> 4%
where the time goes in v3:
time: 1030 us; the launch traced here: 1010 us
  waiting for transfers between devices  324 us (31%)
  local copies, waits for them, and re-layouts  219 us (21%)
  Pallas kernels  203 us (20%)
  starting transfers between devices  134 us (13%)
  other arithmetic  110 us (11%)
  matrix products  21.4 us (2%)
    ppermute x26, waiting for transfers between devices, ring(): lax.ppermute(block, 'blk', [(i, (i + step) % count) for i in range(count)])  194 us
    pallas_call x1, Pallas kernels, middle(): pl.pallas_call(functools.partial(middle_kernel, len(slabs), line), out_sh...  162 us
    ppermute x55, waiting for transfers between devices, swap(): return lax.ppermute(block, axis, [(i, i ^ bit) for i in range(count)])  116 us
    ppermute x55, starting transfers between devices, swap(): return lax.ppermute(block, axis, [(i, i ^ bit) for i in range(count)])  74.2 us
    ppermute x26, starting transfers between devices, ring(): lax.ppermute(block, 'blk', [(i, (i + step) % count) for i in range(count)])  44.4 us
    pallas_call x1, Pallas kernels, attend_back(): pl.pallas_call(attend_back_kernel, out_shape=(jax.ShapeDtypeStruct((heads...  26.2 us
    dynamic_update_slice x15, local copies, waits for them, and re-layouts, put(): return lax.dynamic_update_index_in_dim(full, part, index, axis)  22.6 us
  transfers between devices with their start and end apart: 85, of which 35 were waited for; matrix products, arithmetic and copies ran while one was open for 29% of the time, Pallas kernels for 4%

profile of v3, /device:TPU:0, one launch (start us, length us, event | category | flops | bytes accessed | tf_op | source)
XLA Modules:
  0.0 1013.6 jit_solution(3811098135194517531)
XLA Ops:
  16.2 5.1 stack_reshape.6
  34.7 5.9 maximum_bitcast_fusion
  61.1 5.8 collective-permute-done.1
  82.2 9.1 collective-permute-done.8
  98.4 6.1 collective-permute-done.4
  110.8 9.0 collective-permute-done.6
  133.8 6.0 fusion.15
  145.0 5.5 collective-permute-done.12
  161.5 11.5 %all-to-all-done.1 = bf16[4,2,64,1280]{3,2,1,0:T(8,128)(2,1)} async-done(((bf16[4,2,64,1280]{3,2,1,0:T(8,128)(2,1)}), bf16[4,2,64,1280]{3,2,1,0:T(8,128)(2,1)}, u32[]{:S(2)}, u32[]{:S(2)}) %all-to-all-start.1) | async-done | bytes 1310752 | tf_op jit(solution)/shard_map/all_to_all | solution.py:972
  180.0 25.4 %collective-permute-done.13.refs_1_ = bf16[4,128,1280]{2,1,0:T(8,128)(2,1)S(1)} collective-permute-done((bf16[4,128,1280]{2,1,0:T(8,128)(2,1)}, bf16[4,128,1280]{2,1,0:T(8,128)(2,1)S(1)}, u32[]{:S(2)}, u32[]{:S(2)}) %collective-permute-start.13) | collective-permute-done | bytes 1310752 | tf_op jit(solution)/shard_map/ppermute | solution.py:49
  209.6 10.2 %collective-permute-done.14 = bf16[2,1024,128]{1,2,0:T(8,128)(2,1)S(1)} collective-permute-done((bf16[2,1024,128]{1,2,0:T(8,128)(2,1)S(1)}, bf16[2,1024,128]{1,2,0:T(8,128)(2,1)S(1)}, u32[]{:S(2)}, u32[]{:S(2)}) %collective-permute-start.14) | collective-permute-done | bytes 524320 | tf_op jit(solution)/shard_map/ppermute | solution.py:49
  223.1 10.2 %collective-permute-done.15 = bf16[2,1024,128]{1,2,0:T(8,128)(2,1)S(1)} collective-permute-done((bf16[2,1024,128]{1,2,0:T(8,128)(2,1)S(1)}, bf16[2,1024,128]{1,2,0:T(8,128)(2,1)S(1)}, u32[]{:S(2)}, u32[]{:S(2)}) %collective-permute-start.15) | collective-permute-done | bytes 524320 | tf_op jit(solution)/shard_map/ppermute | solution.py:49
  239.0 6.4 collective-permute-done.16
  280.0 29.1 %collective-permute-done.31 = bf16[48,2048]{1,0:T(8,128)(2,1)S(1)} collective-permute-done((bf16[48,2048]{1,0:T(8,128)(2,1)S(1)}, bf16[48,2048]{1,0:T(8,128)(2,1)S(1)}, u32[]{:S(2)}, u32[]{:S(2)}) %collective-permute-start.31) | collective-permute-done | bytes 196640 | tf_op jit(solution)/shard_map/ppermute | solution.py:49
  310.5 7.4 collective-permute-done.33
  325.2 14.2 %attend.1 = f32[6,1024,128]{2,1,0:T(8,128)} custom-call(s32[9]{0:T(128)S(1)} %pad_add_fusion.3.meta_ref, bf16[6,1024,128]{2,1,0:T(8,128)(2,1)S(1)} %pad_maximum_fusion.query_ref, bf16[2,5120,128]{2,1,0:T(8,128)(2,1)S(1)} %slice.246.key_ref, bf16[2,5120,128]{2,1,0:T(8,128)(2,1)} %copy.306.value_ref, s32[1024,1]{1,0:T(8,128)S(1)} %copy.297.start_ref), custom_call_target="tpu_custom_call" | custom-call | flops 30000001024 | bytes 20000000 | tf_op jit(solution)/shard_map/attend/pallas_call | solution.py:303
  339.5 21.0 %collective-permute-done.36 = bf16[384,2048]{1,0:T(8,128)(2,1)S(1)} collective-permute-done((bf16[384,2048]{1,0:T(8,128)(2,1)S(1)}, bf16[384,2048]{1,0:T(8,128)(2,1)S(1)}, u32[]{:S(2)}, u32[]{:S(2)}) %collective-permute-start.36) | collective-permute-done | bytes 1572896 | tf_op jit(solution)/shard_map/ppermute | solution.py:44
  381.1 162.1 %middle.1 = (f32[256,2048]{1,0:T(8,128)}, f32[256,2048]{1,0:T(8,128)}, bf16[256,2048]{1,0:T(8,128)(2,1)}, bf16[256,1536]{1,0:T(8,128)(2,1)}, bf16[4,256,384]{2,1...) custom-call(bf16[4,256,384]{2,1,0:T(8,128)(2,1)} %copy.299.attn_ref,, ...), custom_call_target="tpu_custom_call" | custom-call | flops 60000002048 | bytes 100000000 | tf_op jit(solution)/shard_map/middle/pallas_call | solution.py:834
  572.6 5.2 convert_add_fusion.9
  587.5 12.1 %concatenate.85 = bf16[6,1024,256]{2,1,0:T(8,128)(2,1)} concatenate(bf16[6,1024,64]{2,1,0:T(8,128)(2,1)S(1)} %copy-done.9, bf16[6,1024,64]{2,1,0:T(8,128)(2,1)S(1)} %copy-done.7, bf16[6,1024,1]{2,1,0:T(8,128)(2,1)} %get-tuple-element.130, bf16[6,1024,1]{2,1,0:T(8,128)(2,1)} %get-tuple-element.129, bf16[6,1024,1]{2,1,0:T(8,128)(2,1)} %get-tuple-element.128, ...), dimensions={2} | concatenate | bytes 6291456 | tf_op jit(solution)/shard_map/concatenate | solution.py:1094
  613.7 10.5 %collective-permute-done.43 = bf16[128,2048]{1,0:T(8,128)(2,1)S(1)} collective-permute-done((bf16[128,2048]{1,0:T(8,128)(2,1)S(1)}, bf16[128,2048]{1,0:T(8,128)(2,1)S(1)}, u32[]{:S(2)}, u32[]{:S(2)}) %collective-permute-start.43) | collective-permute-done | bytes 524320 | tf_op jit(solution)/shard_map/ppermute | solution.py:44
  631.2 26.2 %attend_back.1 = (f32[6,64,1024]{2,1,0:T(8,128)}, f32[2,5120,128]{2,1,0:T(8,128)}) custom-call(s32[9]{0:T(128)} %copy-done, bf16[2,5120,256]{2,1,0:T(8,128)(2,1)} %maximum_maximum_fusion.key_ref, bf16[2,5120,128]{2,1,0:T(8,128)(2,1)} %copy.306.value_ref, bf16[2,64,5120]{2,1,0:T(8,128)(2,1)} %get-tuple-element.133.key_t_ref, ...), custom_call_target="tpu_custom_call" | custom-call | flops 70000001024 | bytes 40000000 | tf_op jit(solution)/shard_map/attend_back/pallas_call | solution.py:379
  660.7 35.0 %collective-permute-start.39 = (bf16[4,128,1280]{2,1,0:T(8,128)(2,1)S(1)}, bf16[4,128,1280]{2,1,0:T(8,128)(2,1)}, u32[]{:S(2)}, u32[]{:S(2)}) collective-permute-start(bf16[4,128,1280]{2,1,0:T(8,128)(2,1)S(1)} %fusion.13), channel_id=1, source_target_pairs={{0,2},{1,3},{2,4},{3,5},{4,6},{5,7},{6,0},{7,1},{8,10},{9,11},{10,... | collective-permute-start | bytes 3932168 | tf_op jit(solution)/shard_map/ppermute | solution.py:49
  704.4 52.6 %collective-permute-done.38 = bf16[160,2048]{1,0:T(8,128)(2,1)S(1)} collective-permute-done((bf16[160,2048]{1,0:T(8,128)(2,1)S(1)}, bf16[160,2048]{1,0:T(8,128)(2,1)S(1)}, u32[]{:S(2)}, u32[]{:S(2)}) %collective-permute-start.38) | collective-permute-done | bytes 655392 | tf_op jit(solution)/shard_map/ppermute | solution.py:49
  757.0 6.0 copy.315
  766.8 27.0 %collective-permute-start.51 = (bf16[2,1024,128]{1,2,0:T(8,128)(2,1)}, bf16[2,1024,128]{1,2,0:T(8,128)(2,1)}, u32[]{:S(2)}, u32[]{:S(2)}) collective-permute-start(bf16[2,1024,128]{1,2,0:T(8,128)(2,1)} %get-tuple-element.132), channel_id=1, source_target_pairs={{0,1},{1,0},{2,3},{3,2},{4,5},{5,4},{6,7},{7,6},{8,9},{9,8},{10,11... | collective-permute-start | bytes 1572872 | tf_op jit(solution)/shard_map/ppermute | solution.py:44
  806.0 16.0 %collective-permute-done.75 = bf16[48,2048]{1,0:T(8,128)(2,1)S(1)} collective-permute-done((bf16[48,2048]{1,0:T(8,128)(2,1)S(1)}, bf16[48,2048]{1,0:T(8,128)(2,1)S(1)}, u32[]{:S(2)}, u32[]{:S(2)}) %collective-permute-start.75) | collective-permute-done | bytes 196640 | tf_op jit(solution)/shard_map/ppermute | solution.py:44
  844.4 27.3 %collective-permute-done.53 = bf16[2,1024,128]{1,2,0:T(8,128)(2,1)S(1)} collective-permute-done((bf16[2,1024,128]{1,2,0:T(8,128)(2,1)S(1)}, bf16[2,1024,128]{1,2,0:T(8,128)(2,1)S(1)}, u32[]{:S(2)}, u32[]{:S(2)}) %collective-permute-start.53) | collective-permute-done | bytes 524320 | tf_op jit(solution)/shard_map/ppermute | solution.py:49
  891.4 5.5 convolution_convert_fusion.1
  897.7 8.1 convolution_convert_fusion.2
  922.2 13.9 %collective-permute-done.59 = bf16[256,2048]{1,0:T(8,128)(2,1)S(1)} collective-permute-done((bf16[256,2048]{1,0:T(8,128)(2,1)S(1)}, bf16[256,2048]{1,0:T(8,128)(2,1)S(1)}, u32[]{:S(2)}, u32[]{:S(2)}) %collective-permute-start.59) | collective-permute-done | bytes 1048608 | tf_op jit(solution)/shard_map/ppermute | solution.py:44
  968.9 6.3 reshape.519
  (520 shorter events, 409.5 us)
Async XLA Ops:
  0.7 76.3 %collective-permute-start.19 = (bf16[256,2048]{1,0:T(8,128)(2,1)}, bf16[256,2048]{1,0:T(8,128)(2,1)}, u32[]{:S(2)}, u32[]{:S(2)}) collective-permute-start(bf16[256,2048]{1,0:T(8,128)(2,1)} %param.27), channel_id=1, source_target_pairs={{0,8},{8,0},{16,24},{24,16},{1,9},{9,1},{17,25},{25,17},{2,10},{10... | collective-permute-start | bytes 3145736 | tf_op jit(solution)/shard_map/ppermute | solution.py:44
  1.2 70.7 %collective-permute-start.20 = (bf16[256,2048]{1,0:T(8,128)(2,1)}, bf16[256,2048]{1,0:T(8,128)(2,1)}, u32[]{:S(2)}, u32[]{:S(2)}) collective-permute-start(bf16[256,2048]{1,0:T(8,128)(2,1)} %param.27), channel_id=1, source_target_pairs={{0,16},{8,24},{16,0},{24,8},{1,17},{9,25},{17,1},{25,9},{2,18},{10... | collective-permute-start | bytes 3145736 | tf_op jit(solution)/shard_map/ppermute | solution.py:44
  3.8 70.7 %collective-permute-start.22 = (bf16[256,2048]{1,0:T(8,128)(2,1)}, bf16[256,2048]{1,0:T(8,128)(2,1)}, u32[]{:S(2)}, u32[]{:S(2)}) collective-permute-start(bf16[256,2048]{1,0:T(8,128)(2,1)} %param.27), channel_id=1, source_target_pairs={{0,1},{1,0},{2,3},{3,2},{4,5},{5,4},{6,7},{7,6},{8,9},{9,8},{10,11... | collective-permute-start | bytes 3145736 | tf_op jit(solution)/shard_map/ppermute | solution.py:44
  13.7 55.8 %collective-permute-start.7 = (bf16[256,2048]{1,0:T(8,128)(2,1)S(1)}, bf16[256,2048]{1,0:T(8,128)(2,1)}, u32[]{:S(2)}, u32[]{:S(2)}) collective-permute-start(bf16[256,2048]{1,0:T(8,128)(2,1)S(1)} %copy-done.4), channel_id=1, source_target_pairs={{0,8},{8,0},{16,24},{24,16},{1,9},{9,1},{17,25},{25,17},{2,10},{10... | collective-permute-start | bytes 3145736 | tf_op jit(solution)/shard_map/ppermute | solution.py:44
  69.6 52.0 %collective-permute-start.10 = (bf16[160,2048]{1,0:T(8,128)(2,1)S(1)}, bf16[160,2048]{1,0:T(8,128)(2,1)}, u32[]{:S(2)}, u32[]{:S(2)}) collective-permute-start(bf16[160,2048]{1,0:T(8,128)(2,1)S(1)} %copy-done.42), channel_id=1, source_target_pairs={{0,2},{1,3},{2,4},{3,5},{4,6},{5,7},{6,0},{7,1},{8,10},{9,11},{10,... | collective-permute-start | bytes 1966088 | tf_op jit(solution)/shard_map/ppermute | solution.py:49
  77.0 31.2 %collective-permute-start.24 = (bf16[128,2048]{1,0:T(8,128)(2,1)S(1)}, bf16[128,2048]{1,0:T(8,128)(2,1)S(1)}, u32[]{:S(2)}, u32[]{:S(2)}) collective-permute-start(bf16[128,2048]{1,0:T(8,128)(2,1)S(1)} %slice.296), channel_id=1, source_target_pairs={{0,1},{1,0},{2,3},{3,2},{4,5},{5,4},{6,7},{7,6},{8,9},{9,8},{10,11... | collective-permute-start | bytes 1572872 | tf_op jit(solution)/shard_map/ppermute | solution.py:44
  107.4 70.2 %collective-permute-start.21 = (bf16[256,2048]{1,0:T(8,128)(2,1)}, bf16[256,2048]{1,0:T(8,128)(2,1)}, u32[]{:S(2)}, u32[]{:S(2)}) collective-permute-start(bf16[256,2048]{1,0:T(8,128)(2,1)} %collective-permute-done.20), channel_id=1, source_target_pairs={{0,8},{8,0},{16,24},{24,16},{1,9},{9,1},{17,25},{25,17},{2,10},{10... | collective-permute-start | bytes 3145736 | tf_op jit(solution)/shard_map/ppermute | solution.py:44
  109.7 110.5 %collective-permute-start.23 = (bf16[256,2048]{1,0:T(8,128)(2,1)}, bf16[256,2048]{1,0:T(8,128)(2,1)}, u32[]{:S(2)}, u32[]{:S(2)}) collective-permute-start(bf16[256,2048]{1,0:T(8,128)(2,1)} %collective-permute-done.22), channel_id=1, source_target_pairs={{0,8},{8,0},{16,24},{24,16},{1,9},{9,1},{17,25},{25,17},{2,10},{10... | collective-permute-start | bytes 3145736 | tf_op jit(solution)/shard_map/ppermute | solution.py:44
  119.7 126.7 %collective-permute-start.26 = (bf16[256,2048]{1,0:T(8,128)(2,1)}, bf16[256,2048]{1,0:T(8,128)(2,1)}, u32[]{:S(2)}, u32[]{:S(2)}) collective-permute-start(bf16[256,2048]{1,0:T(8,128)(2,1)} %constant_dynamic-update-slice_fusion.6), channel_id=1, source_target_pairs={{0,8},{8,0},{16,24},{24,16},{1,9},{9,1},{17,25},{25,17},{2,10},{10... | collective-permute-start | bytes 3145736 | tf_op jit(solution)/shard_map/ppermute | solution.py:44
  130.8 49.2 %collective-permute-start.11 = (bf16[160,2048]{1,0:T(8,128)(2,1)}, bf16[160,2048]{1,0:T(8,128)(2,1)}, u32[]{:S(2)}, u32[]{:S(2)}) collective-permute-start(bf16[160,2048]{1,0:T(8,128)(2,1)} %collective-permute-done.10), channel_id=1, source_target_pairs={{0,2},{1,3},{2,4},{3,5},{4,6},{5,7},{6,0},{7,1},{8,10},{9,11},{10,... | collective-permute-start | bytes 1966088 | tf_op jit(solution)/shard_map/ppermute | solution.py:49
  173.0 32.3 %collective-permute-start.13 = (bf16[4,128,1280]{2,1,0:T(8,128)(2,1)}, bf16[4,128,1280]{2,1,0:T(8,128)(2,1)S(1)}, u32[]{:S(2)}, u32[]{:S(2)}) collective-permute-start(bf16[4,128,1280]{2,1,0:T(8,128)(2,1)} %bitcast.39.refs_0_), channel_id=1, source_target_pairs={{0,2},{1,3},{2,4},{3,5},{4,6},{5,7},{6,0},{7,1},{8,10},{9,11},{10,... | collective-permute-start | bytes 3932168 | tf_op jit(solution)/shard_map/ppermute | solution.py:49
  275.8 95.5 %collective-permute-start.27 = (bf16[4,128,1280]{2,1,0:T(8,128)(2,1)S(1)}, bf16[4,128,1280]{2,1,0:T(8,128)(2,1)S(1)}, u32[]{:S(2)}, u32[]{:S(2)}) collective-permute-start(bf16[4,128,1280]{2,1,0:T(8,128)(2,1)S(1)} %copy-done.69), channel_id=1, source_target_pairs={{0,2},{1,3},{2,4},{3,5},{4,6},{5,7},{6,0},{7,1},{8,10},{9,11},{10,... | collective-permute-start | bytes 3932168 | tf_op jit(solution)/shard_map/ppermute | solution.py:49
  278.5 31.9 %collective-permute-start.30 = (bf16[48,2048]{1,0:T(8,128)(2,1)S(1)}, bf16[48,2048]{1,0:T(8,128)(2,1)S(1)}, u32[]{:S(2)}, u32[]{:S(2)}) collective-permute-start(bf16[48,2048]{1,0:T(8,128)(2,1)S(1)} %collective-permute-done.29), channel_id=1, source_target_pairs={{0,1},{1,0},{2,3},{3,2},{4,5},{5,4},{6,7},{7,6},{8,9},{9,8},{10,11... | collective-permute-start | bytes 589832 | tf_op jit(solution)/shard_map/ppermute | solution.py:44
  323.6 43.7 %collective-permute-start.35 = (bf16[384,2048]{1,0:T(8,128)(2,1)S(1)}, bf16[384,2048]{1,0:T(8,128)(2,1)S(1)}, u32[]{:S(2)}, u32[]{:S(2)}) collective-permute-start(bf16[384,2048]{1,0:T(8,128)(2,1)S(1)} %bitcast.346), channel_id=1, source_target_pairs={{0,8},{8,0},{16,24},{24,16},{1,9},{9,1},{17,25},{25,17},{2,10},{10... | collective-permute-start | bytes 4718600 | tf_op jit(solution)/shard_map/ppermute | solution.py:44
  323.7 36.8 %collective-permute-start.36 = (bf16[384,2048]{1,0:T(8,128)(2,1)S(1)}, bf16[384,2048]{1,0:T(8,128)(2,1)S(1)}, u32[]{:S(2)}, u32[]{:S(2)}) collective-permute-start(bf16[384,2048]{1,0:T(8,128)(2,1)S(1)} %bitcast.347), channel_id=1, source_target_pairs={{0,16},{8,24},{16,0},{24,8},{1,17},{9,25},{17,1},{25,9},{2,18},{10... | collective-permute-start | bytes 4718600 | tf_op jit(solution)/shard_map/ppermute | solution.py:44
  569.0 58.0 %collective-permute-start.49 = (bf16[384,2048]{1,0:T(8,128)(2,1)}, bf16[384,2048]{1,0:T(8,128)(2,1)}, u32[]{:S(2)}, u32[]{:S(2)}) collective-permute-start(bf16[384,2048]{1,0:T(8,128)(2,1)} %get-tuple-element.115), channel_id=1, source_target_pairs={{0,8},{8,0},{16,24},{24,16},{1,9},{9,1},{17,25},{25,17},{2,10},{10... | collective-permute-start | bytes 4718600 | tf_op jit(solution)/shard_map/ppermute | solution.py:44
  578.9 32.0 %collective-permute-start.46 = (bf16[128,2048]{1,0:T(8,128)(2,1)}, bf16[128,2048]{1,0:T(8,128)(2,1)}, u32[]{:S(2)}, u32[]{:S(2)}) collective-permute-start(bf16[128,2048]{1,0:T(8,128)(2,1)} %get-tuple-element.145), channel_id=1, source_target_pairs={{0,16},{8,24},{16,0},{24,8},{1,17},{9,25},{17,1},{25,9},{2,18},{10... | collective-permute-start | bytes 1572872 | tf_op jit(solution)/shard_map/ppermute | solution.py:44
  607.4 53.3 %collective-permute-start.40 = (bf16[256,2048]{1,0:T(8,128)(2,1)}, bf16[256,2048]{1,0:T(8,128)(2,1)}, u32[]{:S(2)}, u32[]{:S(2)}) collective-permute-start(bf16[256,2048]{1,0:T(8,128)(2,1)} %get-tuple-element.107), channel_id=1, source_target_pairs={{0,8},{8,0},{16,24},{24,16},{1,9},{9,1},{17,25},{25,17},{2,10},{10... | collective-permute-start | bytes 3145736 | tf_op jit(solution)/shard_map/ppermute | solution.py:44
  607.7 92.1 %collective-permute-start.48 = (bf16[384,2048]{1,0:T(8,128)(2,1)}, bf16[384,2048]{1,0:T(8,128)(2,1)}, u32[]{:S(2)}, u32[]{:S(2)}) collective-permute-start(bf16[384,2048]{1,0:T(8,128)(2,1)} %get-tuple-element.114), channel_id=1, source_target_pairs={{0,8},{8,0},{16,24},{24,16},{1,9},{9,1},{17,25},{25,17},{2,10},{10... | collective-permute-start | bytes 4718600 | tf_op jit(solution)/shard_map/ppermute | solution.py:44
  613.1 82.7 %collective-permute-start.47 = (bf16[256,2048]{1,0:T(8,128)(2,1)}, bf16[256,2048]{1,0:T(8,128)(2,1)}, u32[]{:S(2)}, u32[]{:S(2)}) collective-permute-start(bf16[256,2048]{1,0:T(8,128)(2,1)} %pad_maximum_fusion.3), channel_id=1, source_target_pairs={{0,1},{1,0},{2,3},{3,2},{4,5},{5,4},{6,7},{7,6},{8,9},{9,8},{10,11... | collective-permute-start | bytes 3145736 | tf_op jit(solution)/shard_map/ppermute | solution.py:44
  625.4 70.4 %collective-permute-start.44 = (bf16[256,2048]{1,0:T(8,128)(2,1)}, bf16[256,2048]{1,0:T(8,128)(2,1)}, u32[]{:S(2)}, u32[]{:S(2)}) collective-permute-start(bf16[256,2048]{1,0:T(8,128)(2,1)} %pad_maximum_fusion.2), channel_id=1, source_target_pairs={{0,16},{8,24},{16,0},{24,8},{1,17},{9,25},{17,1},{25,9},{2,18},{10... | collective-permute-start | bytes 3145736 | tf_op jit(solution)/shard_map/ppermute | solution.py:44
  630.7 69.2 %collective-permute-start.50 = (bf16[384,2048]{1,0:T(8,128)(2,1)}, bf16[384,2048]{1,0:T(8,128)(2,1)}, u32[]{:S(2)}, u32[]{:S(2)}) collective-permute-start(bf16[384,2048]{1,0:T(8,128)(2,1)} %fusion.8), channel_id=1, source_target_pairs={{0,16},{8,24},{16,0},{24,8},{1,17},{9,25},{17,1},{25,9},{2,18},{10... | collective-permute-start | bytes 4718600 | tf_op jit(solution)/shard_map/ppermute | solution.py:44
  660.7 96.2 %collective-permute-start.39 = (bf16[4,128,1280]{2,1,0:T(8,128)(2,1)S(1)}, bf16[4,128,1280]{2,1,0:T(8,128)(2,1)}, u32[]{:S(2)}, u32[]{:S(2)}) collective-permute-start(bf16[4,128,1280]{2,1,0:T(8,128)(2,1)S(1)} %fusion.13), channel_id=1, source_target_pairs={{0,2},{1,3},{2,4},{3,5},{4,6},{5,7},{6,0},{7,1},{8,10},{9,11},{10,... | collective-permute-start | bytes 3932168 | tf_op jit(solution)/shard_map/ppermute | solution.py:49
  695.8 61.2 %collective-permute-start.38 = (bf16[160,2048]{1,0:T(8,128)(2,1)S(1)}, bf16[160,2048]{1,0:T(8,128)(2,1)S(1)}, u32[]{:S(2)}, u32[]{:S(2)}) collective-permute-start(bf16[160,2048]{1,0:T(8,128)(2,1)S(1)} %dynamic-slice_bitcast_fusion.9), channel_id=1, source_target_pairs={{0,2},{1,3},{2,4},{3,5},{4,6},{5,7},{6,0},{7,1},{8,10},{9,11},{10,... | collective-permute-start | bytes 1966088 | tf_op jit(solution)/shard_map/ppermute | solution.py:49
  766.8 76.6 %collective-permute-start.51 = (bf16[2,1024,128]{1,2,0:T(8,128)(2,1)}, bf16[2,1024,128]{1,2,0:T(8,128)(2,1)}, u32[]{:S(2)}, u32[]{:S(2)}) collective-permute-start(bf16[2,1024,128]{1,2,0:T(8,128)(2,1)} %get-tuple-element.132), channel_id=1, source_target_pairs={{0,1},{1,0},{2,3},{3,2},{4,5},{5,4},{6,7},{7,6},{8,9},{9,8},{10,11... | collective-permute-start | bytes 1572872 | tf_op jit(solution)/shard_map/ppermute | solution.py:44
  793.8 37.0 %collective-permute-start.52 = (bf16[2,1024,128]{1,2,0:T(8,128)(2,1)}, bf16[2,1024,128]{1,2,0:T(8,128)(2,1)}, u32[]{:S(2)}, u32[]{:S(2)}) collective-permute-start(bf16[2,1024,128]{1,2,0:T(8,128)(2,1)} %get-tuple-element.131), channel_id=1, source_target_pairs={{0,1},{1,0},{2,3},{3,2},{4,5},{5,4},{6,7},{7,6},{8,9},{9,8},{10,11... | collective-permute-start | bytes 1572872 | tf_op jit(solution)/shard_map/ppermute | solution.py:44
  794.8 95.4 %collective-permute-start.55 = (bf16[160,2048]{1,0:T(8,128)(2,1)}, bf16[160,2048]{1,0:T(8,128)(2,1)}, u32[]{:S(2)}, u32[]{:S(2)}) collective-permute-start(bf16[160,2048]{1,0:T(8,128)(2,1)} %fusion.31), channel_id=1, source_target_pairs={{0,2},{1,3},{2,4},{3,5},{4,6},{5,7},{6,0},{7,1},{8,10},{9,11},{10,... | collective-permute-start | bytes 1966088 | tf_op jit(solution)/shard_map/ppermute | solution.py:49
  832.3 39.4 %collective-permute-start.53 = (bf16[2,1024,128]{1,2,0:T(8,128)(2,1)S(1)}, bf16[2,1024,128]{1,2,0:T(8,128)(2,1)S(1)}, u32[]{:S(2)}, u32[]{:S(2)}) collective-permute-start(bf16[2,1024,128]{1,2,0:T(8,128)(2,1)S(1)} %fusion.40), channel_id=1, source_target_pairs={{0,6},{1,7},{2,0},{3,1},{4,2},{5,3},{6,4},{7,5},{8,14},{9,15},{10,... | collective-permute-start | bytes 1572872 | tf_op jit(solution)/shard_map/ppermute | solution.py:49
  836.2 54.0 %collective-permute-start.56 = (bf16[4,128,1280]{2,1,0:T(8,128)(2,1)S(1)}, bf16[4,128,1280]{2,1,0:T(8,128)(2,1)}, u32[]{:S(2)}, u32[]{:S(2)}) collective-permute-start(bf16[4,128,1280]{2,1,0:T(8,128)(2,1)S(1)} %copy-done.37), channel_id=1, source_target_pairs={{0,2},{1,3},{2,4},{3,5},{4,6},{5,7},{6,0},{7,1},{8,10},{9,11},{10,... | collective-permute-start | bytes 3932168 | tf_op jit(solution)/shard_map/ppermute | solution.py:49
  840.5 38.0 %collective-permute-start.72 = (bf16[48,2048]{1,0:T(8,128)(2,1)}, bf16[48,2048]{1,0:T(8,128)(2,1)}, u32[]{:S(2)}, u32[]{:S(2)}) collective-permute-start(bf16[48,2048]{1,0:T(8,128)(2,1)} %get-tuple-element.136), channel_id=1, source_target_pairs={{0,1},{1,0},{2,3},{3,2},{4,5},{5,4},{6,7},{7,6},{8,9},{9,8},{10,11... | collective-permute-start | bytes 589832 | tf_op jit(solution)/shard_map/ppermute | solution.py:44
  843.4 39.9 %collective-permute-start.78 = (bf16[48,2048]{1,0:T(8,128)(2,1)}, bf16[48,2048]{1,0:T(8,128)(2,1)}, u32[]{:S(2)}, u32[]{:S(2)}) collective-permute-start(bf16[48,2048]{1,0:T(8,128)(2,1)} %fusion.55), channel_id=1, source_target_pairs={{0,2},{1,3},{2,4},{3,5},{4,6},{5,7},{6,0},{7,1},{8,10},{9,11},{10,... | collective-permute-start | bytes 589832 | tf_op jit(solution)/shard_map/ppermute | solution.py:49
  920.9 34.3 %collective-permute-start.80 = (bf16[160,2048]{1,0:T(8,128)(2,1)S(1)}, bf16[160,2048]{1,0:T(8,128)(2,1)}, u32[]{:S(2)}, u32[]{:S(2)}) collective-permute-start(bf16[160,2048]{1,0:T(8,128)(2,1)S(1)} %fusion.30), channel_id=1, source_target_pairs={{0,2},{1,3},{2,4},{3,5},{4,6},{5,7},{6,0},{7,1},{8,10},{9,11},{10,... | collective-permute-start | bytes 1966088 | tf_op jit(solution)/shard_map/ppermute | solution.py:49
  (128 other events, 2300.7 us)

commit v4 on v3

--- a/solution.py
+++ b/solution.py
@@ -81,30 +81,6 @@
 def place_of():
     at = lax.axis_index("blk")
     return at // 2, at % 2, lax.axis_size("blk") // 2
-
-
-class LineGather:
-    def __init__(self, part, axis=0):
-        self.place, _, self.line = place_of()
-        self.axis = axis
-        shape = part.shape[:axis] + (self.line,) + part.shape[axis:]
-        self.full = put(jnp.zeros(shape, part.dtype), part, self.place, axis)
-        self.held = part
-        self.step = 0
-
-    def send(self):
-        self.step += 1
-        self.held = ring(self.held, 2)
-        return self.held
-
-    def keep(self):
-        source = (self.place - self.step) % self.line
-        self.full = put(self.full, self.held, source, self.axis)
-
-    def ahead(self, steps):
-        for _ in range(steps):
-            self.send()
-            self.keep()
 
 
 class LineScatter:
@@ -168,35 +144,6 @@
     return total
 
 
-def gather_pair(part):
-    me = lax.axis_index("head")
-    side = lax.axis_index("blk") % 2
-    half = part.shape[0] // 2
-    near = swap(part, "head", 1)
-    far = swap(part, "head", 2)
-    across = swap(part, "blk", 1)
-    corner = jnp.concatenate(
-        [swap(far[:half], "blk", 1), swap(across[half:], "head", 2)], axis=0
-    )
-    full = jnp.zeros((2, 4) + part.shape, part.dtype)
-
-    def store(full, block, side, head):
-        return lax.dynamic_update_slice(
-            full, block[None, None], [side, head] + [0] * part.ndim
-        )
-
-    full = store(full, part, side, me)
-    full = store(full, near, side, me ^ 1)
-    for block, to_side, to_head in (
-        (far, side, me ^ 2),
-        (across, 1 - side, me),
-        (corner, 1 - side, me ^ 2),
-    ):
-        full = store(full, block, to_side, to_head)
-        full = store(full, swap(block, "head", 1), to_side, to_head ^ 1)
-    return full
-
-
 def scatter_pair(terms):
     me = lax.axis_index("head")
     side = lax.axis_index("blk") % 2
@@ -250,15 +197,45 @@
     )
 
 
+def lanes(shape):
+    return lax.broadcasted_iota(jnp.int32, shape, len(shape) - 1)
+
+
+def transposed(block):
+    return jnp.swapaxes(block, 0, 1)
+
+
 def head_groups(meta_ref):
     odd = meta_ref[0]
     return ((4, 2 * odd, odd), (2, 4 * (1 - odd), 1 - odd))
 
 
-def attend_kernel(meta_ref, query_ref, key_ref, value_ref, start_ref, out_ref, acc_ref):
-    rows = query_ref.shape[1]
-    base = key_ref.shape[1] - rows
-    lane = lax.broadcasted_iota(jnp.int32, (TILE, 2 * HEAD), 1)
+def split_window(kv_ref, keys, values, step):
+    per_block = kv_ref.shape[2] // TILE
+    block, part = step // per_block, step % per_block
+    source = pl.ds(pl.multiple_of(part * TILE, TILE), TILE)
+    target = pl.ds(pl.multiple_of(step * TILE, TILE), TILE)
+    low = lanes((TILE, 128)) < HEAD
+    for slot in range(2):
+        both = kv_ref[block, slot, source, :].astype(F32)
+        moved = pltpu.roll(both, HEAD, 1)
+        keys[slot, target, 0:128] = jnp.where(low, both, moved).astype(BF)
+        values[slot, target, :] = jnp.where(low, moved, 1.0).astype(BF)
+    return target
+
+
+def attend_kernel(
+    meta_ref, query_ref, kv_ref, start_ref, out_ref, low_ref, acc_ref, keys, values
+):
+    heads, rows, _ = query_ref.shape
+    base = keys.shape[1] - rows
+    lane = lanes((TILE, 128))
+
+    def fill(step, carry):
+        split_window(kv_ref, keys, values, step)
+        return carry
+
+    lax.fori_loop(0, keys.shape[1] // TILE, fill, 0)
     for count, first, slot in head_groups(meta_ref):
         for tile in range(rows // TILE):
             q_at = tile * TILE
@@ -273,7 +250,7 @@
 
             def step(at, carry, masked):
                 k_at = pl.multiple_of(at * TILE, TILE)
-                scores = nt(queries, key_ref[slot, pl.ds(k_at, TILE), :])
+                scores = nt(queries, keys[slot, pl.ds(k_at, TILE), :])
                 if masked:
                     k_pos = k_at + lax.broadcasted_iota(jnp.int32, (1, TILE), 1)
                     allowed = (start_col <= k_pos) & (k_pos <= q_pos)
@@ -281,12 +258,12 @@
                         allowed[None], scores.reshape(count, TILE, TILE), NEG
                     ).reshape(count * TILE, TILE)
                 weights = jnp.exp2(scores).astype(BF)
-                acc[...] += nn(weights, value_ref[slot, pl.ds(k_at, TILE), :])
+                acc[...] += nn(weights, values[slot, pl.ds(k_at, TILE), :])
                 return carry
 
             begin = low // TILE
-            clear = jnp.minimum((high + TILE - 1) // TILE, (base + q_at) // TILE)
             last = (base + q_at) // TILE
+            clear = jnp.minimum((high + TILE - 1) // TILE, last)
             lax.fori_loop(begin, clear, functools.partial(step, masked=True), 0)
             lax.fori_loop(clear, last, functools.partial(step, masked=False), 0)
             step(last, 0, True)
@@ -297,41 +274,106 @@
                     lane < HEAD, part / total, jnp.log2(total)
                 )
 
-
-def attend(meta, queries, keys, values, starts):
+    def lay(step, carry):
+        tile = pl.ds(pl.multiple_of(step * TILE, TILE), TILE)
+        for t in range(heads // 2):
+            pair = jnp.where(
+                lane < HEAD, out_ref[2 * t, tile, :], pltpu.roll(out_ref[2 * t + 1, tile, :], HEAD, 1)
+            )
+            low_ref[tile, t * 128 : (t + 1) * 128] = pair.astype(BF)
+        return carry
+
+    lax.fori_loop(0, rows // TILE, lay, 0)
+
+
+def attend(meta, queries, kv, starts):
     heads, rows, _ = queries.shape
+    window = kv.shape[0] * rows
+    vmem = pl.BlockSpec(memory_space=pltpu.VMEM)
     return pl.pallas_call(
         attend_kernel,
-        out_shape=jax.ShapeDtypeStruct((heads, rows, 2 * HEAD), F32),
-        in_specs=[pl.BlockSpec(memory_space=pltpu.SMEM)]
-        + [pl.BlockSpec(memory_space=pltpu.VMEM)] * 4,
-        out_specs=pl.BlockSpec(memory_space=pltpu.VMEM),
-        scratch_shapes=[pltpu.VMEM((4 * TILE, 2 * HEAD), F32)],
+        out_shape=(
+            jax.ShapeDtypeStruct((heads, rows, 2 * HEAD), F32),
+            jax.ShapeDtypeStruct((rows, heads * HEAD), BF),
+        ),
+        in_specs=[pl.BlockSpec(memory_space=pltpu.SMEM)] + [vmem] * 3,
+        out_specs=(vmem, vmem),
+        scratch_shapes=[
+            pltpu.VMEM((4 * TILE, 2 * HEAD), F32),
+            pltpu.VMEM((2, window, 2 * HEAD), BF),
+            pltpu.VMEM((2, window, 2 * HEAD), BF),
+        ],
         compiler_params=pltpu.CompilerParams(vmem_limit_bytes=48 << 20),
         cost_estimate=pl.CostEstimate(
-            flops=30_000_000_000, bytes_accessed=20_000_000, transcendentals=20_000_000
+            flops=60_000_000_000, bytes_accessed=20_000_000, transcendentals=20_000_000
         ),
         name="attend",
-    )(meta, queries, keys, values, starts)
+    )(meta, queries, kv, starts)
 
 
 def attend_back_kernel(
     meta_ref,
-    key_ref,
-    value_ref,
-    key_t_ref,
-    query_t_ref,
-    grad_t_ref,
+    wide_ref,
     query_ref,
+    kv_ref,
+    out_ref,
     grad_ref,
     start_ref,
     dq_ref,
-    dkv_ref,
+    dkv_low_ref,
+    dkv_own_ref,
+    keys,
+    values,
+    keys_t,
+    query_t,
+    grad_t,
+    grads,
+    dq,
+    dkv,
 ):
-    rows = query_ref.shape[1]
-    base = key_ref.shape[1] - rows
-    dkv_ref[...] = jnp.zeros_like(dkv_ref)
-    dq_ref[...] = jnp.zeros_like(dq_ref)
+    heads, rows, _ = query_ref.shape
+    window = keys.shape[1]
+    base = window - rows
+    lane = lanes((TILE, 128))
+    low_lane = lane < HEAD
+
+    def fill(step, carry):
+        target = split_window(kv_ref, keys, values, step)
+        for slot in range(2):
+            keys[slot, target, 128:256] = jnp.ones((TILE, 128), BF)
+            keys_t[slot, :, target] = transposed(keys[slot, target, 0:128])[0:HEAD, :]
+            dkv[slot, target, :] = jnp.zeros((TILE, 128), F32)
+        return carry
+
+    lax.fori_loop(0, window // TILE, fill, 0)
+
+    def low_terms(value, first):
+        out = jnp.zeros_like(value)
+        for i in range(3):
+            term = value.astype(BF).astype(F32)
+            out = jnp.where(lane == first + i, term, out)
+            value = value - term
+        return out
+
+    def turn(step, carry):
+        tile = pl.ds(pl.multiple_of(step * TILE, TILE), TILE)
+        for j in range(heads):
+            query_t[j, 0:128, tile] = transposed(wide_ref[j, tile, :])
+            kept = out_ref[j, tile, :]
+            query_t[j, 128:256, tile] = transposed(low_terms(-kept, HEAD).astype(BF))
+            grad = grad_ref[tile, (j // 2) * 128 : (j // 2) * 128 + 128].astype(F32)
+            moved = pltpu.roll(grad, HEAD, 1)
+            if j % 2:
+                grad, moved = moved, grad
+            dots = jnp.sum(jnp.where(low_lane, grad * kept, 0.0), axis=1, keepdims=True)
+            dots = jnp.broadcast_to(-dots, (TILE, 128))
+            block = jnp.where(low_lane, grad, low_terms(dots, HEAD))
+            grad_t[j, :, tile] = transposed(block.astype(BF))
+            grads[j, tile, :] = jnp.where(low_lane, 0.0, moved).astype(BF)
+            dq[j, :, tile] = jnp.zeros((HEAD, TILE), F32)
+        return carry
+
+    lax.fori_loop(0, rows // TILE, turn, 0)
     for count, first, slot in head_groups(meta_ref):
         for tile in range(rows // TILE):
             q_at = tile * TILE
@@ -343,54 +385,86 @@
             def step(at, carry, masked):
                 k_at = pl.multiple_of(at * TILE, TILE)
                 k_rows = pl.ds(k_at, TILE)
-                keys = key_ref[slot, k_rows, :]
-                values = value_ref[slot, k_rows, :]
-                key_t = key_t_ref[slot, :, k_rows]
+                key_block = keys[slot, k_rows, :]
+                value_block = values[slot, k_rows, :]
+                key_t = keys_t[slot, :, k_rows]
                 if masked:
                     k_pos = k_at + lax.broadcasted_iota(jnp.int32, (TILE, 1), 0)
                     allowed = (start_row <= k_pos) & (k_pos <= q_pos)
-                total = dkv_ref[slot, k_rows, :]
+                total = dkv[slot, k_rows, :]
                 for j in range(count):
-                    scores = nn(keys, query_t_ref[first + j, :, q_cols])
+                    scores = nn(key_block, query_t[first + j, :, q_cols])
                     if masked:
                         scores = jnp.where(allowed, scores, NEG)
                     probs = jnp.exp2(scores)
-                    diff = nn(values, grad_t_ref[first + j, :, q_cols])
+                    diff = nn(value_block, grad_t[first + j, :, q_cols])
                     grad_score = (probs * diff).astype(BF)
                     total = (
                         total
-                        + nn(probs.astype(BF), grad_ref[first + j, q_cols, :])
+                        + nn(probs.astype(BF), grads[first + j, q_cols, :])
                         + nn(grad_score, query_ref[first + j, q_cols, :])
                     )
-                    dq_ref[first + j, :, q_cols] += nn(key_t, grad_score)
-                dkv_ref[slot, k_rows, :] = total
+                    dq[first + j, :, q_cols] += nn(key_t, grad_score)
+                dkv[slot, k_rows, :] = total
                 return carry
 
             begin = low // TILE
-            clear = jnp.minimum((high + TILE - 1) // TILE, (base + q_at) // TILE)
             last = (base + q_at) // TILE
+            clear = jnp.minimum((high + TILE - 1) // TILE, last)
             lax.fori_loop(begin, clear, functools.partial(step, masked=True), 0)
             lax.fori_loop(clear, last, functools.partial(step, masked=False), 0)
             step(last, 0, True)
 
-
-def attend_back(meta, keys, values, keys_t, queries_t, grads_t, queries, grads, starts):
+    def finish(step, carry):
+        tile = pl.ds(pl.multiple_of(step * TILE, TILE), TILE)
+        for t in range(heads // 2):
+            pair = jnp.concatenate([dq[2 * t, :, tile], dq[2 * t + 1, :, tile]], axis=0)
+            dq_ref[tile, t * 128 : (t + 1) * 128] = transposed(pair) * SCALE
+        per_block = rows // TILE
+        for slot in range(2):
+            for block in range(BACK + 1):
+                source = pl.ds(pl.multiple_of(block * rows + step * TILE, TILE), TILE)
+                part = dkv[slot, source, :]
+                part = jnp.where(low_lane, part * SCALE, part)
+                if block < BACK:
+                    dkv_low_ref[block, slot, tile, :] = part.astype(BF)
+                else:
+                    dkv_own_ref[slot, tile, :] = part
+        return carry
+
+    lax.fori_loop(0, rows // TILE, finish, 0)
+
+
+def attend_back(meta, wide, queries, kv, kept, grads, starts):
     heads, rows, _ = queries.shape
+    window = kv.shape[0] * rows
+    vmem = pl.BlockSpec(memory_space=pltpu.VMEM)
+    shape = jax.ShapeDtypeStruct
     return pl.pallas_call(
         attend_back_kernel,
         out_shape=(
-            jax.ShapeDtypeStruct((heads, HEAD, rows), F32),
-            jax.ShapeDtypeStruct((2, keys.shape[1], 2 * HEAD), F32),
+            shape((rows, heads * HEAD), F32),
+            shape((BACK, 2, rows, 128), BF),
+            shape((2, rows, 128), F32),
         ),
-        in_specs=[pl.BlockSpec(memory_space=pltpu.SMEM)]
-        + [pl.BlockSpec(memory_space=pltpu.VMEM)] * 8,
-        out_specs=(pl.BlockSpec(memory_space=pltpu.VMEM),) * 2,
+        in_specs=[pl.BlockSpec(memory_space=pltpu.SMEM)] + [vmem] * 6,
+        out_specs=(vmem,) * 3,
+        scratch_shapes=[
+            pltpu.VMEM((2, window, 256), BF),
+            pltpu.VMEM((2, window, 128), BF),
+            pltpu.VMEM((2, HEAD, window), BF),
+            pltpu.VMEM((heads, 256, rows), BF),
+            pltpu.VMEM((heads, 128, rows), BF),
+            pltpu.VMEM((heads, rows, 128), BF),
+            pltpu.VMEM((heads, HEAD, rows), F32),
+            pltpu.VMEM((2, window, 128), F32),
+        ],
         compiler_params=pltpu.CompilerParams(vmem_limit_bytes=56 << 20),
         cost_estimate=pl.CostEstimate(
-            flops=70_000_000_000, bytes_accessed=40_000_000, transcendentals=20_000_000
+            flops=120_000_000_000, bytes_accessed=40_000_000, transcendentals=20_000_000
         ),
         name="attend_back",
-    )(meta, keys, values, keys_t, queries_t, grads_t, queries, grads, starts)
+    )(meta, wide, queries, kv, kept, grads, starts)
 
 
 MESH = pl.DeviceIdType.MESH
@@ -399,10 +473,6 @@
 BACK_TOP, BACK_LOW, BACK_FAR, BACK_ACROSS, HEADS_BACK, SUM_ON = 19, 20, 21, 22, 23, 26
 TRANSFERS = 30
 SPANS = ((0, 256), (256, 256), (512, 128))
-
-
-def transposed(block):
-    return jnp.swapaxes(block, 0, 1)
 
 
 def middle_kernel(
@@ -880,6 +950,452 @@
     )(attn_out, tokens, w_o, gain, w_d, top, *slabs)
 
 
+TOK_NEAR, TOK_FAR, TOK_ON, IN_QUERY, IN_REST = 0, 1, 2, 3, 6
+TOP_NEAR, TOP_FAR, TOP_ACROSS, TOP_FAR_ON, TOP_ACROSS_ON = 9, 10, 11, 12, 13
+TOP_CORNER_HIGH, TOP_CORNER_LOW, TOP_CORNER_ON = 14, 15, 16
+UNITS_MOVE, SLAB_ON, DOWN_MOVE, DOWN_ONE, DOWN_TWO = 17, 31, 32, 33, 34
+KV_ONE, KV_TWO, KV_PAIR_ONE, KV_PAIR_TWO, FIRST_TRANSFERS = 35, 36, 37, 38, 39
+COLS_Q = QHEADS // 4 * HEAD
+COLS_IN = COLS_Q + 4 * HEAD
+
+
+def head_scale(block):
+    low = lanes(block.shape) < HEAD
+    square = block * block
+    first = jnp.sum(jnp.where(low, square, 0.0), axis=1, keepdims=True)
+    second = jnp.sum(jnp.where(low, 0.0, square), axis=1, keepdims=True)
+    return jnp.where(
+        low, lax.rsqrt(first / HEAD + EPS), lax.rsqrt(second / HEAD + EPS)
+    )
+
+
+def swap_halves(block):
+    low = lanes(block.shape) % HEAD < HEAD // 2
+    return jnp.where(low, pltpu.roll(block, 96, 1), pltpu.roll(block, 32, 1))
+
+
+def first_kernel(
+    line,
+    tokens_ref,
+    query_ref,
+    rest_ref,
+    gate_ref,
+    up_ref,
+    down_ref,
+    top_ref,
+    cos_ref,
+    sin_ref,
+    query_gain_ref,
+    key_gain_ref,
+    wide_out,
+    query_out,
+    kv_out,
+    raw_out,
+    normed_out,
+    w_in_out,
+    tops_out,
+    slab_out,
+    slab_next,
+    down_out,
+    down_one,
+    down_two,
+    gain_out,
+    toks,
+    normed,
+    w_in,
+    raw,
+    wide,
+    query,
+    kv_own,
+    sends,
+    recvs,
+    ring_sends,
+    ring_recvs,
+    swap_sends,
+    swap_recvs,
+    locals_,
+):
+    me, at = lax.axis_index("head"), lax.axis_index("blk")
+    count = lax.axis_size("blk")
+    side, place = at % 2, at // 2
+    odd = me % 2
+    mate, beside, corner = me + 1 - 2 * odd, (me + 2) % 4, (me + 3 - 2 * odd) % 4
+    other = at + 1 - 2 * side
+    after, before = (at + 2) % count, (at + count - 2) % count
+    rows, width = tokens_ref.shape
+    half = rows // 2
+    w_rows = query_ref.shape[0]
+    units = slab_out.shape[2] // 2
+    piece_to = 2 * (at % line) + at // line
+    piece_from = (at % 2) * line + at // 2
+    stays = piece_to == at
+
+    barrier = pltpu.get_barrier_semaphore()
+    peers = [(mate, at), (beside, at), (corner, at), (me, after), (me, before)]
+    peers += [(head, other) for head in (me, mate, beside, corner)]
+    for peer in peers:
+        pl.semaphore_signal(barrier, inc=1, device_id=peer, device_id_type=MESH)
+
+    @pl.when(jnp.logical_not(stays))
+    def _():
+        for peer in ((me, piece_to), (me, piece_from)):
+            pl.semaphore_signal(barrier, inc=1, device_id=peer, device_id_type=MESH)
+
+    pl.semaphore_wait(barrier, jnp.where(stays, len(peers), len(peers) + 2))
+
+    def remote(index, source, target, device, send=sends, recv=recvs):
+        return pltpu.make_async_remote_copy(
+            src_ref=source,
+            dst_ref=target,
+            send_sem=send.at[index],
+            recv_sem=recv.at[index],
+            device_id=device,
+            device_id_type=MESH,
+        )
+
+    def local(index, source, target):
+        return pltpu.make_async_copy(source, target, locals_.at[index])
+
+    def cols_of(ref, start, size):
+        return ref.at[:, pl.ds(pl.multiple_of(start, 128), size)]
+
+    own_q = w_in.at[me, at, :, pl.ds(0, COLS_Q)]
+    own_rest = w_in.at[me, at, :, pl.ds(COLS_Q, COLS_Q)]
+    split = []
+    for i, to in enumerate((mate, beside, corner)):
+        split.append(
+            remote(IN_QUERY + i, cols_of(query_ref, to * COLS_Q, COLS_Q), own_q, (to, at))
+        )
+        split.append(remote(IN_REST + i, rest_ref.at[to], own_rest, (to, at)))
+    for copy in split:
+        copy.start()
+    own = [
+        local(0, cols_of(query_ref, me * COLS_Q, COLS_Q), own_q),
+        local(1, rest_ref.at[me], own_rest),
+        local(2, tokens_ref, toks.at[me]),
+        local(3, top_ref, tops_out.at[side * 4 + me]),
+    ]
+    for copy in own:
+        copy.start()
+    tok_near = remote(TOK_NEAR, tokens_ref, toks.at[me], (mate, at))
+    tok_far = remote(TOK_FAR, tokens_ref, toks.at[me], (beside, at))
+    tok_on = remote(TOK_ON, toks.at[beside], toks.at[beside], (mate, at))
+    tok_far.start()
+    tok_near.start()
+    down_move = remote(DOWN_MOVE, down_ref, down_out, (me, piece_to))
+    down_stay = local(4, down_ref, down_out)
+
+    @pl.when(jnp.logical_not(stays))
+    def _():
+        down_move.start()
+
+    @pl.when(stays)
+    def _():
+        down_stay.start()
+
+    def units_at(ref, to_side, to_head):
+        return cols_of(ref, (to_head * 2 + to_side) * units, units)
+
+    slab_rows = pl.ds(pl.multiple_of(side * w_rows, 16), w_rows)
+    targets = [(side, mate), (side, beside), (side, corner)]
+    targets += [(1 - side, head) for head in (me, mate, beside, corner)]
+    spread = []
+    for i, (to_side, to_head) in enumerate(targets):
+        device = (to_head, at if i < 3 else other)
+        for j, ref in enumerate((gate_ref, up_ref)):
+            spread.append(
+                remote(
+                    UNITS_MOVE + 2 * i + j,
+                    units_at(ref, to_side, to_head),
+                    slab_out.at[me, slab_rows, pl.ds(j * units, units)],
+                    device,
+                )
+            )
+    for copy in spread:
+        copy.start()
+    own_units = [
+        local(
+            5 + j,
+            units_at(ref, side, me),
+            slab_out.at[me, slab_rows, pl.ds(j * units, units)],
+        )
+        for j, ref in enumerate((gate_ref, up_ref))
+    ]
+    for copy in own_units:
+        copy.start()
+
+    def ring_copy(step):
+        block = w_in.at[:, (at + count - 2 * (step - 1)) % count]
+        return remote(step, block, block, (me, after), ring_sends, ring_recvs)
+
+    def swap_copy(step):
+        block = w_in.at[:, (at + count - 2 * step) % count]
+        return remote(step, block, block, (me, other), swap_sends, swap_recvs)
+
+    for copy in split:
+        copy.wait_recv()
+    own[0].wait()
+    own[1].wait()
+    ring_copy(1).start()
+    swap_copy(0).start()
+    tok_far.wait_recv()
+    tok_on.start()
+    top_slot = side * 4 + me
+    far_slot, across_slot = side * 4 + beside, (1 - side) * 4 + me
+    corner_slot = (1 - side) * 4 + beside
+    top_near = remote(TOP_NEAR, top_ref, tops_out.at[top_slot], (mate, at))
+    top_far = remote(TOP_FAR, top_ref, tops_out.at[top_slot], (beside, at))
+    top_across = remote(TOP_ACROSS, top_ref, tops_out.at[top_slot], (me, other))
+    top_far_on = remote(
+        TOP_FAR_ON, tops_out.at[far_slot], tops_out.at[far_slot], (mate, at)
+    )
+    top_across_on = remote(
+        TOP_ACROSS_ON, tops_out.at[across_slot], tops_out.at[across_slot], (mate, at)
+    )
+    top_corner_on = remote(
+        TOP_CORNER_ON, tops_out.at[corner_slot], tops_out.at[corner_slot], (mate, at)
+    )
+    high = tops_out.at[far_slot, pl.ds(0, half)]
+    low = tops_out.at[across_slot, pl.ds(half, half)]
+    top_corner_high = remote(TOP_CORNER_HIGH, high, high, (me, other))
+    top_corner_low = remote(TOP_CORNER_LOW, low, low, (beside, at))
+    top_near.start()
+    top_far.start()
+    for step in range(1, line):
+        ring_copy(step).wait_recv()
+        if step < line - 1:
+            ring_copy(step + 1).start()
+        swap_copy(step).start()
+
+    @pl.when(jnp.logical_not(stays))
+    def _():
+        down_move.wait_recv()
+
+    @pl.when(stays)
+    def _():
+        down_stay.wait()
+
+    down_on = remote(DOWN_ONE, down_out, down_one, (me, after))
+    down_on.start()
+    for copy in spread:
+        copy.wait_recv()
+    for copy in own_units:
+        copy.wait()
+    slab_on = remote(SLAB_ON, slab_out, slab_next, (me, after))
+    slab_on.start()
+    tok_near.wait_recv()
+    tok_on.wait_recv()
+    own[2].wait()
+    own[3].wait()
+    for step in range(line):
+        swap_copy(step).wait_recv()
+    top_across.start()
+    keep_in = [
+        local(7 + h, w_in.at[h], w_in_out.at[h]) for h in range(4)
+    ]
+    for copy in keep_in:
+        copy.start()
+
+    gains = w_in[:, :, :, COLS_IN : COLS_IN + 128].reshape(width, 128).astype(F32)
+    gain_out[...] = transposed(gains)[0:8, :]
+
+    def norm_tile(step, carry):
+        head, tile = step // (rows // 32), pl.ds(pl.multiple_of(step % (rows // 32) * 32, 32), 32)
+        block = toks[head, tile, :].astype(F32)
+        scale = lax.rsqrt(jnp.mean(block * block, axis=1, keepdims=True) + EPS)
+        normed[pl.ds(pl.multiple_of(step * 32, 32), 32), :] = (
+            block * scale * gain_out[0:1, :]
+        ).astype(BF)
+        return carry
+
+    lax.fori_loop(0, 4 * rows // 32, norm_tile, 0)
+    keep_normed = local(11, normed, normed_out)
+    keep_normed.start()
+
+    def project(step, carry):
+        tile = pl.ds(pl.multiple_of(step * 256, 256), 256)
+        for first, size in SPANS:
+            weight = w_in[:, :, :, first : first + size].reshape(width, size)
+            raw[tile, first : first + size] = nn(normed[tile, :], weight)
+        return carry
+
+    lax.fori_loop(0, 4 * rows // 256, project, 0)
+    keep_raw = local(12, raw.at[:, pl.ds(0, COLS_Q + 128)], raw_out)
+    keep_raw.start()
+
+    def rotated(block, gain, tile):
+        block = block * head_scale(block) * gain
+        return block * cos_ref[tile, :] + swap_halves(block) * sin_ref[tile, :]
+
+    def prepare(step, carry):
+        tile = pl.ds(pl.multiple_of(step * 64, 64), 64)
+        first_half = lanes((64, 128)) < HEAD
+        for t in range(QHEADS // 4 // 2):
+            block = rotated(raw[tile, t * 128 : (t + 1) * 128], query_gain_ref[...], tile)
+            block = block.astype(BF).astype(F32)
+            moved = pltpu.roll(block, HEAD, 1)
+            query[2 * t, tile, :] = jnp.where(first_half, block, 0.0).astype(BF)
+            query[2 * t + 1, tile, :] = jnp.where(first_half, moved, 0.0).astype(BF)
+            scaled = block * (SCALE * LOG2E)
+            upper = scaled.astype(BF).astype(F32)
+            lower = scaled - upper
+            wide[2 * t, tile, :] = jnp.where(
+                first_half, upper, pltpu.roll(lower, HEAD, 1)
+            ).astype(BF)
+            wide[2 * t + 1, tile, :] = jnp.where(
+                first_half, pltpu.roll(upper, HEAD, 1), lower
+            ).astype(BF)
+        keys = rotated(raw[tile, COLS_Q : COLS_Q + 128], key_gain_ref[...], tile)
+        values = raw[tile, COLS_Q + 128 : COLS_Q + 256]
+        kv_own[0, tile, :] = jnp.where(
+            first_half, keys, pltpu.roll(values, HEAD, 1)
+        ).astype(BF)
+        kv_own[1, tile, :] = jnp.where(
+            first_half, pltpu.roll(keys, HEAD, 1), values
+        ).astype(BF)
+        return carry
+
+    lax.fori_loop(0, 4 * rows // 64, prepare, 0)
+
+    kv_one = remote(KV_ONE, kv_own, kv_out.at[2], (me, after))
+    kv_two = remote(KV_TWO, kv_out.at[2], kv_out.at[0], (me, after))
+    pair_one_even = remote(KV_PAIR_ONE, kv_own, kv_out.at[3], (me, other))
+    pair_one_odd = remote(KV_PAIR_ONE, kv_out.at[2], kv_out.at[3], (me, other))
+    pair_two_even = remote(KV_PAIR_TWO, kv_out.at[2], kv_out.at[1], (me, other))
+    pair_two_odd = remote(KV_PAIR_TWO, kv_out.at[0], kv_out.at[1], (me, other))
+    kv_one.start()
+
+    @pl.when(side == 0)
+    def _():
+        pair_one_even.start()
+
+    keep = [
+        local(13, kv_own, kv_out.at[4]),
+        local(14, wide, wide_out),
+        local(15, query, query_out),
+    ]
+    for copy in keep:
+        copy.start()
+    top_far.wait_recv()
+    top_far_on.start()
+    top_corner_high.start()
+    kv_one.wait_recv()
+    kv_two.start()
+
+    @pl.when(side == 0)
+    def _():
+        pair_two_even.start()
+
+    @pl.when(side == 1)
+    def _():
+        pair_one_odd.start()
+
+    down_on.wait_recv()
+    top_across.wait_recv()
+    top_across_on.start()
+    top_corner_low.start()
+    kv_two.wait_recv()
+
+    @pl.when(side == 1)
+    def _():
+        pair_two_odd.start()
+
+    down_last = remote(DOWN_TWO, down_one, down_two, (me, after))
+    down_last.start()
+    top_corner_high.wait_recv()
+    top_corner_low.wait_recv()
+    top_corner_on.start()
+
+    pair_one_even.wait_recv()
+    pair_two_even.wait_recv()
+    down_last.wait_recv()
+    slab_on.wait_recv()
+    for copy in (top_near, top_far_on, top_across_on, top_corner_on):
+        copy.wait_recv()
+    for copy in keep + keep_in + [keep_normed, keep_raw]:
+        copy.wait()
+    for copy in split + spread:
+        copy.wait_send()
+    for copy in (tok_near, tok_far, tok_on, top_near, top_far, top_across, top_far_on):
+        copy.wait_send()
+    for copy in (top_across_on, top_corner_high, top_corner_low, top_corner_on):
+        copy.wait_send()
+    for copy in (slab_on, down_on, down_last, kv_one, kv_two):
+        copy.wait_send()
+    pair_one_even.wait_send()
+    pair_two_even.wait_send()
+
+    @pl.when(jnp.logical_not(stays))
+    def _():
+        down_move.wait_send()
+
+    for step in range(line):
+        swap_copy(step).wait_send()
+        if step:
+            ring_copy(step).wait_send()
+
+
+def first(
+    tokens, w_query, rest, w_gate, w_up, w_down, cotangent, cosine, sine, query_gain, key_gain
+):
+    rows, width = tokens.shape
+    count = lax.axis_size("blk")
+    w_rows, ff = w_gate.shape
+    units = ff // 8
+    block = 4 * rows
+    anywhere = pl.BlockSpec(memory_space=pl.ANY)
+    vmem = pl.BlockSpec(memory_space=pltpu.VMEM)
+    shape = jax.ShapeDtypeStruct
+    heads = QHEADS // 4
+    slab = shape((4, 2 * w_rows, 2 * units), BF)
+    dma = pltpu.SemaphoreType.DMA
+    return pl.pallas_call(
+        functools.partial(first_kernel, count // 2),
+        out_shape=(
+            shape((heads, block, 128), BF),
+            shape((heads, block, 128), BF),
+            shape((BACK + 1, 2, block, 128), BF),
+            shape((block, COLS_Q + 128), F32),
+            shape((block, width), BF),
+            shape((4, count, w_rows, 2 * COLS_Q), BF),
+            shape((8, rows, width), BF),
+            slab,
+            slab,
+            shape(w_down.shape, BF),
+            shape(w_down.shape, BF),
+            shape(w_down.shape, BF),
+            shape((8, width), F32),
+        ),
+        in_specs=[anywhere] * 7 + [vmem] * 4,
+        out_specs=(anywhere,) * 12 + (vmem,),
+        scratch_shapes=[
+            pltpu.VMEM((4, rows, width), BF),
+            pltpu.VMEM((block, width), BF),
+            pltpu.VMEM((4, count, w_rows, 2 * COLS_Q), BF),
+            pltpu.VMEM((block, COLS_IN), F32),
+            pltpu.VMEM((heads, block, 128), BF),
+            pltpu.VMEM((heads, block, 128), BF),
+            pltpu.VMEM((2, block, 128), BF),
+            dma((FIRST_TRANSFERS,)),
+            dma((FIRST_TRANSFERS,)),
+            dma((count // 2,)),
+            dma((count // 2,)),
+            dma((count // 2,)),
+            dma((count // 2,)),
+            dma((16,)),
+        ],
+        compiler_params=pltpu.CompilerParams(
+            collective_id=2, has_side_effects=True, vmem_limit_bytes=48 << 20
+        ),
+        cost_estimate=pl.CostEstimate(
+            flops=60_000_000_000, bytes_accessed=60_000_000, transcendentals=1_000_000
+        ),
+        name="first",
+    )(
+        tokens, w_query, rest, w_gate, w_up, w_down, cotangent, cosine, sine, query_gain, key_gain
+    )
+
+
 def norm_rows(tensor, gain_vec):
     return tensor * lax.rsqrt(jnp.mean(tensor * tensor, axis=-1, keepdims=True) + EPS) * gain_vec
 
@@ -892,15 +1408,6 @@
         [first_half * cosine - second * sine_table, second * cosine + first_half * sine_table],
         axis=-1,
     )
-
-
-def split_low(value, parts):
-    out = []
-    for _ in range(parts):
-        term = lax.reduce_precision(value, 8, 7)
-        out.append(term.astype(BF))
-        value = value - term
-    return out
 
 
 def shards(
@@ -936,52 +1443,6 @@
     firsts = [g * per_group // head_ratio for g in range(groups)]
     odd = group_id % 2
 
-    columns = []
-    for g in range(groups):
-        kv = slice(firsts[g] * HEAD, (firsts[g] + 2) * HEAD)
-        columns += [
-            w_query[:, g * q_cols : (g + 1) * q_cols],
-            w_key[:, kv],
-            w_value[:, kv],
-            norm1_gain[:, None],
-            norm2_gain[:, None],
-            jnp.zeros((w_rows, 126), BF),
-        ]
-    qkv_cols = q_cols + 4 * HEAD
-    qkv_wide = qkv_cols + 2 * HEAD
-    w_in = jnp.concatenate(columns, axis=1).reshape(w_rows, groups, qkv_wide)
-    w_in = lax.all_to_all(w_in, "head", split_axis=1, concat_axis=1, tiled=True)
-    down = LineGather(w_down)
-    down.ahead(line - 4)
-    down_moved = down.send()
-    w_in = gather_blk(jnp.swapaxes(w_in, 0, 1), 1).reshape(width, qkv_wide)
-    block_tokens = gather_head(tokens).reshape(block_len, width)
-
-    def by_unit(weight):
-        return weight.reshape(w_rows, groups, line, 2, ff_rows)
-
-    both = jnp.stack([by_unit(w_gate), by_unit(w_up)], axis=3)
-    both = jnp.transpose(both, (4, 1, 0, 3, 2, 5)).reshape(2, groups, w_rows, 2 * ff_cols)
-    w_in, block_tokens, both, down_moved = sync(w_in, block_tokens, both, down_moved)
-    down.held = down_moved
-    down.keep()
-
-    other = swap(take(both, 1 - side), "blk", 1)
-    both = put(jnp.zeros(both.shape, BF), take(both, side), side)
-    both = put(both, other, 1 - side)
-    both = lax.all_to_all(
-        jnp.swapaxes(both, 0, 1), "head", split_axis=0, concat_axis=0, tiled=True
-    )
-    slabs = [both.reshape(groups, 2 * w_rows, 2 * ff_cols)]
-    for _ in range(line - 3):
-        slabs.append(ring(slabs[-1], 2))
-    down_moved = down.send()
-    top = gather_pair(cotangent)
-
-    w_qkv = w_in[:, :qkv_cols]
-    gains = w_in[:, qkv_cols : qkv_cols + 2].astype(F32).T
-    gain_one, gain_two = gains[0], gains[1]
-
     starts = jnp.cumsum(doc_lengths) - doc_lengths
     offsets = jnp.arange(block_len, dtype=jnp.int32)
     token_pos = blk_place * block_len + offsets
@@ -990,8 +1451,9 @@
     in_doc = token_pos - token_start
     rope_freq = jnp.exp(-math.log(10000.0) * jnp.arange(HEAD // 2, dtype=F32) / (HEAD // 2))
     rope_angle = in_doc.astype(F32)[:, None] * rope_freq[None, :]
-    cosine = jnp.cos(rope_angle)[:, None, :]
-    sine_table = jnp.sin(rope_angle)[:, None, :]
+    cosine, sine = jnp.cos(rope_angle), jnp.sin(rope_angle)
+    cosine = jnp.concatenate([cosine] * 4, axis=1)
+    sine = jnp.concatenate([-sine, sine] * 2, axis=1)
     window_start = token_start - (blk_place - BACK) * block_len
     tiles = block_len // TILE
     edges = jnp.stack(
@@ -999,62 +1461,65 @@
     ).reshape(2 * tiles)
     meta = jnp.concatenate([odd[None].astype(jnp.int32), edges.astype(jnp.int32)])
 
+    rest = []
+    for g in range(groups):
+        kv = slice(firsts[g] * HEAD, (firsts[g] + 2) * HEAD)
+        rest += [
+            w_key[:, kv],
+            w_value[:, kv],
+            norm1_gain[:, None],
+            norm2_gain[:, None],
+            jnp.zeros((w_rows, 126), BF),
+        ]
+    rest = jnp.concatenate(rest, axis=1).reshape(w_rows, groups, COLS_Q)
+    rest = jnp.swapaxes(rest, 0, 1)
     query_g = query_gain.astype(F32)
     key_g = key_gain.astype(F32)
-    block_inputs = block_tokens.astype(F32)
-    normed_one = norm_rows(block_inputs, gain_one).astype(BF)
-    raw = matmul(normed_one, w_qkv)
-
-    def prepare(query_raw, key_raw, query_gain_in, key_gain_in):
-        return (
-            rotate(norm_rows(query_raw, query_gain_in), cosine, sine_table),
-            rotate(norm_rows(key_raw, key_gain_in), cosine, sine_table),
-        )
-
-    query_raw = raw[:, :q_cols].reshape(block_len, per_group, HEAD)
-    key_raw = raw[:, q_cols : q_cols + 2 * HEAD].reshape(block_len, 2, HEAD)
-    value_own = raw[:, q_cols + 2 * HEAD :].reshape(block_len, 2, HEAD).astype(BF)
-    (query_rot, key_rot), prep_pull = jax.vjp(prepare, query_raw, key_raw, query_g, key_g)
-    queries = jnp.swapaxes(query_rot.astype(BF), 0, 1)
-    kv_own = jnp.swapaxes(
-        jnp.concatenate([key_rot.astype(BF), value_own], axis=-1), 0, 1
-    )
-    kv_own, down_moved, slabs = sync(kv_own, down_moved, slabs)
-    down.held = down_moved
-    down.keep()
-
-    down_moved = down.send()
-    even = side == 0
-    kv_two = ring(kv_own, 2)
-    kv_one = swap(jnp.where(even, kv_own, kv_two), "blk", 1)
-    kv_four = ring(kv_two, 2)
-    kv_three = swap(jnp.where(even, kv_two, kv_four), "blk", 1)
-    window = jnp.concatenate([kv_four, kv_three, kv_two, kv_one, kv_own], axis=1)
-    key_win, value_win = window[..., :HEAD], window[..., HEAD:]
-    ones = jnp.ones(key_win.shape, BF)
-    keys_wide = jnp.concatenate([key_win, key_win, ones, ones], axis=-1)
-    values_wide = jnp.concatenate([value_win, ones], axis=-1)
-
-    scaled = split_low(queries.astype(F32) * (SCALE * LOG2E), 2)
-    keys_wide, values_wide, down_moved, w_out, top, slabs = sync(
-        keys_wide, values_wide, down_moved, w_out, top, slabs
-    )
-    down.held = down_moved
-    down.keep()
+    (
+        wide,
+        queries,
+        kv_window,
+        raw,
+        normed_one,
+        w_in,
+        top,
+        slab,
+        slab_next,
+        down_own,
+        down_one,
+        down_two,
+        gains,
+    ) = first(
+        tokens,
+        w_query,
+        rest,
+        w_gate,
+        w_up,
+        w_down,
+        cotangent,
+        cosine,
+        sine,
+        jnp.concatenate([query_g, query_g])[None, :],
+        jnp.concatenate([key_g, key_g])[None, :],
+    )
+    w_in = w_in.reshape(width, 2 * q_cols)
+    gain_one, gain_two = gains[0], gains[1]
+    slabs, downs = [slab, slab_next], [down_own, down_one, down_two]
+    for _ in range(line - 4):
+        slabs.append(ring(slabs[-1], 2))
+        downs.append(ring(downs[-1], 2))
+    slabs, downs, w_out, queries = sync(slabs, downs, w_out, queries)
     slabs.append(ring(slabs[-1], 2))
+    downs.append(ring(downs[-1], 2))
     w_o = gather_blk(w_out, 0).reshape(blocks * w_out.shape[0], width)
     w_o = gather_head(w_o).reshape(QHEADS * HEAD, width)
-    attended = attend(
-        meta,
-        jnp.concatenate(scaled, axis=-1),
-        keys_wide[..., : 2 * HEAD],
-        values_wide,
-        window_start[:, None],
-    )
-    attended, slabs, w_o = sync(attended, slabs, w_o)
-    attn_keep = attended[..., :HEAD]
-    log_total = attended[..., HEAD]
-    attn_out = jnp.swapaxes(attn_keep.astype(BF), 0, 1).reshape(groups, tok_rows, q_cols)
+    kept, attn_out = attend(meta, wide, kv_window, window_start[:, None])
+    kept, attn_out, slabs, downs, w_o = sync(kept, attn_out, slabs, downs, w_o)
+    place = blk_place // 2
+    w_d = jnp.zeros((line, ff_rows, width), BF)
+    for step, block in enumerate(downs):
+        w_d = put(w_d, block, (place - step) % line)
+    attn_out = attn_out.reshape(groups, tok_rows, q_cols)
 
     (
         resid,
@@ -1073,8 +1538,8 @@
         w_o,
         gain_two[None, :],
         slabs,
-        down.full.reshape(ff_cols, width),
-        top.reshape(2 * groups, tok_rows, width),
+        w_d.reshape(ff_cols, width),
+        top,
     )
     grad_gain_two = grad_gain_two[0]
     inputs = tokens.astype(F32)
@@ -1086,47 +1551,34 @@
     gu_sum.add()
     out_part = out_part.reshape(2, groups, tok_rows, width)
     out_parts = matmul_tn(mixed, grad_attn).astype(BF).reshape(groups, -1, width)
-    grad_mix = jnp.swapaxes(grad_mix.reshape(block_len, per_group, HEAD), 0, 1)
-    row_dots = jnp.sum(grad_mix.astype(F32) * attn_keep, axis=-1, keepdims=True)
-    low_logs = split_low(-log_total[..., None], 3)
-    low_dots = split_low(-row_dots, 2)
-    blank = jnp.zeros(queries.shape, BF)
-    query_t = jnp.concatenate(
-        scaled + low_logs + [blank, blank[..., : HEAD - 3]], axis=-1
-    )
-    grad_t = jnp.concatenate([grad_mix] + low_dots + [blank[..., : HEAD - 2]], axis=-1)
-    query_t, grad_t = jnp.swapaxes(query_t, 1, 2), jnp.swapaxes(grad_t, 1, 2)
     down_sum.ahead(line - 4)
     gu_sum.ahead(line - 4)
     down_moved, gu_moved = down_sum.send(), gu_sum.send()
     out_act = (resid + scatter_pair(out_part)).astype(BF)
     out_slab = scatter_head(out_parts).astype(BF).reshape(blocks, w_out.shape[0], width)
-    dq_t, dkv = attend_back(
+    dq, dkv, own = attend_back(
         meta,
-        keys_wide,
-        values_wide,
-        jnp.swapaxes(key_win, 1, 2),
-        query_t,
-        grad_t,
-        jnp.concatenate([queries, blank], axis=-1),
-        jnp.concatenate([blank, grad_mix], axis=-1),
+        wide,
+        queries,
+        kv_window,
+        kept,
+        grad_mix.reshape(block_len, q_cols),
         window_start[None, :],
     )
-    dq_t, dkv, down_moved, gu_moved, out_act, out_slab = sync(
-        dq_t, dkv, down_moved, gu_moved, out_act, out_slab
+    dq, dkv, own, down_moved, gu_moved, out_act, out_slab = sync(
+        dq, dkv, own, down_moved, gu_moved, out_act, out_slab
     )
     down_sum.total, gu_sum.total = down_moved, gu_moved
     down_sum.add()
     gu_sum.add()
-    grad_queries = jnp.transpose(dq_t, (2, 0, 1)) * SCALE
-
-    four, three, two, one, own = [
-        dkv[:, i * block_len : (i + 1) * block_len] for i in range(BACK + 1)
-    ]
-    got_three = swap(three.astype(BF), "blk", 1).astype(F32)
-    got_one = swap(one.astype(BF), "blk", 1).astype(F32)
-    four = four + jnp.where(even, 0.0, got_three)
-    two = two + jnp.where(even, got_three, got_one)
+    grad_queries = dq.reshape(block_len, per_group, HEAD)
+
+    even = side == 0
+    four, three, two, one = [dkv[i] for i in range(BACK)]
+    got_three = swap(three, "blk", 1).astype(F32)
+    got_one = swap(one, "blk", 1).astype(F32)
+    four = four.astype(F32) + jnp.where(even, 0.0, got_three)
+    two = two.astype(F32) + jnp.where(even, got_three, got_one)
     own = own + jnp.where(even, got_one, 0.0)
     two = two + ring(four.astype(BF), -2).astype(F32)
     own = own + ring(two.astype(BF), -2).astype(F32)
@@ -1137,9 +1589,13 @@
     gu_sum.add()
     down_sum.send()
     down_sum.add()
-    d_w_down = down_sum.total
+    d_w_down = lax.ppermute(
+        down_sum.total.astype(BF),
+        "blk",
+        [(i, i % 2 * line + i // 2) for i in range(blocks)],
+    ).astype(F32)
     kv_grad = jnp.swapaxes(own, 0, 1)
-    grad_keys = kv_grad[..., :HEAD] * SCALE
+    grad_keys = kv_grad[..., :HEAD]
     grad_values = kv_grad[..., HEAD:]
 
     def to_owner(grad):
@@ -1154,12 +1610,25 @@
     gu_own = put(jnp.zeros((groups, w_rows, 2, 2 * ff_cols), BF), mine, side, 2)
     gu_own = put(gu_own, got, 1 - side, 2)
     gu_own = to_owner(gu_own)
-    gu_own = gu_own.reshape(w_rows, groups, 2, 2, line, ff_rows)
-    gu_own = jnp.transpose(gu_own, (3, 0, 1, 4, 2, 5)).reshape((2,) + w_gate.shape)
-    d_w_gate, d_w_up = gu_own[0], gu_own[1]
+    gu_own = gu_own.reshape(w_rows, groups, 2, 2, ff_cols)
+    d_w_gate = gu_own[:, :, :, 0].reshape(w_gate.shape)
+    d_w_up = gu_own[:, :, :, 1].reshape(w_up.shape)
 
     d_w_out = scatter_blk(lambda b: take(out_slab, b))
 
+    def prepare(query_raw, key_raw, query_gain_in, key_gain_in):
+        cos_half, sin_half = (
+            cosine[:, None, : HEAD // 2],
+            sine[:, None, HEAD // 2 : HEAD],
+        )
+        return (
+            rotate(norm_rows(query_raw, query_gain_in), cos_half, sin_half),
+            rotate(norm_rows(key_raw, key_gain_in), cos_half, sin_half),
+        )
+
+    query_raw = raw[:, :q_cols].reshape(block_len, per_group, HEAD)
+    key_raw = raw[:, q_cols:].reshape(block_len, 2, HEAD)
+    rot_out, prep_pull = jax.vjp(prepare, query_raw, key_raw, query_g, key_g)
     grad_query_raw, grad_key_raw, grad_query_g, grad_key_g = prep_pull((grad_queries, grad_keys))
     gain_sums = sum_all(jnp.stack([grad_query_g, grad_key_g]))
     raw_grads = jnp.concatenate(
@@ -1171,7 +1640,7 @@
         axis=1,
     ).astype(BF)
     grad_w_in = matmul_tn(normed_one, raw_grads)
-    normed_part = matmul_nt(raw_grads, w_qkv).astype(BF)
+    normed_part = matmul_nt(raw_grads, w_in[:, : q_cols + 4 * HEAD]).astype(BF)
     grad_normed_one = scatter_head(normed_part.reshape(groups, tok_rows, width))
     norm_one_out, norm_one_pull = jax.vjp(norm_rows, inputs, gain_one)
     grad_input_part, grad_gain_one = norm_one_pull(grad_normed_one)
@@ -1185,7 +1654,7 @@
         ],
         axis=1,
     )
-    in_parts = grad_w_in.astype(BF).reshape(groups, blocks, w_rows, qkv_wide)
+    in_parts = grad_w_in.astype(BF).reshape(groups, blocks, w_rows, 2 * q_cols)
     owned = to_owner(scatter_blk(lambda b: take(in_parts, b, 1)))
     d_w_query = owned[:, :, :q_cols].reshape(w_rows, QHEADS * HEAD)
     key_heads, value_heads = [], []
@@ -1202,8 +1671,8 @@
         value_heads.append(functools.reduce(jnp.add, values_of))
     d_w_key = jnp.concatenate(key_heads, axis=1)
     d_w_value = jnp.concatenate(value_heads, axis=1)
-    d_norm1_gain = jnp.sum(owned[:, :, qkv_cols], axis=1)
-    d_norm2_gain = jnp.sum(owned[:, :, qkv_cols + 1], axis=1)
+    d_norm1_gain = jnp.sum(owned[:, :, q_cols + 4 * HEAD], axis=1)
+    d_norm2_gain = jnp.sum(owned[:, :, q_cols + 4 * HEAD + 1], axis=1)
     return (
         out_act,
         d_tokens,

time: 1030 us -> 903 us (0.88)
  Pallas kernels: 203 us -> 353 us
  local copies, waits for them, and re-layouts: 219 us -> 87 us
  waiting for transfers between devices: 324 us -> 202 us
  other arithmetic: 110 us -> 79.9 us
  starting transfers between devices: 134 us -> 156 us
    pallas_call x2 -> x3, Pallas kernels: 40.4 us -> 181 us  [the longest x1 133 us: first(): pl.pallas_call(functools.partial(first_kernel, count // 2), out_shape=(sh...]
    ppermute x26 -> x18, waiting for transfers between devices: 194 us -> 127 us  [ring(): lax.ppermute(block, 'blk', [(i, (i + step) % count) for i in range(count)])]
    ppermute x55 -> x37, waiting for transfers between devices: 116 us -> 73.1 us  [swap(): return lax.ppermute(block, axis, [(i, i ^ bit) for i in range(count)])]
    ppermute x26 -> x18, starting transfers between devices: 44.4 us -> 86.4 us  [ring(): lax.ppermute(block, 'blk', [(i, (i + step) % count) for i in range(count)])]
    transpose x7 -> x0, local copies, waits for them, and re-layouts: 23.6 us -> none  [the longest x2 7.84 us: shards(): query_t, grad_t = (jnp.swapaxes(query_t, 1, 2), jnp.swapaxes(grad_t, 1, 2))]
    dynamic_update_slice x8 -> x0, local copies, waits for them, and re-layouts: 18.5 us -> none  [store(): lax.dynamic_update_slice(full, block[None, None], [side, head] + [0] * pa...]
    concatenate x9 -> x1, local copies, waits for them, and re-layouts: 16.9 us -> 0.14 us  [shards(): rest = jnp.concatenate(rest, axis=1).reshape(w_rows, groups, COLS_Q)]
    dynamic_update_slice x15 -> x10, local copies, waits for them, and re-layouts: 22.6 us -> 8.15 us  [put(): return lax.dynamic_update_index_in_dim(full, part, index, axis)]
  transfers between devices with their start and end apart: 85 -> 58, of which waited for: 35 -> 23; matrix products, arithmetic and copies ran while one was open for 29% -> 16% of each run, Pallas kernels for 4% -> 5%
where the time goes in v4:
time: 903 us; the launch traced here: 893 us
  Pallas kernels  353 us (39%)
  waiting for transfers between devices  202 us (22%)
  starting transfers between devices  156 us (17%)
  local copies, waits for them, and re-layouts  87 us (10%)
  other arithmetic  79.9 us (9%)
  matrix products  12.3 us (1%)
    pallas_call x1, Pallas kernels, middle(): pl.pallas_call(functools.partial(middle_kernel, len(slabs), line), out_sh...  171 us
    pallas_call x1, Pallas kernels, first(): pl.pallas_call(functools.partial(first_kernel, count // 2), out_shape=(sh...  133 us
    ppermute x18, waiting for transfers between devices, ring(): lax.ppermute(block, 'blk', [(i, (i + step) % count) for i in range(count)])  127 us
    ppermute x18, starting transfers between devices, ring(): lax.ppermute(block, 'blk', [(i, (i + step) % count) for i in range(count)])  86.4 us
    ppermute x37, waiting for transfers between devices, swap(): return lax.ppermute(block, axis, [(i, i ^ bit) for i in range(count)])  73.1 us
    ppermute x37, starting transfers between devices, swap(): return lax.ppermute(block, axis, [(i, i ^ bit) for i in range(count)])  61.2 us
    pallas_call x1, Pallas kernels, attend_back(): pl.pallas_call(attend_back_kernel, out_shape=(shape((rows, heads * HEAD),...  32.9 us
  transfers between devices with their start and end apart: 58, of which 23 were waited for; matrix products, arithmetic and copies ran while one was open for 16% of the time, Pallas kernels for 5%

profile of v4, /device:TPU:0, one launch (start us, length us, event | category | flops | bytes accessed | tf_op | source)
XLA Modules:
  0.0 892.6 jit_solution(6263941668695630123)
XLA Ops:
  9.3 132.9 %first.1 = (bf16[6,1024,128]{2,1,0:T(8,128)(2,1)}, bf16[6,1024,128]{2,1,0:T(8,128)(2,1)}, bf16[5,2,1024,128]{3,2,1,0:T(8,128)(2,1)}, f32[1024,512]{1,0:T(8,128)}...) custom-call(bf16[256,2048]{1,0:T(8,128)(2,1)} %tokens_ref.3, ...), custom_call_target="tpu_custom_call" | custom-call | flops 60000002048 | bytes 60000000 | tf_op jit(solution)/shard_map/first/pallas_call | solution.py:1352
  147.3 5.1 collective-permute-done.3
  155.5 38.4 %collective-permute-done.5 = bf16[48,2048]{1,0:T(8,128)(2,1)S(1)} collective-permute-done((bf16[48,2048]{1,0:T(8,128)(2,1)S(1)}, bf16[48,2048]{1,0:T(8,128)(2,1)S(1)}, u32[]{:S(2)}, u32[]{:S(2)}) %collective-permute-start.5) | collective-permute-done | bytes 196640 | tf_op jit(solution)/shard_map/ppermute | solution.py:49
  197.0 6.1 collective-permute-done.7
  204.8 4.0 collective-permute-done.8
  212.4 15.6 %attend.1 = (f32[6,1024,128]{2,1,0:T(8,128)}, bf16[1024,384]{1,0:T(8,128)(2,1)S(1)}) custom-call(s32[9]{0:T(128)S(1)} %pad_add_fusion.3.meta_ref, bf16[6,1024,128]{2,1,0:T(8,128)(2,1)S(1)} %copy-done.7, bf16[5,2,1024,128]{3,2,1,0:T(8,128)(2,1)S(1)} %copy-done.6, s32[1024,1]{1,0:T(8,128)S(1)} %copy.137.start_ref), custom_call_target="tpu_custom_call" | custom-call | flops 60000002048 | bytes 20000000 | tf_op jit(solution)/shard_map/attend/pallas_call | solution.py:293
  237.4 9.2 %collective-permute-done.10 = bf16[384,2048]{1,0:T(8,128)(2,1)} collective-permute-done((bf16[384,2048]{1,0:T(8,128)(2,1)}, bf16[384,2048]{1,0:T(8,128)(2,1)}, u32[]{:S(2)}, u32[]{:S(2)}) %collective-permute-start.10) | collective-permute-done | bytes 1572896 | tf_op jit(solution)/shard_map/ppermute | solution.py:44
  259.1 171.3 %middle.1 = (f32[256,2048]{1,0:T(8,128)}, f32[256,2048]{1,0:T(8,128)}, bf16[256,2048]{1,0:T(8,128)(2,1)}, bf16[256,1536]{1,0:T(8,128)(2,1)}, bf16[4,256,384]{2,1...) custom-call(bf16[4,256,384]{2,1,0:T(8,128)(2,1)} %bitcast.252, ...), custom_call_target="tpu_custom_call" | custom-call | flops 60000002048 | bytes 100000000 | tf_op jit(solution)/shard_map/middle/pallas_call | solution.py:904
  439.8 5.2 convert_add_fusion.9
  456.5 3.8 collective-permute-done.20
  463.3 6.3 collective-permute-done.17
  472.3 3.7 fusion
  476.5 32.9 %attend_back.1 = (f32[1024,384]{1,0:T(8,128)}, bf16[4,2,1024,128]{3,2,1,0:T(8,128)(2,1)}, f32[2,1024,128]{2,1,0:T(8,128)}) custom-call(s32[9]{0:T(128)} %copy-done.5, bf16[6,1024,128]{2,1,0:T(8,128)(2,1)} %get-tuple-element.68.query_ref.wide_ref, bf16[6,1024,128]{2,1,0:T(8,128)(2,1)} %get-tuple-element.75.query_ref, ...), custom_call_target="tpu_custom_call" | custom-call | flops 120000004096 | bytes 40000000 | tf_op jit(solution)/shard_map/attend_back/pallas_call | solution.py:443
  512.9 55.8 %collective-permute-start.13 = (bf16[4,128,1280]{2,1,0:T(8,128)(2,1)S(1)}, bf16[4,128,1280]{2,1,0:T(8,128)(2,1)S(1)}, u32[]{:S(2)}, u32[]{:S(2)}) collective-permute-start(bf16[4,128,1280]{2,1,0:T(8,128)(2,1)S(1)} %fusion.6), channel_id=1, source_target_pairs={{0,2},{1,3},{2,4},{3,5},{4,6},{5,7},{6,0},{7,1},{8,10},{9,11},{10,... | collective-permute-start | bytes 3932168 | tf_op jit(solution)/shard_map/ppermute | solution.py:49
  569.1 4.0 fusion.18
  573.1 4.6 fusion.2
  577.7 31.9 %collective-permute-done.12 = bf16[160,2048]{1,0:T(8,128)(2,1)S(1)} collective-permute-done((bf16[160,2048]{1,0:T(8,128)(2,1)S(1)}, bf16[160,2048]{1,0:T(8,128)(2,1)S(1)}, u32[]{:S(2)}, u32[]{:S(2)}) %collective-permute-start.12) | collective-permute-done | bytes 655392 | tf_op jit(solution)/shard_map/ppermute | solution.py:49
  610.6 27.4 %collective-permute-start.25 = (bf16[2,1024,128]{2,1,0:T(8,128)(2,1)}, bf16[2,1024,128]{2,1,0:T(8,128)(2,1)}, u32[]{:S(2)}, u32[]{:S(2)}) collective-permute-start(bf16[2,1024,128]{2,1,0:T(8,128)(2,1)} %get-tuple-element.151), channel_id=1, source_target_pairs={{0,1},{1,0},{2,3},{3,2},{4,5},{5,4},{6,7},{7,6},{8,9},{9,8},{10,11... | collective-permute-start | bytes 1572872 | tf_op jit(solution)/shard_map/ppermute | solution.py:44
  652.4 13.2 %collective-permute-done.49 = bf16[48,2048]{1,0:T(8,128)(2,1)S(1)} collective-permute-done((bf16[48,2048]{1,0:T(8,128)(2,1)S(1)}, bf16[48,2048]{1,0:T(8,128)(2,1)S(1)}, u32[]{:S(2)}, u32[]{:S(2)}) %collective-permute-start.49) | collective-permute-done | bytes 196640 | tf_op jit(solution)/shard_map/ppermute | solution.py:44
  671.5 5.0 collective-permute-done.50
  681.3 31.0 %collective-permute-done.27 = bf16[2,1024,128]{2,1,0:T(8,128)(2,1)S(1)} collective-permute-done((bf16[2,1024,128]{2,1,0:T(8,128)(2,1)S(1)}, bf16[2,1024,128]{2,1,0:T(8,128)(2,1)S(1)}, u32[]{:S(2)}, u32[]{:S(2)}) %collective-permute-start.27) | collective-permute-done | bytes 524320 | tf_op jit(solution)/shard_map/ppermute | solution.py:49
  721.2 3.9 collective-permute-done.28
  734.0 5.6 convolution_convert_fusion.1
  741.3 4.9 convolution_convert_fusion.2
  758.7 8.2 collective-permute-done.43
  774.1 4.5 all-to-all-start.1
  793.9 19.8 %collective-permute-done.37 = bf16[4,64,768]{2,1,0:T(8,128)(2,1)S(1)} collective-permute-done((bf16[4,64,768]{2,1,0:T(8,128)(2,1)S(1)}, bf16[4,64,768]{2,1,0:T(8,128)(2,1)S(1)}, u32[]{:S(2)}, u32[]{:S(2)}) %collective-permute-start.37) | collective-permute-done | bytes 393248 | tf_op jit(solution)/shard_map/ppermute | solution.py:44
  821.2 5.0 collective-permute-done.36
  829.3 15.2 %collective-permute-start.39 = (bf16[4,64,768]{2,1,0:T(8,128)(2,1)}, bf16[4,64,768]{2,1,0:T(8,128)(2,1)}, u32[]{:S(2)}, u32[]{:S(2)}) collective-permute-start(bf16[4,64,768]{2,1,0:T(8,128)(2,1)} %fusion.35), channel_id=1, source_target_pairs={{0,2},{1,3},{2,4},{3,5},{4,6},{5,7},{6,0},{7,1},{8,10},{9,11},{10,... | collective-permute-start | bytes 1179656 | tf_op jit(solution)/shard_map/ppermute | solution.py:49
  847.6 4.3 reshape.435
  856.9 6.1 fusion.57
  881.6 5.2 fusion.7
  (341 shorter events, 200.4 us)
Async XLA Ops:
  144.3 109.6 %collective-permute-start = (bf16[4,128,1280]{2,1,0:T(8,128)(2,1)}, bf16[4,128,1280]{2,1,0:T(8,128)(2,1)}, u32[]{:S(2)}, u32[]{:S(2)}) collective-permute-start(bf16[4,128,1280]{2,1,0:T(8,128)(2,1)} %get-tuple-element.95.refs_1_), channel_id=1, source_target_pairs={{0,2},{1,3},{2,4},{3,5},{4,6},{5,7},{6,0},{7,1},{8,10},{9,11},{10,... | collective-permute-start | bytes 3932168 | tf_op jit(solution)/shard_map/ppermute | solution.py:49
  144.5 109.4 %collective-permute-start.1 = (bf16[160,2048]{1,0:T(8,128)(2,1)S(1)}, bf16[160,2048]{1,0:T(8,128)(2,1)}, u32[]{:S(2)}, u32[]{:S(2)}) collective-permute-start(bf16[160,2048]{1,0:T(8,128)(2,1)S(1)} %get-tuple-element.91), channel_id=1, source_target_pairs={{0,2},{1,3},{2,4},{3,5},{4,6},{5,7},{6,0},{7,1},{8,10},{9,11},{10,... | collective-permute-start | bytes 1966088 | tf_op jit(solution)/shard_map/ppermute | solution.py:49
  152.4 43.2 %collective-permute-start.4 = (bf16[48,2048]{1,0:T(8,128)(2,1)S(1)}, bf16[48,2048]{1,0:T(8,128)(2,1)S(1)}, u32[]{:S(2)}, u32[]{:S(2)}) collective-permute-start(bf16[48,2048]{1,0:T(8,128)(2,1)S(1)} %collective-permute-done.3), channel_id=1, source_target_pairs={{0,1},{1,0},{2,3},{3,2},{4,5},{5,4},{6,7},{7,6},{8,9},{9,8},{10,11... | collective-permute-start | bytes 589832 | tf_op jit(solution)/shard_map/ppermute | solution.py:44
  154.0 39.9 %collective-permute-start.5 = (bf16[48,2048]{1,0:T(8,128)(2,1)S(1)}, bf16[48,2048]{1,0:T(8,128)(2,1)S(1)}, u32[]{:S(2)}, u32[]{:S(2)}) collective-permute-start(bf16[48,2048]{1,0:T(8,128)(2,1)S(1)} %collective-permute-done.3), channel_id=1, source_target_pairs={{0,2},{1,3},{2,4},{3,5},{4,6},{5,7},{6,0},{7,1},{8,10},{9,11},{10,... | collective-permute-start | bytes 589832 | tf_op jit(solution)/shard_map/ppermute | solution.py:49
  209.5 40.9 %collective-permute-start.9 = (bf16[384,2048]{1,0:T(8,128)(2,1)}, bf16[384,2048]{1,0:T(8,128)(2,1)}, u32[]{:S(2)}, u32[]{:S(2)}) collective-permute-start(bf16[384,2048]{1,0:T(8,128)(2,1)} %bitcast.20), channel_id=1, source_target_pairs={{0,8},{8,0},{16,24},{24,16},{1,9},{9,1},{17,25},{25,17},{2,10},{10... | collective-permute-start | bytes 4718600 | tf_op jit(solution)/shard_map/ppermute | solution.py:44
  209.5 37.1 %collective-permute-start.10 = (bf16[384,2048]{1,0:T(8,128)(2,1)}, bf16[384,2048]{1,0:T(8,128)(2,1)}, u32[]{:S(2)}, u32[]{:S(2)}) collective-permute-start(bf16[384,2048]{1,0:T(8,128)(2,1)} %bitcast.20), channel_id=1, source_target_pairs={{0,16},{8,24},{16,0},{24,8},{1,17},{9,25},{17,1},{25,9},{2,18},{10... | collective-permute-start | bytes 4718600 | tf_op jit(solution)/shard_map/ppermute | solution.py:44
  448.3 24.0 %collective-permute-start.23 = (bf16[384,2048]{1,0:T(8,128)(2,1)}, bf16[384,2048]{1,0:T(8,128)(2,1)}, u32[]{:S(2)}, u32[]{:S(2)}) collective-permute-start(bf16[384,2048]{1,0:T(8,128)(2,1)} %get-tuple-element.139), channel_id=1, source_target_pairs={{0,8},{8,0},{16,24},{24,16},{1,9},{9,1},{17,25},{25,17},{2,10},{10... | collective-permute-start | bytes 4718600 | tf_op jit(solution)/shard_map/ppermute | solution.py:44
  451.3 61.6 %collective-permute-start.14 = (bf16[256,2048]{1,0:T(8,128)(2,1)}, bf16[256,2048]{1,0:T(8,128)(2,1)}, u32[]{:S(2)}, u32[]{:S(2)}) collective-permute-start(bf16[256,2048]{1,0:T(8,128)(2,1)} %get-tuple-element.131), channel_id=1, source_target_pairs={{0,8},{8,0},{16,24},{24,16},{1,9},{9,1},{17,25},{25,17},{2,10},{10... | collective-permute-start | bytes 3145736 | tf_op jit(solution)/shard_map/ppermute | solution.py:44
  451.8 121.3 %collective-permute-start.22 = (bf16[384,2048]{1,0:T(8,128)(2,1)}, bf16[384,2048]{1,0:T(8,128)(2,1)}, u32[]{:S(2)}, u32[]{:S(2)}) collective-permute-start(bf16[384,2048]{1,0:T(8,128)(2,1)} %get-tuple-element.138), channel_id=1, source_target_pairs={{0,8},{8,0},{16,24},{24,16},{1,9},{9,1},{17,25},{25,17},{2,10},{10... | collective-permute-start | bytes 4718600 | tf_op jit(solution)/shard_map/ppermute | solution.py:44
  462.5 106.3 %collective-permute-start.21 = (bf16[256,2048]{1,0:T(8,128)(2,1)}, bf16[256,2048]{1,0:T(8,128)(2,1)}, u32[]{:S(2)}, u32[]{:S(2)}) collective-permute-start(bf16[256,2048]{1,0:T(8,128)(2,1)} %pad_maximum_fusion.2), channel_id=1, source_target_pairs={{0,1},{1,0},{2,3},{3,2},{4,5},{5,4},{6,7},{7,6},{8,9},{9,8},{10,11... | collective-permute-start | bytes 3145736 | tf_op jit(solution)/shard_map/ppermute | solution.py:44
  470.8 98.4 %collective-permute-start.18 = (bf16[256,2048]{1,0:T(8,128)(2,1)}, bf16[256,2048]{1,0:T(8,128)(2,1)}, u32[]{:S(2)}, u32[]{:S(2)}) collective-permute-start(bf16[256,2048]{1,0:T(8,128)(2,1)} %pad_maximum_fusion.1), channel_id=1, source_target_pairs={{0,16},{8,24},{16,0},{24,8},{1,17},{9,25},{17,1},{25,9},{2,18},{10... | collective-permute-start | bytes 3145736 | tf_op jit(solution)/shard_map/ppermute | solution.py:44
  476.0 97.1 %collective-permute-start.24 = (bf16[384,2048]{1,0:T(8,128)(2,1)}, bf16[384,2048]{1,0:T(8,128)(2,1)}, u32[]{:S(2)}, u32[]{:S(2)}) collective-permute-start(bf16[384,2048]{1,0:T(8,128)(2,1)} %fusion), channel_id=1, source_target_pairs={{0,16},{8,24},{16,0},{24,8},{1,17},{9,25},{17,1},{25,9},{2,18},{10... | collective-permute-start | bytes 4718600 | tf_op jit(solution)/shard_map/ppermute | solution.py:44
  512.9 96.7 %collective-permute-start.13 = (bf16[4,128,1280]{2,1,0:T(8,128)(2,1)S(1)}, bf16[4,128,1280]{2,1,0:T(8,128)(2,1)S(1)}, u32[]{:S(2)}, u32[]{:S(2)}) collective-permute-start(bf16[4,128,1280]{2,1,0:T(8,128)(2,1)S(1)} %fusion.6), channel_id=1, source_target_pairs={{0,2},{1,3},{2,4},{3,5},{4,6},{5,7},{6,0},{7,1},{8,10},{9,11},{10,... | collective-permute-start | bytes 3932168 | tf_op jit(solution)/shard_map/ppermute | solution.py:49
  568.8 40.8 %collective-permute-start.12 = (bf16[160,2048]{1,0:T(8,128)(2,1)S(1)}, bf16[160,2048]{1,0:T(8,128)(2,1)S(1)}, u32[]{:S(2)}, u32[]{:S(2)}) collective-permute-start(bf16[160,2048]{1,0:T(8,128)(2,1)S(1)} %dynamic-slice_bitcast_fusion.9), channel_id=1, source_target_pairs={{0,2},{1,3},{2,4},{3,5},{4,6},{5,7},{6,0},{7,1},{8,10},{9,11},{10,... | collective-permute-start | bytes 1966088 | tf_op jit(solution)/shard_map/ppermute | solution.py:49
  610.6 68.6 %collective-permute-start.25 = (bf16[2,1024,128]{2,1,0:T(8,128)(2,1)}, bf16[2,1024,128]{2,1,0:T(8,128)(2,1)}, u32[]{:S(2)}, u32[]{:S(2)}) collective-permute-start(bf16[2,1024,128]{2,1,0:T(8,128)(2,1)} %get-tuple-element.151), channel_id=1, source_target_pairs={{0,1},{1,0},{2,3},{3,2},{4,5},{5,4},{6,7},{7,6},{8,9},{9,8},{10,11... | collective-permute-start | bytes 1572872 | tf_op jit(solution)/shard_map/ppermute | solution.py:44
  638.1 31.1 %collective-permute-start.26 = (bf16[2,1024,128]{2,1,0:T(8,128)(2,1)}, bf16[2,1024,128]{2,1,0:T(8,128)(2,1)S(1)}, u32[]{:S(2)}, u32[]{:S(2)}) collective-permute-start(bf16[2,1024,128]{2,1,0:T(8,128)(2,1)} %get-tuple-element.150), channel_id=1, source_target_pairs={{0,1},{1,0},{2,3},{3,2},{4,5},{5,4},{6,7},{7,6},{8,9},{9,8},{10,11... | collective-permute-start | bytes 1572872 | tf_op jit(solution)/shard_map/ppermute | solution.py:44
  639.2 87.1 %collective-permute-start.29 = (bf16[160,2048]{1,0:T(8,128)(2,1)}, bf16[160,2048]{1,0:T(8,128)(2,1)}, u32[]{:S(2)}, u32[]{:S(2)}) collective-permute-start(bf16[160,2048]{1,0:T(8,128)(2,1)} %fusion.22), channel_id=1, source_target_pairs={{0,2},{1,3},{2,4},{3,5},{4,6},{5,7},{6,0},{7,1},{8,10},{9,11},{10,... | collective-permute-start | bytes 1966088 | tf_op jit(solution)/shard_map/ppermute | solution.py:49
  669.4 42.9 %collective-permute-start.27 = (bf16[2,1024,128]{2,1,0:T(8,128)(2,1)S(1)}, bf16[2,1024,128]{2,1,0:T(8,128)(2,1)S(1)}, u32[]{:S(2)}, u32[]{:S(2)}) collective-permute-start(bf16[2,1024,128]{2,1,0:T(8,128)(2,1)S(1)} %fusion.29), channel_id=1, source_target_pairs={{0,6},{1,7},{2,0},{3,1},{4,2},{5,3},{6,4},{7,5},{8,14},{9,15},{10,... | collective-permute-start | bytes 1572872 | tf_op jit(solution)/shard_map/ppermute | solution.py:49
  670.8 55.5 %collective-permute-start.30 = (bf16[4,128,1280]{2,1,0:T(8,128)(2,1)S(1)}, bf16[4,128,1280]{2,1,0:T(8,128)(2,1)S(1)}, u32[]{:S(2)}, u32[]{:S(2)}) collective-permute-start(bf16[4,128,1280]{2,1,0:T(8,128)(2,1)S(1)} %copy-done.33), channel_id=1, source_target_pairs={{0,2},{1,3},{2,4},{3,5},{4,6},{5,7},{6,0},{7,1},{8,10},{9,11},{10,... | collective-permute-start | bytes 3932168 | tf_op jit(solution)/shard_map/ppermute | solution.py:49
  676.5 38.7 %collective-permute-start.47 = (bf16[48,2048]{1,0:T(8,128)(2,1)S(1)}, bf16[48,2048]{1,0:T(8,128)(2,1)S(1)}, u32[]{:S(2)}, u32[]{:S(2)}) collective-permute-start(bf16[48,2048]{1,0:T(8,128)(2,1)S(1)} %get-tuple-element.157), channel_id=1, source_target_pairs={{0,1},{1,0},{2,3},{3,2},{4,5},{5,4},{6,7},{7,6},{8,9},{9,8},{10,11... | collective-permute-start | bytes 589832 | tf_op jit(solution)/shard_map/ppermute | solution.py:44
  679.2 40.2 %collective-permute-start.51 = (bf16[48,2048]{1,0:T(8,128)(2,1)S(1)}, bf16[48,2048]{1,0:T(8,128)(2,1)S(1)}, u32[]{:S(2)}, u32[]{:S(2)}) collective-permute-start(bf16[48,2048]{1,0:T(8,128)(2,1)S(1)} %fusion.42), channel_id=1, source_target_pairs={{0,2},{1,3},{2,4},{3,5},{4,6},{5,7},{6,0},{7,1},{8,10},{9,11},{10,... | collective-permute-start | bytes 589832 | tf_op jit(solution)/shard_map/ppermute | solution.py:49
  715.1 101.2 %collective-permute-start.46 = (bf16[48,2048]{1,0:T(8,128)(2,1)}, bf16[48,2048]{1,0:T(8,128)(2,1)}, u32[]{:S(2)}, u32[]{:S(2)}) collective-permute-start(bf16[48,2048]{1,0:T(8,128)(2,1)} %get-tuple-element.154), channel_id=1, source_target_pairs={{0,1},{1,0},{2,3},{3,2},{4,5},{5,4},{6,7},{7,6},{8,9},{9,8},{10,11... | collective-permute-start | bytes 589832 | tf_op jit(solution)/shard_map/ppermute | solution.py:44
  740.8 37.9 %collective-permute-start.31 = (bf16[256,2048]{1,0:T(8,128)(2,1)}, bf16[256,2048]{1,0:T(8,128)(2,1)S(1)}, u32[]{:S(2)}, u32[]{:S(2)}) collective-permute-start(bf16[256,2048]{1,0:T(8,128)(2,1)} %get-tuple-element.140), channel_id=1, source_target_pairs={{0,8},{8,0},{16,24},{24,16},{1,9},{9,1},{17,25},{25,17},{2,10},{10... | collective-permute-start | bytes 3145736 | tf_op jit(solution)/shard_map/ppermute | solution.py:44
  754.4 26.5 %collective-permute-start.33 = (bf16[256,2048]{1,0:T(8,128)(2,1)}, bf16[256,2048]{1,0:T(8,128)(2,1)S(1)}, u32[]{:S(2)}, u32[]{:S(2)}) collective-permute-start(bf16[256,2048]{1,0:T(8,128)(2,1)} %fusion.12), channel_id=1, source_target_pairs={{0,16},{8,24},{16,0},{24,8},{1,17},{9,25},{17,1},{25,9},{2,18},{10... | collective-permute-start | bytes 3145736 | tf_op jit(solution)/shard_map/ppermute | solution.py:44
  770.5 46.5 %collective-permute-start.52 = (bf16[48,2048]{1,0:T(8,128)(2,1)S(1)}, bf16[48,2048]{1,0:T(8,128)(2,1)S(1)}, u32[]{:S(2)}, u32[]{:S(2)}) collective-permute-start(bf16[48,2048]{1,0:T(8,128)(2,1)S(1)} %copy-done.38), channel_id=1, source_target_pairs={{0,2},{1,3},{2,4},{3,5},{4,6},{5,7},{6,0},{7,1},{8,10},{9,11},{10,... | collective-permute-start | bytes 589832 | tf_op jit(solution)/shard_map/ppermute | solution.py:49
  774.1 70.4 %all-to-all-start.1 = ((bf16[4,64,2,1280]{3,1,2,0:T(8,128)(2,1)}), bf16[4,64,2,1280]{3,1,2,0:T(8,128)(2,1)}, u32[]{:S(2)}, u32[]{:S(2)}) async-start(bf16[4,64,2,1280]{3,1,2,0:T(8,128)(2,1)} %bitcast_dynamic-update-slice_fusion.3), calls=%async_computation.1 | async-start | bytes 2621440 | tf_op jit(solution)/shard_map/all_to_all | solution.py:1602
  778.7 40.2 %collective-permute-start.45 = (f32[2,64]{1,0:T(2,128)}, f32[2,64]{1,0:T(2,128)}, u32[]{:S(2)}, u32[]{:S(2)}) collective-permute-start(f32[2,64]{1,0:T(2,128)} %add.514), channel_id=1, source_target_pairs={{0,4},{1,5},{2,6},{3,7},{4,0},{5,1},{6,2},{7,3},{8,12},{9,13},{10,... | collective-permute-start | bytes 1544 | tf_op jit(solution)/shard_map/ppermute | solution.py:44
  789.5 24.2 %collective-permute-start.37 = (bf16[4,64,768]{2,1,0:T(8,128)(2,1)S(1)}, bf16[4,64,768]{2,1,0:T(8,128)(2,1)S(1)}, u32[]{:S(2)}, u32[]{:S(2)}) collective-permute-start(bf16[4,64,768]{2,1,0:T(8,128)(2,1)S(1)} %get-tuple-element.143), channel_id=1, source_target_pairs={{0,1},{1,0},{2,3},{3,2},{4,5},{5,4},{6,7},{7,6},{8,9},{9,8},{10,11... | collective-permute-start | bytes 1179656 | tf_op jit(solution)/shard_map/ppermute | solution.py:44
  793.2 26.8 %collective-permute-start.55 = (bf16[160,2048]{1,0:T(8,128)(2,1)S(1)}, bf16[160,2048]{1,0:T(8,128)(2,1)S(1)}, u32[]{:S(2)}, u32[]{:S(2)}) collective-permute-start(bf16[160,2048]{1,0:T(8,128)(2,1)S(1)} %fusion.20), channel_id=1, source_target_pairs={{0,0},{1,4},{2,1},{3,5},{4,2},{5,6},{6,3},{7,7},{8,8},{9,12},{10,9... | collective-permute-start | bytes 1966088 | tf_op jit(solution)/shard_map/ppermute | solution.py:1592
  821.2 32.7 %collective-permute-start.35 = (bf16[4,64,768]{2,1,0:T(8,128)(2,1)}, bf16[4,64,768]{2,1,0:T(8,128)(2,1)}, u32[]{:S(2)}, u32[]{:S(2)}) collective-permute-start(bf16[4,64,768]{2,1,0:T(8,128)(2,1)} %get-tuple-element.145), channel_id=1, source_target_pairs={{0,1},{1,0},{2,3},{3,2},{4,5},{5,4},{6,7},{7,6},{8,9},{9,8},{10,11... | collective-permute-start | bytes 1179656 | tf_op jit(solution)/shard_map/ppermute | solution.py:44
  829.3 24.6 %collective-permute-start.39 = (bf16[4,64,768]{2,1,0:T(8,128)(2,1)}, bf16[4,64,768]{2,1,0:T(8,128)(2,1)}, u32[]{:S(2)}, u32[]{:S(2)}) collective-permute-start(bf16[4,64,768]{2,1,0:T(8,128)(2,1)} %fusion.35), channel_id=1, source_target_pairs={{0,2},{1,3},{2,4},{3,5},{4,6},{5,7},{6,0},{7,1},{8,10},{9,11},{10,... | collective-permute-start | bytes 1179656 | tf_op jit(solution)/shard_map/ppermute | solution.py:49
  851.9 24.3 %collective-permute-start.34 = (bf16[4,64,768]{2,1,0:T(8,128)(2,1)}, bf16[4,64,768]{2,1,0:T(8,128)(2,1)S(1)}, u32[]{:S(2)}, u32[]{:S(2)}) collective-permute-start(bf16[4,64,768]{2,1,0:T(8,128)(2,1)} %get-tuple-element.142), channel_id=1, source_target_pairs={{0,1},{1,0},{2,3},{3,2},{4,5},{5,4},{6,7},{7,6},{8,9},{9,8},{10,11... | collective-permute-start | bytes 1179656 | tf_op jit(solution)/shard_map/ppermute | solution.py:44
  (80 other events, 1539.7 us)

commit v5 on v4

--- a/solution.py
+++ b/solution.py
@@ -127,23 +127,6 @@
     return full
 
 
-def scatter_blk(chunk):
-    place, side, line = place_of()
-    total = None
-    for step in range(1, line + 1):
-        target = (place - step) % line
-        mine = chunk(2 * target + side)
-        got = swap(chunk(2 * target + 1 - side), "blk", 1)
-        term = mine.astype(F32) + got.astype(F32)
-        if total is not None:
-            term = term + total.astype(F32)
-        if step < line:
-            total = ring(term.astype(BF), 2)
-        else:
-            total = term
-    return total
-
-
 def scatter_pair(terms):
     me = lax.axis_index("head")
     side = lax.axis_index("blk") % 2
@@ -171,16 +154,6 @@
     return both(side, me) + got_far.astype(F32) + got_across.astype(F32)
 
 
-def sum_all(values):
-    for bit in (1, 2):
-        values = values + swap(values, "head", bit)
-    bit = 1
-    while bit < lax.axis_size("blk"):
-        values = values + swap(values, "blk", bit)
-        bit *= 2
-    return values
-
-
 def sync(*trees):
     return lax.optimization_barrier(trees)
 
@@ -210,17 +183,16 @@
     return ((4, 2 * odd, odd), (2, 4 * (1 - odd), 1 - odd))
 
 
-def split_window(kv_ref, keys, values, step):
+def split_window(kv_ref, keys, values, step, slot):
     per_block = kv_ref.shape[2] // TILE
     block, part = step // per_block, step % per_block
     source = pl.ds(pl.multiple_of(part * TILE, TILE), TILE)
     target = pl.ds(pl.multiple_of(step * TILE, TILE), TILE)
     low = lanes((TILE, 128)) < HEAD
-    for slot in range(2):
-        both = kv_ref[block, slot, source, :].astype(F32)
-        moved = pltpu.roll(both, HEAD, 1)
-        keys[slot, target, 0:128] = jnp.where(low, both, moved).astype(BF)
-        values[slot, target, :] = jnp.where(low, moved, 1.0).astype(BF)
+    both = kv_ref[block, slot, source, :].astype(F32)
+    moved = pltpu.roll(both, HEAD, 1)
+    keys[target, 0:128] = jnp.where(low, both, moved).astype(BF)
+    values[target, :] = jnp.where(low, moved, 1.0).astype(BF)
     return target
 
 
@@ -232,7 +204,8 @@
     lane = lanes((TILE, 128))
 
     def fill(step, carry):
-        split_window(kv_ref, keys, values, step)
+        for slot in range(2):
+            split_window(kv_ref, keys.at[slot], values.at[slot], step, slot)
         return carry
 
     lax.fori_loop(0, keys.shape[1] // TILE, fill, 0)
@@ -312,6 +285,7 @@
 
 
 def attend_back_kernel(
+    which,
     meta_ref,
     wide_ref,
     query_ref,
@@ -320,8 +294,8 @@
     grad_ref,
     start_ref,
     dq_ref,
-    dkv_low_ref,
-    dkv_own_ref,
+    low_ref,
+    own_ref,
     keys,
     values,
     keys_t,
@@ -331,18 +305,18 @@
     dq,
     dkv,
 ):
-    heads, rows, _ = query_ref.shape
-    window = keys.shape[1]
+    rows = query_ref.shape[1]
+    window = keys.shape[0]
     base = window - rows
     lane = lanes((TILE, 128))
     low_lane = lane < HEAD
+    count, first, slot = head_groups(meta_ref)[which]
 
     def fill(step, carry):
-        target = split_window(kv_ref, keys, values, step)
-        for slot in range(2):
-            keys[slot, target, 128:256] = jnp.ones((TILE, 128), BF)
-            keys_t[slot, :, target] = transposed(keys[slot, target, 0:128])[0:HEAD, :]
-            dkv[slot, target, :] = jnp.zeros((TILE, 128), F32)
+        target = split_window(kv_ref, keys, values, step, slot)
+        keys[target, 128:256] = jnp.ones((TILE, 128), BF)
+        keys_t[:, target] = transposed(keys[target, 0:128])[0:HEAD, :]
+        dkv[target, :] = jnp.zeros((TILE, 128), F32)
         return carry
 
     lax.fori_loop(0, window // TILE, fill, 0)
@@ -357,11 +331,12 @@
 
     def turn(step, carry):
         tile = pl.ds(pl.multiple_of(step * TILE, TILE), TILE)
-        for j in range(heads):
-            query_t[j, 0:128, tile] = transposed(wide_ref[j, tile, :])
-            kept = out_ref[j, tile, :]
+        for j in range(count):
+            query_t[j, 0:128, tile] = transposed(wide_ref[first + j, tile, :])
+            kept = out_ref[first + j, tile, :]
             query_t[j, 128:256, tile] = transposed(low_terms(-kept, HEAD).astype(BF))
-            grad = grad_ref[tile, (j // 2) * 128 : (j // 2) * 128 + 128].astype(F32)
+            pair = pl.ds(pl.multiple_of((first // 2 + j // 2) * 128, 128), 128)
+            grad = grad_ref[tile, pair].astype(F32)
             moved = pltpu.roll(grad, HEAD, 1)
             if j % 2:
                 grad, moved = moved, grad
@@ -374,96 +349,94 @@
         return carry
 
     lax.fori_loop(0, rows // TILE, turn, 0)
-    for count, first, slot in head_groups(meta_ref):
-        for tile in range(rows // TILE):
-            q_at = tile * TILE
-            q_cols = slice(q_at, q_at + TILE)
-            low, high = meta_ref[1 + 2 * tile], meta_ref[2 + 2 * tile]
-            start_row = start_ref[:, q_cols]
-            q_pos = base + q_at + lax.broadcasted_iota(jnp.int32, (1, TILE), 1)
-
-            def step(at, carry, masked):
-                k_at = pl.multiple_of(at * TILE, TILE)
-                k_rows = pl.ds(k_at, TILE)
-                key_block = keys[slot, k_rows, :]
-                value_block = values[slot, k_rows, :]
-                key_t = keys_t[slot, :, k_rows]
+    for tile in range(rows // TILE):
+        q_at = tile * TILE
+        q_cols = slice(q_at, q_at + TILE)
+        low, high = meta_ref[1 + 2 * tile], meta_ref[2 + 2 * tile]
+        start_row = start_ref[:, q_cols]
+        q_pos = base + q_at + lax.broadcasted_iota(jnp.int32, (1, TILE), 1)
+
+        def step(at, carry, masked):
+            k_at = pl.multiple_of(at * TILE, TILE)
+            k_rows = pl.ds(k_at, TILE)
+            key_block = keys[k_rows, :]
+            value_block = values[k_rows, :]
+            key_t = keys_t[:, k_rows]
+            if masked:
+                k_pos = k_at + lax.broadcasted_iota(jnp.int32, (TILE, 1), 0)
+                allowed = (start_row <= k_pos) & (k_pos <= q_pos)
+            total = dkv[k_rows, :]
+            for j in range(count):
+                scores = nn(key_block, query_t[j, :, q_cols])
                 if masked:
-                    k_pos = k_at + lax.broadcasted_iota(jnp.int32, (TILE, 1), 0)
-                    allowed = (start_row <= k_pos) & (k_pos <= q_pos)
-                total = dkv[slot, k_rows, :]
-                for j in range(count):
-                    scores = nn(key_block, query_t[first + j, :, q_cols])
-                    if masked:
-                        scores = jnp.where(allowed, scores, NEG)
-                    probs = jnp.exp2(scores)
-                    diff = nn(value_block, grad_t[first + j, :, q_cols])
-                    grad_score = (probs * diff).astype(BF)
-                    total = (
-                        total
-                        + nn(probs.astype(BF), grads[first + j, q_cols, :])
-                        + nn(grad_score, query_ref[first + j, q_cols, :])
-                    )
-                    dq[first + j, :, q_cols] += nn(key_t, grad_score)
-                dkv[slot, k_rows, :] = total
-                return carry
-
-            begin = low // TILE
-            last = (base + q_at) // TILE
-            clear = jnp.minimum((high + TILE - 1) // TILE, last)
-            lax.fori_loop(begin, clear, functools.partial(step, masked=True), 0)
-            lax.fori_loop(clear, last, functools.partial(step, masked=False), 0)
-            step(last, 0, True)
+                    scores = jnp.where(allowed, scores, NEG)
+                probs = jnp.exp2(scores)
+                diff = nn(value_block, grad_t[j, :, q_cols])
+                grad_score = (probs * diff).astype(BF)
+                total = (
+                    total
+                    + nn(probs.astype(BF), grads[j, q_cols, :])
+                    + nn(grad_score, query_ref[first + j, q_cols, :])
+                )
+                dq[j, :, q_cols] += nn(key_t, grad_score)
+            dkv[k_rows, :] = total
+            return carry
+
+        begin = low // TILE
+        last = (base + q_at) // TILE
+        clear = jnp.minimum((high + TILE - 1) // TILE, last)
+        lax.fori_loop(begin, clear, functools.partial(step, masked=True), 0)
+        lax.fori_loop(clear, last, functools.partial(step, masked=False), 0)
+        step(last, 0, True)
 
     def finish(step, carry):
         tile = pl.ds(pl.multiple_of(step * TILE, TILE), TILE)
-        for t in range(heads // 2):
+        for t in range(count // 2):
             pair = jnp.concatenate([dq[2 * t, :, tile], dq[2 * t + 1, :, tile]], axis=0)
             dq_ref[tile, t * 128 : (t + 1) * 128] = transposed(pair) * SCALE
-        per_block = rows // TILE
-        for slot in range(2):
-            for block in range(BACK + 1):
-                source = pl.ds(pl.multiple_of(block * rows + step * TILE, TILE), TILE)
-                part = dkv[slot, source, :]
-                part = jnp.where(low_lane, part * SCALE, part)
-                if block < BACK:
-                    dkv_low_ref[block, slot, tile, :] = part.astype(BF)
-                else:
-                    dkv_own_ref[slot, tile, :] = part
+        for block in range(BACK + 1):
+            source = pl.ds(pl.multiple_of(block * rows + step * TILE, TILE), TILE)
+            part = dkv[source, :]
+            part = jnp.where(low_lane, part * SCALE, part)
+            if block < BACK:
+                low_ref[block, tile, :] = part.astype(BF)
+            else:
+                own_ref[tile, :] = part
         return carry
 
     lax.fori_loop(0, rows // TILE, finish, 0)
 
 
-def attend_back(meta, wide, queries, kv, kept, grads, starts):
-    heads, rows, _ = queries.shape
+def attend_back(which, meta, wide, queries, kv, kept, grads, starts):
+    _, rows, _ = queries.shape
     window = kv.shape[0] * rows
+    count = (4, 2)[which]
     vmem = pl.BlockSpec(memory_space=pltpu.VMEM)
     shape = jax.ShapeDtypeStruct
     return pl.pallas_call(
-        attend_back_kernel,
+        functools.partial(attend_back_kernel, which),
         out_shape=(
-            shape((rows, heads * HEAD), F32),
-            shape((BACK, 2, rows, 128), BF),
-            shape((2, rows, 128), F32),
+            shape((rows, count * HEAD), F32),
+            shape((BACK, rows, 128), BF),
+            shape((rows, 128), F32),
         ),
         in_specs=[pl.BlockSpec(memory_space=pltpu.SMEM)] + [vmem] * 6,
         out_specs=(vmem,) * 3,
         scratch_shapes=[
-            pltpu.VMEM((2, window, 256), BF),
-            pltpu.VMEM((2, window, 128), BF),
-            pltpu.VMEM((2, HEAD, window), BF),
-            pltpu.VMEM((heads, 256, rows), BF),
-            pltpu.VMEM((heads, 128, rows), BF),
-            pltpu.VMEM((heads, rows, 128), BF),
-            pltpu.VMEM((heads, HEAD, rows), F32),
-            pltpu.VMEM((2, window, 128), F32),
+            pltpu.VMEM((window, 256), BF),
+            pltpu.VMEM((window, 128), BF),
+            pltpu.VMEM((HEAD, window), BF),
+            pltpu.VMEM((count, 256, rows), BF),
+            pltpu.VMEM((count, 128, rows), BF),
+            pltpu.VMEM((count, rows, 128), BF),
+            pltpu.VMEM((count, HEAD, rows), F32),
+            pltpu.VMEM((window, 128), F32),
         ],
-        compiler_params=pltpu.CompilerParams(vmem_limit_bytes=56 << 20),
+        compiler_params=pltpu.CompilerParams(vmem_limit_bytes=48 << 20),
         cost_estimate=pl.CostEstimate(
-            flops=120_000_000_000, bytes_accessed=40_000_000, transcendentals=20_000_000
+            flops=count * 20_000_000_000, bytes_accessed=40_000_000, transcendentals=20_000_000
         ),
-        name="attend_back",
+        name=("attend_back_four", "attend_back_two")[which],
     )(meta, wide, queries, kv, kept, grads, starts)
 
 
@@ -999,6 +972,7 @@
     down_out,
     down_one,
     down_two,
+    toks_out,
     gain_out,
     toks,
     normed,
@@ -1211,6 +1185,8 @@
     lax.fori_loop(0, 4 * rows // 32, norm_tile, 0)
     keep_normed = local(11, normed, normed_out)
     keep_normed.start()
+    keep_toks = local(16, toks, toks_out)
+    keep_toks.start()
 
     def project(step, carry):
         tile = pl.ds(pl.multiple_of(step * 256, 256), 256)
@@ -1312,7 +1288,7 @@
     slab_on.wait_recv()
     for copy in (top_near, top_far_on, top_across_on, top_corner_on):
         copy.wait_recv()
-    for copy in keep + keep_in + [keep_normed, keep_raw]:
+    for copy in keep + keep_in + [keep_normed, keep_raw, keep_toks]:
         copy.wait()
     for copy in split + spread:
         copy.wait_send()
@@ -1364,10 +1340,11 @@
             shape(w_down.shape, BF),
             shape(w_down.shape, BF),
             shape(w_down.shape, BF),
+            shape((4, rows, width), BF),
             shape((8, width), F32),
         ),
         in_specs=[anywhere] * 7 + [vmem] * 4,
-        out_specs=(anywhere,) * 12 + (vmem,),
+        out_specs=(anywhere,) * 13 + (vmem,),
         scratch_shapes=[
             pltpu.VMEM((4, rows, width), BF),
             pltpu.VMEM((block, width), BF),
@@ -1382,7 +1359,7 @@
             dma((count // 2,)),
             dma((count // 2,)),
             dma((count // 2,)),
-            dma((16,)),
+            dma((17,)),
         ],
         compiler_params=pltpu.CompilerParams(
             collective_id=2, has_side_effects=True, vmem_limit_bytes=48 << 20
@@ -1396,17 +1373,572 @@
     )
 
 
-def norm_rows(tensor, gain_vec):
-    return tensor * lax.rsqrt(jnp.mean(tensor * tensor, axis=-1, keepdims=True) + EPS) * gain_vec
-
-
-def rotate(tensor, cosine, sine_table):
-    half_width = tensor.shape[-1] // 2
-    first_half = tensor[..., :half_width]
-    second = tensor[..., half_width:]
-    return jnp.concatenate(
-        [first_half * cosine - second * sine_table, second * cosine + first_half * sine_table],
-        axis=-1,
+THREE, ONE, FOUR_ON, TWO_ON = 0, 2, 4, 6
+UNITS_HOME, DOWN_ON, DOWN_HOME = 8, 15, 16
+PART_MATE, PART_CORNER, PART_FAR, QUERY_HOME, REST_HOME = 17, 18, 19, 20, 23
+LAST_TRANSFERS = 26
+
+
+def head_means(block):
+    low = lanes(block.shape) < HEAD
+    first = jnp.sum(jnp.where(low, block, 0.0), axis=1, keepdims=True)
+    second = jnp.sum(jnp.where(low, 0.0, block), axis=1, keepdims=True)
+    return jnp.where(low, first, second) * (1.0 / HEAD)
+
+
+class LineSum:
+    def __init__(self, part, got, hold, arrive, sems, places, remote):
+        self.part, self.got, self.hold, self.arrive = part, got, hold, arrive
+        self.swap_sems, self.ring_sems = sems
+        self.side, self.place, self.line, self.other, self.after = places
+        self.remote = remote
+
+    def target(self, step):
+        return (self.place + self.line - step) % self.line
+
+    def swap(self, step):
+        to = self.target(step)
+        return self.remote(
+            step - 1,
+            self.part(2 * to + 1 - self.side),
+            self.got.at[to],
+            self.other,
+            *self.swap_sems,
+        )
+
+    def pass_on(self, step):
+        return self.remote(
+            step - 1, self.hold.at[step - 1], self.arrive.at[step - 1], self.after, *self.ring_sems
+        )
+
+    def start(self):
+        for step in range(1, self.line + 1):
+            self.swap(step).start()
+
+    def step(self, step, out=None):
+        to = self.target(step)
+        self.swap(step).wait_recv()
+        total = self.part(2 * to + self.side)[...].astype(F32) + self.got[to].astype(F32)
+        if step > 1:
+            self.pass_on(step - 1).wait_recv()
+            total = total + self.arrive[step - 2].astype(F32)
+        if step < self.line:
+            self.hold[step - 1] = total.astype(BF)
+            self.pass_on(step).start()
+        else:
+            out[...] = total.astype(out.dtype)
+
+    def drain(self):
+        for step in range(1, self.line + 1):
+            self.swap(step).wait_send()
+            if step < self.line:
+                self.pass_on(step).wait_send()
+
+
+def last_kernel(
+    line,
+    dq_four_ref,
+    dq_two_ref,
+    low_four_ref,
+    low_two_ref,
+    own_four_ref,
+    own_two_ref,
+    raw_ref,
+    cos_ref,
+    sin_ref,
+    query_gain_ref,
+    key_gain_ref,
+    normed_ref,
+    w_in_ref,
+    toks_ref,
+    gain_ref,
+    gain_two_ref,
+    units_ref,
+    down_ref,
+    down_parts_ref,
+    slab_ref,
+    dx_out,
+    query_out,
+    rest_out,
+    units_out,
+    down_out,
+    w_out_out,
+    gains_out,
+    low,
+    three,
+    one,
+    four_in,
+    two_in,
+    raw,
+    normed,
+    turned,
+    w_in,
+    toks,
+    scales,
+    grads,
+    query_part,
+    rest_part,
+    query_got,
+    rest_got,
+    query_hold,
+    rest_hold,
+    query_arrive,
+    rest_arrive,
+    query_sum,
+    rest_sum,
+    slab,
+    slab_got,
+    slab_hold,
+    slab_arrive,
+    down_own,
+    down_in,
+    parts,
+    part_got,
+    part_far,
+    gain_rows,
+    head_gains,
+    gains_in,
+    sends,
+    recvs,
+    line_sems,
+    gain_sends,
+    gain_recvs,
+    locals_,
+):
+    me, at = lax.axis_index("head"), lax.axis_index("blk")
+    count = lax.axis_size("blk")
+    side, place = at % 2, at // 2
+    odd = me % 2
+    mate, beside, corner = me + 1 - 2 * odd, (me + 2) % 4, (me + 3 - 2 * odd) % 4
+    other = at + 1 - 2 * side
+    after, before = (at + 2) % count, (at + count - 2) % count
+    rows, width = dx_out.shape
+    block = 4 * rows
+    w_rows = w_in_ref.shape[2]
+    piece_from = (at % 2) * line + at // 2
+    piece_to = 2 * (at % line) + at // line
+    stays = piece_to == at
+
+    rounds = [(mate, at), (beside, at), (me, other)]
+    bit = 1
+    while bit < line:
+        rounds.append((me, at + 2 * bit * (1 - 2 * ((place // bit) % 2))))
+        bit *= 2
+    barrier = pltpu.get_barrier_semaphore()
+    peers = [(corner, at), (me, after), (me, before)]
+    peers += [(head, other) for head in (mate, beside, corner)] + rounds
+    for peer in peers:
+        pl.semaphore_signal(barrier, inc=1, device_id=peer, device_id_type=MESH)
+
+    @pl.when(jnp.logical_not(stays))
+    def _():
+        for peer in ((me, piece_to), (me, piece_from)):
+            pl.semaphore_signal(barrier, inc=1, device_id=peer, device_id_type=MESH)
+
+    pl.semaphore_wait(barrier, jnp.where(stays, len(peers), len(peers) + 2))
+
+    def remote(index, source, target, device, send=sends, recv=recvs):
+        return pltpu.make_async_remote_copy(
+            src_ref=source,
+            dst_ref=target,
+            send_sem=send.at[index],
+            recv_sem=recv.at[index],
+            device_id=device,
+            device_id_type=MESH,
+        )
+
+    def local(index, source, target):
+        return pltpu.make_async_copy(source, target, locals_.at[index])
+
+    low_refs, own_refs = (low_four_ref, low_two_ref), (own_four_ref, own_two_ref)
+    three_on = [remote(THREE + g, low_refs[g].at[1], three.at[g], (me, other)) for g in (0, 1)]
+    one_on = [remote(ONE + g, low_refs[g].at[3], one.at[g], (me, other)) for g in (0, 1)]
+    for copy in three_on + one_on:
+        copy.start()
+    loads = [
+        local(0, normed_ref, normed),
+        local(1, raw_ref, raw),
+        local(2, w_in_ref, w_in),
+        local(3, toks_ref, toks),
+        local(4, slab_ref, slab),
+        local(5, down_parts_ref.at[place], down_own),
+    ]
+    for copy in loads:
+        copy.start()
+    low_loads = [
+        local(6 + 2 * g + i, low_refs[g].at[2 * i], low.at[g, i]) for g in (0, 1) for i in (0, 1)
+    ]
+    for copy in low_loads:
+        copy.start()
+    down_on = remote(DOWN_ON, down_ref, down_in, (me, after))
+    down_on.start()
+    targets = [(side, mate), (side, beside), (side, corner)]
+    targets += [(1 - side, head) for head in (me, mate, beside, corner)]
+    homes = []
+    for i, (to_side, to_head) in enumerate(targets):
+        device = (to_head, at if i < 3 else other)
+        source = units_ref.at[to_head, pl.ds(pl.multiple_of(to_side * w_rows, 16), w_rows)]
+        homes.append(remote(UNITS_HOME + i, source, units_out.at[side * 4 + me], device))
+    units_own = local(
+        10,
+        units_ref.at[me, pl.ds(pl.multiple_of(side * w_rows, 16), w_rows)],
+        units_out.at[side * 4 + me],
+    )
+
+    places = (side, place, line, (me, other), (me, after))
+
+    def line_sum(which, part, got, hold, arrive):
+        sems = [(line_sems.at[which, i, 0], line_sems.at[which, i, 1]) for i in (0, 1)]
+        return LineSum(part, got, hold, arrive, sems, places, remote)
+
+    query_line = line_sum(
+        0, lambda b: query_part.at[:, b], query_got, query_hold, query_arrive
+    )
+    rest_line = line_sum(1, lambda b: rest_part.at[:, b], rest_got, rest_hold, rest_arrive)
+    slab_line = line_sum(2, lambda b: slab.at[b], slab_got, slab_hold, slab_arrive)
+
+    head_gains[...] = jnp.zeros_like(head_gains)
+    gain_rows[...] = jnp.zeros_like(gain_rows)
+    loads[0].wait()
+    loads[1].wait()
+
+    def head_back(out, cols, tile, gain_tile, gain_row):
+        value = raw[tile, cols]
+        scale = head_scale(value)
+        grad = out * cos_ref[tile, :] + swap_halves(out * sin_ref[tile, :])
+        head_gains[0, gain_row : gain_row + 1, :] += jnp.sum(
+            grad * value * scale, axis=0, keepdims=True
+        )
+        inner = grad * gain_tile
+        mean = head_means(inner * value)
+        return (scale * inner - value * (scale * scale * scale * mean)).astype(BF)
+
+    def query_rows(step, carry):
+        tile = pl.ds(pl.multiple_of(step * 64, 64), 64)
+        for i in range(3):
+            t = odd + i if i < 2 else 2 * (1 - odd)
+            cols = pl.ds(pl.multiple_of(t * 128, 128), 128)
+            if i < 2:
+                out = dq_four_ref[tile, i * 128 : (i + 1) * 128]
+            else:
+                out = dq_two_ref[tile, :]
+            grads[tile, cols] = head_back(out, cols, tile, query_gain_ref[...], 0)
+        return carry
+
+    lax.fori_loop(0, block // 64, query_rows, 0)
+    per_tile = 256 // w_rows
+    tiles_per_head = count // per_tile
+
+    def query_weights(step, carry):
+        span = pl.ds(pl.multiple_of(step * 256, 256), 256)
+        turned[span, :] = transposed(normed[:, span])
+        first = pl.ds(step % tiles_per_head * per_tile, per_tile)
+        part = nn(turned[span, :], grads[:, 0:COLS_Q])
+        query_part[step // tiles_per_head, first] = part.astype(BF).reshape(
+            per_tile, w_rows, COLS_Q
+        )
+        return carry
+
+    lax.fori_loop(0, width // 256, query_weights, 0)
+    for copy in low_loads:
+        copy.wait()
+
+    for copy in three_on + one_on:
+        copy.wait_recv()
+
+    def add_pair(step, carry):
+        tile = pl.ds(pl.multiple_of(step * 128, 128), 128)
+        for g in (0, 1):
+            got_three, got_one = three[g, tile, :].astype(F32), one[g, tile, :].astype(F32)
+            to_four = jnp.where(side == 0, 0.0, got_three)
+            to_two = jnp.where(side == 0, got_three, got_one)
+            low[g, 0, tile, :] = (low[g, 0, tile, :].astype(F32) + to_four).astype(BF)
+            low[g, 1, tile, :] = (low[g, 1, tile, :].astype(F32) + to_two).astype(BF)
+        return carry
+
+    lax.fori_loop(0, block // 128, add_pair, 0)
+    four_on = [remote(FOUR_ON + g, low.at[g, 0], four_in.at[g], (me, before)) for g in (0, 1)]
+    two_on = [remote(TWO_ON + g, low.at[g, 1], two_in.at[g], (me, before)) for g in (0, 1)]
+    for copy in four_on:
+        copy.start()
+    query_line.start()
+    for copy in homes:
+        copy.start()
+    units_own.start()
+    loads[4].wait()
+    slab_line.start()
+
+    loads[3].wait()
+
+    def token_scales(step, carry):
+        tile = pl.ds(pl.multiple_of(step % (rows // 32) * 32, 32), 32)
+        value = toks[step // (rows // 32), tile, :].astype(F32)
+        scales[pl.ds(pl.multiple_of(step * 32, 32), 32), :] = lax.rsqrt(
+            jnp.mean(value * value, axis=1, keepdims=True) + EPS
+        )
+        return carry
+
+    lax.fori_loop(0, block // 32, token_scales, 0)
+    query_line.step(1)
+    for copy in four_on:
+        copy.wait_recv()
+
+    def add_four(step, carry):
+        tile = pl.ds(pl.multiple_of(step * 128, 128), 128)
+        for g in (0, 1):
+            low[g, 1, tile, :] = (
+                low[g, 1, tile, :].astype(F32) + four_in[g, tile, :].astype(F32)
+            ).astype(BF)
+        return carry
+
+    lax.fori_loop(0, block // 128, add_four, 0)
+    for copy in two_on:
+        copy.start()
+    loads[5].wait()
+    down_on.wait_recv()
+
+    def add_down(step, carry):
+        span = pl.ds(pl.multiple_of(step * 256, 256), 256)
+        down_own[:, span] = (
+            down_own[:, span].astype(F32) + down_in[:, span].astype(F32)
+        ).astype(BF)
+        return carry
+
+    lax.fori_loop(0, width // 256, add_down, 0)
+    down_home = remote(DOWN_HOME, down_own, down_out, (me, piece_from))
+    down_stay = local(11, down_own, down_out)
+
+    @pl.when(jnp.logical_not(stays))
+    def _():
+        down_home.start()
+
+    @pl.when(stays)
+    def _():
+        down_stay.start()
+
+    slab_line.step(1)
+    for step in range(2, line + 1):
+        query_line.step(step, query_sum)
+    query_home = [
+        remote(QUERY_HOME + i, query_sum.at[to], query_out.at[me], (to, at))
+        for i, to in enumerate((mate, beside, corner))
+    ]
+    query_own = local(12, query_sum.at[me], query_out.at[me])
+    for copy in query_home:
+        copy.start()
+    query_own.start()
+    for copy in two_on:
+        copy.wait_recv()
+
+    def key_rows(step, carry):
+        tile = pl.ds(pl.multiple_of(step * 64, 64), 64)
+        first_half = lanes((64, 128)) < HEAD
+        both = []
+        for g in (0, 1):
+            from_pair = jnp.where(side == 0, one[g, tile, :].astype(F32), 0.0)
+            both.append(own_refs[g][tile, :] + from_pair + two_in[g, tile, :].astype(F32))
+        zero = jnp.where(odd == 0, both[0], both[1])
+        unit = jnp.where(odd == 0, both[1], both[0])
+        keys = jnp.where(first_half, zero, pltpu.roll(unit, HEAD, 1))
+        values = jnp.where(first_half, pltpu.roll(zero, HEAD, 1), unit)
+        cols = pl.ds(COLS_Q, 128)
+        grads[tile, cols] = head_back(keys, cols, tile, key_gain_ref[...], 1)
+        grads[tile, COLS_Q + 128 : COLS_Q + 256] = values.astype(BF)
+        return carry
+
+    lax.fori_loop(0, block // 64, key_rows, 0)
+
+    loads[2].wait()
+
+    def token_cols(step, carry):
+        span = pl.ds(pl.multiple_of(step * 256, 256), 256)
+        first = pl.ds(step % tiles_per_head * per_tile, per_tile)
+        weight = w_in[step // tiles_per_head, first, :, 0:COLS_IN].reshape(256, COLS_IN)
+        part = nt(grads[...], weight)
+        parts[:, :, span] = part.astype(BF).reshape(4, rows, 256)
+        value = toks[:, :, span].reshape(block, 256).astype(F32)
+        gain_rows[0:1, span] = jnp.sum(part * value * scales[...], axis=0, keepdims=True)
+        return carry
+
+    lax.fori_loop(0, width // 256, token_cols, 0)
+    to_mate = [
+        remote(PART_CORNER, parts.at[corner], part_got.at[1], (mate, at)),
+        remote(PART_MATE, parts.at[mate], part_got.at[0], (mate, at)),
+    ]
+    for copy in to_mate:
+        copy.start()
+    gain_rows[1:2, :] = gain_two_ref[...]
+
+    def rest_weights(step, carry):
+        span = pl.ds(pl.multiple_of(step * 256, 256), 256)
+        first = pl.ds(step % tiles_per_head * per_tile, per_tile)
+        head = step // tiles_per_head
+        part = nn(turned[span, :], grads[:, COLS_Q : COLS_Q + 256])
+        rest_part[head, first, :, 0:256] = part.astype(BF).reshape(per_tile, w_rows, 256)
+        gain_cols = transposed(gain_rows[:, span])
+        rest_part[head, first, :, 256:384] = gain_cols.astype(BF).reshape(per_tile, w_rows, 128)
+        return carry
+
+    lax.fori_loop(0, width // 256, rest_weights, 0)
+    rest_line.start()
+    to_mate[0].wait_recv()
+
+    def add_part(step, carry):
+        tile = pl.ds(pl.multiple_of(step * 32, 32), 32)
+        parts[beside, tile, :] = (
+            parts[beside, tile, :].astype(F32) + part_got[1, tile, :].astype(F32)
+        ).astype(BF)
+        return carry
+
+    lax.fori_loop(0, rows // 32, add_part, 0)
+    part_on = remote(PART_FAR, parts.at[beside], part_far, (beside, at))
+    part_on.start()
+
+    def gain_round(i):
+        return remote(i, head_gains.at[i], gains_in.at[i], rounds[i], gain_sends, gain_recvs)
+
+    rest_line.step(1)
+    for i in range(len(rounds)):
+        gain_round(i).start()
+        gain_round(i).wait_recv()
+        head_gains[i + 1] = head_gains[i] + gains_in[i]
+        if i + 2 <= line:
+            slab_line.step(i + 2, w_out_out)
+            rest_line.step(i + 2, rest_sum)
+    for step in range(len(rounds) + 2, line + 1):
+        slab_line.step(step, w_out_out)
+        rest_line.step(step, rest_sum)
+    gains_out[...] = head_gains[len(rounds)]
+    rest_home = [
+        remote(REST_HOME + i, rest_sum.at[to], rest_out.at[me], (to, at))
+        for i, to in enumerate((mate, beside, corner))
+    ]
+    rest_own = local(13, rest_sum.at[me], rest_out.at[me])
+    for copy in rest_home:
+        copy.start()
+    rest_own.start()
+
+    to_mate[1].wait_recv()
+    part_on.wait_recv()
+
+    def norm_back(step, carry):
+        tile = pl.ds(pl.multiple_of(step * 32, 32), 32)
+        grad = (
+            parts[me, tile, :].astype(F32)
+            + part_got[0, tile, :].astype(F32)
+            + part_far[tile, :].astype(F32)
+        )
+        value = toks[me, tile, :].astype(F32)
+        scale = lax.rsqrt(jnp.mean(value * value, axis=1, keepdims=True) + EPS)
+        inner = grad * gain_ref[0:1, :]
+        mean = jnp.mean(inner * value, axis=1, keepdims=True)
+        dx_out[tile, :] = scale * inner - value * (scale * scale * scale * mean)
+        return carry
+
+    lax.fori_loop(0, rows // 32, norm_back, 0)
+
+    for copy in homes + query_home + rest_home:
+        copy.wait()
+    for copy in (units_own, query_own, rest_own):
+        copy.wait()
+    for copy in three_on + one_on + four_on + two_on + to_mate + [down_on, part_on]:
+        copy.wait_send()
+
+    @pl.when(jnp.logical_not(stays))
+    def _():
+        down_home.wait()
+
+    @pl.when(stays)
+    def _():
+        down_stay.wait()
+
+    for total in (query_line, rest_line, slab_line):
+        total.drain()
+    for i in range(len(rounds)):
+        gain_round(i).wait_send()
+
+
+def last(
+    dq, dkv_low, dkv_own, raw, cosine, sine, query_gain, key_gain, normed, w_in, toks, gains,
+    gain_two, units, down, down_parts, slab,
+):
+    _, rows, width = toks.shape
+    _, count, w_rows, _ = w_in.shape
+    line = count // 2
+    block = 4 * rows
+    anywhere = pl.BlockSpec(memory_space=pl.ANY)
+    vmem = pl.BlockSpec(memory_space=pltpu.VMEM)
+    shape = jax.ShapeDtypeStruct
+    dma = pltpu.SemaphoreType.DMA
+    rounds = 3 + int(math.log2(line))
+    part = (4, w_rows, COLS_Q)
+    out_rows = slab.shape[1]
+    return pl.pallas_call(
+        functools.partial(last_kernel, line),
+        out_shape=(
+            shape((rows, width), F32),
+            shape(part, BF),
+            shape(part, BF),
+            shape((8, w_rows, units.shape[2]), BF),
+            shape(down.shape, BF),
+            shape((out_rows, width), F32),
+            shape((8, 128), F32),
+        ),
+        in_specs=[vmem] * 2 + [anywhere] * 2 + [vmem] * 2 + [anywhere] + [vmem] * 4
+        + [anywhere] * 3 + [vmem] * 2 + [anywhere] * 4,
+        out_specs=(vmem,) + (anywhere,) * 4 + (vmem,) * 2,
+        scratch_shapes=[
+            pltpu.VMEM((2, 2, block, 128), BF),
+            pltpu.VMEM((2, block, 128), BF),
+            pltpu.VMEM((2, block, 128), BF),
+            pltpu.VMEM((2, block, 128), BF),
+            pltpu.VMEM((2, block, 128), BF),
+            pltpu.VMEM((block, COLS_Q + 128), F32),
+            pltpu.VMEM((block, width), BF),
+            pltpu.VMEM((width, block), BF),
+            pltpu.VMEM(w_in.shape, BF),
+            pltpu.VMEM(toks.shape, BF),
+            pltpu.VMEM((block, 1), F32),
+            pltpu.VMEM((block, COLS_IN), BF),
+            pltpu.VMEM((4, count, w_rows, COLS_Q), BF),
+            pltpu.VMEM((4, count, w_rows, COLS_Q), BF),
+            pltpu.VMEM((line,) + part, BF),
+            pltpu.VMEM((line,) + part, BF),
+            pltpu.VMEM((line - 1,) + part, BF),
+            pltpu.VMEM((line - 1,) + part, BF),
+            pltpu.VMEM((line - 1,) + part, BF),
+            pltpu.VMEM((line - 1,) + part, BF),
+            pltpu.VMEM(part, BF),
+            pltpu.VMEM(part, BF),
+            pltpu.VMEM(slab.shape, BF),
+            pltpu.VMEM((line,) + slab.shape[1:], BF),
+            pltpu.VMEM((line - 1,) + slab.shape[1:], BF),
+            pltpu.VMEM((line - 1,) + slab.shape[1:], BF),
+            pltpu.VMEM(down.shape, BF),
+            pltpu.VMEM(down.shape, BF),
+            pltpu.VMEM((4, rows, width), BF),
+            pltpu.VMEM((2, rows, width), BF),
+            pltpu.VMEM((rows, width), BF),
+            pltpu.VMEM((128, width), F32),
+            pltpu.VMEM((rounds + 1, 8, 128), F32),
+            pltpu.VMEM((rounds, 8, 128), F32),
+            dma((LAST_TRANSFERS,)),
+            dma((LAST_TRANSFERS,)),
+            dma((3, 2, 2, line)),
+            dma((rounds,)),
+            dma((rounds,)),
+            dma((14,)),
+        ],
+        compiler_params=pltpu.CompilerParams(
+            collective_id=3, has_side_effects=True, vmem_limit_bytes=58 << 20
+        ),
+        cost_estimate=pl.CostEstimate(
+            flops=60_000_000_000, bytes_accessed=60_000_000, transcendentals=1_000_000
+        ),
+        name="last",
+    )(
+        *dq, *dkv_low, *dkv_own, raw, cosine, sine, query_gain, key_gain, normed, w_in, toks, gains,
+        gain_two, units, down, down_parts, slab,
     )
 
 
@@ -1473,8 +2005,8 @@
         ]
     rest = jnp.concatenate(rest, axis=1).reshape(w_rows, groups, COLS_Q)
     rest = jnp.swapaxes(rest, 0, 1)
-    query_g = query_gain.astype(F32)
-    key_g = key_gain.astype(F32)
+    query_row = jnp.concatenate([query_gain, query_gain]).astype(F32)[None, :]
+    key_row = jnp.concatenate([key_gain, key_gain]).astype(F32)[None, :]
     (
         wide,
         queries,
@@ -1488,6 +2020,7 @@
         down_own,
         down_one,
         down_two,
+        toks,
         gains,
     ) = first(
         tokens,
@@ -1499,11 +2032,9 @@
         cotangent,
         cosine,
         sine,
-        jnp.concatenate([query_g, query_g])[None, :],
-        jnp.concatenate([key_g, key_g])[None, :],
+        query_row,
+        key_row,
     )
-    w_in = w_in.reshape(width, 2 * q_cols)
-    gain_one, gain_two = gains[0], gains[1]
     slabs, downs = [slab, slab_next], [down_own, down_one, down_two]
     for _ in range(line - 4):
         slabs.append(ring(slabs[-1], 2))
@@ -1536,13 +2067,11 @@
         attn_out,
         tokens,
         w_o,
-        gain_two[None, :],
+        gains[1:2],
         slabs,
         w_d.reshape(ff_cols, width),
         top,
     )
-    grad_gain_two = grad_gain_two[0]
-    inputs = tokens.astype(F32)
     down_parts = down_parts.reshape(line, ff_rows, width)
     gu_parts = gu_parts.reshape(groups, line, 2 * w_rows, 2 * ff_cols)
     down_sum = LineScatter(lambda p: take(down_parts, p))
@@ -1555,107 +2084,59 @@
     gu_sum.ahead(line - 4)
     down_moved, gu_moved = down_sum.send(), gu_sum.send()
     out_act = (resid + scatter_pair(out_part)).astype(BF)
-    out_slab = scatter_head(out_parts).astype(BF).reshape(blocks, w_out.shape[0], width)
-    dq, dkv, own = attend_back(
-        meta,
-        wide,
-        queries,
-        kv_window,
-        kept,
-        grad_mix.reshape(block_len, q_cols),
-        window_start[None, :],
+    back = functools.partial(
+        attend_back,
+        meta=meta,
+        wide=wide,
+        queries=queries,
+        kv=kv_window,
+        kept=kept,
+        grads=grad_mix.reshape(block_len, q_cols),
+        starts=window_start[None, :],
     )
-    dq, dkv, own, down_moved, gu_moved, out_act, out_slab = sync(
-        dq, dkv, own, down_moved, gu_moved, out_act, out_slab
+    four = back(0)
+    four, down_moved, gu_moved, out_act, kv_window = sync(
+        four, down_moved, gu_moved, out_act, kv_window
     )
     down_sum.total, gu_sum.total = down_moved, gu_moved
     down_sum.add()
     gu_sum.add()
-    grad_queries = dq.reshape(block_len, per_group, HEAD)
-
-    even = side == 0
-    four, three, two, one = [dkv[i] for i in range(BACK)]
-    got_three = swap(three, "blk", 1).astype(F32)
-    got_one = swap(one, "blk", 1).astype(F32)
-    four = four.astype(F32) + jnp.where(even, 0.0, got_three)
-    two = two.astype(F32) + jnp.where(even, got_three, got_one)
-    own = own + jnp.where(even, got_one, 0.0)
-    two = two + ring(four.astype(BF), -2).astype(F32)
-    own = own + ring(two.astype(BF), -2).astype(F32)
     down_moved, gu_moved = down_sum.send(), gu_sum.send()
-    own, down_moved, gu_moved = sync(own, down_moved, gu_moved)
+    out_slab = scatter_head(out_parts).astype(BF).reshape(blocks, w_out.shape[0], width)
+    two = back(1, kv=kv_window)
+    four, two, down_moved, gu_moved, out_slab = sync(
+        four, two, down_moved, gu_moved, out_slab
+    )
     down_sum.total, gu_sum.total = down_moved, gu_moved
     down_sum.add()
     gu_sum.add()
-    down_sum.send()
-    down_sum.add()
-    d_w_down = lax.ppermute(
+    token_part, query_owned, rest_owned, units_owned, down_owned, d_w_out, head_gains = last(
+        (four[0], two[0]),
+        (four[1], two[1]),
+        (four[2], two[2]),
+        raw,
+        cosine,
+        sine,
+        query_row,
+        key_row,
+        normed_one,
+        w_in,
+        toks,
+        gains,
+        grad_gain_two,
+        gu_sum.total.astype(BF),
         down_sum.total.astype(BF),
-        "blk",
-        [(i, i % 2 * line + i // 2) for i in range(blocks)],
-    ).astype(F32)
-    kv_grad = jnp.swapaxes(own, 0, 1)
-    grad_keys = kv_grad[..., :HEAD]
-    grad_values = kv_grad[..., HEAD:]
-
-    def to_owner(grad):
-        back = lax.all_to_all(
-            grad.astype(BF), "head", split_axis=0, concat_axis=0, tiled=True
-        )
-        return jnp.swapaxes(back, 0, 1).astype(F32)
-
-    gu_own = gu_sum.total.astype(BF).reshape(groups, 2, w_rows, 2 * ff_cols)
-    mine = take(gu_own, side, 1)
-    got = swap(take(gu_own, 1 - side, 1), "blk", 1)
-    gu_own = put(jnp.zeros((groups, w_rows, 2, 2 * ff_cols), BF), mine, side, 2)
-    gu_own = put(gu_own, got, 1 - side, 2)
-    gu_own = to_owner(gu_own)
-    gu_own = gu_own.reshape(w_rows, groups, 2, 2, ff_cols)
-    d_w_gate = gu_own[:, :, :, 0].reshape(w_gate.shape)
-    d_w_up = gu_own[:, :, :, 1].reshape(w_up.shape)
-
-    d_w_out = scatter_blk(lambda b: take(out_slab, b))
-
-    def prepare(query_raw, key_raw, query_gain_in, key_gain_in):
-        cos_half, sin_half = (
-            cosine[:, None, : HEAD // 2],
-            sine[:, None, HEAD // 2 : HEAD],
-        )
-        return (
-            rotate(norm_rows(query_raw, query_gain_in), cos_half, sin_half),
-            rotate(norm_rows(key_raw, key_gain_in), cos_half, sin_half),
-        )
-
-    query_raw = raw[:, :q_cols].reshape(block_len, per_group, HEAD)
-    key_raw = raw[:, q_cols:].reshape(block_len, 2, HEAD)
-    rot_out, prep_pull = jax.vjp(prepare, query_raw, key_raw, query_g, key_g)
-    grad_query_raw, grad_key_raw, grad_query_g, grad_key_g = prep_pull((grad_queries, grad_keys))
-    gain_sums = sum_all(jnp.stack([grad_query_g, grad_key_g]))
-    raw_grads = jnp.concatenate(
-        [
-            grad_query_raw.reshape(block_len, q_cols),
-            grad_key_raw.reshape(block_len, 2 * HEAD),
-            grad_values.reshape(block_len, 2 * HEAD),
-        ],
-        axis=1,
-    ).astype(BF)
-    grad_w_in = matmul_tn(normed_one, raw_grads)
-    normed_part = matmul_nt(raw_grads, w_in[:, : q_cols + 4 * HEAD]).astype(BF)
-    grad_normed_one = scatter_head(normed_part.reshape(groups, tok_rows, width))
-    norm_one_out, norm_one_pull = jax.vjp(norm_rows, inputs, gain_one)
-    grad_input_part, grad_gain_one = norm_one_pull(grad_normed_one)
-    d_tokens = grad_resid + grad_input_part
-    grad_w_in = jnp.concatenate(
-        [
-            grad_w_in,
-            grad_gain_one[:, None],
-            grad_gain_two[:, None],
-            jnp.zeros((width, 126), F32),
-        ],
-        axis=1,
+        down_parts,
+        out_slab,
     )
-    in_parts = grad_w_in.astype(BF).reshape(groups, blocks, w_rows, 2 * q_cols)
-    owned = to_owner(scatter_blk(lambda b: take(in_parts, b, 1)))
+    d_tokens = grad_resid + token_part
+    d_w_down = down_owned.astype(F32)
+    units = units_owned.reshape(2, groups, w_rows, 2, ff_cols).astype(F32)
+    units = jnp.transpose(units, (3, 2, 1, 0, 4)).reshape((2,) + w_gate.shape)
+    d_w_gate, d_w_up = units[0], units[1]
+    gain_sums = head_gains[:2, :HEAD] + head_gains[:2, HEAD:]
+    owned = jnp.concatenate([query_owned, rest_owned], axis=2).astype(F32)
+    owned = jnp.swapaxes(owned, 0, 1)
     d_w_query = owned[:, :, :q_cols].reshape(w_rows, QHEADS * HEAD)
     key_heads, value_heads = [], []
     for head_id in range(KVHEADS):

time: 903 us -> 800 us (0.89)
  Pallas kernels: 353 us -> 533 us
  waiting for transfers between devices: 202 us -> 81 us
  starting transfers between devices: 156 us -> 75.2 us
  other arithmetic: 79.9 us -> 42.2 us
  local copies, waits for them, and re-layouts: 87 us -> 52.5 us
  matrix products: 12.3 us -> 1.83 us
    pallas_call x1 -> x3, Pallas kernels: 32.9 us -> 197 us  [the longest x1 162 us: last(): pl.pallas_call(functools.partial(last_kernel, line), out_shape=(shape((ro...]
    ppermute x18 -> x9, waiting for transfers between devices: 127 us -> 35.8 us  [ring(): lax.ppermute(block, 'blk', [(i, (i + step) % count) for i in range(count)])]
    ppermute x37 -> x18, starting transfers between devices: 61.2 us -> 12 us  [swap(): return lax.ppermute(block, axis, [(i, i ^ bit) for i in range(count)])]
    ppermute x37 -> x18, waiting for transfers between devices: 73.1 us -> 45.2 us  [swap(): return lax.ppermute(block, axis, [(i, i ^ bit) for i in range(count)])]
    ppermute x18 -> x9, starting transfers between devices: 86.4 us -> 63.2 us  [ring(): lax.ppermute(block, 'blk', [(i, (i + step) % count) for i in range(count)])]
    slice x10 -> x4, local copies, waits for them, and re-layouts: 22.3 us -> 5.71 us  [the longest x3 5.1 us: shards(): d_w_gate, d_w_up = (units[0], units[1])]
    pallas_call x1, Pallas kernels: 171 us -> 187 us  [middle(): pl.pallas_call(functools.partial(middle_kernel, len(slabs), line), out_sh...]
    convert_element_type x14 -> x3, other arithmetic: 14.2 us -> 4.69 us  [the longest x1 2.69 us: shards(): gu_sum.total.astype(BF)]
  transfers between devices with their start and end apart: 58 -> 27, of which waited for: 23 -> 12; matrix products, arithmetic and copies ran while one was open for 16% -> 6% of each run, Pallas kernels for 5% -> 6%
where the time goes in v5:
time: 800 us; the launch traced here: 787 us
  Pallas kernels  533 us (67%)
  waiting for transfers between devices  81 us (10%)
  starting transfers between devices  75.2 us (9%)
  local copies, waits for them, and re-layouts  52.5 us (7%)
  other arithmetic  42.2 us (5%)
    pallas_call x1, Pallas kernels, middle(): pl.pallas_call(functools.partial(middle_kernel, len(slabs), line), out_sh...  187 us
    pallas_call x1, Pallas kernels, last(): pl.pallas_call(functools.partial(last_kernel, line), out_shape=(shape((ro...  162 us
    pallas_call x1, Pallas kernels, first(): pl.pallas_call(functools.partial(first_kernel, count // 2), out_shape=(sh...  133 us
    ppermute x9, starting transfers between devices, ring(): lax.ppermute(block, 'blk', [(i, (i + step) % count) for i in range(count)])  63.2 us
    ppermute x18, waiting for transfers between devices, swap(): return lax.ppermute(block, axis, [(i, i ^ bit) for i in range(count)])  45.2 us
    ppermute x9, waiting for transfers between devices, ring(): lax.ppermute(block, 'blk', [(i, (i + step) % count) for i in range(count)])  35.8 us
    pallas_call x2, Pallas kernels, attend_back(): pl.pallas_call(functools.partial(attend_back_kernel, which), out_shape=(s...  35.4 us
  transfers between devices with their start and end apart: 27, of which 12 were waited for; matrix products, arithmetic and copies ran while one was open for 6% of the time, Pallas kernels for 6%

profile of v5, /device:TPU:0, one launch (start us, length us, event | category | flops | bytes accessed | tf_op | source)
XLA Modules:
  0.0 787.4 jit_solution(15564067291863750054)
XLA Ops:
  8.7 132.9 %first.1 = (bf16[6,1024,128]{2,1,0:T(8,128)(2,1)}, bf16[6,1024,128]{2,1,0:T(8,128)(2,1)}, bf16[5,2,1024,128]{3,2,1,0:T(8,128)(2,1)}, f32[1024,512]{1,0:T(8,128)}...) custom-call(bf16[256,2048]{1,0:T(8,128)(2,1)} %tokens_ref.3, ...), custom_call_target="tpu_custom_call" | custom-call | flops 60000002048 | bytes 60000000 | tf_op jit(solution)/shard_map/first/pallas_call | solution.py:1328
  146.4 2.9 collective-permute-done.3
  152.8 5.2 collective-permute-done.5
  161.6 3.9 collective-permute-done.7
  165.5 2.2 collective-permute-start.8
  169.1 2.3 collective-permute-done.8
  173.8 28.5 %collective-permute-done.10 = bf16[384,2048]{1,0:T(8,128)(2,1)} collective-permute-done((bf16[384,2048]{1,0:T(8,128)(2,1)}, bf16[384,2048]{1,0:T(8,128)(2,1)}, u32[]{:S(2)}, u32[]{:S(2)}) %collective-permute-start.10) | collective-permute-done | bytes 1572896 | tf_op jit(solution)/shard_map/ppermute | solution.py:44
  205.5 15.7 %attend.1 = (f32[6,1024,128]{2,1,0:T(8,128)}, bf16[1024,384]{1,0:T(8,128)(2,1)S(1)}) custom-call(s32[9]{0:T(128)S(1)} %pad_add_fusion.1.meta_ref, bf16[6,1024,128]{2,1,0:T(8,128)(2,1)S(1)} %copy-done.12, bf16[5,2,1024,128]{3,2,1,0:T(8,128)(2,1)S(1)} %copy-done.11, s32[1024,1]{1,0:T(8,128)S(1)} %copy.83.start_ref), custom_call_target="tpu_custom_call" | custom-call | flops 60000002048 | bytes 20000000 | tf_op jit(solution)/shard_map/attend/pallas_call | solution.py:266
  234.1 187.3 %middle.1 = (f32[256,2048]{1,0:T(8,128)}, f32[256,2048]{1,0:T(8,128)}, bf16[256,2048]{1,0:T(8,128)(2,1)}, bf16[256,1536]{1,0:T(8,128)(2,1)}, bf16[4,256,384]{2,1...) custom-call(bf16[4,256,384]{2,1,0:T(8,128)(2,1)} %bitcast.155, ...), custom_call_target="tpu_custom_call" | custom-call | flops 60000002048 | bytes 100000000 | tf_op jit(solution)/shard_map/middle/pallas_call | solution.py:877
  421.4 4.5 dynamic-slice_bitcast_fusion.5
  427.2 2.7 fusion.5
  432.3 4.2 convert_add_fusion.7
  439.7 2.1 dynamic-slice_bitcast_fusion.1
  443.4 7.5 collective-permute-done.20
  452.8 4.4 collective-permute-done.17
  458.9 21.1 %attend_back_four.1 = (f32[1024,256]{1,0:T(8,128)S(1)}, bf16[4,1024,128]{2,1,0:T(8,128)(2,1)S(1)}, f32[1024,128]{1,0:T(8,128)S(1)}) custom-call(s32[9]{0:T(128)S(1)} %pad_add_fusion.1.meta_ref, bf16[6,1024,128]{2,1,0:T(8,128)(2,1)S(1)} %copy-done.13, bf16[6,1024,128]{2,1,0:T(8,128)(2,1)} %get-tuple-element.92.query_ref, ...), custom_call_target="tpu_custom_call" | custom-call | flops 80000000000 | bytes 40000000 | tf_op jit(solution)/shard_map/attend_back_four/pallas_call | solution.py:416
  482.9 20.1 %collective-permute-start.12 = (bf16[160,2048]{1,0:T(8,128)(2,1)S(1)}, bf16[160,2048]{1,0:T(8,128)(2,1)S(1)}, u32[]{:S(2)}, u32[]{:S(2)}) collective-permute-start(bf16[160,2048]{1,0:T(8,128)(2,1)S(1)} %dynamic-slice_bitcast_fusion.6), channel_id=1, source_target_pairs={{0,2},{1,3},{2,4},{3,5},{4,6},{5,7},{6,0},{7,1},{8,10},{9,11},{10,... | collective-permute-start | bytes 1966088 | tf_op jit(solution)/shard_map/ppermute | solution.py:49
  506.8 4.0 fusion.10
  510.8 4.9 collective-permute-done.12
  515.8 2.1 fusion.12
  517.9 36.4 %collective-permute-start.22 = (bf16[160,2048]{1,0:T(8,128)(2,1)}, bf16[160,2048]{1,0:T(8,128)(2,1)S(1)}, u32[]{:S(2)}, u32[]{:S(2)}) collective-permute-start(bf16[160,2048]{1,0:T(8,128)(2,1)} %fusion.12), channel_id=1, source_target_pairs={{0,2},{1,3},{2,4},{3,5},{4,6},{5,7},{6,0},{7,1},{8,10},{9,11},{10,... | collective-permute-start | bytes 1966088 | tf_op jit(solution)/shard_map/ppermute | solution.py:49
  554.3 2.7 fusion.4
  557.0 2.5 collective-permute-start.23
  559.4 14.3 %attend_back_two.1 = (f32[1024,128]{1,0:T(8,128)S(1)}, bf16[4,1024,128]{2,1,0:T(8,128)(2,1)S(1)}, f32[1024,128]{1,0:T(8,128)S(1)}) custom-call(s32[9]{0:T(128)S(1)} %pad_add_fusion.1.meta_ref, bf16[6,1024,128]{2,1,0:T(8,128)(2,1)S(1)} %copy-done.13, bf16[6,1024,128]{2,1,0:T(8,128)(2,1)S(1)} %copy-done.14, ...), custom_call_target="tpu_custom_call" | custom-call | flops 40000000000 | bytes 40000000 | tf_op jit(solution)/shard_map/attend_back_two/pallas_call | solution.py:416
  573.8 4.7 fusion.2
  578.5 18.9 %collective-permute-done.23 = bf16[4,128,1280]{2,1,0:T(8,128)(2,1)S(1)} collective-permute-done((bf16[4,128,1280]{2,1,0:T(8,128)(2,1)}, bf16[4,128,1280]{2,1,0:T(8,128)(2,1)S(1)}, u32[]{:S(2)}, u32[]{:S(2)}) %collective-permute-start.23) | collective-permute-done | bytes 1310752 | tf_op jit(solution)/shard_map/ppermute | solution.py:49
  597.4 2.1 fusion.11.down_ref
  599.5 2.7 fusion.3.units_ref
  602.2 161.9 %last.1 = (f32[256,2048]{1,0:T(8,128)}, bf16[4,64,384]{2,1,0:T(8,128)(2,1)}, bf16[4,64,384]{2,1,0:T(8,128)(2,1)}, bf16[8,64,1280]{2,1,0:T(8,128)(2,1)}, bf16[160...) custom-call(f32[1024,256]{1,0:T(8,128)} %copy-done.18, f32[1024,128]{1,0:T(8,128)} %copy-done.16, ...), custom_call_target="tpu_custom_call" | custom-call | flops 60000002048 | bytes 60000000 | tf_op jit(solution)/shard_map/last/pallas_call | solution.py:1876
  768.8 3.0 reshape.296
  771.8 3.1 fusion.20
  781.1 3.9 add.250
  (174 shorter events, 71.2 us)
Async XLA Ops:
  8.6 133.0 %copy-start = (f32[1024,128]{1,0:T(8,128)}, f32[1024,128]{1,0:T(8,128)S(1)}, u32[]{:S(2)}) copy-start(f32[1024,128]{1,0:T(8,128)S(1)} %get-tuple-element.203.cos_ref) | copy-start | bytes 1572868
  8.6 133.0 %copy-start.1 = (f32[1024,128]{1,0:T(8,128)}, f32[1024,128]{1,0:T(8,128)S(1)}, u32[]{:S(2)}) copy-start(f32[1024,128]{1,0:T(8,128)S(1)} %get-tuple-element.204.sin_ref) | copy-start | bytes 1572868
  8.7 133.0 %copy-start.31 = (bf16[48,2048]{1,0:T(8,128)(2,1)S(1)}, bf16[48,2048]{1,0:T(8,128)(2,1)}, u32[]{:S(2)}) copy-start(bf16[48,2048]{1,0:T(8,128)(2,1)} %param.22) | copy-start | bytes 589828
  141.6 80.4 %copy-start.2 = (f32[8,2048]{1,0:T(8,128)}, f32[8,2048]{1,0:T(8,128)S(1)}, u32[]{:S(2)}) copy-start(f32[8,2048]{1,0:T(8,128)S(1)} %get-tuple-element.105.gain_ref) | copy-start | bytes 196612
  141.7 7.6 collective-permute-start.3
  143.7 7.7 collective-permute-start.2
  149.3 8.7 %collective-permute-start.5 = (bf16[48,2048]{1,0:T(8,128)(2,1)S(1)}, bf16[48,2048]{1,0:T(8,128)(2,1)S(1)}, u32[]{:S(2)}, u32[]{:S(2)}) collective-permute-start(bf16[48,2048]{1,0:T(8,128)(2,1)S(1)} %collective-permute-done.3), channel_id=1, source_target_pairs={{0,2},{1,3},{2,4},{3,5},{4,6},{5,7},{6,0},{7,1},{8,10},{9,11},{10,... | collective-permute-start | bytes 589832 | tf_op jit(solution)/shard_map/ppermute | solution.py:49
  151.2 9.0 %collective-permute-start.4 = (bf16[48,2048]{1,0:T(8,128)(2,1)S(1)}, bf16[48,2048]{1,0:T(8,128)(2,1)S(1)}, u32[]{:S(2)}, u32[]{:S(2)}) collective-permute-start(bf16[48,2048]{1,0:T(8,128)(2,1)S(1)} %collective-permute-done.3), channel_id=1, source_target_pairs={{0,1},{1,0},{2,3},{3,2},{4,5},{5,4},{6,7},{7,6},{8,9},{9,8},{10,11... | collective-permute-start | bytes 589832 | tf_op jit(solution)/shard_map/ppermute | solution.py:44
  158.0 7.5 collective-permute-start.7
  158.3 9.4 %collective-permute-start.6 = (bf16[48,2048]{1,0:T(8,128)(2,1)S(1)}, bf16[48,2048]{1,0:T(8,128)(2,1)S(1)}, u32[]{:S(2)}, u32[]{:S(2)}) collective-permute-start(bf16[48,2048]{1,0:T(8,128)(2,1)S(1)} %collective-permute-done.5), channel_id=1, source_target_pairs={{0,1},{1,0},{2,3},{3,2},{4,5},{5,4},{6,7},{7,6},{8,9},{9,8},{10,11... | collective-permute-start | bytes 589832 | tf_op jit(solution)/shard_map/ppermute | solution.py:44
  165.5 5.9 collective-permute-start.8
  172.0 30.3 %collective-permute-start.10 = (bf16[384,2048]{1,0:T(8,128)(2,1)}, bf16[384,2048]{1,0:T(8,128)(2,1)}, u32[]{:S(2)}, u32[]{:S(2)}) collective-permute-start(bf16[384,2048]{1,0:T(8,128)(2,1)} %bitcast.20), channel_id=1, source_target_pairs={{0,16},{8,24},{16,0},{24,8},{1,17},{9,25},{17,1},{25,9},{2,18},{10... | collective-permute-start | bytes 4718600 | tf_op jit(solution)/shard_map/ppermute | solution.py:44
  173.1 56.8 %collective-permute-start.1 = (bf16[160,2048]{1,0:T(8,128)(2,1)S(1)}, bf16[160,2048]{1,0:T(8,128)(2,1)S(1)}, u32[]{:S(2)}, u32[]{:S(2)}) collective-permute-start(bf16[160,2048]{1,0:T(8,128)(2,1)S(1)} %get-tuple-element.108), channel_id=1, source_target_pairs={{0,2},{1,3},{2,4},{3,5},{4,6},{5,7},{6,0},{7,1},{8,10},{9,11},{10,... | collective-permute-start | bytes 1966088 | tf_op jit(solution)/shard_map/ppermute | solution.py:49
  173.1 56.8 %collective-permute-start = (bf16[4,128,1280]{2,1,0:T(8,128)(2,1)}, bf16[4,128,1280]{2,1,0:T(8,128)(2,1)}, u32[]{:S(2)}, u32[]{:S(2)}) collective-permute-start(bf16[4,128,1280]{2,1,0:T(8,128)(2,1)} %get-tuple-element.112.refs_1_), channel_id=1, source_target_pairs={{0,2},{1,3},{2,4},{3,5},{4,6},{5,7},{6,0},{7,1},{8,10},{9,11},{10,... | collective-permute-start | bytes 3932168 | tf_op jit(solution)/shard_map/ppermute | solution.py:49
  173.8 51.3 %collective-permute-start.9 = (bf16[384,2048]{1,0:T(8,128)(2,1)}, bf16[384,2048]{1,0:T(8,128)(2,1)}, u32[]{:S(2)}, u32[]{:S(2)}) collective-permute-start(bf16[384,2048]{1,0:T(8,128)(2,1)} %bitcast.20), channel_id=1, source_target_pairs={{0,8},{8,0},{16,24},{24,16},{1,9},{9,1},{17,25},{25,17},{2,10},{10... | collective-permute-start | bytes 4718600 | tf_op jit(solution)/shard_map/ppermute | solution.py:44
  202.3 26.0 %collective-permute-start.11 = (bf16[384,2048]{1,0:T(8,128)(2,1)}, bf16[384,2048]{1,0:T(8,128)(2,1)}, u32[]{:S(2)}, u32[]{:S(2)}) collective-permute-start(bf16[384,2048]{1,0:T(8,128)(2,1)} %collective-permute-done.10), channel_id=1, source_target_pairs={{0,8},{8,0},{16,24},{24,16},{1,9},{9,1},{17,25},{25,17},{2,10},{10... | collective-permute-start | bytes 4718600 | tf_op jit(solution)/shard_map/ppermute | solution.py:44
  425.8 4.0 collective-permute-start.19
  426.6 4.1 collective-permute-start.16
  426.6 5.6 collective-permute-start.15
  429.8 85.9 %collective-permute-start.13 = (bf16[4,128,1280]{2,1,0:T(8,128)(2,1)}, bf16[4,128,1280]{2,1,0:T(8,128)(2,1)S(1)}, u32[]{:S(2)}, u32[]{:S(2)}) collective-permute-start(bf16[4,128,1280]{2,1,0:T(8,128)(2,1)} %fusion.5), channel_id=1, source_target_pairs={{0,2},{1,3},{2,4},{3,5},{4,6},{5,7},{6,0},{7,1},{8,10},{9,11},{10,... | collective-permute-start | bytes 3932168 | tf_op jit(solution)/shard_map/ppermute | solution.py:49
  429.8 75.2 %collective-permute-start.14 = (bf16[256,2048]{1,0:T(8,128)(2,1)}, bf16[256,2048]{1,0:T(8,128)(2,1)}, u32[]{:S(2)}, u32[]{:S(2)}) collective-permute-start(bf16[256,2048]{1,0:T(8,128)(2,1)} %get-tuple-element.159), channel_id=1, source_target_pairs={{0,8},{8,0},{16,24},{24,16},{1,9},{9,1},{17,25},{25,17},{2,10},{10... | collective-permute-start | bytes 3145736 | tf_op jit(solution)/shard_map/ppermute | solution.py:44
  436.6 14.3 %collective-permute-start.20 = (bf16[128,2048]{1,0:T(8,128)(2,1)S(1)}, bf16[128,2048]{1,0:T(8,128)(2,1)S(1)}, u32[]{:S(2)}, u32[]{:S(2)}) collective-permute-start(bf16[128,2048]{1,0:T(8,128)(2,1)S(1)} %get-tuple-element.171), channel_id=1, source_target_pairs={{0,16},{8,24},{16,0},{24,8},{1,17},{9,25},{17,1},{25,9},{2,18},{10... | collective-permute-start | bytes 1572872 | tf_op jit(solution)/shard_map/ppermute | solution.py:44
  441.9 39.8 %collective-permute-start.25 = (bf16[384,2048]{1,0:T(8,128)(2,1)}, bf16[384,2048]{1,0:T(8,128)(2,1)S(1)}, u32[]{:S(2)}, u32[]{:S(2)}) collective-permute-start(bf16[384,2048]{1,0:T(8,128)(2,1)} %get-tuple-element.167), channel_id=1, source_target_pairs={{0,8},{8,0},{16,24},{24,16},{1,9},{9,1},{17,25},{25,17},{2,10},{10... | collective-permute-start | bytes 4718600 | tf_op jit(solution)/shard_map/ppermute | solution.py:44
  442.4 14.8 %collective-permute-start.17 = (bf16[128,2048]{1,0:T(8,128)(2,1)S(1)}, bf16[128,2048]{1,0:T(8,128)(2,1)S(1)}, u32[]{:S(2)}, u32[]{:S(2)}) collective-permute-start(bf16[128,2048]{1,0:T(8,128)(2,1)S(1)} %get-tuple-element.170), channel_id=1, source_target_pairs={{0,1},{1,0},{2,3},{3,2},{4,5},{5,4},{6,7},{7,6},{8,9},{9,8},{10,11... | collective-permute-start | bytes 1572872 | tf_op jit(solution)/shard_map/ppermute | solution.py:44
  452.1 53.1 %collective-permute-start.21 = (bf16[256,2048]{1,0:T(8,128)(2,1)}, bf16[256,2048]{1,0:T(8,128)(2,1)}, u32[]{:S(2)}, u32[]{:S(2)}) collective-permute-start(bf16[256,2048]{1,0:T(8,128)(2,1)} %pad_maximum_fusion.1), channel_id=1, source_target_pairs={{0,1},{1,0},{2,3},{3,2},{4,5},{5,4},{6,7},{7,6},{8,9},{9,8},{10,11... | collective-permute-start | bytes 3145736 | tf_op jit(solution)/shard_map/ppermute | solution.py:44
  458.4 48.4 %collective-permute-start.18 = (bf16[256,2048]{1,0:T(8,128)(2,1)}, bf16[256,2048]{1,0:T(8,128)(2,1)}, u32[]{:S(2)}, u32[]{:S(2)}) collective-permute-start(bf16[256,2048]{1,0:T(8,128)(2,1)} %pad_maximum_fusion), channel_id=1, source_target_pairs={{0,16},{8,24},{16,0},{24,8},{1,17},{9,25},{17,1},{25,9},{2,18},{10... | collective-permute-start | bytes 3145736 | tf_op jit(solution)/shard_map/ppermute | solution.py:44
  482.9 32.9 %collective-permute-start.12 = (bf16[160,2048]{1,0:T(8,128)(2,1)S(1)}, bf16[160,2048]{1,0:T(8,128)(2,1)S(1)}, u32[]{:S(2)}, u32[]{:S(2)}) collective-permute-start(bf16[160,2048]{1,0:T(8,128)(2,1)S(1)} %dynamic-slice_bitcast_fusion.6), channel_id=1, source_target_pairs={{0,2},{1,3},{2,4},{3,5},{4,6},{5,7},{6,0},{7,1},{8,10},{9,11},{10,... | collective-permute-start | bytes 1966088 | tf_op jit(solution)/shard_map/ppermute | solution.py:49
  505.0 68.7 %collective-permute-start.24 = (bf16[384,2048]{1,0:T(8,128)(2,1)}, bf16[384,2048]{1,0:T(8,128)(2,1)}, u32[]{:S(2)}, u32[]{:S(2)}) collective-permute-start(bf16[384,2048]{1,0:T(8,128)(2,1)} %get-tuple-element.166), channel_id=1, source_target_pairs={{0,8},{8,0},{16,24},{24,16},{1,9},{9,1},{17,25},{25,17},{2,10},{10... | collective-permute-start | bytes 4718600 | tf_op jit(solution)/shard_map/ppermute | solution.py:44
  505.1 68.6 %collective-permute-start.26 = (bf16[384,2048]{1,0:T(8,128)(2,1)S(1)}, bf16[384,2048]{1,0:T(8,128)(2,1)}, u32[]{:S(2)}, u32[]{:S(2)}) collective-permute-start(bf16[384,2048]{1,0:T(8,128)(2,1)S(1)} %fusion), channel_id=1, source_target_pairs={{0,16},{8,24},{16,0},{24,8},{1,17},{9,25},{17,1},{25,9},{2,18},{10... | collective-permute-start | bytes 4718600 | tf_op jit(solution)/shard_map/ppermute | solution.py:44
  517.9 41.5 %copy-start.14 = (bf16[6,1024,128]{2,1,0:T(8,128)(2,1)S(1)}, bf16[6,1024,128]{2,1,0:T(8,128)(2,1)}, u32[]{:S(2)}) copy-start(bf16[6,1024,128]{2,1,0:T(8,128)(2,1)} %get-tuple-element.92.query_ref) | copy-start | bytes 4718596
  517.9 60.6 %collective-permute-start.22 = (bf16[160,2048]{1,0:T(8,128)(2,1)}, bf16[160,2048]{1,0:T(8,128)(2,1)S(1)}, u32[]{:S(2)}, u32[]{:S(2)}) collective-permute-start(bf16[160,2048]{1,0:T(8,128)(2,1)} %fusion.12), channel_id=1, source_target_pairs={{0,2},{1,3},{2,4},{3,5},{4,6},{5,7},{6,0},{7,1},{8,10},{9,11},{10,... | collective-permute-start | bytes 1966088 | tf_op jit(solution)/shard_map/ppermute | solution.py:49
  557.0 40.4 %collective-permute-start.23 = (bf16[4,128,1280]{2,1,0:T(8,128)(2,1)}, bf16[4,128,1280]{2,1,0:T(8,128)(2,1)S(1)}, u32[]{:S(2)}, u32[]{:S(2)}) collective-permute-start(bf16[4,128,1280]{2,1,0:T(8,128)(2,1)} %fusion.4), channel_id=1, source_target_pairs={{0,2},{1,3},{2,4},{3,5},{4,6},{5,7},{6,0},{7,1},{8,10},{9,11},{10,... | collective-permute-start | bytes 3932168 | tf_op jit(solution)/shard_map/ppermute | solution.py:49
  (28 other events, 177.1 us)

commit v6 on v5

--- a/solution.py
+++ b/solution.py
@@ -57,27 +57,6 @@
     return lax.dynamic_index_in_dim(full, index, axis, keepdims=False)
 
 
-def gather_head(part):
-    me = lax.axis_index("head")
-    far = swap(part, "head", 2)
-    near = swap(part, "head", 1)
-    diagonal = swap(far, "head", 1)
-    full = jnp.zeros((4,) + part.shape, part.dtype)
-    full = put(full, part, me)
-    full = put(full, near, me ^ 1)
-    full = put(full, far, me ^ 2)
-    return put(full, diagonal, me ^ 3)
-
-
-def scatter_head(terms):
-    me = lax.axis_index("head")
-    got_far = swap(take(terms, me ^ 3), "head", 1)
-    far = (take(terms, me ^ 2).astype(F32) + got_far.astype(F32)).astype(terms.dtype)
-    got_near = swap(take(terms, me ^ 1), "head", 1)
-    arrived = swap(far, "head", 2)
-    return take(terms, me).astype(F32) + got_near.astype(F32) + arrived.astype(F32)
-
-
 def place_of():
     at = lax.axis_index("blk")
     return at // 2, at % 2, lax.axis_size("blk") // 2
@@ -125,33 +104,6 @@
         full = store(full, held, source, side)
         full = store(full, other, source, 1 - side)
     return full
-
-
-def scatter_pair(terms):
-    me = lax.axis_index("head")
-    side = lax.axis_index("blk") % 2
-    half = terms.shape[2] // 2
-
-    def pick(to_side, to_head):
-        rest = [0] * (terms.ndim - 2)
-        return lax.dynamic_slice(
-            terms, [to_side, to_head] + rest, (1, 1) + terms.shape[2:]
-        ).reshape(terms.shape[2:])
-
-    def both(to_side, to_head):
-        got = swap(pick(to_side, to_head ^ 1), "head", 1)
-        return pick(to_side, to_head).astype(F32) + got.astype(F32)
-
-    corner = both(1 - side, me ^ 2).astype(BF)
-    top = swap(corner[:half], "blk", 1)
-    bottom = swap(corner[half:], "head", 2)
-    far = both(side, me ^ 2)
-    across = both(1 - side, me)
-    far = jnp.concatenate([far[:half] + top.astype(F32), far[half:]], axis=0)
-    across = jnp.concatenate([across[:half], across[half:] + bottom.astype(F32)], axis=0)
-    got_far = swap(far.astype(BF), "head", 2)
-    got_across = swap(across.astype(BF), "blk", 1)
-    return both(side, me) + got_far.astype(F32) + got_across.astype(F32)
 
 
 def sync(*trees):
@@ -444,22 +396,27 @@
 HEADS_OUT, SLAB, NEAR, FAR, ACROSS, FAR_ON, ACROSS_ON = 0, 3, 7, 8, 9, 10, 11
 CORNER_TOP, CORNER_LOW, CORNER_ON, TO_MATE = 12, 13, 14, 15
 BACK_TOP, BACK_LOW, BACK_FAR, BACK_ACROSS, HEADS_BACK, SUM_ON = 19, 20, 21, 22, 23, 26
-TRANSFERS = 30
+WEIGHT_ON, TOP_ON, OUT_MATE, TRANSFERS = 30, 32, 37, 41
 SPANS = ((0, 256), (256, 256), (512, 128))
 
 
 def middle_kernel(
     slabs,
+    downs,
     line,
     attn_ref,
     tokens_ref,
-    w_out_ref,
+    w_own_ref,
+    w_far_ref,
     gain_ref,
-    w_down_ref,
     top_ref,
+    top_far_ref,
+    top_across_ref,
+    top_high_ref,
+    top_low_ref,
     *refs,
 ):
-    slab_refs = refs[:slabs]
+    slab_refs, down_refs = refs[:slabs], refs[slabs : slabs + downs]
     (
         resid_out,
         grad_out,
@@ -467,6 +424,8 @@
         mixed_out,
         heads_out,
         part_out,
+        part_in,
+        w_out_ref,
         gu_out,
         gu_next,
         down_out,
@@ -491,7 +450,7 @@
         sends,
         recvs,
         locals_,
-    ) = refs[slabs:]
+    ) = refs[slabs + downs :]
     me, at = lax.axis_index("head"), lax.axis_index("blk")
     count = lax.axis_size("blk")
     side, place = at % 2, at // 2
@@ -535,8 +494,19 @@
         copy.start()
     own_heads = local(0, attn_ref.at[me], mixed_cols(me))
     own_heads.start()
+
+    def w_rows_of(head):
+        return pairs.at[pl.ds(pl.multiple_of(head * cols, 128), cols)]
+
+    weight_on = [
+        remote(WEIGHT_ON, w_own_ref, w_rows_of(me), (mate, at)),
+        remote(WEIGHT_ON + 1, w_far_ref, w_rows_of(beside), (mate, at)),
+    ]
+    for copy in weight_on:
+        copy.start()
     load_out = [
-        local(1 + i, w_out_ref.at[pl.ds(i * rows, rows)], pairs.at[i]) for i in range(6)
+        local(1, w_own_ref, w_rows_of(me)),
+        local(2, w_far_ref, w_rows_of(beside)),
     ]
     for copy in load_out:
         copy.start()
@@ -558,28 +528,53 @@
     ]
     for copy in load_slabs:
         copy.start()
-    base_sem = 7 + 4 * slabs
-    load_down = local(base_sem, w_down_ref, w_dn)
-    load_down.start()
-    load_top = local(base_sem + 1, top_ref, tops)
-    load_top.start()
-
-    for copy in heads:
+    base_sem = 14 + 4 * slabs + downs
+    part_rows = units // downs
+    load_down = []
+    for i, ref in enumerate(down_refs):
+        start = pl.multiple_of((place + line - i) % line * part_rows, 16) if i or downs > 1 else 0
+        load_down.append(
+            local(14 + 4 * slabs + i, ref, w_dn.at[pl.ds(start, part_rows)])
+        )
+    slot = side * 4 + me
+    far_slot, across_slot = side * 4 + beside, (1 - side) * 4 + me
+    corner_slot = (1 - side) * 4 + beside
+    top_parts = (
+        (top_ref, tops.at[slot]),
+        (top_far_ref, tops.at[far_slot]),
+        (top_across_ref, tops.at[across_slot]),
+        (top_high_ref, tops.at[corner_slot, pl.ds(0, half)]),
+        (top_low_ref, tops.at[corner_slot, pl.ds(half, half)]),
+    )
+    load_top = [
+        local(7 + 4 * slabs + i, source, target) for i, (source, target) in enumerate(top_parts)
+    ]
+    for copy in load_down + load_top:
+        copy.start()
+
+    for copy in heads + weight_on:
         copy.wait_recv()
     own_heads.wait()
     for copy in load_out:
         copy.wait()
+    top_on = [
+        remote(TOP_ON + i, source, target, (mate, at))
+        for i, (source, target) in enumerate(top_parts)
+    ]
+    for copy in top_on:
+        copy.start()
+    keep_weight = local(base_sem, pairs.at[pl.ds(0, 4 * cols)], w_out_ref)
+    keep_weight.start()
     keep_mixed = local(base_sem + 2, mixed, mixed_out)
     keep_mixed.start()
 
     def resid_cols(step, carry):
         span = pl.ds(pl.multiple_of(step * 256, 256), 256)
-        weight = pairs[0:6, :, span].reshape(6 * rows, 256)
+        weight = pairs[0 : 4 * cols, span]
         resid[:, span] = tokens_ref[:, span].astype(F32) + nn(mixed[...], weight)
         return carry
 
     lax.fori_loop(0, width // 256, resid_cols, 0)
-    slot = side * 4 + me
 
     def norm_tile(step, carry):
         tile = pl.ds(pl.multiple_of(step * 32, 32), 32)
@@ -592,8 +587,6 @@
     keep_resid = local(base_sem + 3, resid, resid_out)
     keep_resid.start()
 
-    far_slot, across_slot = side * 4 + beside, (1 - side) * 4 + me
-    corner_slot = (1 - side) * 4 + beside
     near = remote(NEAR, acts.at[slot], acts.at[slot], (mate, at))
     far = remote(FAR, acts.at[slot], acts.at[slot], (beside, at))
     across = remote(ACROSS, acts.at[slot], acts.at[slot], (me, other))
@@ -611,8 +604,24 @@
         copy.wait()
     for copy in slab_on:
         copy.wait_recv()
-    load_down.wait()
-    load_top.wait()
+    for copy in load_down + load_top + [keep_weight]:
+        copy.wait()
+    for copy in top_on:
+        copy.wait_recv()
+
+    def pair_rows(index, first=0, size=rows):
+        return pl.ds(pl.multiple_of(index * rows + first, 16), size)
+
+    def to_mate(c):
+        return remote(
+            TO_MATE + c, pairs.at[pair_rows(2 * c + 1 - odd)], got.at[c], (mate, at)
+        )
+
+    def keep_part(c):
+        return local(base_sem + 4, stage.at[odd], part_out.at[c])
+
+    def part_on(c):
+        return remote(OUT_MATE + c, stage.at[1 - odd], part_in.at[c], (mate, at))
 
     def chunk(c, carry):
         its_side = (side + c // 2) % 2
@@ -668,15 +677,16 @@
             span = pl.ds(pl.multiple_of(step * 256, 256), 256)
             block = grad_gu[pl.ds(pair, 2)].reshape(2 * rows, 2 * units)
             part = nt(block, w_gu[span, :])
-            pairs[pl.ds(2 * c, 2), :, span] = part.astype(BF).reshape(2, rows, 256)
+            pairs[pl.ds(pl.multiple_of(2 * c * rows, 128), 2 * rows), span] = part.astype(BF)
             return carry
 
         lax.fori_loop(0, width // 256, grad_cols, 0)
-        remote(TO_MATE + c, pairs.at[2 * c + 1 - odd], got.at[c], (mate, at)).start()
+        to_mate(c).start()
 
         @pl.when(c > 0)
         def _():
-            local(base_sem + 4, stage, part_out.at[pl.ds(0, 2)]).wait()
+            keep_part(c - 1).wait()
+            part_on(c - 1).wait_send()
 
         def out_cols(step, carry):
             span = pl.ds(pl.multiple_of(step * 256, 256), 256)
@@ -686,33 +696,32 @@
             return carry
 
         lax.fori_loop(0, width // 256, out_cols, 0)
-        local(base_sem + 4, stage, part_out.at[pl.ds(pair, 2)]).start()
+        keep_part(c).start()
+        part_on(c).start()
         return carry
 
     lax.fori_loop(0, 4, chunk, 0)
-
-    def to_mate(c):
-        return remote(TO_MATE + c, pairs.at[2 * c + 1 - odd], got.at[c], (mate, at))
 
     def add_rows(c, first, extra):
         def tile(step, carry):
             span = pl.ds(pl.multiple_of(first + step * 32, 32), 32)
-            total = pairs[2 * c + odd, span, :].astype(F32) + got[c, span, :].astype(F32)
+            mine = pair_rows(2 * c + odd, first + step * 32, 32)
+            total = pairs[mine, :].astype(F32) + got[c, span, :].astype(F32)
             for ref in extra:
                 total = total + ref[pl.ds(pl.multiple_of(step * 32, 32), 32), :].astype(F32)
-            pairs[2 * c + odd, span, :] = total.astype(BF)
+            pairs[mine, :] = total.astype(BF)
             return carry
 
         lax.fori_loop(0, half // 32, tile, 0)
 
     back_top = remote(
-        BACK_TOP, pairs.at[6 + odd, pl.ds(0, half)], in_top, (me, other)
+        BACK_TOP, pairs.at[pair_rows(6 + odd, 0, half)], in_top, (me, other)
     )
     back_low = remote(
-        BACK_LOW, pairs.at[6 + odd, pl.ds(half, half)], in_low, (beside, at)
+        BACK_LOW, pairs.at[pair_rows(6 + odd, half, half)], in_low, (beside, at)
     )
-    back_far = remote(BACK_FAR, pairs.at[2 + odd], in_far, (beside, at))
-    back_across = remote(BACK_ACROSS, pairs.at[4 + odd], in_across, (me, other))
+    back_far = remote(BACK_FAR, pairs.at[pair_rows(2 + odd)], in_far, (beside, at))
+    back_across = remote(BACK_ACROSS, pairs.at[pair_rows(4 + odd)], in_across, (me, other))
     to_mate(3).wait_recv()
     add_rows(3, 0, ())
     back_top.start()
@@ -723,7 +732,8 @@
     add_rows(1, half, ())
     add_rows(2, 0, ())
 
-    local(base_sem + 4, stage, part_out.at[pl.ds(0, 2)]).wait()
+    keep_part(3).wait()
+    part_on(3).wait_send()
 
     def gu_rows(step, carry):
         span = pl.ds(pl.multiple_of(step * 256, 256), 256)
@@ -806,7 +816,7 @@
     def norm_back(step, carry):
         tile = pl.ds(pl.multiple_of(step * 32, 32), 32)
         grad = (
-            pairs[odd, tile, :].astype(F32)
+            pairs[pair_rows(odd, step * 32, 32), :].astype(F32)
             + got[0, tile, :].astype(F32)
             + in_far[tile, :].astype(F32)
             + in_across[tile, :].astype(F32)
@@ -858,39 +868,44 @@
         copy.wait()
     for copy in heads + slab_on:
         copy.wait_send()
+    for copy in weight_on + top_on:
+        copy.wait_send()
     for c in range(4):
         to_mate(c).wait_send()
+        part_on(c).wait_recv()
     for copy in (back_top, back_low, back_far, back_across):
         copy.wait_send()
 
 
-def middle(attn_out, tokens, w_o, gain, slabs, w_d, top):
+def middle(attn_out, tokens, w_own, w_far, gain, tops, slabs, downs):
     rows, width = tokens.shape
-    units = w_d.shape[0]
+    units = sum(block.shape[0] for block in downs)
     cols = attn_out.shape[2]
     line = lax.axis_size("blk") // 2
     slab_shape = slabs[0].shape
     anywhere = pl.BlockSpec(memory_space=pl.ANY)
     vmem = pl.BlockSpec(memory_space=pltpu.VMEM)
     shape = jax.ShapeDtypeStruct
-    eight = (8, rows, width)
+    eight, four = (8, rows, width), (4, rows, width)
     return pl.pallas_call(
-        functools.partial(middle_kernel, len(slabs), line),
+        functools.partial(middle_kernel, len(slabs), len(downs), line),
         out_shape=(
             shape((rows, width), F32),
             shape((rows, width), F32),
             shape((rows, width), BF),
             shape((rows, 4 * cols), BF),
             shape(attn_out.shape, BF),
-            shape(eight, BF),
+            shape(four, BF),
+            shape(four, BF),
+            shape((4 * cols, width), BF),
             shape((width, 2 * units), BF),
             shape(slab_shape, BF),
             shape((units, width), BF),
             shape((1, width), F32),
         ),
-        in_specs=[anywhere, vmem, anywhere, vmem, anywhere, anywhere]
-        + [anywhere] * len(slabs),
-        out_specs=(anywhere,) * 9 + (vmem,),
+        in_specs=[anywhere, vmem, anywhere, anywhere, vmem]
+        + [anywhere] * (len(tops) + len(slabs) + len(downs)),
+        out_specs=(anywhere,) * 11 + (vmem,),
         scratch_shapes=[
             pltpu.VMEM((rows, 4 * cols), BF),
             pltpu.VMEM(eight, BF),
@@ -899,8 +914,8 @@
             pltpu.VMEM((units, width), BF),
             pltpu.VMEM((8, rows, units), BF),
             pltpu.VMEM((8, rows, 2 * units), BF),
-            pltpu.VMEM(eight, BF),
-            pltpu.VMEM((4, rows, width), BF),
+            pltpu.VMEM((8 * rows, width), BF),
+            pltpu.VMEM(four, BF),
             pltpu.VMEM((2, rows, width), BF),
             pltpu.VMEM((rows, width), BF),
             pltpu.VMEM((rows, width), BF),
@@ -911,7 +926,7 @@
             pltpu.VMEM((2, 256, 2 * units), BF),
             pltpu.SemaphoreType.DMA((TRANSFERS,)),
             pltpu.SemaphoreType.DMA((TRANSFERS,)),
-            pltpu.SemaphoreType.DMA((16 + 4 * len(slabs),)),
+            pltpu.SemaphoreType.DMA((24 + 4 * len(slabs) + len(downs),)),
         ],
         compiler_params=pltpu.CompilerParams(
             collective_id=1, has_side_effects=True, vmem_limit_bytes=60 << 20
@@ -920,12 +935,11 @@
             flops=60_000_000_000, bytes_accessed=100_000_000, transcendentals=2_000_000
         ),
         name="middle",
-    )(attn_out, tokens, w_o, gain, w_d, top, *slabs)
+    )(attn_out, tokens, w_own, w_far, gain, *tops, *slabs, *downs)
 
 
 TOK_NEAR, TOK_FAR, TOK_ON, IN_QUERY, IN_REST = 0, 1, 2, 3, 6
-TOP_NEAR, TOP_FAR, TOP_ACROSS, TOP_FAR_ON, TOP_ACROSS_ON = 9, 10, 11, 12, 13
-TOP_CORNER_HIGH, TOP_CORNER_LOW, TOP_CORNER_ON = 14, 15, 16
+TOP_FAR, TOP_ACROSS = 9, 10
 UNITS_MOVE, SLAB_ON, DOWN_MOVE, DOWN_ONE, DOWN_TWO = 17, 31, 32, 33, 34
 KV_ONE, KV_TWO, KV_PAIR_ONE, KV_PAIR_TWO, FIRST_TRANSFERS = 35, 36, 37, 38, 39
 COLS_Q = QHEADS // 4 * HEAD
@@ -955,6 +969,7 @@
     gate_ref,
     up_ref,
     down_ref,
+    w_out_ref,
     top_ref,
     cos_ref,
     sin_ref,
@@ -966,7 +981,9 @@
     raw_out,
     normed_out,
     w_in_out,
-    tops_out,
+    top_far_out,
+    top_across_out,
+    w_out_all,
     slab_out,
     slab_next,
     down_out,
@@ -987,6 +1004,10 @@
     ring_recvs,
     swap_sends,
     swap_recvs,
+    out_ring_sends,
+    out_ring_recvs,
+    out_swap_sends,
+    out_swap_recvs,
     locals_,
 ):
     me, at = lax.axis_index("head"), lax.axis_index("blk")
@@ -1047,7 +1068,7 @@
         local(0, cols_of(query_ref, me * COLS_Q, COLS_Q), own_q),
         local(1, rest_ref.at[me], own_rest),
         local(2, tokens_ref, toks.at[me]),
-        local(3, top_ref, tops_out.at[side * 4 + me]),
+        local(3, w_out_ref, w_out_all.at[at]),
     ]
     for copy in own:
         copy.start()
@@ -1106,6 +1127,22 @@
         block = w_in.at[:, (at + count - 2 * step) % count]
         return remote(step, block, block, (me, other), swap_sends, swap_recvs)
 
+    def out_ring(step):
+        index = (at + count - 2 * (step - 1)) % count
+        source = w_out_ref if step == 1 else w_out_all.at[index]
+        return remote(
+            step, source, w_out_all.at[index], (me, after), out_ring_sends, out_ring_recvs
+        )
+
+    def out_swap(step):
+        index = (at + count - 2 * step) % count
+        source = w_out_ref if step == 0 else w_out_all.at[index]
+        return remote(
+            step, source, w_out_all.at[index], (me, other), out_swap_sends, out_swap_recvs
+        )
+
+    out_ring(1).start()
+    out_swap(0).start()
     for copy in split:
         copy.wait_recv()
     own[0].wait()
@@ -1114,32 +1151,17 @@
     swap_copy(0).start()
     tok_far.wait_recv()
     tok_on.start()
-    top_slot = side * 4 + me
-    far_slot, across_slot = side * 4 + beside, (1 - side) * 4 + me
-    corner_slot = (1 - side) * 4 + beside
-    top_near = remote(TOP_NEAR, top_ref, tops_out.at[top_slot], (mate, at))
-    top_far = remote(TOP_FAR, top_ref, tops_out.at[top_slot], (beside, at))
-    top_across = remote(TOP_ACROSS, top_ref, tops_out.at[top_slot], (me, other))
-    top_far_on = remote(
-        TOP_FAR_ON, tops_out.at[far_slot], tops_out.at[far_slot], (mate, at)
-    )
-    top_across_on = remote(
-        TOP_ACROSS_ON, tops_out.at[across_slot], tops_out.at[across_slot], (mate, at)
-    )
-    top_corner_on = remote(
-        TOP_CORNER_ON, tops_out.at[corner_slot], tops_out.at[corner_slot], (mate, at)
-    )
-    high = tops_out.at[far_slot, pl.ds(0, half)]
-    low = tops_out.at[across_slot, pl.ds(half, half)]
-    top_corner_high = remote(TOP_CORNER_HIGH, high, high, (me, other))
-    top_corner_low = remote(TOP_CORNER_LOW, low, low, (beside, at))
-    top_near.start()
+    top_far = remote(TOP_FAR, top_ref, top_far_out, (beside, at))
+    top_across = remote(TOP_ACROSS, top_ref, top_across_out, (me, other))
     top_far.start()
     for step in range(1, line):
         ring_copy(step).wait_recv()
         if step < line - 1:
             ring_copy(step + 1).start()
         swap_copy(step).start()
+        out_ring(step).wait_recv()
+        if step < line - 1:
+            out_ring(step + 1).start()
 
     @pl.when(jnp.logical_not(stays))
     def _():
@@ -1163,6 +1185,8 @@
     own[3].wait()
     for step in range(line):
         swap_copy(step).wait_recv()
+    for step in range(1, line):
+        out_swap(step).start()
     top_across.start()
     keep_in = [
         local(7 + h, w_in.at[h], w_in_out.at[h]) for h in range(4)
@@ -1252,9 +1276,6 @@
     ]
     for copy in keep:
         copy.start()
-    top_far.wait_recv()
-    top_far_on.start()
-    top_corner_high.start()
     kv_one.wait_recv()
     kv_two.start()
 
@@ -1267,9 +1288,6 @@
         pair_one_odd.start()
 
     down_on.wait_recv()
-    top_across.wait_recv()
-    top_across_on.start()
-    top_corner_low.start()
     kv_two.wait_recv()
 
     @pl.when(side == 1)
@@ -1278,23 +1296,17 @@
 
     down_last = remote(DOWN_TWO, down_one, down_two, (me, after))
     down_last.start()
-    top_corner_high.wait_recv()
-    top_corner_low.wait_recv()
-    top_corner_on.start()
-
     pair_one_even.wait_recv()
     pair_two_even.wait_recv()
     down_last.wait_recv()
     slab_on.wait_recv()
-    for copy in (top_near, top_far_on, top_across_on, top_corner_on):
+    for copy in (top_far, top_across):
         copy.wait_recv()
     for copy in keep + keep_in + [keep_normed, keep_raw, keep_toks]:
         copy.wait()
     for copy in split + spread:
         copy.wait_send()
-    for copy in (tok_near, tok_far, tok_on, top_near, top_far, top_across, top_far_on):
-        copy.wait_send()
-    for copy in (top_across_on, top_corner_high, top_corner_low, top_corner_on):
+    for copy in (tok_near, tok_far, tok_on, top_far, top_across):
         copy.wait_send()
     for copy in (slab_on, down_on, down_last, kv_one, kv_two):
         copy.wait_send()
@@ -1307,12 +1319,14 @@
 
     for step in range(line):
         swap_copy(step).wait_send()
+        out_swap(step).wait()
         if step:
             ring_copy(step).wait_send()
+            out_ring(step).wait_send()
 
 
 def first(
-    tokens, w_query, rest, w_gate, w_up, w_down, cotangent, cosine, sine, query_gain, key_gain
+    tokens, w_query, rest, w_gate, w_up, w_down, w_out, cotangent, cosine, sine, query_gain, key_gain
 ):
     rows, width = tokens.shape
     count = lax.axis_size("blk")
@@ -1334,7 +1348,9 @@
             shape((block, COLS_Q + 128), F32),
             shape((block, width), BF),
             shape((4, count, w_rows, 2 * COLS_Q), BF),
-            shape((8, rows, width), BF),
+            shape((rows, width), BF),
+            shape((rows, width), BF),
+            shape((count,) + w_out.shape, BF),
             slab,
             slab,
             shape(w_down.shape, BF),
@@ -1343,8 +1359,8 @@
             shape((4, rows, width), BF),
             shape((8, width), F32),
         ),
-        in_specs=[anywhere] * 7 + [vmem] * 4,
-        out_specs=(anywhere,) * 13 + (vmem,),
+        in_specs=[anywhere] * 8 + [vmem] * 4,
+        out_specs=(anywhere,) * 15 + (vmem,),
         scratch_shapes=[
             pltpu.VMEM((4, rows, width), BF),
             pltpu.VMEM((block, width), BF),
@@ -1359,6 +1375,10 @@
             dma((count // 2,)),
             dma((count // 2,)),
             dma((count // 2,)),
+            dma((count // 2,)),
+            dma((count // 2,)),
+            dma((count // 2,)),
+            dma((count // 2,)),
             dma((17,)),
         ],
         compiler_params=pltpu.CompilerParams(
@@ -1369,7 +1389,8 @@
         ),
         name="first",
     )(
-        tokens, w_query, rest, w_gate, w_up, w_down, cotangent, cosine, sine, query_gain, key_gain
+        tokens, w_query, rest, w_gate, w_up, w_down, w_out, cotangent, cosine, sine,
+        query_gain, key_gain,
     )
 
 
@@ -1640,6 +1661,7 @@
         return carry
 
     lax.fori_loop(0, width // 256, query_weights, 0)
+    query_line.start()
     for copy in low_loads:
         copy.wait()
 
@@ -1661,10 +1683,6 @@
     two_on = [remote(TWO_ON + g, low.at[g, 1], two_in.at[g], (me, before)) for g in (0, 1)]
     for copy in four_on:
         copy.start()
-    query_line.start()
-    for copy in homes:
-        copy.start()
-    units_own.start()
     loads[4].wait()
     slab_line.start()
 
@@ -1679,7 +1697,6 @@
         return carry
 
     lax.fori_loop(0, block // 32, token_scales, 0)
-    query_line.step(1)
     for copy in four_on:
         copy.wait_recv()
 
@@ -1716,17 +1733,12 @@
     def _():
         down_stay.start()
 
+    for copy in homes:
+        copy.start()
+    units_own.start()
+    query_line.step(1)
     slab_line.step(1)
-    for step in range(2, line + 1):
-        query_line.step(step, query_sum)
-    query_home = [
-        remote(QUERY_HOME + i, query_sum.at[to], query_out.at[me], (to, at))
-        for i, to in enumerate((mate, beside, corner))
-    ]
-    query_own = local(12, query_sum.at[me], query_out.at[me])
-    for copy in query_home:
-        copy.start()
-    query_own.start()
+    query_line.step(2)
     for copy in two_on:
         copy.wait_recv()
 
@@ -1781,6 +1793,17 @@
 
     lax.fori_loop(0, width // 256, rest_weights, 0)
     rest_line.start()
+
+    for step in range(3, line + 1):
+        query_line.step(step, query_sum)
+    query_home = [
+        remote(QUERY_HOME + i, query_sum.at[to], query_out.at[me], (to, at))
+        for i, to in enumerate((mate, beside, corner))
+    ]
+    query_own = local(12, query_sum.at[me], query_out.at[me])
+    for copy in query_home:
+        copy.start()
+    query_own.start()
     to_mate[0].wait_recv()
 
     def add_part(step, carry):
@@ -2014,7 +2037,9 @@
         raw,
         normed_one,
         w_in,
-        top,
+        top_far,
+        top_across,
+        w_blk,
         slab,
         slab_next,
         down_own,
@@ -2029,6 +2054,7 @@
         w_gate,
         w_up,
         w_down,
+        w_out,
         cotangent,
         cosine,
         sine,
@@ -2039,17 +2065,25 @@
     for _ in range(line - 4):
         slabs.append(ring(slabs[-1], 2))
         downs.append(ring(downs[-1], 2))
-    slabs, downs, w_out, queries = sync(slabs, downs, w_out, queries)
+    w_own = w_blk.reshape(q_cols, width)
+    slabs, downs, w_own, top_far, top_across, queries = sync(
+        slabs, downs, w_own, top_far, top_across, queries
+    )
     slabs.append(ring(slabs[-1], 2))
     downs.append(ring(downs[-1], 2))
-    w_o = gather_blk(w_out, 0).reshape(blocks * w_out.shape[0], width)
-    w_o = gather_head(w_o).reshape(QHEADS * HEAD, width)
+    w_far = swap(w_own, "head", 2)
+    half = tok_rows // 2
+    top_high = swap(top_far[:half], "blk", 1)
+    top_low = swap(top_across[half:], "head", 2)
     kept, attn_out = attend(meta, wide, kv_window, window_start[:, None])
-    kept, attn_out, slabs, downs, w_o = sync(kept, attn_out, slabs, downs, w_o)
-    place = blk_place // 2
-    w_d = jnp.zeros((line, ff_rows, width), BF)
-    for step, block in enumerate(downs):
-        w_d = put(w_d, block, (place - step) % line)
+    kept, attn_out, slabs, downs, w_far, top_high, top_low = sync(
+        kept, attn_out, slabs, downs, w_far, top_high, top_low
+    )
+    if ff_rows % 16:
+        w_d = jnp.zeros((line, ff_rows, width), BF)
+        for step, part in enumerate(downs):
+            w_d = put(w_d, part, (blk_place // 2 - step) % line)
+        downs = [w_d.reshape(ff_cols, width)]
     attn_out = attn_out.reshape(groups, tok_rows, q_cols)
 
     (
@@ -2058,7 +2092,9 @@
         grad_attn,
         mixed,
         grad_mix,
-        out_part,
+        out_mine,
+        out_got,
+        w_o,
         gu_parts,
         gu_moved,
         down_parts,
@@ -2066,11 +2102,12 @@
     ) = middle(
         attn_out,
         tokens,
-        w_o,
+        w_own,
+        w_far,
         gains[1:2],
+        (cotangent, top_far, top_across, top_high, top_low),
         slabs,
-        w_d.reshape(ff_cols, width),
-        top,
+        downs,
     )
     down_parts = down_parts.reshape(line, ff_rows, width)
     gu_parts = gu_parts.reshape(groups, line, 2 * w_rows, 2 * ff_cols)
@@ -2078,12 +2115,18 @@
     gu_sum = LineScatter(lambda p: take(gu_parts, p, 1))
     gu_sum.total = gu_moved
     gu_sum.add()
-    out_part = out_part.reshape(2, groups, tok_rows, width)
     out_parts = matmul_tn(mixed, grad_attn).astype(BF).reshape(groups, -1, width)
     down_sum.ahead(line - 4)
     gu_sum.ahead(line - 4)
     down_moved, gu_moved = down_sum.send(), gu_sum.send()
-    out_act = (resid + scatter_pair(out_part)).astype(BF)
+
+    def out_sum(i):
+        return out_mine[i].astype(F32) + out_got[i].astype(F32)
+
+    corner = out_sum(3).astype(BF)
+    out_top = swap(corner[:half], "blk", 1)
+    out_low = swap(corner[half:], "head", 2)
+    near_parts = [swap(take(out_parts, group_id ^ bit), "head", 1) for bit in (1, 3)]
     back = functools.partial(
         attend_back,
         meta=meta,
@@ -2095,18 +2138,29 @@
         starts=window_start[None, :],
     )
     four = back(0)
-    four, down_moved, gu_moved, out_act, kv_window = sync(
-        four, down_moved, gu_moved, out_act, kv_window
+    four, down_moved, gu_moved, out_top, out_low, near_parts, kv_window = sync(
+        four, down_moved, gu_moved, out_top, out_low, near_parts, kv_window
     )
     down_sum.total, gu_sum.total = down_moved, gu_moved
     down_sum.add()
     gu_sum.add()
     down_moved, gu_moved = down_sum.send(), gu_sum.send()
-    out_slab = scatter_head(out_parts).astype(BF).reshape(blocks, w_out.shape[0], width)
+    none = jnp.zeros((half, width), F32)
+    out_far = out_sum(1) + jnp.concatenate([out_top.astype(F32), none], axis=0)
+    out_across = out_sum(2) + jnp.concatenate([none, out_low.astype(F32)], axis=0)
+    out_far = swap(out_far.astype(BF), "head", 2)
+    out_across = swap(out_across.astype(BF), "blk", 1)
+    far_parts = take(out_parts, group_id ^ 2).astype(F32) + near_parts[1].astype(F32)
+    far_parts = swap(far_parts.astype(BF), "head", 2)
     two = back(1, kv=kv_window)
-    four, two, down_moved, gu_moved, out_slab = sync(
-        four, two, down_moved, gu_moved, out_slab
+    four, two, down_moved, gu_moved, out_far, out_across, far_parts = sync(
+        four, two, down_moved, gu_moved, out_far, out_across, far_parts
     )
+    out_act = resid + out_sum(0) + out_far.astype(F32) + out_across.astype(F32)
+    out_act = out_act.astype(BF)
+    out_slab = take(out_parts, group_id).astype(F32) + near_parts[0].astype(F32)
+    out_slab = (out_slab + far_parts.astype(F32)).astype(BF)
+    out_slab = out_slab.reshape(blocks, w_out.shape[0], width)
     down_sum.total, gu_sum.total = down_moved, gu_moved
     down_sum.add()
     gu_sum.add()

time: 800 us -> 710 us (0.89)
  Pallas kernels: 533 us -> 504 us
  local copies, waits for them, and re-layouts: 52.5 us -> 30.6 us
  starting transfers between devices: 75.2 us -> 55.9 us
  waiting for transfers between devices: 81 us -> 63.3 us
    ppermute x18 -> x10, waiting for transfers between devices: 45.2 us -> 22.3 us  [swap(): return lax.ppermute(block, axis, [(i, i ^ bit) for i in range(count)])]
    pallas_call x1, Pallas kernels: 187 us -> 165 us  [middle(): pl.pallas_call(functools.partial(middle_kernel, len(slabs), len(downs), l...]
    ppermute x9 -> x6, starting transfers between devices: 63.2 us -> 45.3 us  [ring(): lax.ppermute(block, 'blk', [(i, (i + step) % count) for i in range(count)])]
    pallas_call x1, Pallas kernels: 162 us -> 144 us  [last(): pl.pallas_call(functools.partial(last_kernel, line), out_shape=(shape((ro...]
    dynamic_update_slice x16 -> x0, local copies, waits for them, and re-layouts: 12.2 us -> none  [the longest x8 6.71 us: put(): return lax.dynamic_update_index_in_dim(full, part, index, axis)]
    pallas_call x1, Pallas kernels: 133 us -> 143 us  [first(): pl.pallas_call(functools.partial(first_kernel, count // 2), out_shape=(sh...]
    ppermute x9 -> x6, waiting for transfers between devices: 35.8 us -> 40.9 us  [ring(): lax.ppermute(block, 'blk', [(i, (i + step) % count) for i in range(count)])]
  transfers between devices with their start and end apart: 27 -> 16, of which waited for: 12 -> 5; matrix products, arithmetic and copies ran while one was open for 6% -> 3% of each run, Pallas kernels for 6% -> 7%
where the time goes in v6:
time: 710 us; the launch traced here: 697 us
  Pallas kernels  504 us (71%)
  waiting for transfers between devices  63.3 us (9%)
  starting transfers between devices  55.9 us (8%)
  other arithmetic  38.6 us (5%)
  local copies, waits for them, and re-layouts  30.6 us (4%)
    pallas_call x1, Pallas kernels, middle(): pl.pallas_call(functools.partial(middle_kernel, len(slabs), len(downs), l...  165 us
    pallas_call x1, Pallas kernels, last(): pl.pallas_call(functools.partial(last_kernel, line), out_shape=(shape((ro...  144 us
    pallas_call x1, Pallas kernels, first(): pl.pallas_call(functools.partial(first_kernel, count // 2), out_shape=(sh...  143 us
    ppermute x6, starting transfers between devices, ring(): lax.ppermute(block, 'blk', [(i, (i + step) % count) for i in range(count)])  45.3 us
    ppermute x6, waiting for transfers between devices, ring(): lax.ppermute(block, 'blk', [(i, (i + step) % count) for i in range(count)])  40.9 us
    pallas_call x2, Pallas kernels, attend_back(): pl.pallas_call(functools.partial(attend_back_kernel, which), out_shape=(s...  35.6 us
    ppermute x10, waiting for transfers between devices, swap(): return lax.ppermute(block, axis, [(i, i ^ bit) for i in range(count)])  22.3 us
    pallas_call x1, Pallas kernels, attend(): pl.pallas_call(attend_kernel, out_shape=(jax.ShapeDtypeStruct((heads, row...  15.7 us
  transfers between devices with their start and end apart: 16, of which 5 were waited for; matrix products, arithmetic and copies ran while one was open for 3% of the time, Pallas kernels for 7%

profile of v6, /device:TPU:0, one launch (start us, length us, event | category | flops | bytes accessed | tf_op | source)
XLA Modules:
  0.0 697.1 jit_solution(1841855770789584893)
XLA Ops:
  5.0 1.9 fusion.13
  8.0 143.3 %first.1 = (bf16[6,1024,128]{2,1,0:T(8,128)(2,1)}, bf16[6,1024,128]{2,1,0:T(8,128)(2,1)}, bf16[5,2,1024,128]{3,2,1,0:T(8,128)(2,1)}, f32[1024,512]{1,0:T(8,128)}...) custom-call(bf16[256,2048]{1,0:T(8,128)(2,1)} %tokens_ref.3, ...), custom_call_target="tpu_custom_call" | custom-call | flops 60000002048 | bytes 60000000 | tf_op jit(solution)/shard_map/first/pallas_call | solution.py:1342
  160.8 15.7 %attend.1 = (f32[6,1024,128]{2,1,0:T(8,128)}, bf16[1024,384]{1,0:T(8,128)(2,1)S(1)}) custom-call(s32[9]{0:T(128)S(1)} %pad_add_fusion.1.meta_ref, bf16[6,1024,128]{2,1,0:T(8,128)(2,1)S(1)} %copy-done.14, bf16[5,2,1024,128]{3,2,1,0:T(8,128)(2,1)S(1)} %copy-done.13, s32[1024,1]{1,0:T(8,128)S(1)} %copy.83.start_ref), custom_call_target="tpu_custom_call" | custom-call | flops 60000002048 | bytes 20000000 | tf_op jit(solution)/shard_map/attend/pallas_call | solution.py:218
  178.0 16.7 %collective-permute-done.4.top_low_ref = bf16[128,2048]{1,0:T(8,128)(2,1)} collective-permute-done((bf16[128,2048]{1,0:T(8,128)(2,1)}, bf16[128,2048]{1,0:T(8,128)(2,1)}, u32[]{:S(2)}, u32[]{:S(2)}) %collective-permute-start.4) | collective-permute-done | bytes 524320 | tf_op jit(solution)/shard_map/ppermute | solution.py:44
  195.1 164.8 %middle.1 = (f32[256,2048]{1,0:T(8,128)}, f32[256,2048]{1,0:T(8,128)}, bf16[256,2048]{1,0:T(8,128)(2,1)}, bf16[256,1536]{1,0:T(8,128)(2,1)}, bf16[4,256,384]{2,1...) custom-call(bf16[4,256,384]{2,1,0:T(8,128)(2,1)} %bitcast.119, ...), custom_call_target="tpu_custom_call" | custom-call | flops 60000002048 | bytes 100000000 | tf_op jit(solution)/shard_map/middle/pallas_call | solution.py:890
  359.9 3.3 convolution_convert_fusion
  363.2 1.9 dynamic-slice_bitcast_fusion
  365.6 2.0 add_convert_fusion
  368.5 1.9 collective-permute-start.7
  370.9 2.7 fusion.5
  373.7 2.1 collective-permute-start.6
  376.9 5.6 collective-permute-done.7
  382.5 2.7 collective-permute-start.5
  385.2 20.9 %attend_back_four.1 = (f32[1024,256]{1,0:T(8,128)S(1)}, bf16[4,1024,128]{2,1,0:T(8,128)(2,1)S(1)}, f32[1024,128]{1,0:T(8,128)S(1)}) custom-call(s32[9]{0:T(128)S(1)} %pad_add_fusion.1.meta_ref, bf16[6,1024,128]{2,1,0:T(8,128)(2,1)S(1)} %copy-done.14, bf16[6,1024,128]{2,1,0:T(8,128)(2,1)} %get-tuple-element.133.query_ref, ...), custom_call_target="tpu_custom_call" | custom-call | flops 80000000000 | bytes 40000000 | tf_op jit(solution)/shard_map/attend_back_four/pallas_call | solution.py:368
  406.2 15.8 %collective-permute-done.5 = bf16[160,2048]{1,0:T(8,128)(2,1)S(1)} collective-permute-done((bf16[160,2048]{1,0:T(8,128)(2,1)S(1)}, bf16[160,2048]{1,0:T(8,128)(2,1)S(1)}, u32[]{:S(2)}, u32[]{:S(2)}) %collective-permute-start.5) | collective-permute-done | bytes 655392 | tf_op jit(solution)/shard_map/ppermute | solution.py:49
  425.3 4.1 fusion.6
  430.9 1.9 collective-permute-start.14
  432.9 3.1 fusion.4
  435.9 39.4 %collective-permute-start.12 = (bf16[4,128,1280]{2,1,0:T(8,128)(2,1)}, bf16[4,128,1280]{2,1,0:T(8,128)(2,1)}, u32[]{:S(2)}, u32[]{:S(2)}) collective-permute-start(bf16[4,128,1280]{2,1,0:T(8,128)(2,1)} %fusion.4), channel_id=1, source_target_pairs={{0,2},{1,3},{2,4},{3,5},{4,6},{5,7},{6,0},{7,1},{8,10},{9,11},{10,... | collective-permute-start | bytes 3932168 | tf_op jit(solution)/shard_map/ppermute | solution.py:49
  475.4 2.1 fusion.12
  477.5 14.7 %attend_back_two.1 = (f32[1024,128]{1,0:T(8,128)S(1)}, bf16[4,1024,128]{2,1,0:T(8,128)(2,1)S(1)}, f32[1024,128]{1,0:T(8,128)S(1)}) custom-call(s32[9]{0:T(128)S(1)} %pad_add_fusion.1.meta_ref, bf16[6,1024,128]{2,1,0:T(8,128)(2,1)S(1)} %copy-done.14, bf16[6,1024,128]{2,1,0:T(8,128)(2,1)S(1)} %copy-done.15, ...), custom_call_target="tpu_custom_call" | custom-call | flops 40000000000 | bytes 40000000 | tf_op jit(solution)/shard_map/attend_back_two/pallas_call | solution.py:368
  492.3 24.7 %collective-permute-done.11 = bf16[160,2048]{1,0:T(8,128)(2,1)S(1)} collective-permute-done((bf16[160,2048]{1,0:T(8,128)(2,1)}, bf16[160,2048]{1,0:T(8,128)(2,1)S(1)}, u32[]{:S(2)}, u32[]{:S(2)}) %collective-permute-start.11) | collective-permute-done | bytes 655392 | tf_op jit(solution)/shard_map/ppermute | solution.py:49
  517.0 2.5 fusion.11.down_ref
  519.5 3.2 fusion.3.units_ref
  522.7 3.4 fusion.1
  526.1 144.5 %last.1 = (f32[256,2048]{1,0:T(8,128)}, bf16[4,64,384]{2,1,0:T(8,128)(2,1)}, bf16[4,64,384]{2,1,0:T(8,128)(2,1)}, bf16[8,64,1280]{2,1,0:T(8,128)(2,1)}, bf16[160...) custom-call(f32[1024,256]{1,0:T(8,128)} %copy-done.19, f32[1024,128]{1,0:T(8,128)} %copy-done.17, ...), custom_call_target="tpu_custom_call" | custom-call | flops 60000002048 | bytes 60000000 | tf_op jit(solution)/shard_map/last/pallas_call | solution.py:1899
  672.6 3.1 reshape.234
  675.7 3.1 fusion.18
  679.8 2.1 squeeze.86
  683.0 2.1 squeeze.87
  687.7 3.4 add.196
  691.0 3.7 fusion.10
  (139 shorter events, 33.1 us)
Async XLA Ops:
  0.6 6.3 copy-start.36
  7.0 144.3 %copy-start.3 = (f32[1,128]{1,0:T(1,128)}, f32[1,128]{1,0:T(1,128)S(1)}, u32[]{:S(2)}) copy-start(f32[1,128]{1,0:T(1,128)S(1)} %get-tuple-element.224.query_gain_ref) | copy-start | bytes 1540
  7.0 144.3 %copy-start.4 = (f32[1,128]{1,0:T(1,128)}, f32[1,128]{1,0:T(1,128)S(1)}, u32[]{:S(2)}) copy-start(f32[1,128]{1,0:T(1,128)S(1)} %get-tuple-element.225.key_gain_ref) | copy-start | bytes 1540
  7.9 143.4 %copy-start = (f32[1024,128]{1,0:T(8,128)}, f32[1024,128]{1,0:T(8,128)S(1)}, u32[]{:S(2)}) copy-start(f32[1024,128]{1,0:T(8,128)S(1)} %get-tuple-element.222.cos_ref) | copy-start | bytes 1572868
  7.9 143.4 %copy-start.1 = (f32[1024,128]{1,0:T(8,128)}, f32[1024,128]{1,0:T(8,128)S(1)}, u32[]{:S(2)}) copy-start(f32[1024,128]{1,0:T(8,128)S(1)} %get-tuple-element.223.sin_ref) | copy-start | bytes 1572868
  151.4 25.1 %copy-start.8 = (bf16[160,2048]{1,0:T(8,128)(2,1)}, bf16[160,2048]{1,0:T(8,128)(2,1)S(1)}, u32[]{:S(2)}) copy-start(bf16[160,2048]{1,0:T(8,128)(2,1)S(1)} %get-tuple-element.128.refs_5_) | copy-start | bytes 1966084
  151.4 26.0 %copy-start.2 = (f32[8,2048]{1,0:T(8,128)}, f32[8,2048]{1,0:T(8,128)S(1)}, u32[]{:S(2)}) copy-start(f32[8,2048]{1,0:T(8,128)S(1)} %get-tuple-element.120.gain_ref) | copy-start | bytes 196612
  151.4 7.6 %copy-start.14 = (bf16[6,1024,128]{2,1,0:T(8,128)(2,1)S(1)}, bf16[6,1024,128]{2,1,0:T(8,128)(2,1)}, u32[]{:S(2)}) copy-start(bf16[6,1024,128]{2,1,0:T(8,128)(2,1)} %get-tuple-element.97.query_ref.wide_ref) | copy-start | bytes 4718596
  151.4 43.7 %collective-permute-start.2 = (bf16[384,2048]{1,0:T(8,128)(2,1)}, bf16[384,2048]{1,0:T(8,128)(2,1)}, u32[]{:S(2)}, u32[]{:S(2)}) collective-permute-start(bf16[384,2048]{1,0:T(8,128)(2,1)} %bitcast.142), channel_id=1, source_target_pairs={{0,16},{8,24},{16,0},{24,8},{1,17},{9,25},{17,1},{25,9},{2,18},{10... | collective-permute-start | bytes 4718600 | tf_op jit(solution)/shard_map/ppermute | solution.py:44
  153.0 42.1 %collective-permute-start = (bf16[4,128,1280]{2,1,0:T(8,128)(2,1)}, bf16[4,128,1280]{2,1,0:T(8,128)(2,1)}, u32[]{:S(2)}, u32[]{:S(2)}) collective-permute-start(bf16[4,128,1280]{2,1,0:T(8,128)(2,1)} %get-tuple-element.124.refs_1_), channel_id=1, source_target_pairs={{0,2},{1,3},{2,4},{3,5},{4,6},{5,7},{6,0},{7,1},{8,10},{9,11},{10,... | collective-permute-start | bytes 3932168 | tf_op jit(solution)/shard_map/ppermute | solution.py:49
  154.1 23.9 %collective-permute-start.3 = (bf16[128,2048]{1,0:T(8,128)(2,1)S(1)}, bf16[128,2048]{1,0:T(8,128)(2,1)}, u32[]{:S(2)}, u32[]{:S(2)}) collective-permute-start(bf16[128,2048]{1,0:T(8,128)(2,1)S(1)} %slice.162), channel_id=1, source_target_pairs={{0,1},{1,0},{2,3},{3,2},{4,5},{5,4},{6,7},{7,6},{8,9},{9,8},{10,11... | collective-permute-start | bytes 1572872 | tf_op jit(solution)/shard_map/ppermute | solution.py:44
  156.2 38.5 %collective-permute-start.4 = (bf16[128,2048]{1,0:T(8,128)(2,1)}, bf16[128,2048]{1,0:T(8,128)(2,1)}, u32[]{:S(2)}, u32[]{:S(2)}) collective-permute-start(bf16[128,2048]{1,0:T(8,128)(2,1)} %slice.163), channel_id=1, source_target_pairs={{0,16},{8,24},{16,0},{24,8},{1,17},{9,25},{17,1},{25,9},{2,18},{10... | collective-permute-start | bytes 1572872 | tf_op jit(solution)/shard_map/ppermute | solution.py:44
  157.3 37.8 %collective-permute-start.1 = (bf16[160,2048]{1,0:T(8,128)(2,1)S(1)}, bf16[160,2048]{1,0:T(8,128)(2,1)}, u32[]{:S(2)}, u32[]{:S(2)}) collective-permute-start(bf16[160,2048]{1,0:T(8,128)(2,1)S(1)} %get-tuple-element.128.refs_5_), channel_id=1, source_target_pairs={{0,2},{1,3},{2,4},{3,5},{4,6},{5,7},{6,0},{7,1},{8,10},{9,11},{10,... | collective-permute-start | bytes 1966088 | tf_op jit(solution)/shard_map/ppermute | solution.py:49
  365.1 56.9 %collective-permute-start.10 = (bf16[384,2048]{1,0:T(8,128)(2,1)}, bf16[384,2048]{1,0:T(8,128)(2,1)S(1)}, u32[]{:S(2)}, u32[]{:S(2)}) collective-permute-start(bf16[384,2048]{1,0:T(8,128)(2,1)} %get-tuple-element.185), channel_id=1, source_target_pairs={{0,8},{8,0},{16,24},{24,16},{1,9},{9,1},{17,25},{25,17},{2,10},{10... | collective-permute-start | bytes 4718600 | tf_op jit(solution)/shard_map/ppermute | solution.py:44
  365.1 56.9 %collective-permute-start.9 = (bf16[384,2048]{1,0:T(8,128)(2,1)}, bf16[384,2048]{1,0:T(8,128)(2,1)S(1)}, u32[]{:S(2)}, u32[]{:S(2)}) collective-permute-start(bf16[384,2048]{1,0:T(8,128)(2,1)} %get-tuple-element.186), channel_id=1, source_target_pairs={{0,8},{8,0},{16,24},{24,16},{1,9},{9,1},{17,25},{25,17},{2,10},{10... | collective-permute-start | bytes 4718600 | tf_op jit(solution)/shard_map/ppermute | solution.py:44
  368.5 14.0 %collective-permute-start.7 = (bf16[128,2048]{1,0:T(8,128)(2,1)S(1)}, bf16[128,2048]{1,0:T(8,128)(2,1)S(1)}, u32[]{:S(2)}, u32[]{:S(2)}) collective-permute-start(bf16[128,2048]{1,0:T(8,128)(2,1)S(1)} %get-tuple-element.190), channel_id=1, source_target_pairs={{0,1},{1,0},{2,3},{3,2},{4,5},{5,4},{6,7},{7,6},{8,9},{9,8},{10,11... | collective-permute-start | bytes 1572872 | tf_op jit(solution)/shard_map/ppermute | solution.py:44
  370.4 35.8 %collective-permute-start.8 = (bf16[128,2048]{1,0:T(8,128)(2,1)}, bf16[128,2048]{1,0:T(8,128)(2,1)}, u32[]{:S(2)}, u32[]{:S(2)}) collective-permute-start(bf16[128,2048]{1,0:T(8,128)(2,1)} %get-tuple-element.189), channel_id=1, source_target_pairs={{0,16},{8,24},{16,0},{24,8},{1,17},{9,25},{17,1},{25,9},{2,18},{10... | collective-permute-start | bytes 1572872 | tf_op jit(solution)/shard_map/ppermute | solution.py:44
  370.9 14.3 %copy-start.12 = (bf16[4,256,384]{2,1,0:T(8,128)(2,1)S(1)}, bf16[4,256,384]{2,1,0:T(8,128)(2,1)}, u32[]{:S(2)}) copy-start(bf16[4,256,384]{2,1,0:T(8,128)(2,1)} %get-tuple-element.135) | copy-start | bytes 2359300
  373.7 48.3 %collective-permute-start.6 = (bf16[4,128,1280]{2,1,0:T(8,128)(2,1)}, bf16[4,128,1280]{2,1,0:T(8,128)(2,1)}, u32[]{:S(2)}, u32[]{:S(2)}) collective-permute-start(bf16[4,128,1280]{2,1,0:T(8,128)(2,1)} %fusion.5), channel_id=1, source_target_pairs={{0,2},{1,3},{2,4},{3,5},{4,6},{5,7},{6,0},{7,1},{8,10},{9,11},{10,... | collective-permute-start | bytes 3932168 | tf_op jit(solution)/shard_map/ppermute | solution.py:49
  382.5 39.5 %collective-permute-start.5 = (bf16[160,2048]{1,0:T(8,128)(2,1)S(1)}, bf16[160,2048]{1,0:T(8,128)(2,1)S(1)}, u32[]{:S(2)}, u32[]{:S(2)}) collective-permute-start(bf16[160,2048]{1,0:T(8,128)(2,1)S(1)} %dynamic-slice_bitcast_fusion.2), channel_id=1, source_target_pairs={{0,2},{1,3},{2,4},{3,5},{4,6},{5,7},{6,0},{7,1},{8,10},{9,11},{10,... | collective-permute-start | bytes 1966088 | tf_op jit(solution)/shard_map/ppermute | solution.py:49
  406.2 17.6 %copy-start.19 = (f32[1024,256]{1,0:T(8,128)}, f32[1024,256]{1,0:T(8,128)S(1)}, u32[]{:S(2)}) copy-start(f32[1024,256]{1,0:T(8,128)S(1)} %get-tuple-element.159.dq_four_ref) | copy-start | bytes 3145732
  406.2 17.6 %copy-start.20 = (bf16[4,1024,128]{2,1,0:T(8,128)(2,1)}, bf16[4,1024,128]{2,1,0:T(8,128)(2,1)S(1)}, u32[]{:S(2)}) copy-start(bf16[4,1024,128]{2,1,0:T(8,128)(2,1)S(1)} %get-tuple-element.161.low_four_ref) | copy-start | bytes 3145732
  406.2 17.6 %copy-start.23 = (f32[1024,128]{1,0:T(8,128)}, f32[1024,128]{1,0:T(8,128)S(1)}, u32[]{:S(2)}) copy-start(f32[1024,128]{1,0:T(8,128)S(1)} %get-tuple-element.163.own_four_ref) | copy-start | bytes 1572868
  423.8 93.2 %collective-permute-start.15 = (bf16[384,2048]{1,0:T(8,128)(2,1)S(1)}, bf16[384,2048]{1,0:T(8,128)(2,1)}, u32[]{:S(2)}, u32[]{:S(2)}) collective-permute-start(bf16[384,2048]{1,0:T(8,128)(2,1)S(1)} %fusion.2), channel_id=1, source_target_pairs={{0,16},{8,24},{16,0},{24,8},{1,17},{9,25},{17,1},{25,9},{2,18},{10... | collective-permute-start | bytes 4718600 | tf_op jit(solution)/shard_map/ppermute | solution.py:44
  429.5 87.5 %collective-permute-start.13 = (bf16[256,2048]{1,0:T(8,128)(2,1)}, bf16[256,2048]{1,0:T(8,128)(2,1)S(1)}, u32[]{:S(2)}, u32[]{:S(2)}) collective-permute-start(bf16[256,2048]{1,0:T(8,128)(2,1)} %get-tuple-element.184), channel_id=1, source_target_pairs={{0,16},{8,24},{16,0},{24,8},{1,17},{9,25},{17,1},{25,9},{2,18},{10... | collective-permute-start | bytes 3145736 | tf_op jit(solution)/shard_map/ppermute | solution.py:44
  430.9 46.6 %copy-start.15 = (bf16[6,1024,128]{2,1,0:T(8,128)(2,1)S(1)}, bf16[6,1024,128]{2,1,0:T(8,128)(2,1)}, u32[]{:S(2)}) copy-start(bf16[6,1024,128]{2,1,0:T(8,128)(2,1)} %get-tuple-element.133.query_ref) | copy-start | bytes 4718596
  430.9 86.0 %collective-permute-start.14 = (bf16[256,2048]{1,0:T(8,128)(2,1)}, bf16[256,2048]{1,0:T(8,128)(2,1)}, u32[]{:S(2)}, u32[]{:S(2)}) collective-permute-start(bf16[256,2048]{1,0:T(8,128)(2,1)} %get-tuple-element.183), channel_id=1, source_target_pairs={{0,1},{1,0},{2,3},{3,2},{4,5},{5,4},{6,7},{7,6},{8,9},{9,8},{10,11... | collective-permute-start | bytes 3145736 | tf_op jit(solution)/shard_map/ppermute | solution.py:44
  435.9 81.0 %collective-permute-start.12 = (bf16[4,128,1280]{2,1,0:T(8,128)(2,1)}, bf16[4,128,1280]{2,1,0:T(8,128)(2,1)}, u32[]{:S(2)}, u32[]{:S(2)}) collective-permute-start(bf16[4,128,1280]{2,1,0:T(8,128)(2,1)} %fusion.4), channel_id=1, source_target_pairs={{0,2},{1,3},{2,4},{3,5},{4,6},{5,7},{6,0},{7,1},{8,10},{9,11},{10,... | collective-permute-start | bytes 3932168 | tf_op jit(solution)/shard_map/ppermute | solution.py:49
  477.5 39.5 %collective-permute-start.11 = (bf16[160,2048]{1,0:T(8,128)(2,1)}, bf16[160,2048]{1,0:T(8,128)(2,1)S(1)}, u32[]{:S(2)}, u32[]{:S(2)}) collective-permute-start(bf16[160,2048]{1,0:T(8,128)(2,1)} %fusion.12), channel_id=1, source_target_pairs={{0,2},{1,3},{2,4},{3,5},{4,6},{5,7},{6,0},{7,1},{8,10},{9,11},{10,... | collective-permute-start | bytes 1966088 | tf_op jit(solution)/shard_map/ppermute | solution.py:49
  492.2 30.5 %copy-start.16 = (bf16[4,1024,128]{2,1,0:T(8,128)(2,1)}, bf16[4,1024,128]{2,1,0:T(8,128)(2,1)S(1)}, u32[]{:S(2)}) copy-start(bf16[4,1024,128]{2,1,0:T(8,128)(2,1)S(1)} %get-tuple-element.162.low_two_ref) | copy-start | bytes 3145732
  492.2 30.4 %copy-start.17 = (f32[1024,128]{1,0:T(8,128)}, f32[1024,128]{1,0:T(8,128)S(1)}, u32[]{:S(2)}) copy-start(f32[1024,128]{1,0:T(8,128)S(1)} %get-tuple-element.160.dq_two_ref) | copy-start | bytes 1572868
  492.2 30.4 %copy-start.18 = (f32[1024,128]{1,0:T(8,128)}, f32[1024,128]{1,0:T(8,128)S(1)}, u32[]{:S(2)}) copy-start(f32[1024,128]{1,0:T(8,128)S(1)} %get-tuple-element.164.own_two_ref) | copy-start | bytes 1572868
  (22 other events, 76.6 us)
